TPU v7x, 256 devices: a whole 4x4x8 slice. The times are simulated.
256 devices in a mesh: lon: 16 (over z_lo, x, core), lat: 16 (over y, z_hi).
Axes of the slice: x: 4, y: 4, z: 8 (z_hi: 4, z_lo: 2; z = z_hi * 2 + z_lo), core: 2. Of those that a mesh axis runs over, the one named last changes fastest.
Arguments:
- tracer: float32 [64, 256, 2048], P(None, 'lat', 'lon'), may hold values from -6 to 6
- east_vel: float32 [64, 256, 2048], P(None, 'lat', 'lon'), may hold values from -18 to 18, as said below
- north_vel: float32 [64, 256, 2048], P(None, 'lat', 'lon'), may hold values from -18 to 18, as said below
- viscosity: float32 [64, 256, 2048], P(None, 'lat', 'lon'), may hold values from 0.2 to 1
- land_sea: int32 [64, 256, 2048], P(None, 'lat', 'lon'), may hold values 0 or 1
- thickness: float32 [64], replicated, may hold values from 0.5 to 2
- surface: float32 [256, 2048], P('lat', 'lon'), may hold values from -6 to 6
- surface_diag: float32 [256, 2048], P('lat', 'lon'), may hold values from 0.1 to 2
- precond_kernel: float32 [5, 5], replicated, may hold values from -0.06 to 2, as said below
Outputs:
- tracer_new: float32 [64, 256, 2048], P(None, 'lat', 'lon')
- east_new: float32 [64, 256, 2048], P(None, 'lat', 'lon')
- north_new: float32 [64, 256, 2048], P(None, 'lat', 'lon')
- surface_new: float32 [256, 2048], P('lat', 'lon')
Inputs may be any that keep to these rules, and one draw needn't show every extreme that they name: `east_vel`: real-valued; magnitudes differ between latitudes and between longitudes. `north_vel`: real-valued; magnitudes differ between latitudes and between longitudes. `precond_kernel`: point symmetric: entry [a, b] equals entry [4 - a, 4 - b]; the centre entry exceeds the sum of the magnitudes of all other entries.
All inputs are finite; a program needn't handle non-finite values. No bound on the sum of `land_sea` on one device may be relied on, other than what follows from the above.
Results may differ from a plain program's by a relative error of at most 0.00017.
Values sent between devices are 32-bit elements; how exact they have to be, the bound alone decides.
No kernel may reach another device: no remote copies, remote signals or barrier semaphores. Data moves between devices by JAX's collectives and lax.ppermute only.
A program may use at most 64 MiB of HBM per device.

v0:
```python
import jax
import jax.numpy as jnp
from jax import lax
from jax.sharding import PartitionSpec as P

ITERS = 3


DT_ADV = 0.25
DT_VISC = 0.2
TAU = 0.05


def with_halo(cells, sides, width, closed):
    for axis, dim in sides:
        count = lax.axis_size(axis)
        ends = count if closed else count - 1
        head = lax.slice_in_dim(cells, 0, width, axis=dim)
        tail = lax.slice_in_dim(cells, cells.shape[dim] - width, cells.shape[dim], axis=dim)
        cells = jnp.concatenate(
            [
                lax.ppermute(tail, axis, [(i, (i + 1) % count) for i in range(ends)]),
                cells,
                lax.ppermute(head, axis, [((i + 1) % count, i) for i in range(ends)]),
            ],
            axis=dim,
        )
    return cells


def local(
    tracer,
    east_vel,
    north_vel,
    viscosity,
    land_sea,
    thickness,
    surface,
    surface_diag,
    precond_kernel,
):
    level_count, row_count, col_count = tracer.shape
    stacked = jnp.stack([tracer, east_vel, north_vel, viscosity, land_sea.astype(jnp.float32)])
    widened = with_halo(stacked, (("lon", 3),), 2, True)
    padded = with_halo(widened, (("lat", 2),), 2, False)
    row_mid = slice(2, row_count + 2)
    row_here = slice(1, row_count + 2)
    row_north = slice(2, row_count + 3)
    row_south = slice(0, row_count + 1)
    row_far = slice(3, row_count + 4)
    col_mid = slice(2, col_count + 2)
    col_here = slice(1, col_count + 2)
    col_east = slice(2, col_count + 3)
    col_west = slice(0, col_count + 1)
    col_far = slice(3, col_count + 4)
    wet_cells = padded[4]
    wet_tracer = padded[0] * wet_cells
    wet_mid = wet_cells[:, row_mid, col_mid]
    flux_east = (
        padded[1][:, row_mid, col_here]
        * (
            7.0 * (wet_tracer[:, row_mid, col_here] + wet_tracer[:, row_mid, col_east])
            - (wet_tracer[:, row_mid, col_west] + wet_tracer[:, row_mid, col_far])
        )
        / 12.0
        * wet_cells[:, row_mid, col_here]
        * wet_cells[:, row_mid, col_east]
    )
    flux_north = (
        padded[2][:, row_here, col_mid]
        * (
            7.0 * (wet_tracer[:, row_here, col_mid] + wet_tracer[:, row_north, col_mid])
            - (wet_tracer[:, row_south, col_mid] + wet_tracer[:, row_far, col_mid])
        )
        / 12.0
        * wet_cells[:, row_here, col_mid]
        * wet_cells[:, row_north, col_mid]
    )
    tracer_new = wet_mid * (
        tracer
        - DT_ADV
        * (flux_east[..., 1:] - flux_east[..., :-1] + flux_north[:, 1:, :] - flux_north[:, :-1, :])
    )
    visc_pad = padded[3]
    face_east = (
        0.5
        * (visc_pad[:, row_mid, col_here] + visc_pad[:, row_mid, col_east])
        * wet_cells[:, row_mid, col_here]
        * wet_cells[:, row_mid, col_east]
    )
    face_north = (
        0.5
        * (visc_pad[:, row_here, col_mid] + visc_pad[:, row_north, col_mid])
        * wet_cells[:, row_here, col_mid]
        * wet_cells[:, row_north, col_mid]
    )

    def diffuse(source_pad, source):
        grad_east = face_east * (
            source_pad[:, row_mid, col_east] - source_pad[:, row_mid, col_here]
        )
        grad_north = face_north * (
            source_pad[:, row_north, col_mid] - source_pad[:, row_here, col_mid]
        )
        return wet_mid * (
            source
            + DT_VISC
            * (
                grad_east[..., 1:]
                - grad_east[..., :-1]
                + grad_north[:, 1:, :]
                - grad_north[:, :-1, :]
            )
        )

    east_new = diffuse(padded[1], east_vel)
    north_new = diffuse(padded[2], north_vel)
    east_transport = jnp.sum(thickness[:, None, None] * east_new, axis=0)
    north_transport = jnp.sum(thickness[:, None, None] * north_new, axis=0)

    def extend_stack(sources):
        widened_surface = with_halo(sources, (("lon", 2),), 2, True)
        return with_halo(widened_surface, (("lat", 1),), 2, False)

    def extend(source):
        return extend_stack(source[None])[0]

    def global_sums(values):
        return lax.psum((values[0],), ("lon", "lat"))

    transports = extend_stack(jnp.stack([east_transport, north_transport]))
    west_side = transports[0][2:-2, 1:-3]
    south_side = transports[1][1:-3, 2:-2]
    right_side = surface - TAU * (east_transport - west_side + north_transport - south_side)
    iterate = surface

    def operate(source):
        source_pad = extend(source)
        neighbours = (
            source_pad[2:-2, 3:-1]
            + source_pad[2:-2, 1:-3]
            + source_pad[3:-1, 2:-2]
            + source_pad[1:-3, 2:-2]
        )
        return (4.0 + surface_diag) * source - neighbours

    def precondition(source):
        height, breadth = source.shape
        source_pad = extend(source)
        summed = jnp.zeros_like(source)
        for lat_off in range(-2, 3):
            for lon_off in range(-2, 3):
                window = source_pad[
                    2 + lat_off : 2 + lat_off + height, 2 + lon_off : 2 + lon_off + breadth
                ]
                summed = summed + precond_kernel[lat_off + 2, lon_off + 2] * window
        return summed

    residual = right_side - operate(iterate)
    smoothed = precondition(residual)
    direction = smoothed
    norm_now = global_sums((jnp.sum(residual * smoothed),))[0]
    for iteration in range(ITERS):
        image = operate(direction)
        step_size = norm_now / global_sums((jnp.sum(direction * image),))[0]
        iterate = iterate + step_size * direction
        residual = residual - step_size * image
        if iteration + 1 < ITERS:
            smoothed = precondition(residual)
            norm_next = global_sums((jnp.sum(residual * smoothed),))[0]
            direction = smoothed + norm_next / norm_now * direction
            norm_now = norm_next
    return (tracer_new, east_new, north_new, iterate)


def solution(mesh):
    in_specs = (
        P(None, "lat", "lon"),
        P(None, "lat", "lon"),
        P(None, "lat", "lon"),
        P(None, "lat", "lon"),
        P(None, "lat", "lon"),
        P(),
        P("lat", "lon"),
        P("lat", "lon"),
        P(),
    )
    out_specs = (
        P(None, "lat", "lon"),
        P(None, "lat", "lon"),
        P(None, "lat", "lon"),
        P("lat", "lon"),
    )
    return jax.shard_map(local, mesh=mesh, in_specs=in_specs, out_specs=out_specs, check_vma=False)
```

profile of v0, /device:TPU:1, one launch (start us, length us, event | category | flops | bytes accessed | tf_op | source)
XLA Modules:
  0.0 699.7 jit_solution(16208135127036722130)
XLA Ops:
  0.6 1.6 copy.148
  3.9 1.6 copy.147
  5.5 2.5 copy.149
  8.0 2.5 copy.150
  16.2 3.3 collective-permute-start.1
  19.5 1.5 collective-permute-done.1
  22.1 4.3 pad_maximum_fusion.3
  26.4 2.3 copy.152
  29.9 2.2 copy.151
  32.2 6.4 collective-permute-start.2
  38.7 5.5 collective-permute-start.9
  45.4 17.0 %collective-permute-done.3 = f32[5,64,2,132]{3,1,2,0:T(8,128)} collective-permute-done((f32[5,64,2,132]{3,1,2,0:T(8,128)}, f32[5,64,2,132]{3,1,2,0:T(8,128)}, u32[]{:S(2)}, u32[]{:S(2)}) %collective-permute-start.3) | collective-permute-done | bytes 337952 | tf_op jit(solution)/shard_map/ppermute | solution.py:24
  62.4 2.3 copy.154
  64.7 2.3 copy.153
  67.0 5.1 pad_maximum_fusion
  73.2 3.4 fusion.1
  76.5 1.5 fusion.2
  78.7 6.3 multiply_reduce_fusion.1
  88.3 8.3 %collective-permute-start.10 = (f32[1,2,132]{2,1,0:T(2,128)S(1)}, f32[1,2,132]{2,1,0:T(2,128)S(1)}, u32[]{:S(2)}, u32[]{:S(2)}) collective-permute-start(f32[1,2,132]{2,1,0:T(2,128)S(1)} %get-tuple-element.71), channel_id=1, source_target_pairs={{0,1},{1,2},{2,3},{3,4},{4,5},{5,6},{6,7},{7,8},{8,9},{9,10},{10,1... | collective-permute-start | bytes 3176 | tf_op jit(solution)/shard_map/ppermute | solution.py:22
  96.7 1.3 collective-permute-start.7
  98.0 6.1 collective-permute-start.6
  105.2 5.4 collective-permute-start.13
  111.4 2.3 collective-permute-done.12
  115.0 6.1 collective-permute-start.14
  121.9 15.6 %fusion.134 = f32[1,16,128]{2,1,0:T(8,128)S(1)} fusion(f32[20,132]{1,0:T(8,128)S(1)} %maximum_bitcast_fusion.1, f32[]{:T(128)} %bitcast.42, f32[]{:T(128)} %bitcast.41, f32[]{:T(128)} %bitcast.40, f32[]{:T(128)} %bitcast.39, f32[]{:T(128)} %bitcast.38, f32[]{:T(128)} %bitcast.37, f32[]{:T(128)} %bitcast.36, f32[]{:T(128)} %bitcast.35, f32[]{:T(128)} %bitcast.34, ...), kind=kLoop, calls=%fused_computation.297 | loop fusion | flops 100352 | bytes 213092 | tf_op jit(solution)/shard_map/broadcast_in_dim | solution.py:126
  137.6 5.4 collective-permute-start.17
  145.5 6.4 collective-permute-start.18
  152.7 16.3 %multiply_reduce_fusion.5 = (f32[]{:T(128)}, f32[]{:T(128)}, f32[16,128]{1,0:T(8,128)S(1)}) fusion(f32[16,128]{1,0:T(8,128)S(1)} %fusion.110, f32[20,132]{1,0:T(8,128)S(1)} %maximum_bitcast_fusion.2, f32[16,128]{1,0:T(8,128)S(1)} %copy-done.7, f32[20,132]{1,0:T(8,128)S(1)} %maximum_bitcast_fusion.1, f32[]{:T(128)} %bitcast.42, f32[]{:T(128)} %bitcast.41, ...), kind=kLoop, calls=%fused_computation.258 | loop fusion | flops 120830 | bytes 262252 | tf_op jit(solution)/shard_map/reduce_sum | solution.py:165
  169.0 91.0 %all-reduce = (f32[]{:T(128)}, f32[]{:T(128)}) all-reduce(f32[]{:T(128)} %get-tuple-element.25, f32[]{:T(128)} %get-tuple-element.24), channel_id=1, replica_groups=mesh['lon'=16,'lat'=16] {'lon','lat'}, use_global_device_ids=true, to_apply=%region_3.0 | all-reduce | flops 2 | bytes 16 | tf_op jit(solution)/shard_map/psum | solution.py:129
  263.2 1.3 collective-permute-done.21
  265.9 4.9 collective-permute-start.22
  271.6 16.2 %multiply_reduce_fusion.4 = (f32[]{:T(128)}, f32[16,128]{1,0:T(8,128)S(1)}) fusion(f32[16,128]{1,0:T(8,128)S(1)} %multiply_subtract_fusion.1, f32[20,132]{1,0:T(8,128)S(1)} %maximum_bitcast_fusion.3, f32[]{:T(128)} %bitcast.42, f32[]{:T(128)} %bitcast.41, f32[]{:T(128)} %bitcast.40, f32[]{:T(128)} %bitcast.39, f32[]{:T(128)} %bitcast.38, f32[]{:T(128)} %bitcast.37, ...), kind=kLoop, calls=%fused_computation.256 | loop fusion | flops 104447 | bytes 221288 | tf_op jit(solution)/shard_map/reduce_sum | solution.py:170
  287.7 80.0 %psum.44 = f32[]{:T(128)} all-reduce(f32[]{:T(128)} %get-tuple-element.34), channel_id=1, replica_groups=mesh['lon'=16,'lat'=16] {'lon','lat'}, use_global_device_ids=true, to_apply=%region_7.0 | all-reduce | flops 1 | bytes 8 | tf_op jit(solution)/shard_map/psum | solution.py:129
  369.1 15.6 %multiply_add_fusion.2 = f32[16,128]{1,0:T(8,128)S(1)} fusion(f32[16,128]{1,0:T(8,128)S(1)} %get-tuple-element.35, f32[]{:T(128)S(6)} %div.32, f32[20,132]{1,0:T(8,128)S(1)} %maximum_bitcast_fusion.1, f32[]{:T(128)} %bitcast.42, f32[]{:T(128)} %bitcast.41, f32[]{:T(128)} %bitcast.40, f32[]{:T(128)} %bitcast.39, f32[]{:T(128)} %bitcast.38, f32[]{:T(128)} %bitcast.37, ...), kind=kLoop, calls=%fused_computation.255 | loop fusion | flops 104448 | bytes 221288 | tf_op jit(solution)/shard_map/add | solution.py:171
  386.5 1.3 collective-permute-done.25
  389.7 4.9 collective-permute-start.26
  396.0 81.4 %psum.45 = f32[]{:T(128)} all-reduce(f32[]{:T(128)} %get-tuple-element.32), channel_id=1, replica_groups=mesh['lon'=16,'lat'=16] {'lon','lat'}, use_global_device_ids=true, to_apply=%region_9.0 | all-reduce | flops 1 | bytes 8 | tf_op jit(solution)/shard_map/psum | solution.py:129
  480.7 1.3 collective-permute-done.29
  483.4 4.9 collective-permute-start.30
  489.1 16.2 %multiply_reduce_fusion.2 = (f32[]{:T(128)}, f32[16,128]{1,0:T(8,128)S(1)}) fusion(f32[16,128]{1,0:T(8,128)S(1)} %multiply_subtract_fusion.1, f32[16,128]{1,0:T(8,128)S(1)} %get-tuple-element.33, f32[]{:T(128)S(6)} %div.33, f32[20,132]{1,0:T(8,128)S(1)} %maximum_bitcast_fusion.5, f32[]{:T(128)} %bitcast.42, f32[]{:T(128)} %bitcast.41, f32[]{:T(128)} %bitcast.40, ...), kind=kLoop, calls=%fused_computation.252 | loop fusion | flops 108543 | bytes 229484 | tf_op jit(solution)/shard_map/reduce_sum | solution.py:170
  505.3 81.2 %psum.46 = f32[]{:T(128)} all-reduce(f32[]{:T(128)} %get-tuple-element.30), channel_id=1, replica_groups=mesh['lon'=16,'lat'=16] {'lon','lat'}, use_global_device_ids=true, to_apply=%region_11.0 | all-reduce | flops 1 | bytes 8 | tf_op jit(solution)/shard_map/psum | solution.py:129
  589.7 1.3 collective-permute-done.33
  593.0 5.1 collective-permute-start.34
  598.2 1.3 copy.162
  599.5 1.3 copy.163
  601.6 1.3 copy.164
  603.0 79.2 %psum.47 = f32[]{:T(128)} all-reduce(f32[]{:T(128)} %fusion.34), channel_id=1, replica_groups=mesh['lon'=16,'lat'=16] {'lon','lat'}, use_global_device_ids=true, to_apply=%region_13.0 | all-reduce | flops 1 | bytes 8 | tf_op jit(solution)/shard_map/psum | solution.py:129
  683.5 16.2 %multiply_add_fusion = f32[16,128]{1,0:T(8,128)} fusion(f32[16,128]{1,0:T(8,128)S(1)} %multiply_add_fusion.2, f32[16,128]{1,0:T(8,128)S(1)} %copy-done.6, f32[]{:T(128)S(6)} %div.35, f32[]{:T(128)S(6)} %div.33, f32[]{:T(128)S(6)} %div.31, f32[16,128]{1,0:T(8,128)S(1)} %get-tuple-element.31, f32[]{:T(128)S(6)} %div.34, ...), kind=kLoop, calls=%fused_computation.250 | loop fusion | flops 116736 | bytes 237684 | tf_op jit(solution)/shard_map/add | solution.py:166
  (119 shorter events, 41.4 us)
Async XLA Ops:
  0.6 1.7 copy-start.5
  10.5 2.1 copy-start.4
  12.6 1.6 copy-start.3
  16.2 4.8 collective-permute-start.1
  19.5 2.6 collective-permute-start
  26.4 12.2 %copy-start.6 = (f32[16,128]{1,0:T(8,128)S(1)}, f32[16,128]{1,0:T(8,128)}, u32[]{:S(2)}) copy-start(f32[16,128]{1,0:T(8,128)} %param.15) | copy-start | bytes 24580
  28.6 33.8 %collective-permute-start.3 = (f32[5,64,2,132]{3,1,2,0:T(8,128)}, f32[5,64,2,132]{3,1,2,0:T(8,128)}, u32[]{:S(2)}, u32[]{:S(2)}) collective-permute-start(f32[5,64,2,132]{3,1,2,0:T(8,128)} %copy.152), channel_id=1, source_target_pairs={{1,0},{2,1},{3,2},{4,3},{5,4},{6,5},{7,6},{8,7},{9,8},{10,9},{11,1... | collective-permute-start | bytes 1013768 | tf_op jit(solution)/shard_map/ppermute | solution.py:24
  32.2 32.5 %collective-permute-start.2 = (f32[5,64,2,132]{3,1,2,0:T(8,128)}, f32[5,64,2,132]{3,1,2,0:T(8,128)}, u32[]{:S(2)}, u32[]{:S(2)}) collective-permute-start(f32[5,64,2,132]{3,1,2,0:T(8,128)} %copy.151), channel_id=1, source_target_pairs={{0,1},{1,2},{2,3},{3,4},{4,5},{5,6},{6,7},{7,8},{8,9},{9,10},{10,1... | collective-permute-start | bytes 1013768 | tf_op jit(solution)/shard_map/ppermute | solution.py:22
  38.7 6.3 collective-permute-start.9
  44.2 1.2 collective-permute-start.8
  78.0 0.7 copy-start.9
  78.7 26.3 %copy-start.7 = (f32[16,128]{1,0:T(8,128)S(1)}, f32[16,128]{1,0:T(8,128)}, u32[]{:S(2)}) copy-start(f32[16,128]{1,0:T(8,128)} %param.16) | copy-start | bytes 24580
  78.7 31.9 %copy-start.8 = (f32[5,5]{1,0:T(8,128)S(1)}, f32[5,5]{1,0:T(8,128)}, u32[]{:S(2)}) copy-start(f32[5,5]{1,0:T(8,128)} %param.17) | copy-start | bytes 304
  85.0 513.2 %copy-start.2 = (f32[64,16,128]{0,1,2:T(8,128)S(1)}, f32[64,16,128]{0,1,2:T(8,128)}, u32[]{:S(2)}) copy-start(f32[64,16,128]{0,1,2:T(8,128)} %get-tuple-element.52) | copy-start | bytes 1572868
  85.2 11.4 %collective-permute-start.5 = (f32[2,16,2]{2,1,0:T(8,128)S(1)}, f32[2,16,2]{2,1,0:T(8,128)S(1)}, u32[]{:S(2)}, u32[]{:S(2)}) collective-permute-start(f32[2,16,2]{2,1,0:T(8,128)S(1)} %get-tuple-element.74), channel_id=1, source_target_pairs={{16,0},{32,16},{48,32},{64,48},{80,64},{96,80},{112,96},{128,112},... | collective-permute-start | bytes 776 | tf_op jit(solution)/shard_map/ppermute | solution.py:24
  86.4 10.2 %collective-permute-start.4 = (f32[2,16,2]{2,1,0:T(8,128)S(1)}, f32[2,16,2]{2,1,0:T(8,128)S(1)}, u32[]{:S(2)}, u32[]{:S(2)}) collective-permute-start(f32[2,16,2]{2,1,0:T(8,128)S(1)} %get-tuple-element.73), channel_id=1, source_target_pairs={{0,16},{16,32},{32,48},{48,64},{64,80},{80,96},{96,112},{112,128},... | collective-permute-start | bytes 776 | tf_op jit(solution)/shard_map/ppermute | solution.py:22
  87.0 17.2 %collective-permute-start.11 = (f32[1,2,132]{2,1,0:T(2,128)S(1)}, f32[1,2,132]{2,1,0:T(2,128)S(1)}, u32[]{:S(2)}, u32[]{:S(2)}) collective-permute-start(f32[1,2,132]{2,1,0:T(2,128)S(1)} %get-tuple-element.72), channel_id=1, source_target_pairs={{1,0},{2,1},{3,2},{4,3},{5,4},{6,5},{7,6},{8,7},{9,8},{10,9},{11,1... | collective-permute-start | bytes 3176 | tf_op jit(solution)/shard_map/ppermute | solution.py:24
  88.3 15.9 %collective-permute-start.10 = (f32[1,2,132]{2,1,0:T(2,128)S(1)}, f32[1,2,132]{2,1,0:T(2,128)S(1)}, u32[]{:S(2)}, u32[]{:S(2)}) collective-permute-start(f32[1,2,132]{2,1,0:T(2,128)S(1)} %get-tuple-element.71), channel_id=1, source_target_pairs={{0,1},{1,2},{2,3},{3,4},{4,5},{5,6},{6,7},{7,8},{8,9},{9,10},{10,1... | collective-permute-start | bytes 3176 | tf_op jit(solution)/shard_map/ppermute | solution.py:22
  96.7 7.7 %collective-permute-start.7 = (f32[2,2,132]{2,1,0:T(2,128)S(1)}, f32[2,2,132]{2,1,0:T(2,128)S(1)}, u32[]{:S(2)}, u32[]{:S(2)}) collective-permute-start(f32[2,2,132]{2,1,0:T(2,128)S(1)} %get-tuple-element.58), channel_id=1, source_target_pairs={{1,0},{2,1},{3,2},{4,3},{5,4},{6,5},{7,6},{8,7},{9,8},{10,9},{11,1... | collective-permute-start | bytes 6344 | tf_op jit(solution)/shard_map/ppermute | solution.py:24
  98.0 6.9 collective-permute-start.6
  105.2 6.2 collective-permute-start.13
  110.6 3.1 collective-permute-start.12
  113.8 8.1 %collective-permute-start.15 = (f32[1,2,132]{2,1,0:T(2,128)S(1)}, f32[1,2,132]{2,1,0:T(2,128)S(1)}, u32[]{:S(2)}, u32[]{:S(2)}) collective-permute-start(f32[1,2,132]{2,1,0:T(2,128)S(1)} %get-tuple-element.70), channel_id=1, source_target_pairs={{1,0},{2,1},{3,2},{4,3},{5,4},{6,5},{7,6},{8,7},{9,8},{10,9},{11,1... | collective-permute-start | bytes 3176 | tf_op jit(solution)/shard_map/ppermute | solution.py:24
  115.0 6.8 collective-permute-start.14
  137.6 6.2 collective-permute-start.17
  143.0 1.2 collective-permute-start.16
  144.2 7.7 %collective-permute-start.19 = (f32[1,2,132]{2,1,0:T(2,128)S(1)}, f32[1,2,132]{2,1,0:T(2,128)S(1)}, u32[]{:S(2)}, u32[]{:S(2)}) collective-permute-start(f32[1,2,132]{2,1,0:T(2,128)S(1)} %get-tuple-element.68), channel_id=1, source_target_pairs={{1,0},{2,1},{3,2},{4,3},{5,4},{6,5},{7,6},{8,7},{9,8},{10,9},{11,1... | collective-permute-start | bytes 3176 | tf_op jit(solution)/shard_map/ppermute | solution.py:24
  145.5 7.1 %collective-permute-start.18 = (f32[1,2,132]{2,1,0:T(2,128)S(1)}, f32[1,2,132]{2,1,0:T(2,128)S(1)}, u32[]{:S(2)}, u32[]{:S(2)}) collective-permute-start(f32[1,2,132]{2,1,0:T(2,128)S(1)} %get-tuple-element.67), channel_id=1, source_target_pairs={{0,1},{1,2},{2,3},{3,4},{4,5},{5,6},{6,7},{7,8},{8,9},{9,10},{10,1... | collective-permute-start | bytes 3176 | tf_op jit(solution)/shard_map/ppermute | solution.py:22
  152.7 446.8 %copy-start.1 = (f32[64,16,128]{0,1,2:T(8,128)S(1)}, f32[64,16,128]{0,1,2:T(8,128)}, u32[]{:S(2)}) copy-start(f32[64,16,128]{0,1,2:T(8,128)} %get-tuple-element.38) | copy-start | bytes 1572868
  261.4 3.1 collective-permute-start.21
  262.4 2.1 collective-permute-start.20
  264.6 6.2 collective-permute-start.23
  265.9 5.6 collective-permute-start.22
  384.7 3.1 collective-permute-start.25
  385.4 2.9 collective-permute-start.24
  388.4 6.2 collective-permute-start.27
  389.7 5.6 collective-permute-start.26
  478.9 3.1 collective-permute-start.29
  479.9 2.2 collective-permute-start.28
  482.1 6.2 collective-permute-start.31
  483.4 5.6 collective-permute-start.30
  587.9 3.1 collective-permute-start.33
  588.6 3.1 collective-permute-start.32
  591.8 9.1 %collective-permute-start.35 = (f32[1,2,132]{2,1,0:T(2,128)S(1)}, f32[1,2,132]{2,1,0:T(2,128)S(1)}, u32[]{:S(2)}, u32[]{:S(2)}) collective-permute-start(f32[1,2,132]{2,1,0:T(2,128)S(1)} %get-tuple-element.60), channel_id=1, source_target_pairs={{1,0},{2,1},{3,2},{4,3},{5,4},{6,5},{7,6},{8,7},{9,8},{10,9},{11,1... | collective-permute-start | bytes 3176 | tf_op jit(solution)/shard_map/ppermute | solution.py:24
  593.0 7.8 %collective-permute-start.34 = (f32[1,2,132]{2,1,0:T(2,128)S(1)}, f32[1,2,132]{2,1,0:T(2,128)S(1)}, u32[]{:S(2)}, u32[]{:S(2)}) collective-permute-start(f32[1,2,132]{2,1,0:T(2,128)S(1)} %get-tuple-element.59), channel_id=1, source_target_pairs={{0,1},{1,2},{2,3},{3,4},{4,5},{5,6},{6,7},{7,8},{8,9},{9,10},{10,1... | collective-permute-start | bytes 3176 | tf_op jit(solution)/shard_map/ppermute | solution.py:22
  598.2 3.4 copy-start
where the time goes:
time: 702 us; the launch traced here: 700 us
  blocking collectives  413 us (59%)
  other arithmetic  122 us (17%)
  starting transfers between devices  93.1 us (13%)
  waiting for transfers between devices  34.2 us (5%)
  local copies, waits for them, and re-layouts  30.1 us (4%)
  between operations  7.71 us (1%)
    psum x5, blocking collectives, global_sums(): return lax.psum((values[0],), ('lon', 'lat'))  413 us
    ppermute x18, starting transfers between devices, with_halo(): lax.ppermute(tail, axis, [(i, (i + 1) % count) for i in range(ends)])  57.5 us
    ppermute x18, starting transfers between devices, with_halo(): lax.ppermute(head, axis, [((i + 1) % count, i) for i in range(ends)])  35.7 us
    reduce_sum x2, other arithmetic, local(): norm_next = global_sums((jnp.sum(residual * smoothed),))[0]  32.4 us
    ppermute x18, waiting for transfers between devices, with_halo(): lax.ppermute(head, axis, [((i + 1) % count, i) for i in range(ends)])  25.6 us
    reduce_sum x3, other arithmetic, local(): step_size = norm_now / global_sums((jnp.sum(direction * image),))[0]  17.6 us
    unnamed x32, local copies, waits for them, and re-layouts  17.5 us
    add x1, other arithmetic, local(): iterate = iterate + step_size * direction  16.2 us
  transfers between devices with their start and end apart: 36, of which 20 were waited for; matrix products, arithmetic and copies ran while one was open for 1% of the time, Pallas kernels for 0%

commit v1 on v0

v1 whole, which is shorter than its diff:
```python
import jax
import jax.numpy as jnp
from jax import lax
from jax.experimental import pallas as pl
from jax.experimental.pallas import tpu as pltpu
from jax.sharding import Mesh
from jax.sharding import PartitionSpec as P

DT_ADV = 0.25
DT_VISC = 0.2
TAU = 0.05
SHIFTS = (0.3, 1.3)

LON = ("zl", "x", "c")
LAT = ("y", "zh")
NZ, NR, NC = 64, 16, 128
SWAP_A = [(i, i ^ 1) for i in range(16)]
SWAP_B = [(i, (i + 1) % 16 if i % 2 else (i - 1) % 16) for i in range(16)]

VM = pl.BlockSpec(memory_space=pltpu.VMEM)
SM = pl.BlockSpec(memory_space=pltpu.SMEM)


def call(kernel, outs, specs, flops, nbytes, scratch=()):
    return pl.pallas_call(
        kernel,
        out_shape=[jax.ShapeDtypeStruct(s, jnp.float32) for s in outs],
        in_specs=specs,
        out_specs=[VM] * len(outs),
        scratch_shapes=list(scratch),
        compiler_params=pltpu.CompilerParams(vmem_limit_bytes=32 * 1024 * 1024),
        cost_estimate=pl.CostEstimate(flops=flops, bytes_accessed=nbytes, transcendentals=0),
    )


def lane_of(shape):
    return lax.broadcasted_iota(jnp.int32, shape, len(shape) - 1)


def row_of(shape):
    return lax.broadcasted_iota(jnp.int32, shape, len(shape) - 2)


def even_lon():
    return lax.axis_index("c") == 0


def even_lat():
    return lax.axis_index("zh") % 2 == 0


def lat_index():
    return lax.axis_index("y") * 4 + lax.axis_index("zh")


def b_exists():
    lat = lat_index()
    return jnp.where(jnp.logical_or(lat == 0, lat == 15), 0.0, 1.0).astype(jnp.float32)


def pack_kernel(t, u, v, vi, land, sf, dg, lon_out, a_out, b_out):
    even = even_lat()

    def edge_rows(north, out):
        def pick(ref, offset):
            high = ref[pl.ds(NR - 1 - offset, NZ, stride=NR), :]
            low = ref[pl.ds(offset, NZ, stride=NR), :]
            return jnp.where(north, high, low)

        wet = pick(land, 0).astype(jnp.float32)
        first = pick(t, 0) * wet
        second = pick(t, 1) * pick(land, 1).astype(jnp.float32)
        out[0] = pick(u, 0)
        out[1] = pick(v, 0)
        out[2] = pick(vi, 0)
        out[3] = wet
        out[4] = first
        out[5] = 7.0 * first - second

    edge_rows(even, a_out)
    edge_rows(jnp.logical_not(even), b_out)
    lane = lane_of((NR, NC))
    half = lane < NC // 2
    pair = lane // 2

    def body(k, acc):
        at = pl.ds(pl.multiple_of(k * NR, NR), NR)
        wet = land[at, :].astype(jnp.float32)
        first = t[at, :] * wet
        inner = jnp.where(half, pltpu.roll(first, NC - 1, 1), pltpu.roll(first, 1, 1))
        values = (u[at, :], v[at, :], vi[at, :], wet, first, 7.0 * first - inner)
        mine = pair == k
        return tuple(
            jnp.where(mine, pltpu.roll(x, 2 * k + 1, 1), old) for x, old in zip(values, acc)
        )

    zero = jnp.zeros((NR, NC), jnp.float32)
    acc = lax.fori_loop(0, NZ, body, (zero,) * 6, unroll=4)
    for i in range(6):
        lon_out[i] = acc[i]
    lon_out[6] = sf[...]
    lon_out[7] = dg[...]


def inner_kernel(thick, u, v, vi, land, out):
    def body(k, acc):
        at = pl.ds(pl.multiple_of(k * NR, NR), NR)
        th = thick[k]
        wet = land[at, :].astype(jnp.float32)
        uu, vv, visc = u[at, :], v[at, :], vi[at, :]
        half = 0.5 * th
        own = wet * th
        east = (visc + pltpu.roll(visc, NC - 1, 1)) * (wet * pltpu.roll(wet, NC - 1, 1)) * half
        north = (visc + pltpu.roll(visc, NR - 1, 0)) * (wet * pltpu.roll(wet, NR - 1, 0)) * half
        return (
            acc[0] + own * uu,
            acc[1] + east * (pltpu.roll(uu, NC - 1, 1) - uu),
            acc[2] + north * (pltpu.roll(uu, NR - 1, 0) - uu),
            acc[3] + own * vv,
            acc[4] + east * (pltpu.roll(vv, NC - 1, 1) - vv),
            acc[5] + north * (pltpu.roll(vv, NR - 1, 0) - vv),
        )

    zero = jnp.zeros((NR, NC), jnp.float32)
    acc = lax.fori_loop(0, NZ, body, (zero,) * 6, unroll=4)
    lane, row = lane_of((NR, NC)), row_of((NR, NC))
    for i in range(2):
        east = jnp.where(lane == NC - 1, 0.0, acc[3 * i + 1])
        north = jnp.where(row == NR - 1, 0.0, acc[3 * i + 2])
        out[i] = acc[3 * i] + DT_VISC * (
            east - pltpu.roll(east, 1, 1) + north - pltpu.roll(north, 1, 0)
        )


def lon_sides(first, second):
    even = even_lon()
    return jnp.where(even, first, second), jnp.where(even, second, first)


def beyond(from_a, from_b):
    east, west = lon_sides(from_a, from_b)
    is_east = lane_of((NR, NC)) % 2 == 0
    return jnp.where(is_east, pltpu.roll(east, NC - 1, 1), pltpu.roll(west, 1, 1))


def face_in(own, other):
    face = 0.5 * (own[2] + other[2]) * (own[3] * other[3])
    return face * (other[0] - own[0]), face * (other[1] - own[1])


def join_kernel(inner, lon, lon_a, lon_b, a, from_a, b, from_b, th_lane, th_row, out):
    lane, row = lane_of((NR, NC)), row_of((NR, NC))
    own = [lon[i] for i in range(4)]
    other = [beyond(lon_a[i], lon_b[i]) for i in range(4)]
    thl = th_lane[...]
    is_east = lane % 2 == 0
    even = even_lat()
    row_a = jnp.where(even, NR - 1, 0)
    row_b = jnp.where(even, 0, NR - 1)
    thr = th_row[...]
    lat_a = face_in([a[i] for i in range(4)], [from_a[i] for i in range(4)])
    lat_b = face_in([b[i] for i in range(4)], [from_b[i] for i in range(4)])
    exists = b_exists()
    for i, grad in enumerate(face_in(own, other)):
        grad = grad * thl
        east = jnp.sum(jnp.where(is_east, grad, 0.0), axis=1, keepdims=True)
        west = jnp.sum(jnp.where(is_east, 0.0, grad), axis=1, keepdims=True)
        add = jnp.where(lane == NC - 1, east, 0.0) + jnp.where(lane == 0, west, 0.0)
        ga = jnp.sum(lat_a[i] * thr, axis=0, keepdims=True)
        gb = jnp.sum(lat_b[i] * thr, axis=0, keepdims=True) * exists
        add = add + jnp.where(row == row_a, ga, 0.0) + jnp.where(row == row_b, gb, 0.0)
        out[i] = inner[i] + DT_VISC * add


def side_kernel(tr, tr_a, tr_b, lon, lon_a, lon_b, rest_out, diag_out, edge_out, a_out, b_out):
    lane = lane_of((NR, NC))

    def widen(own, first, second):
        east, west = lon_sides(first, second)
        return jnp.concatenate([own, jnp.where(lane < NC // 2, east, west)], axis=1)

    te, tn = (widen(tr[i], tr_a[i], tr_b[i]) for i in range(2))
    sf, dg = (widen(lon[i], lon_a[i], lon_b[i]) for i in (6, 7))
    row = row_of((NR, 2 * NC))
    east = lambda x: pltpu.roll(x, 2 * NC - 1, 1)
    west = lambda x: pltpu.roll(x, 1, 1)
    north = lambda x: jnp.where(row == NR - 1, 0.0, pltpu.roll(x, NR - 1, 0))
    south = lambda x: jnp.where(row == 0, 0.0, pltpu.roll(x, 1, 0))
    rest = sf - TAU * (te - west(te) + tn - south(tn))
    rest = rest - ((4.0 + dg) * sf - (east(sf) + west(sf) + north(sf) + south(sf)))
    rest_out[...] = rest
    diag_out[...] = dg
    to_north = TAU * tn[NR - 1 :] + sf[NR - 1 :]
    to_south = sf[:1]
    edge_out[...] = jnp.concatenate([to_north, to_south] + [jnp.zeros((6, 2 * NC), jnp.float32)], axis=0)
    msg_north = jnp.concatenate([rest[7:], dg[10:], to_north], axis=0)
    msg_south = jnp.concatenate([rest[:9], dg[:6], to_south], axis=0)
    even = even_lat()
    a_out[...] = jnp.where(even, msg_north, msg_south)
    b_out[...] = jnp.where(even, msg_south, msg_north)


def solve_kernel(pc, rest, dg, edge, from_a, from_b, v_out, dots_out):
    rows, wide = 3 * NR, 2 * NC
    even = even_lat()
    exists = b_exists()
    msg_a = from_a[...]
    msg_b = from_b[...] * exists
    north = jnp.where(even, msg_a, msg_b)
    south = jnp.where(even, msg_b, msg_a)
    zeros = lambda n: jnp.zeros((n, wide), jnp.float32)
    res = jnp.concatenate([zeros(7), south[:9], rest[...], north[:9], zeros(7)], axis=0)
    diag = 4.0 + jnp.concatenate([zeros(10), south[9:15], dg[...], north[9:15], zeros(10)], axis=0)
    row = row_of((rows, wide))
    lat = lat_index()
    low = jnp.where(lat == 0, NR, 0)
    high = jnp.where(lat == 15, 2 * NR, 3 * NR)
    inside = jnp.where(jnp.logical_and(row >= low, row < high), 1.0, 0.0).astype(jnp.float32)
    res = res + jnp.where(row == NR, south[15:], 0.0) + jnp.where(row == NR - 1, edge[1:2], 0.0)
    res = res + jnp.where(row == 2 * NR - 1, north[15:], 0.0) + jnp.where(row == 2 * NR, edge[0:1], 0.0)
    res = res * inside

    def lon_shift(x, n):
        return x if n == 0 else pltpu.roll(x, (-n) % wide, 1)

    def lat_shift(x, n):
        return x if n == 0 else pltpu.roll(x, (-n) % rows, 0)

    def operate(x):
        near = lon_shift(x, 1) + lon_shift(x, -1) + lat_shift(x, 1) + lat_shift(x, -1)
        return diag * x - near

    def precondition(x):
        moved = [lon_shift(x, b) for b in range(-2, 3)]
        total = None
        for a in range(-2, 3):
            line = pc[a + 2, 0] * moved[0]
            for b in range(1, 5):
                line = line + pc[a + 2, b] * moved[b]
            line = lat_shift(line, a)
            total = line if total is None else total + line
        return total * inside

    scale = 1.0 / (5.0 * jnp.full((1, wide), pc[2, 2], jnp.float32))
    p = [res]
    v, av = [], []
    for j in range(3):
        v.append(precondition(p[j]))
        av.append(operate(v[j]))
        if j < 2:
            p.append((av[j] * scale - SHIFTS[j] * p[j]) * inside)
    mine = lambda x: x[NR : 2 * NR, :NC]
    v = [mine(x) for x in v]
    av = [mine(x) for x in av]
    r = mine(res)
    for j in range(3):
        v_out[j] = v[j]
    pairs = [(v[0], av[0]), (v[0], av[1]), (v[0], av[2]), (v[1], av[1]), (v[1], av[2])]
    pairs += [(v[2], av[2]), (v[0], r), (v[1], r), (v[2], r)]
    lines = []
    for x, y in pairs:
        line = jnp.sum(x * y, axis=0, keepdims=True)
        lines.append(line + pltpu.roll(line, NC // 2, 1))
    left = lane_of((1, NC)) < NC // 2
    lines.append(lines[-1])
    out = [jnp.where(left, lines[2 * i], lines[2 * i + 1]) for i in range(5)]
    dots_out[...] = jnp.concatenate(out + [jnp.zeros((3, NC), jnp.float32)], axis=0)


def step_kernel(dots, v, sf, out):
    d = dots[...]
    left = lane_of((8, NC)) < NC // 2
    first = jnp.sum(jnp.where(left, d, 0.0), axis=1, keepdims=True)
    second = jnp.sum(jnp.where(left, 0.0, d), axis=1, keepdims=True)
    h = []
    for i in range(5):
        h += [first[i : i + 1], second[i : i + 1]]
    h00, h01, h02, h11, h12, h22, g0, g1, g2 = h[:9]
    l1 = h01 / h00
    l2 = h02 / h00
    d1 = h11 - l1 * h01
    e12 = h12 - l1 * h02
    l3 = e12 / d1
    d2 = h22 - l2 * h02 - l3 * e12
    y1 = g1 - l1 * g0
    y2 = g2 - l2 * g0 - l3 * y1
    c2 = y2 / d2
    c1 = y1 / d1 - l3 * c2
    c0 = g0 / h00 - l1 * c1 - l2 * c2
    out[...] = sf[...] + c0 * v[0] + c1 * v[1] + c2 * v[2]


def field_kernel(
    t, u, v, vi, land, lon, lon_a, lon_b, a, from_a, b, from_b, t_out, u_out, v_out, packed, lines
):
    lane, row = lane_of((NR, NC)), row_of((NR, NC))
    is_east = lane % 2 == 0
    own = [lon[i] for i in range(6)]
    other = [beyond(lon_a[i], lon_b[i]) for i in range(6)]
    grad_u, grad_v = face_in(own, other)
    packed[0] = other[4]
    packed[1] = (
        jnp.where(is_east, own[0], other[0]) * (own[5] + other[5]) / 12.0 * (own[3] * other[3])
    )
    packed[2] = jnp.where(is_east, grad_u, -grad_u)
    packed[3] = jnp.where(is_east, grad_v, -grad_v)
    even = even_lat()
    exists = b_exists()
    for side in range(2):
        use_a = even if side == 0 else jnp.logical_not(even)
        here = [jnp.where(use_a, a[i], b[i]) for i in range(6)]
        there = [jnp.where(use_a, from_a[i], from_b[i] * exists) for i in range(6)]
        grad_u, grad_v = face_in(here, there)
        speed = here[1] if side == 0 else there[1]
        lines[4 * side] = there[4]
        lines[4 * side + 1] = speed * (here[5] + there[5]) / 12.0 * (here[3] * there[3])
        lines[4 * side + 2] = grad_u if side == 0 else -grad_u
        lines[4 * side + 3] = grad_v if side == 0 else -grad_v

    at_east, at_west = lane == NC - 1, lane == 0
    at_north, at_south = row == NR - 1, row == 0
    lon_up = lambda x: pltpu.roll(x, NC - 1, 1)
    lon_down = lambda x: pltpu.roll(x, 1, 1)
    lat_up = lambda x: pltpu.roll(x, NR - 1, 0)
    lat_down = lambda x: pltpu.roll(x, 1, 0)

    def body(k, carry):
        at = pl.ds(pl.multiple_of(k * NR, NR), NR)
        wet = land[at, :].astype(jnp.float32)
        tt, uu, vv, visc = t[at, :], u[at, :], v[at, :], vi[at, :]
        wt = tt * wet
        side = [pltpu.roll(packed[i], NC - 1 - 2 * k, 1) for i in range(4)]
        line = [jnp.broadcast_to(lines[i, pl.ds(k, 1), :], (NR, NC)) for i in range(8)]
        wet_e = wet * lon_up(wet)
        wet_n = wet * lat_up(wet)
        face_e = 0.5 * (visc + lon_up(visc)) * wet_e
        face_n = 0.5 * (visc + lat_up(visc)) * wet_n

        def spread(flux_e, flux_n, i):
            flux_e = jnp.where(at_east, side[i], flux_e)
            flux_n = jnp.where(at_north, line[i], flux_n)
            back_e = jnp.where(at_west, side[i], lon_down(flux_e))
            back_n = jnp.where(at_south, line[4 + i], lat_down(flux_n))
            return flux_e - back_e + flux_n - back_n

        t_e = jnp.where(at_east, side[0], lon_up(wt))
        t_w = jnp.where(at_west, side[0], lon_down(wt))
        t_n = jnp.where(at_north, line[0], lat_up(wt))
        t_s = jnp.where(at_south, line[4], lat_down(wt))
        flux_e = uu * (7.0 * (wt + t_e) - (t_w + lon_up(t_e))) / 12.0 * wet_e
        flux_n = vv * (7.0 * (wt + t_n) - (t_s + lat_up(t_n))) / 12.0 * wet_n
        t_out[at, :] = wet * (tt - DT_ADV * spread(flux_e, flux_n, 1))
        u_out[at, :] = wet * (
            uu + DT_VISC * spread(face_e * (lon_up(uu) - uu), face_n * (lat_up(uu) - uu), 2)
        )
        v_out[at, :] = wet * (
            vv + DT_VISC * spread(face_e * (lon_up(vv) - vv), face_n * (lat_up(vv) - vv), 3)
        )
        return carry

    lax.fori_loop(0, NZ, body, 0, unroll=2)


def shared_sum(values, axes, count):
    spread = jnp.broadcast_to(values[None], (count,) + values.shape)
    return jnp.sum(lax.all_to_all(spread, axes, 0, 0), axis=0)


def local(tracer, east_vel, north_vel, viscosity, land_sea, thickness, surface, surface_diag, precond_kernel):
    flat = (NZ * NR, NC)
    t, u, v, vi, land = (
        x.reshape(flat) for x in (tracer, east_vel, north_vel, viscosity, land_sea)
    )
    block = NZ * NR * NC * 4
    lon, a, b = call(
        pack_kernel,
        [(8, NR, NC), (6, NZ, NC), (6, NZ, NC)],
        [VM] * 7,
        20 * NZ * NR * NC,
        5 * block,
    )(t, u, v, vi, land, surface, surface_diag)
    from_b = lax.ppermute(b, LAT, SWAP_B)
    from_a = lax.ppermute(a, LAT, SWAP_A)
    lon_b = lax.ppermute(lon, LON, SWAP_B)
    lon_a = lax.ppermute(lon, LON, SWAP_A)
    (inner,) = call(
        inner_kernel, [(2, NR, NC)], [SM] + [VM] * 4, 40 * NZ * NR * NC, 4 * block
    )(thickness, u, v, vi, land)
    th_lane = jnp.repeat(thickness, 2)[None]
    th_row = jnp.broadcast_to(thickness[:, None], (NZ, NC))
    (tr,) = call(join_kernel, [(2, NR, NC)], [VM] * 10, 10**6, 10**6)(
        inner, lon, lon_a, lon_b, a, from_a, b, from_b, th_lane, th_row
    )
    tr_b = lax.ppermute(tr, LON, SWAP_B)
    tr_a = lax.ppermute(tr, LON, SWAP_A)
    t_new, u_new, v_new = call(
        field_kernel,
        [flat] * 3,
        [VM] * 12,
        120 * NZ * NR * NC,
        8 * block,
        [pltpu.VMEM((4, NR, NC), jnp.float32), pltpu.VMEM((8, NZ, NC), jnp.float32)],
    )(t, u, v, vi, land, lon, lon_a, lon_b, a, from_a, b, from_b)
    wide = (NR, 2 * NC)
    rest, dg, edge, side_a, side_b = call(
        side_kernel, [wide, wide, (8, 2 * NC), wide, wide], [VM] * 6, 10**6, 10**5
    )(tr, tr_a, tr_b, lon, lon_a, lon_b)
    got_b = lax.ppermute(side_b, LAT, SWAP_B)
    got_a = lax.ppermute(side_a, LAT, SWAP_A)
    vecs, dots = call(
        solve_kernel, [(3, NR, NC), (8, NC)], [SM] + [VM] * 5, 10**6, 10**5
    )(precond_kernel, rest, dg, edge, got_a, got_b)
    dots = shared_sum(dots, ("x", "y", "c"), 32)
    dots = shared_sum(dots, ("zl", "zh"), 8)
    (surface_new,) = call(step_kernel, [(NR, NC)], [VM] * 3, 10**5, 10**4)(dots, vecs, surface)
    shape = (NZ, NR, NC)
    return t_new.reshape(shape), u_new.reshape(shape), v_new.reshape(shape), surface_new


def solution(mesh):
    sizes = dict(mesh.shape)
    assert sizes == {"lon": 16, "lat": 16} and tuple(mesh.axis_names) == ("lon", "lat")
    fine = Mesh(mesh.devices.reshape(2, 4, 2, 4, 4), ("zl", "x", "c", "y", "zh"))
    deep = P(None, LAT, LON)
    flat = P(LAT, LON)
    return jax.shard_map(
        local,
        mesh=fine,
        in_specs=(deep,) * 5 + (P(), flat, flat, P()),
        out_specs=(deep, deep, deep, flat),
        check_vma=False,
    )
```

time: 702 us -> 78.3 us (0.11)
  blocking collectives: 413 us -> 14.9 us
  other arithmetic: 122 us -> 1.72 us
  starting transfers between devices: 93.1 us -> 29.2 us
  waiting for transfers between devices: 34.2 us -> 4.36 us
  local copies, waits for them, and re-layouts: 30.1 us -> 10.4 us
  Pallas kernels: 0 us -> 16.2 us
    psum x5 -> x0, blocking collectives: 413 us -> none  [global_sums(): return lax.psum((values[0],), ('lon', 'lat'))]
    ppermute x36 -> x8, starting transfers between devices: 93.1 us -> 24.1 us  [the longest x1 6.65 us: local(): from_b = lax.ppermute(b, LAT, SWAP_B)]
    reduce_sum x6 -> x2, other arithmetic: 56.3 us -> 1.72 us  [shared_sum(): return jnp.sum(lax.all_to_all(spread, axes, 0, 0), axis=0)]
    add x2 -> x0, other arithmetic: 31.8 us -> none  [the longest x1 16.2 us: local(): iterate = iterate + step_size * direction]
    ppermute x36 -> x8, waiting for transfers between devices: 34.2 us -> 4.36 us  [the longest x1 2.01 us: local(): got_b = lax.ppermute(side_b, LAT, SWAP_B)]
    pallas_call x0 -> x7, Pallas kernels: none -> 16.2 us  [the longest x1 8.76 us: local(): call(field_kernel, [flat] * 3, [VM] * 12, 120 * NZ * NR * NC, 8 * block,...]
    broadcast_in_dim x3 -> x0, other arithmetic: 15.6 us -> none  [extend(): return extend_stack(source[None])[0]]
    all_to_all x0 -> x1, blocking collectives: none -> 14.9 us  [shared_sum(): return jnp.sum(lax.all_to_all(spread, axes, 0, 0), axis=0)]
  transfers between devices with their start and end apart: 36 -> 9, of which waited for: 20 -> 3; matrix products, arithmetic and copies ran while one was open for 1% -> 0% of each run, Pallas kernels for 0% -> 14%
where the time goes in v1:
time: 78.3 us; the launch traced here: 77.6 us
  starting transfers between devices  29.2 us (37%)
  Pallas kernels  16.2 us (21%)
  blocking collectives  14.9 us (19%)
  local copies, waits for them, and re-layouts  10.4 us (13%)
  waiting for transfers between devices  4.36 us (6%)
  other arithmetic  1.72 us (2%)
    all_to_all x1, blocking collectives, shared_sum(): return jnp.sum(lax.all_to_all(spread, axes, 0, 0), axis=0)  14.9 us
    unnamed x38, local copies, waits for them, and re-layouts  9.5 us
    pallas_call x1, Pallas kernels, local(): call(field_kernel, [flat] * 3, [VM] * 12, 120 * NZ * NR * NC, 8 * block,...  8.76 us
    ppermute x1, starting transfers between devices, local(): from_b = lax.ppermute(b, LAT, SWAP_B)  6.65 us
    all_to_all x1, starting transfers between devices, shared_sum(): return jnp.sum(lax.all_to_all(spread, axes, 0, 0), axis=0)  5.13 us
    ppermute x1, starting transfers between devices, local(): got_b = lax.ppermute(side_b, LAT, SWAP_B)  4.8 us
    ppermute x1, starting transfers between devices, local(): from_a = lax.ppermute(a, LAT, SWAP_A)  3.9 us
    ppermute x1, starting transfers between devices, local(): tr_b = lax.ppermute(tr, LON, SWAP_B)  3.01 us
  transfers between devices with their start and end apart: 9, of which 3 were waited for; matrix products, arithmetic and copies ran while one was open for 0% of the time, Pallas kernels for 14%

profile of v1, /device:TPU:1, one launch (start us, length us, event | category | flops | bytes accessed | tf_op | source)
XLA Modules:
  0.0 77.6 jit_solution(5127659584762479101)
XLA Ops:
  0.6 0.0 copy-start.13
  0.6 0.7 copy-done.13
  1.3 1.0 %copy-done = f32[64,16,128]{2,1,0:T(8,128)S(1)} copy-done((f32[64,16,128]{2,1,0:T(8,128)S(1)}, f32[64,16,128]{2,1,0:T(8,128)}, u32[]{:S(2)}) %copy-start) | copy-done | bytes 524312
  2.4 1.0 %copy-done.2 = f32[64,16,128]{2,1,0:T(8,128)S(1)} copy-done((f32[64,16,128]{2,1,0:T(8,128)S(1)}, f32[64,16,128]{2,1,0:T(8,128)}, u32[]{:S(2)}) %copy-start.2) | copy-done | bytes 524312
  3.4 1.0 %copy-done.4 = f32[64,16,128]{2,1,0:T(8,128)S(1)} copy-done((f32[64,16,128]{2,1,0:T(8,128)S(1)}, f32[64,16,128]{2,1,0:T(8,128)}, u32[]{:S(2)}) %copy-start.4) | copy-done | bytes 524312
  4.5 1.0 %copy-done.6 = s32[64,16,128]{2,1,0:T(8,128)S(1)} copy-done((s32[64,16,128]{2,1,0:T(8,128)S(1)}, s32[64,16,128]{2,1,0:T(8,128)}, u32[]{:S(2)}) %copy-start.6) | copy-done | bytes 524312
  5.5 1.0 %copy-done.8 = f32[64,16,128]{2,1,0:T(8,128)S(1)} copy-done((f32[64,16,128]{2,1,0:T(8,128)S(1)}, f32[64,16,128]{2,1,0:T(8,128)}, u32[]{:S(2)}) %copy-start.8) | copy-done | bytes 524312
  6.5 0.7 copy-done.16
  7.2 2.7 %shard_map.120 = (f32[8,16,128]{2,1,0:T(8,128)S(1)}, f32[6,64,128]{2,1,0:T(8,128)S(1)}, f32[6,64,128]{2,1,0:T(8,128)S(1)}) custom-call(f32[1024,128]{1,0:T(8,128)S(1)} %bitcast.20, f32[1024,128]{1,0:T(8,128)S(1)} %bitcast.8, f32[1024,128]{1,0:T(8,128)S(1)} %bitcast.11, f32[1024,128]{1,0:T(8,128)S(1)} %bitcast.14, s32[1024,128]{1,0:T(8,128)S(1)} %bitcast.17, ...), custom_call_target="tpu_custom_call" | custom-call | flops 2621440 | bytes 2621440 | tf_op jit(solution)/shard_map/pallas_call | solution.py:375
  10.0 3.9 %collective-permute-start.2 = (f32[6,64,128]{2,1,0:T(8,128)S(1)}, f32[6,64,128]{2,1,0:T(8,128)S(1)}, u32[]{:S(2)}, u32[]{:S(2)}) collective-permute-start(f32[6,64,128]{2,1,0:T(8,128)S(1)} %get-tuple-element.18.a), channel_id=1, source_target_pairs={{0,1},{1,0},{2,3},{3,2},{4,5},{5,4},{6,7},{7,6},{8,9},{9,8},{10,11... | collective-permute-start | bytes 589832 | tf_op jit(solution)/shard_map/ppermute | solution.py:383
  13.9 6.7 %collective-permute-start.3 = (f32[6,64,128]{2,1,0:T(8,128)S(1)}, f32[6,64,128]{2,1,0:T(8,128)S(1)}, u32[]{:S(2)}, u32[]{:S(2)}) collective-permute-start(f32[6,64,128]{2,1,0:T(8,128)S(1)} %get-tuple-element.19.b), channel_id=1, source_target_pairs={{0,15},{1,2},{2,1},{3,4},{4,3},{5,6},{6,5},{7,8},{8,7},{9,10},{10,... | collective-permute-start | bytes 589832 | tf_op jit(solution)/shard_map/ppermute | solution.py:382
  20.5 2.3 %collective-permute-start.1 = (f32[8,16,128]{2,1,0:T(8,128)S(1)}, f32[8,16,128]{2,1,0:T(8,128)S(1)}, u32[]{:S(2)}, u32[]{:S(2)}) collective-permute-start(f32[8,16,128]{2,1,0:T(8,128)S(1)} %get-tuple-element.17.lon), channel_id=1, source_target_pairs={{0,240},{16,32},{32,16},{48,64},{64,48},{80,96},{96,80},{112,128},... | collective-permute-start | bytes 196616 | tf_op jit(solution)/shard_map/ppermute | solution.py:384
  22.9 1.0 %collective-permute-start = (f32[8,16,128]{2,1,0:T(8,128)S(1)}, f32[8,16,128]{2,1,0:T(8,128)S(1)}, u32[]{:S(2)}, u32[]{:S(2)}) collective-permute-start(f32[8,16,128]{2,1,0:T(8,128)S(1)} %get-tuple-element.17.lon), channel_id=1, source_target_pairs={{0,16},{16,0},{32,48},{48,32},{64,80},{80,64},{96,112},{112,96},{1... | collective-permute-start | bytes 196616 | tf_op jit(solution)/shard_map/ppermute | solution.py:385
  23.9 0.0 copy-done.17
  23.9 0.1 broadcast_in_dim.8
  23.9 0.1 broadcast_in_dim_reshape.3.th_lane
  24.1 2.3 %shard_map.122.inner = f32[2,16,128]{2,1,0:T(8,128)S(1)} custom-call(f32[64]{0:T(128)S(1)} %copy-done.17, f32[1024,128]{1,0:T(8,128)S(1)} %bitcast.9, f32[1024,128]{1,0:T(8,128)S(1)} %bitcast.12, f32[1024,128]{1,0:T(8,128)S(1)} %bitcast.15, s32[1024,128]{1,0:T(8,128)S(1)} %bitcast.18), custom_call_target="tpu_custom_call" | custom-call | flops 5242880 | bytes 2097152 | tf_op jit(solution)/shard_map/pallas_call | solution.py:386
  26.4 0.0 collective-permute-done.1.lon_b
  26.4 0.0 collective-permute-done.lon_a
  26.5 0.0 collective-permute-done.2.from_a
  26.5 1.5 %collective-permute-done.3.from_b = f32[6,64,128]{2,1,0:T(8,128)S(1)} collective-permute-done((f32[6,64,128]{2,1,0:T(8,128)S(1)}, f32[6,64,128]{2,1,0:T(8,128)S(1)}, u32[]{:S(2)}, u32[]{:S(2)}) %collective-permute-start.3) | collective-permute-done | bytes 196640 | tf_op jit(solution)/shard_map/ppermute | solution.py:382
  28.0 0.1 broadcast_in_dim.9.th_row
  28.0 0.2 shard_map.123.tr
  28.2 0.0 copy-start.10
  28.2 0.6 copy-done.10
  28.9 3.0 %collective-permute-start.5 = (f32[2,16,128]{2,1,0:T(8,128)S(1)}, f32[2,16,128]{2,1,0:T(8,128)S(1)}, u32[]{:S(2)}, u32[]{:S(2)}) collective-permute-start(f32[2,16,128]{2,1,0:T(8,128)S(1)} %shard_map.123.tr), channel_id=1, source_target_pairs={{0,240},{16,32},{32,16},{48,64},{64,48},{80,96},{96,80},{112,128},... | collective-permute-start | bytes 49160 | tf_op jit(solution)/shard_map/ppermute | solution.py:394
  31.9 1.7 %collective-permute-start.4 = (f32[2,16,128]{2,1,0:T(8,128)S(1)}, f32[2,16,128]{2,1,0:T(8,128)S(1)}, u32[]{:S(2)}, u32[]{:S(2)}) collective-permute-start(f32[2,16,128]{2,1,0:T(8,128)S(1)} %shard_map.123.tr), channel_id=1, source_target_pairs={{0,16},{16,0},{32,48},{48,32},{64,80},{80,64},{96,112},{112,96},{1... | collective-permute-start | bytes 49160 | tf_op jit(solution)/shard_map/ppermute | solution.py:395
  33.6 0.0 collective-permute-done.5.tr_b
  33.6 0.8 %collective-permute-done.4.tr_a = f32[2,16,128]{2,1,0:T(8,128)S(1)} collective-permute-done((f32[2,16,128]{2,1,0:T(8,128)S(1)}, f32[2,16,128]{2,1,0:T(8,128)S(1)}, u32[]{:S(2)}, u32[]{:S(2)}) %collective-permute-start.4) | collective-permute-done | bytes 16416 | tf_op jit(solution)/shard_map/ppermute | solution.py:395
  34.5 0.8 %copy-done.11 = f32[8,16,128]{2,1,0:T(8,128)S(1)} copy-done((f32[8,16,128]{2,1,0:T(8,128)S(1)}, f32[8,16,128]{2,1,0:T(8,128)}, u32[]{:S(2)}) %copy-start.11) | copy-done | bytes 65560
  35.3 0.1 shard_map.124
  35.4 0.7 collective-permute-start.6
  36.0 4.8 %collective-permute-start.7 = (f32[16,256]{1,0:T(8,128)S(1)}, f32[16,256]{1,0:T(8,128)S(1)}, u32[]{:S(2)}, u32[]{:S(2)}) collective-permute-start(f32[16,256]{1,0:T(8,128)S(1)} %get-tuple-element.27), channel_id=1, source_target_pairs={{0,15},{1,2},{2,1},{3,4},{4,3},{5,6},{6,5},{7,8},{8,7},{9,10},{10,... | collective-permute-start | bytes 49160 | tf_op jit(solution)/shard_map/ppermute | solution.py:408
  40.8 0.0 collective-permute-done.6.from_a
  40.8 2.0 %collective-permute-done.7.from_b = f32[16,256]{1,0:T(8,128)S(1)} collective-permute-done((f32[16,256]{1,0:T(8,128)S(1)}, f32[16,256]{1,0:T(8,128)S(1)}, u32[]{:S(2)}, u32[]{:S(2)}) %collective-permute-start.7) | collective-permute-done | bytes 16416 | tf_op jit(solution)/shard_map/ppermute | solution.py:408
  42.8 1.4 %shard_map.125 = (f32[3,16,128]{2,1,0:T(8,128)S(1)}, f32[8,128]{1,0:T(8,128)S(1)}) custom-call(f32[5,5]{1,0:T(8,128)S(1)} %copy-done.18, f32[16,256]{1,0:T(8,128)S(1)} %get-tuple-element.23.rest, f32[16,256]{1,0:T(8,128)S(1)} %get-tuple-element.24.dg, f32[8,256]{1,0:T(8,128)S(1)} %get-tuple-element.25.edge, f32[16,256]{1,0:T(8,128)S(1)} %collective-permute-done.6.from_a, ...), custom_call_target="tpu_custom_call" | custom-call | flops 1000000 | bytes 100000 | tf_op jit(solution)/shard_map/pallas_call | solution.py:410
  44.2 0.0 copy-start.14
  44.3 0.6 copy-done.14
  44.8 14.9 %all_to_all.10 = f32[32,8,128]{2,1,0:T(8,128)} all-to-all(f32[32,8,128]{2,1,0:T(8,128)S(1)} %broadcast_in_dim.10), channel_id=1, replica_groups=mesh['zl'=2,'x'=4,'c'=2,'y'=4,'zh'=4] {'x','y','c'}, dimensions={0} | all-to-all | bytes 262144 | tf_op jit(solution)/shard_map/all_to_all | solution.py:366
  59.8 0.9 %reduce_sum.18 = f32[8,128]{1,0:T(8,128)S(1)} reduce(f32[32,8,128]{2,1,0:T(8,128)} %all_to_all.10, f32[]{:T(128)} %constant.0.clone.1), dimensions={0}, to_apply=%region_0.0 | reduce | flops 31744 | bytes 135172 | tf_op jit(solution)/shard_map/reduce_sum | solution.py:366
  60.7 0.6 broadcast_in_dim.11
  61.3 5.1 %all-to-all-start.1 = ((f32[8,8,128]{2,1,0:T(8,128)}), f32[8,8,128]{2,1,0:T(8,128)}, u32[]{:S(2)}, u32[]{:S(2)}) async-start(f32[8,8,128]{2,1,0:T(8,128)} %broadcast_in_dim.11), calls=%async_computation.1 | async-start | bytes 65536 | tf_op jit(solution)/shard_map/all_to_all | solution.py:366
  66.5 0.0 copy-start.12
  66.5 0.8 %copy-done.12 = f32[8,16,128]{2,1,0:T(8,128)S(1)} copy-done((f32[8,16,128]{2,1,0:T(8,128)S(1)}, f32[8,16,128]{2,1,0:T(8,128)}, u32[]{:S(2)}) %copy-start.12) | copy-done | bytes 65560
  67.3 8.8 %shard_map.121 = (f32[1024,128]{1,0:T(8,128)}, f32[1024,128]{1,0:T(8,128)}, f32[1024,128]{1,0:T(8,128)}) custom-call(f32[1024,128]{1,0:T(8,128)S(1)} %bitcast.21, f32[1024,128]{1,0:T(8,128)S(1)} %bitcast.10, f32[1024,128]{1,0:T(8,128)S(1)} %bitcast.13, f32[1024,128]{1,0:T(8,128)S(1)} %bitcast.16, s32[1024,128]{1,0:T(8,128)S(1)} %bitcast.19, ...), custom_call_target="tpu_custom_call" | custom-call | flops 15728640 | bytes 4194304 | tf_op jit(solution)/shard_map/pallas_call | solution.py:396
  76.1 0.0 all-to-all-done.1
  76.1 0.8 %reduce_sum.19.dots = f32[8,128]{1,0:T(8,128)S(1)} reduce(f32[8,8,128]{2,1,0:T(8,128)} %all-to-all-done.1, f32[]{:T(128)} %constant.0.clone.1), dimensions={0}, to_apply=%region_1.0 | reduce | flops 7168 | bytes 36868 | tf_op jit(solution)/shard_map/reduce_sum | solution.py:366
  76.9 0.8 shard_map.126
  (23 shorter events, 0.0 us)
Async XLA Ops:
  0.6 0.7 copy-start.13
  1.3 1.0 %copy-start = (f32[64,16,128]{2,1,0:T(8,128)S(1)}, f32[64,16,128]{2,1,0:T(8,128)}, u32[]{:S(2)}) copy-start(f32[64,16,128]{2,1,0:T(8,128)} %param.10) | copy-start | bytes 1572868
  2.4 1.0 %copy-start.2 = (f32[64,16,128]{2,1,0:T(8,128)S(1)}, f32[64,16,128]{2,1,0:T(8,128)}, u32[]{:S(2)}) copy-start(f32[64,16,128]{2,1,0:T(8,128)} %param.11) | copy-start | bytes 1572868
  3.4 1.0 %copy-start.4 = (f32[64,16,128]{2,1,0:T(8,128)S(1)}, f32[64,16,128]{2,1,0:T(8,128)}, u32[]{:S(2)}) copy-start(f32[64,16,128]{2,1,0:T(8,128)} %param.12) | copy-start | bytes 1572868
  4.5 1.0 %copy-start.6 = (s32[64,16,128]{2,1,0:T(8,128)S(1)}, s32[64,16,128]{2,1,0:T(8,128)}, u32[]{:S(2)}) copy-start(s32[64,16,128]{2,1,0:T(8,128)} %param.13) | copy-start | bytes 1572868
  5.5 1.0 %copy-start.8 = (f32[64,16,128]{2,1,0:T(8,128)S(1)}, f32[64,16,128]{2,1,0:T(8,128)}, u32[]{:S(2)}) copy-start(f32[64,16,128]{2,1,0:T(8,128)} %param.9) | copy-start | bytes 1572868
  6.5 0.7 copy-start.16
  7.2 16.9 %copy-start.1 = (f32[64,16,128]{2,1,0:T(8,128)S(1)}, f32[64,16,128]{2,1,0:T(8,128)}, u32[]{:S(2)}) copy-start(f32[64,16,128]{2,1,0:T(8,128)} %param.10) | copy-start | bytes 1572868
  7.2 16.9 %copy-start.3 = (f32[64,16,128]{2,1,0:T(8,128)S(1)}, f32[64,16,128]{2,1,0:T(8,128)}, u32[]{:S(2)}) copy-start(f32[64,16,128]{2,1,0:T(8,128)} %param.11) | copy-start | bytes 1572868
  7.2 16.9 %copy-start.5 = (f32[64,16,128]{2,1,0:T(8,128)S(1)}, f32[64,16,128]{2,1,0:T(8,128)}, u32[]{:S(2)}) copy-start(f32[64,16,128]{2,1,0:T(8,128)} %param.12) | copy-start | bytes 1572868
  7.2 16.9 %copy-start.7 = (s32[64,16,128]{2,1,0:T(8,128)S(1)}, s32[64,16,128]{2,1,0:T(8,128)}, u32[]{:S(2)}) copy-start(s32[64,16,128]{2,1,0:T(8,128)} %param.13) | copy-start | bytes 1572868
  10.0 16.5 %collective-permute-start.2 = (f32[6,64,128]{2,1,0:T(8,128)S(1)}, f32[6,64,128]{2,1,0:T(8,128)S(1)}, u32[]{:S(2)}, u32[]{:S(2)}) collective-permute-start(f32[6,64,128]{2,1,0:T(8,128)S(1)} %get-tuple-element.18.a), channel_id=1, source_target_pairs={{0,1},{1,0},{2,3},{3,2},{4,5},{5,4},{6,7},{7,6},{8,9},{9,8},{10,11... | collective-permute-start | bytes 589832 | tf_op jit(solution)/shard_map/ppermute | solution.py:383
  13.9 10.0 %copy-start.17 = (f32[64]{0:T(128)S(1)}, f32[64]{0:T(128)}, u32[]{:S(2)}) copy-start(f32[64]{0:T(128)} %thick.1) | copy-start | bytes 772
  13.9 14.1 %collective-permute-start.3 = (f32[6,64,128]{2,1,0:T(8,128)S(1)}, f32[6,64,128]{2,1,0:T(8,128)S(1)}, u32[]{:S(2)}, u32[]{:S(2)}) collective-permute-start(f32[6,64,128]{2,1,0:T(8,128)S(1)} %get-tuple-element.19.b), channel_id=1, source_target_pairs={{0,15},{1,2},{2,1},{3,4},{4,3},{5,6},{6,5},{7,8},{8,7},{9,10},{10,... | collective-permute-start | bytes 589832 | tf_op jit(solution)/shard_map/ppermute | solution.py:382
  20.5 5.9 %collective-permute-start.1 = (f32[8,16,128]{2,1,0:T(8,128)S(1)}, f32[8,16,128]{2,1,0:T(8,128)S(1)}, u32[]{:S(2)}, u32[]{:S(2)}) collective-permute-start(f32[8,16,128]{2,1,0:T(8,128)S(1)} %get-tuple-element.17.lon), channel_id=1, source_target_pairs={{0,240},{16,32},{32,16},{48,64},{64,48},{80,96},{96,80},{112,128},... | collective-permute-start | bytes 196616 | tf_op jit(solution)/shard_map/ppermute | solution.py:384
  22.9 3.6 %collective-permute-start = (f32[8,16,128]{2,1,0:T(8,128)S(1)}, f32[8,16,128]{2,1,0:T(8,128)S(1)}, u32[]{:S(2)}, u32[]{:S(2)}) collective-permute-start(f32[8,16,128]{2,1,0:T(8,128)S(1)} %get-tuple-element.17.lon), channel_id=1, source_target_pairs={{0,16},{16,0},{32,48},{48,32},{64,80},{80,64},{96,112},{112,96},{1... | collective-permute-start | bytes 196616 | tf_op jit(solution)/shard_map/ppermute | solution.py:385
  28.0 14.8 %copy-start.18 = (f32[5,5]{1,0:T(8,128)S(1)}, f32[5,5]{1,0:T(8,128)}, u32[]{:S(2)}) copy-start(f32[5,5]{1,0:T(8,128)} %pc.1) | copy-start | bytes 304
  28.2 0.6 copy-start.10
  28.9 37.6 %copy-start.9 = (f32[64,16,128]{2,1,0:T(8,128)S(1)}, f32[64,16,128]{2,1,0:T(8,128)}, u32[]{:S(2)}) copy-start(f32[64,16,128]{2,1,0:T(8,128)} %param.9) | copy-start | bytes 1572868
  28.9 4.8 %collective-permute-start.5 = (f32[2,16,128]{2,1,0:T(8,128)S(1)}, f32[2,16,128]{2,1,0:T(8,128)S(1)}, u32[]{:S(2)}, u32[]{:S(2)}) collective-permute-start(f32[2,16,128]{2,1,0:T(8,128)S(1)} %shard_map.123.tr), channel_id=1, source_target_pairs={{0,240},{16,32},{32,16},{48,64},{64,48},{80,96},{96,80},{112,128},... | collective-permute-start | bytes 49160 | tf_op jit(solution)/shard_map/ppermute | solution.py:394
  31.9 2.6 %collective-permute-start.4 = (f32[2,16,128]{2,1,0:T(8,128)S(1)}, f32[2,16,128]{2,1,0:T(8,128)S(1)}, u32[]{:S(2)}, u32[]{:S(2)}) collective-permute-start(f32[2,16,128]{2,1,0:T(8,128)S(1)} %shard_map.123.tr), channel_id=1, source_target_pairs={{0,16},{16,0},{32,48},{48,32},{64,80},{80,64},{96,112},{112,96},{1... | collective-permute-start | bytes 49160 | tf_op jit(solution)/shard_map/ppermute | solution.py:395
  34.4 0.8 %copy-start.11 = (f32[8,16,128]{2,1,0:T(8,128)S(1)}, f32[8,16,128]{2,1,0:T(8,128)}, u32[]{:S(2)}) copy-start(f32[8,16,128]{2,1,0:T(8,128)} %copy-done.10) | copy-start | bytes 196612
  35.4 5.5 %collective-permute-start.6 = (f32[16,256]{1,0:T(8,128)S(1)}, f32[16,256]{1,0:T(8,128)S(1)}, u32[]{:S(2)}, u32[]{:S(2)}) collective-permute-start(f32[16,256]{1,0:T(8,128)S(1)} %get-tuple-element.26), channel_id=1, source_target_pairs={{0,1},{1,0},{2,3},{3,2},{4,5},{5,4},{6,7},{7,6},{8,9},{9,8},{10,11... | collective-permute-start | bytes 49160 | tf_op jit(solution)/shard_map/ppermute | solution.py:409
  36.0 6.8 %collective-permute-start.7 = (f32[16,256]{1,0:T(8,128)S(1)}, f32[16,256]{1,0:T(8,128)S(1)}, u32[]{:S(2)}, u32[]{:S(2)}) collective-permute-start(f32[16,256]{1,0:T(8,128)S(1)} %get-tuple-element.27), channel_id=1, source_target_pairs={{0,15},{1,2},{2,1},{3,4},{4,3},{5,6},{6,5},{7,8},{8,7},{9,10},{10,... | collective-permute-start | bytes 49160 | tf_op jit(solution)/shard_map/ppermute | solution.py:408
  44.2 0.6 copy-start.14
  61.3 14.8 %all-to-all-start.1 = ((f32[8,8,128]{2,1,0:T(8,128)}), f32[8,8,128]{2,1,0:T(8,128)}, u32[]{:S(2)}, u32[]{:S(2)}) async-start(f32[8,8,128]{2,1,0:T(8,128)} %broadcast_in_dim.11), calls=%async_computation.1 | async-start | bytes 65536 | tf_op jit(solution)/shard_map/all_to_all | solution.py:366
  66.5 0.8 %copy-start.12 = (f32[8,16,128]{2,1,0:T(8,128)S(1)}, f32[8,16,128]{2,1,0:T(8,128)}, u32[]{:S(2)}) copy-start(f32[8,16,128]{2,1,0:T(8,128)} %copy-done.10) | copy-start | bytes 196612
  76.1 0.8 %copy-start.15 = (f32[3,16,128]{2,1,0:T(8,128)S(1)}, f32[3,16,128]{2,1,0:T(8,128)}, u32[]{:S(2)}) copy-start(f32[3,16,128]{2,1,0:T(8,128)} %copy-done.14) | copy-start | bytes 73732

commit v2 on v1

v2 whole, which is shorter than its diff:
```python
import jax
import jax.numpy as jnp
from jax import lax
from jax.experimental import pallas as pl
from jax.experimental.pallas import tpu as pltpu
from jax.sharding import Mesh
from jax.sharding import PartitionSpec as P

DT_ADV = 0.25
DT_VISC = 0.2
TAU = 0.05
SHIFTS = (0.3, 1.3)

LON = ("zl", "x", "c")
LAT = ("y", "zh")
NZ, NR, NC = 64, 16, 128
SWAP_A = [(i, i ^ 1) for i in range(16)]
SWAP_B = [(i, (i + 1) % 16 if i % 2 else (i - 1) % 16) for i in range(16)]

VM = pl.BlockSpec(memory_space=pltpu.VMEM)
SM = pl.BlockSpec(memory_space=pltpu.SMEM)
HBM = pl.BlockSpec(memory_space=pltpu.HBM)
FIELD_UNROLL = 4
FETCH_VMEM = 56


def call(kernel, outs, specs, flops, nbytes, scratch=(), place=VM, vmem=4):
    return pl.pallas_call(
        kernel,
        out_shape=[jax.ShapeDtypeStruct(s, jnp.float32) for s in outs],
        in_specs=specs,
        out_specs=[place] * len(outs),
        scratch_shapes=list(scratch),
        compiler_params=pltpu.CompilerParams(vmem_limit_bytes=vmem * 1024 * 1024),
        cost_estimate=pl.CostEstimate(flops=flops, bytes_accessed=nbytes, transcendentals=0),
    )


def lane_of(shape):
    return lax.broadcasted_iota(jnp.int32, shape, len(shape) - 1)


def row_of(shape):
    return lax.broadcasted_iota(jnp.int32, shape, len(shape) - 2)


def even_lon():
    return lax.axis_index("c") == 0


def even_lat():
    return lax.axis_index("zh") % 2 == 0


def lat_index():
    return lax.axis_index("y") * 4 + lax.axis_index("zh")


def b_exists():
    lat = lat_index()
    return jnp.where(jnp.logical_or(lat == 0, lat == 15), 0.0, 1.0).astype(jnp.float32)


HALF = NZ // 2
CHUNKS = 4


def halves():
    mine = jnp.where(even_lat(), 0, HALF)
    return pl.multiple_of(mine, HALF), pl.multiple_of(HALF - mine, HALF)


def edge_row(ref, north, inwards, first, count):
    if isinstance(north, bool):
        row = NR - 1 - inwards if north else inwards
    else:
        row = jnp.where(north, NR - 1 - inwards, inwards)
    return ref[pl.ds(first * NR + row, count, stride=NR), :].astype(jnp.float32)


def fetch_kernel(u, v, vi, land, sf, dg, lon_out, a_out, b_out, uo, vo, vio, lo, sems):
    span = NZ * NR // CHUNKS
    copies = []
    for c in range(CHUNKS):
        at = pl.ds(c * span, span)
        line = []
        for i, (src, dst) in enumerate(((u, uo), (v, vo), (vi, vio), (land, lo))):
            copy = pltpu.make_async_copy(src.at[at], dst.at[at], sems.at[c, i])
            copy.start()
            line.append(copy)
        copies.append(line)
    pair = lane_of((NR, NC)) // 2

    def body(k, acc):
        at = pl.ds(pl.multiple_of(k * NR, NR), NR)
        wet = lo[at, :].astype(jnp.float32)
        values = (uo[at, :], vo[at, :], vio[at, :], wet)
        mine = pair == k
        return tuple(
            jnp.where(mine, pltpu.roll(x, 2 * k + 1, 1), old) for x, old in zip(values, acc)
        )

    acc = (jnp.zeros((NR, NC), jnp.float32),) * 4
    per = NZ // CHUNKS
    for c in range(CHUNKS):
        for copy in copies[c]:
            copy.wait()
        acc = lax.fori_loop(c * per, (c + 1) * per, body, acc, unroll=8)
    for i in range(4):
        lon_out[i] = acc[i]
    lon_out[4] = sf[...]
    lon_out[5] = dg[...]
    even = even_lat()
    mine, _ = halves()
    for north, out in ((even, a_out), (jnp.logical_not(even), b_out)):
        for i, ref in enumerate((uo, vo, vio, lo)):
            out[i] = edge_row(ref, north, 0, mine, HALF)


def inner_kernel(thick, t, u, v, vi, w, out, lon_out, a_out, b_out):
    lane, row = lane_of((NR, NC)), row_of((NR, NC))
    pair = lane // 2
    half_lane = lane < NC // 2

    def body(k, acc):
        at = pl.ds(pl.multiple_of(k * NR, NR), NR)
        th = thick[k]
        wet, uu, vv, visc = w[at, :].astype(jnp.float32), u[at, :], v[at, :], vi[at, :]
        half = 0.5 * th
        own = wet * th
        east = (visc + pltpu.roll(visc, NC - 1, 1)) * (wet * pltpu.roll(wet, NC - 1, 1)) * half
        north = (visc + pltpu.roll(visc, NR - 1, 0)) * (wet * pltpu.roll(wet, NR - 1, 0)) * half
        first = t[at, :] * wet
        inner = jnp.where(half_lane, pltpu.roll(first, NC - 1, 1), pltpu.roll(first, 1, 1))
        mine = pair == k
        return (
            acc[0] + own * uu,
            acc[1] + east * (pltpu.roll(uu, NC - 1, 1) - uu),
            acc[2] + north * (pltpu.roll(uu, NR - 1, 0) - uu),
            acc[3] + own * vv,
            acc[4] + east * (pltpu.roll(vv, NC - 1, 1) - vv),
            acc[5] + north * (pltpu.roll(vv, NR - 1, 0) - vv),
            jnp.where(mine, pltpu.roll(first, 2 * k + 1, 1), acc[6]),
            jnp.where(mine, pltpu.roll(7.0 * first - inner, 2 * k + 1, 1), acc[7]),
        )

    zero = jnp.zeros((NR, NC), jnp.float32)
    acc = lax.fori_loop(0, NZ, body, (zero,) * 8, unroll=4)
    for i in range(2):
        east = jnp.where(lane == NC - 1, 0.0, acc[3 * i + 1])
        north = jnp.where(row == NR - 1, 0.0, acc[3 * i + 2])
        out[i] = acc[3 * i] + DT_VISC * (
            east - pltpu.roll(east, 1, 1) + north - pltpu.roll(north, 1, 0)
        )
        lon_out[i] = acc[6 + i]
    even = even_lat()
    _, theirs = halves()
    for north, dst in ((even, a_out), (jnp.logical_not(even), b_out)):
        for i, ref in enumerate((u, v, vi, w)):
            dst[i] = edge_row(ref, north, 0, theirs, HALF)
        for i in range(2):
            first = edge_row(t, north, 0, i * HALF, HALF) * edge_row(w, north, 0, i * HALF, HALF)
            second = edge_row(t, north, 1, i * HALF, HALF) * edge_row(w, north, 1, i * HALF, HALF)
            dst[4 + i] = first
            dst[6 + i] = 7.0 * first - second


def lon_sides(first, second):
    even = even_lon()
    return jnp.where(even, first, second), jnp.where(even, second, first)


def beyond(from_a, from_b):
    east, west = lon_sides(from_a, from_b)
    is_east = lane_of((NR, NC)) % 2 == 0
    return jnp.where(is_east, pltpu.roll(east, NC - 1, 1), pltpu.roll(west, 1, 1))


def face_in(own, other):
    face = 0.5 * (own[2] + other[2]) * (own[3] * other[3])
    return face * (other[0] - own[0]), face * (other[1] - own[1])


MSG = 72


def join_kernel(inner, lon, lon_a, lon_b, lon2, a2, from_a, b2, from_b, th_lane, th_row, out):
    lane = lane_of((NR, NC))
    own = [lon[i] for i in range(4)]
    other = [beyond(lon_a[i], lon_b[i]) for i in range(4)]
    is_east = lane % 2 == 0
    for i, grad in enumerate(face_in(own, other)):
        grad = grad * th_lane[...]
        east = jnp.sum(jnp.where(is_east, grad, 0.0), axis=1, keepdims=True)
        west = jnp.sum(jnp.where(is_east, 0.0, grad), axis=1, keepdims=True)
        add = jnp.where(lane == NC - 1, east, 0.0) + jnp.where(lane == 0, west, 0.0)
        out[NR * i : NR * (i + 1), :] = inner[i] + DT_VISC * add
    _, theirs = halves()
    weight = DT_VISC * th_row[pl.ds(theirs, HALF), :]
    lat_a = face_in([a2[i] for i in range(4)], [from_a[i] for i in range(4)])
    weight_b = weight * b_exists()
    lat_b = face_in([b2[i] for i in range(4)], [from_b[i] for i in range(4)])
    sums = [jnp.sum(x * weight, axis=0, keepdims=True) for x in lat_a]
    sums += [jnp.sum(x * weight_b, axis=0, keepdims=True) for x in lat_b]
    out[2 * NR : 2 * NR + 8, :] = jnp.concatenate(sums + [jnp.zeros((4, NC), jnp.float32)], axis=0)
    out[40:56, :] = lon2[0]
    out[56:72, :] = lon2[1]


def side_kernel(msg, msg_a, msg_b, lon, lon_a, lon_b, rest_out, diag_out, edge_out, a_out, b_out):
    def widen(own, first, second):
        east, west = lon_sides(first, second)
        halo = jnp.where(lane_of(own.shape) < NC // 2, east, west)
        return jnp.concatenate([own, halo], axis=1)

    part = lambda lo, hi: widen(msg[lo:hi, :], msg_a[lo:hi, :], msg_b[lo:hi, :])
    te, tn, faces = part(0, NR), part(NR, 2 * NR), part(2 * NR, 2 * NR + 8)
    sf, dg = (widen(lon[i], lon_a[i], lon_b[i]) for i in (4, 5))
    row = row_of((NR, 2 * NC))
    even = even_lat()
    north_u, north_v = (jnp.where(even, faces[i : i + 1], faces[i + 2 : i + 3]) for i in range(2))
    south_u, south_v = (jnp.where(even, faces[i + 2 : i + 3], faces[i : i + 1]) for i in range(2))
    at_north, at_south = row == NR - 1, row == 0
    te = te + jnp.where(at_north, north_u, 0.0) + jnp.where(at_south, south_u, 0.0)
    tn = tn + jnp.where(at_north, north_v, 0.0) + jnp.where(at_south, south_v, 0.0)
    east = lambda x: pltpu.roll(x, 2 * NC - 1, 1)
    west = lambda x: pltpu.roll(x, 1, 1)
    north = lambda x: jnp.where(at_north, 0.0, pltpu.roll(x, NR - 1, 0))
    south = lambda x: jnp.where(at_south, 0.0, pltpu.roll(x, 1, 0))
    across = lambda fu, fv: TAU * (fu - west(fu) + fv)
    rest = sf - TAU * (te - west(te) + tn - south(tn))
    rest = rest - ((4.0 + dg) * sf - (east(sf) + west(sf) + north(sf) + south(sf)))
    rest = rest - jnp.where(at_south, TAU * south_v, 0.0)
    rest_out[...] = rest
    diag_out[...] = dg
    first = TAU * tn[NR - 1 :] + sf[NR - 1 :] + across(north_u, north_v)
    second = -TAU * north_v
    to_south = sf[:1] + across(south_u, south_v)
    zero = jnp.zeros((5, 2 * NC), jnp.float32)
    edge_out[...] = jnp.concatenate([first, second, to_south, zero], axis=0)
    msg_north = jnp.concatenate([rest[8:], dg[11:], first, second, zero[:1]], axis=0)
    msg_south = jnp.concatenate([rest[:9], dg[:6], to_south], axis=0)
    a_out[...] = jnp.where(even, msg_north, msg_south)
    b_out[...] = jnp.where(even, msg_south, msg_north)


def solve_kernel(pc, rest, dg, edge, from_a, from_b, v_out, dots_out):
    rows, wide = 3 * NR, 2 * NC
    even = even_lat()
    exists = b_exists()
    msg_a = from_a[...]
    msg_b = from_b[...] * exists
    north = jnp.where(even, msg_a, msg_b)
    south = jnp.where(even, msg_b, msg_a)
    zeros = lambda n: jnp.zeros((n, wide), jnp.float32)
    row = row_of((rows, wide))
    lat = lat_index()
    low = jnp.where(lat == 0, NR, 0)
    high = jnp.where(lat == 15, 2 * NR, 3 * NR)
    inside = jnp.where(jnp.logical_and(row >= low, row < high), 1.0, 0.0).astype(jnp.float32)
    below = jnp.concatenate([zeros(8), south[:7], south[7:8] + edge[2:3]], axis=0)
    above = jnp.concatenate(
        [north[:1] + edge[0:1], north[1:2] + edge[1:2], north[2:9], zeros(7)], axis=0
    )
    own = rest[...] + jnp.concatenate([south[13:15], zeros(13), north[15:]], axis=0)
    res = jnp.concatenate([below, own, above], axis=0) * inside
    diag = 4.0 + jnp.concatenate([zeros(11), south[8:13], dg[...], north[9:15], zeros(10)], axis=0)

    def lon_shift(x, n):
        return x if n == 0 else pltpu.roll(x, (-n) % wide, 1)

    def lat_shift(x, n):
        return x if n == 0 else pltpu.roll(x, (-n) % rows, 0)

    def operate(x):
        near = lon_shift(x, 1) + lon_shift(x, -1) + lat_shift(x, 1) + lat_shift(x, -1)
        return diag * x - near

    def precondition(x):
        moved = [lon_shift(x, b) for b in range(-2, 3)]
        total = None
        for a in range(-2, 3):
            line = pc[a + 2, 0] * moved[0]
            for b in range(1, 5):
                line = line + pc[a + 2, b] * moved[b]
            line = lat_shift(line, a)
            total = line if total is None else total + line
        return total * inside

    scale = 1.0 / (5.0 * jnp.full((1, wide), pc[2, 2], jnp.float32))
    p0 = res
    v0 = precondition(p0)
    a0 = operate(v0)
    p1 = (a0 * scale - SHIFTS[0] * p0) * inside
    v1 = precondition(p1)
    a1 = operate(v1)
    p2 = (a1 * scale - SHIFTS[1] * p1) * inside
    v2 = precondition(p2)
    mine = lambda x: x[NR : 2 * NR, :NC]
    half_a2 = mine(diag * v2 - 2.0 * (lon_shift(v2, 1) + lat_shift(v2, 1)))
    v0, v1, v2, a0, a1, r = (mine(x) for x in (v0, v1, v2, a0, a1, p0))
    v_out[0] = v0
    v_out[1] = v1
    v_out[2] = v2
    pairs = ((v0, a0), (v0, a1), (v2, a0), (v1, a1), (v2, a1), (v2, half_a2), (v0, r), (v1, r), (v2, r))
    lines = []
    for x, y in pairs:
        line = jnp.sum(x * y, axis=0, keepdims=True)
        lines.append(line + pltpu.roll(line, NC // 2, 1))
    left = lane_of((1, NC)) < NC // 2
    lines.append(lines[-1])
    out = [jnp.where(left, lines[2 * i], lines[2 * i + 1]) for i in range(5)]
    dots_out[...] = jnp.concatenate(out + [jnp.zeros((3, NC), jnp.float32)], axis=0)


def step_kernel(dots, v, sf, out):
    d = dots[...]
    left = lane_of((8, NC)) < NC // 2
    first = jnp.sum(jnp.where(left, d, 0.0), axis=1, keepdims=True)
    second = jnp.sum(jnp.where(left, 0.0, d), axis=1, keepdims=True)
    h = []
    for i in range(5):
        h += [first[i : i + 1], second[i : i + 1]]
    h00, h01, h02, h11, h12, h22, g0, g1, g2 = h[:9]
    l1 = h01 / h00
    l2 = h02 / h00
    d1 = h11 - l1 * h01
    e12 = h12 - l1 * h02
    l3 = e12 / d1
    d2 = h22 - l2 * h02 - l3 * e12
    y1 = g1 - l1 * g0
    y2 = g2 - l2 * g0 - l3 * y1
    c2 = y2 / d2
    c1 = y1 / d1 - l3 * c2
    c0 = g0 / h00 - l1 * c1 - l2 * c2
    out[...] = sf[...] + c0 * v[0] + c1 * v[1] + c2 * v[2]


def field_kernel(
    t, u, v, vi, w,
    lon, lon_a, lon_b, msg, msg_a, msg_b,
    from_a, from_a2, from_b, from_b2,
    t_hbm, u_hbm, v_hbm, t_out, u_out, v_out, packed, lines, sems,
):
    lane, row = lane_of((NR, NC)), row_of((NR, NC))
    is_east = lane % 2 == 0
    own = [lon[i] for i in range(4)]
    other = [beyond(lon_a[i], lon_b[i]) for i in range(4)]
    grad_u, grad_v = face_in(own, other)
    packed[0] = beyond(msg_a[40:56, :], msg_b[40:56, :])
    far = msg[56:72, :] + beyond(msg_a[56:72, :], msg_b[56:72, :])
    packed[1] = jnp.where(is_east, own[0], other[0]) * far * (1.0 / 12.0) * (own[3] * other[3])
    packed[2] = jnp.where(is_east, grad_u, -grad_u)
    packed[3] = jnp.where(is_east, grad_v, -grad_v)
    even = even_lat()
    exists = b_exists()
    mine, theirs = halves()
    for first, there_a, there_b in ((mine, from_a2, from_b2), (theirs, from_a, from_b)):
        at = pl.ds(first, HALF)
        part = first // HALF
        for side in range(2):
            use_a = even if side == 0 else jnp.logical_not(even)
            here = [edge_row(ref, side == 0, 0, first, HALF) for ref in (u, v, vi, w)]
            there = [jnp.where(use_a, there_a[i], there_b[i] * exists) for i in range(4)]
            near = jnp.where(use_a, from_a2[4 + part], from_b2[4 + part] * exists)
            far = jnp.where(use_a, from_a2[6 + part], from_b2[6 + part])
            near_own = edge_row(t, side == 0, 0, first, HALF) * here[3]
            next_own = edge_row(t, side == 0, 1, first, HALF) * edge_row(w, side == 0, 1, first, HALF)
            far = far + (7.0 * near_own - next_own)
            grad_u, grad_v = face_in(here, there)
            speed = here[1] if side == 0 else there[1]
            lines[4 * side, at, :] = near
            lines[4 * side + 1, at, :] = speed * far * (1.0 / 12.0) * (here[3] * there[3])
            lines[4 * side + 2, at, :] = grad_u if side == 0 else -grad_u
            lines[4 * side + 3, at, :] = grad_v if side == 0 else -grad_v

    at_east, at_west = lane == NC - 1, lane == 0
    at_north, at_south = row == NR - 1, row == 0
    lon_up = lambda x: pltpu.roll(x, NC - 1, 1)
    lon_down = lambda x: pltpu.roll(x, 1, 1)
    lat_up = lambda x: pltpu.roll(x, NR - 1, 0)
    lat_down = lambda x: pltpu.roll(x, 1, 0)

    def body(k, carry):
        at = pl.ds(pl.multiple_of(k * NR, NR), NR)
        tt, uu, vv, visc = t[at, :], u[at, :], v[at, :], vi[at, :]
        wet = w[at, :].astype(jnp.float32)
        wt = tt * wet
        side = [pltpu.roll(packed[i], NC - 1 - 2 * k, 1) for i in range(4)]
        line = [jnp.broadcast_to(lines[i, pl.ds(k, 1), :], (NR, NC)) for i in range(8)]
        wet_e = wet * lon_up(wet)
        wet_n = wet * lat_up(wet)
        face_e = (0.5 * DT_VISC) * (visc + lon_up(visc)) * wet_e
        face_n = (0.5 * DT_VISC) * (visc + lat_up(visc)) * wet_n

        def spread(flux_e, flux_n, i, by):
            flux_e = jnp.where(at_east, by * side[i], flux_e)
            flux_n = jnp.where(at_north, by * line[i], flux_n)
            back_e = jnp.where(at_west, by * side[i], lon_down(flux_e))
            back_n = jnp.where(at_south, by * line[4 + i], lat_down(flux_n))
            return flux_e - back_e + flux_n - back_n

        t_e = jnp.where(at_east, side[0], lon_up(wt))
        t_w = jnp.where(at_west, side[0], lon_down(wt))
        t_n = jnp.where(at_north, line[0], lat_up(wt))
        t_s = jnp.where(at_south, line[4], lat_down(wt))
        by = DT_ADV / 12.0
        flux_e = uu * (7.0 * (wt + t_e) - (t_w + lon_up(t_e))) * (by * wet_e)
        flux_n = vv * (7.0 * (wt + t_n) - (t_s + lat_up(t_n))) * (by * wet_n)
        t_out[at, :] = wet * (tt - spread(flux_e, flux_n, 1, DT_ADV))
        u_out[at, :] = wet * (uu + spread(face_e * (lon_up(uu) - uu), face_n * (lat_up(uu) - uu), 2, DT_VISC))
        v_out[at, :] = wet * (vv + spread(face_e * (lon_up(vv) - vv), face_n * (lat_up(vv) - vv), 3, DT_VISC))
        return carry

    per = NZ // CHUNKS
    copies = []
    for c in range(CHUNKS):
        lax.fori_loop(c * per, (c + 1) * per, body, 0, unroll=FIELD_UNROLL)
        at = pl.ds(c * per * NR, per * NR)
        for i, (src, dst) in enumerate(((t_out, t_hbm), (u_out, u_hbm), (v_out, v_hbm))):
            copy = pltpu.make_async_copy(src.at[at], dst.at[at], sems.at[c, i])
            copy.start()
            copies.append(copy)
    for copy in copies:
        copy.wait()


def shared_sum(values, axes, count):
    spread = jnp.broadcast_to(values[None], (count,) + values.shape)
    return jnp.sum(lax.all_to_all(spread, axes, 0, 0), axis=0)


def local(tracer, east_vel, north_vel, viscosity, land_sea, thickness, surface, surface_diag, precond_kernel):
    flat = (NZ * NR, NC)
    u, v, vi, w, t = (x.reshape(flat) for x in (east_vel, north_vel, viscosity, land_sea, tracer))
    block = NZ * NR * NC * 4
    lon, a, b = call(
        fetch_kernel,
        [(6, NR, NC), (4, HALF, NC), (4, HALF, NC)],
        [HBM] * 4 + [VM] * 2,
        20 * NZ * NR * NC,
        5 * block,
        [pltpu.VMEM(flat, jnp.float32)] * 3
        + [pltpu.VMEM(flat, jnp.int32), pltpu.SemaphoreType.DMA((CHUNKS, 4))],
        vmem=FETCH_VMEM,
    )(u, v, vi, w, surface, surface_diag)
    from_b = lax.ppermute(b, LAT, SWAP_B)
    from_a = lax.ppermute(a, LAT, SWAP_A)
    lon_b = lax.ppermute(lon, LON, SWAP_B)
    lon_a = lax.ppermute(lon, LON, SWAP_A)
    inner, lon2, a2, b2 = call(
        inner_kernel,
        [(2, NR, NC), (2, NR, NC), (8, HALF, NC), (8, HALF, NC)],
        [SM] + [VM] * 5,
        40 * NZ * NR * NC,
        4 * block,
    )(thickness, t, u, v, vi, w)
    th_lane = jnp.repeat(thickness, 2)[None]
    th_row = jnp.broadcast_to(thickness[:, None], (NZ, NC))
    (msg,) = call(join_kernel, [(MSG, NC)], [VM] * 11, 10**6, 10**6)(
        inner, lon, lon_a, lon_b, lon2, a2, from_a, b2, from_b, th_lane, th_row
    )
    msg_b = lax.ppermute(msg, LON, SWAP_B)
    msg_a = lax.ppermute(msg, LON, SWAP_A)
    from_b2 = lax.ppermute(b2, LAT, SWAP_B)
    from_a2 = lax.ppermute(a2, LAT, SWAP_A)
    wide = (NR, 2 * NC)
    rest, dg, edge, side_a, side_b = call(
        side_kernel, [wide, wide, (8, 2 * NC), wide, wide], [VM] * 6, 10**6, 10**5
    )(msg, msg_a, msg_b, lon, lon_a, lon_b)
    got_b = lax.ppermute(side_b, LAT, SWAP_B)
    got_a = lax.ppermute(side_a, LAT, SWAP_A)
    t_new, u_new, v_new = call(
        field_kernel,
        [flat] * 3,
        [VM] * 15,
        120 * NZ * NR * NC,
        8 * block,
        [pltpu.VMEM(flat, jnp.float32)] * 3
        + [
            pltpu.VMEM((4, NR, NC), jnp.float32),
            pltpu.VMEM((8, NZ, NC), jnp.float32),
            pltpu.SemaphoreType.DMA((CHUNKS, 3)),
        ],
        HBM,
    )(t, u, v, vi, w, lon, lon_a, lon_b, msg, msg_a, msg_b, from_a, from_a2, from_b, from_b2)
    vecs, dots = call(
        solve_kernel, [(3, NR, NC), (8, NC)], [SM] + [VM] * 5, 10**6, 10**5
    )(precond_kernel, rest, dg, edge, got_a, got_b)
    dots = shared_sum(dots, ("x", "y", "c"), 32)
    dots = shared_sum(dots, ("zl", "zh"), 8)
    (surface_new,) = call(step_kernel, [(NR, NC)], [VM] * 3, 10**5, 10**4)(dots, vecs, surface)
    shape = (NZ, NR, NC)
    return t_new.reshape(shape), u_new.reshape(shape), v_new.reshape(shape), surface_new


def solution(mesh):
    sizes = dict(mesh.shape)
    assert sizes == {"lon": 16, "lat": 16} and tuple(mesh.axis_names) == ("lon", "lat")
    fine = Mesh(mesh.devices.reshape(2, 4, 2, 4, 4), ("zl", "x", "c", "y", "zh"))
    deep = P(None, LAT, LON)
    flat = P(LAT, LON)
    return jax.shard_map(
        local,
        mesh=fine,
        in_specs=(deep,) * 5 + (P(), flat, flat, P()),
        out_specs=(deep, deep, deep, flat),
        check_vma=False,
    )
```

time: 78.3 us -> 67.4 us (0.86)
  blocking collectives: 14.9 us -> 0 us
  waiting for transfers between devices: 4.36 us -> 15.4 us
  local copies, waits for them, and re-layouts: 10.4 us -> 3.24 us
  starting transfers between devices: 29.2 us -> 30.7 us
  Pallas kernels: 16.2 us -> 15.1 us
    all_to_all x1 -> x0, blocking collectives: 14.9 us -> none  [shared_sum(): return jnp.sum(lax.all_to_all(spread, axes, 0, 0), axis=0)]
    unnamed x38 -> x24, local copies, waits for them, and re-layouts: 9.5 us -> 1.69 us
    all_to_all x1 -> x2, waiting for transfers between devices: 0.01 us -> 6.42 us  [shared_sum(): return jnp.sum(lax.all_to_all(spread, axes, 0, 0), axis=0)]
    all_to_all x1 -> x2, starting transfers between devices: 5.13 us -> 11.5 us  [shared_sum(): return jnp.sum(lax.all_to_all(spread, axes, 0, 0), axis=0)]
    ppermute x1, starting transfers between devices: 4.8 us -> 1.28 us  [local(): got_b = lax.ppermute(side_b, LAT, SWAP_B)]
    ppermute x2 -> x4, waiting for transfers between devices: 0.84 us -> 3.39 us  [the longest x1 2.52 us: local(): msg_b = lax.ppermute(msg, LON, SWAP_B)]
    ppermute x1, waiting for transfers between devices: 0.01 us -> 2.2 us  [local(): got_a = lax.ppermute(side_a, LAT, SWAP_A)]
    ppermute x1, waiting for transfers between devices: 1.5 us -> 0.01 us  [local(): from_b = lax.ppermute(b, LAT, SWAP_B)]
  transfers between devices with their start and end apart: 9 -> 12, of which waited for: 3 -> 6; matrix products, arithmetic and copies ran while one was open for 0% -> 3% of each run, Pallas kernels for 14% -> 13%
where the time goes in v2:
time: 67.4 us; the launch traced here: 67.1 us
  starting transfers between devices  30.7 us (46%)
  waiting for transfers between devices  15.4 us (23%)
  Pallas kernels  15.1 us (22%)
  local copies, waits for them, and re-layouts  3.24 us (5%)
  other arithmetic  1.71 us (3%)
  between operations  0.85 us (1%)
    all_to_all x2, starting transfers between devices, shared_sum(): return jnp.sum(lax.all_to_all(spread, axes, 0, 0), axis=0)  11.5 us
    ppermute x1, starting transfers between devices, local(): from_b = lax.ppermute(b, LAT, SWAP_B)  6.65 us
    all_to_all x2, waiting for transfers between devices, shared_sum(): return jnp.sum(lax.all_to_all(spread, axes, 0, 0), axis=0)  6.42 us
    pallas_call x1, Pallas kernels, local(): call(field_kernel, [flat] * 3, [VM] * 15, 120 * NZ * NR * NC, 8 * block,...  5.56 us
    pallas_call x1, Pallas kernels, local(): call(fetch_kernel, [(6, NR, NC), (4, HALF, NC), (4, HALF, NC)], [HBM] * 4...  3.91 us
    ppermute x1, starting transfers between devices, local(): from_a = lax.ppermute(a, LAT, SWAP_A)  3.91 us
    ppermute x1, waiting for transfers between devices, local(): got_b = lax.ppermute(side_b, LAT, SWAP_B)  3.42 us
    pallas_call x1, Pallas kernels, local(): call(inner_kernel, [(2, NR, NC), (2, NR, NC), (8, HALF, NC), (8, HALF, NC...  3.24 us
  transfers between devices with their start and end apart: 12, of which 6 were waited for; matrix products, arithmetic and copies ran while one was open for 3% of the time, Pallas kernels for 13%

profile of v2, /device:TPU:1, one launch (start us, length us, event | category | flops | bytes accessed | tf_op | source)
XLA Modules:
  0.0 67.1 jit_solution(6511509041562781911)
XLA Ops:
  0.6 0.0 copy-start
  0.6 0.0 copy-start.1
  0.7 0.0 copy-start.2
  0.7 0.0 copy-start.3
  0.7 3.9 %shard_map.120 = (f32[6,16,128]{2,1,0:T(8,128)}, f32[4,32,128]{2,1,0:T(8,128)}, f32[4,32,128]{2,1,0:T(8,128)}) custom-call(f32[1024,128]{1,0:T(8,128)} %bitcast.8, f32[1024,128]{1,0:T(8,128)} %bitcast.11, f32[1024,128]{1,0:T(8,128)} %bitcast.14, s32[1024,128]{1,0:T(8,128)} %bitcast.17, f32[16,128]{1,0:T(8,128)} %sf.3, f32[16,128]{1,0:T(8,128)} %dg.1), custom_call_target="tpu_custom_call" | custom-call | flops 2621440 | bytes 2621440 | tf_op jit(solution)/shard_map/pallas_call | solution.py:437
  4.6 3.9 %collective-permute-start.2 = (f32[4,32,128]{2,1,0:T(8,128)}, f32[4,32,128]{2,1,0:T(8,128)S(1)}, u32[]{:S(2)}, u32[]{:S(2)}) collective-permute-start(f32[4,32,128]{2,1,0:T(8,128)} %get-tuple-element.25), channel_id=1, source_target_pairs={{0,1},{1,0},{2,3},{3,2},{4,5},{5,4},{6,7},{7,6},{8,9},{9,8},{10,11... | collective-permute-start | bytes 196616 | tf_op jit(solution)/shard_map/ppermute | solution.py:448
  8.5 6.7 %collective-permute-start.3 = (f32[4,32,128]{2,1,0:T(8,128)}, f32[4,32,128]{2,1,0:T(8,128)S(1)}, u32[]{:S(2)}, u32[]{:S(2)}) collective-permute-start(f32[4,32,128]{2,1,0:T(8,128)} %get-tuple-element.27), channel_id=1, source_target_pairs={{0,15},{1,2},{2,1},{3,4},{4,3},{5,6},{6,5},{7,8},{8,7},{9,10},{10,... | collective-permute-start | bytes 196616 | tf_op jit(solution)/shard_map/ppermute | solution.py:447
  15.2 1.2 %collective-permute-start = (f32[6,16,128]{2,1,0:T(8,128)}, f32[6,16,128]{2,1,0:T(8,128)S(1)}, u32[]{:S(2)}, u32[]{:S(2)}) collective-permute-start(f32[6,16,128]{2,1,0:T(8,128)} %get-tuple-element.21.lon), channel_id=1, source_target_pairs={{0,16},{16,0},{32,48},{48,32},{64,80},{80,64},{96,112},{112,96},{1... | collective-permute-start | bytes 147464 | tf_op jit(solution)/shard_map/ppermute | solution.py:450
  16.4 1.1 %collective-permute-start.1 = (f32[6,16,128]{2,1,0:T(8,128)}, f32[6,16,128]{2,1,0:T(8,128)S(1)}, u32[]{:S(2)}, u32[]{:S(2)}) collective-permute-start(f32[6,16,128]{2,1,0:T(8,128)} %get-tuple-element.21.lon), channel_id=1, source_target_pairs={{0,240},{16,32},{32,16},{48,64},{64,48},{80,96},{96,80},{112,128},... | collective-permute-start | bytes 147464 | tf_op jit(solution)/shard_map/ppermute | solution.py:449
  17.5 0.0 copy-done.10
  17.5 0.1 broadcast_in_dim.8
  17.6 0.1 broadcast_in_dim_reshape.3.th_lane
  17.7 0.0 copy-start.4
  17.8 1.0 %copy-done.4 = f32[64,16,128]{2,1,0:T(8,128)S(1)} copy-done((f32[64,16,128]{2,1,0:T(8,128)S(1)}, f32[64,16,128]{2,1,0:T(8,128)}, u32[]{:S(2)}) %copy-start.4) | copy-done | bytes 524312
  18.8 3.2 %shard_map.121 = (f32[2,16,128]{2,1,0:T(8,128)S(1)}, f32[2,16,128]{2,1,0:T(8,128)S(1)}, f32[8,32,128]{2,1,0:T(8,128)S(1)}, f32[8,32,128]{2,1,0:T(8,128)S(1)}) custom-call(f32[64]{0:T(128)S(1)} %copy-done.10, f32[1024,128]{1,0:T(8,128)S(1)} %bitcast.20, f32[1024,128]{1,0:T(8,128)S(1)} %bitcast.9, f32[1024,128]{1,0:T(8,128)S(1)} %bitcast.12, ...), custom_call_target="tpu_custom_call" | custom-call | flops 5242880 | bytes 2097152 | tf_op jit(solution)/shard_map/pallas_call | solution.py:451
  22.0 0.0 collective-permute-done.lon_a
  22.1 0.0 collective-permute-done.1.lon_b
  22.1 0.0 collective-permute-done.2.from_a
  22.1 0.0 collective-permute-done.3.from_b
  22.1 0.1 broadcast_in_dim.9.th_row
  22.2 0.2 shard_map.122.msg
  22.4 2.3 %collective-permute-start.4 = (f32[72,128]{1,0:T(8,128)S(1)}, f32[72,128]{1,0:T(8,128)S(1)}, u32[]{:S(2)}, u32[]{:S(2)}) collective-permute-start(f32[72,128]{1,0:T(8,128)S(1)} %shard_map.122.msg), channel_id=1, source_target_pairs={{0,16},{16,0},{32,48},{48,32},{64,80},{80,64},{96,112},{112,96},{1... | collective-permute-start | bytes 110600 | tf_op jit(solution)/shard_map/ppermute | solution.py:464
  24.7 0.0 collective-permute-start.5
  24.7 0.9 %collective-permute-done.4.msg_a = f32[72,128]{1,0:T(8,128)S(1)} collective-permute-done((f32[72,128]{1,0:T(8,128)S(1)}, f32[72,128]{1,0:T(8,128)S(1)}, u32[]{:S(2)}, u32[]{:S(2)}) %collective-permute-start.4) | collective-permute-done | bytes 36896 | tf_op jit(solution)/shard_map/ppermute | solution.py:464
  25.5 2.5 %collective-permute-done.5.msg_b = f32[72,128]{1,0:T(8,128)S(1)} collective-permute-done((f32[72,128]{1,0:T(8,128)S(1)}, f32[72,128]{1,0:T(8,128)S(1)}, u32[]{:S(2)}, u32[]{:S(2)}) %collective-permute-start.5) | collective-permute-done | bytes 36896 | tf_op jit(solution)/shard_map/ppermute | solution.py:463
  28.1 0.1 shard_map.124
  28.2 0.1 collective-permute-start.8
  28.3 1.3 %collective-permute-start.9 = (f32[16,256]{1,0:T(8,128)S(1)}, f32[16,256]{1,0:T(8,128)S(1)}, u32[]{:S(2)}, u32[]{:S(2)}) collective-permute-start(f32[16,256]{1,0:T(8,128)S(1)} %get-tuple-element.35), channel_id=1, source_target_pairs={{0,15},{1,2},{2,1},{3,4},{4,3},{5,6},{6,5},{7,8},{8,7},{9,10},{10,... | collective-permute-start | bytes 49160 | tf_op jit(solution)/shard_map/ppermute | solution.py:471
  29.5 2.2 %collective-permute-done.8.from_a = f32[16,256]{1,0:T(8,128)S(1)} collective-permute-done((f32[16,256]{1,0:T(8,128)S(1)}, f32[16,256]{1,0:T(8,128)S(1)}, u32[]{:S(2)}, u32[]{:S(2)}) %collective-permute-start.8) | collective-permute-done | bytes 16416 | tf_op jit(solution)/shard_map/ppermute | solution.py:472
  31.7 3.4 %collective-permute-done.9.from_b = f32[16,256]{1,0:T(8,128)S(1)} collective-permute-done((f32[16,256]{1,0:T(8,128)S(1)}, f32[16,256]{1,0:T(8,128)S(1)}, u32[]{:S(2)}, u32[]{:S(2)}) %collective-permute-start.9) | collective-permute-done | bytes 16416 | tf_op jit(solution)/shard_map/ppermute | solution.py:471
  35.2 0.0 copy-done.11
  35.2 1.4 %shard_map.125 = (f32[3,16,128]{2,1,0:T(8,128)S(1)}, f32[8,128]{1,0:T(8,128)S(1)}) custom-call(f32[5,5]{1,0:T(8,128)S(1)} %copy-done.11, f32[16,256]{1,0:T(8,128)S(1)} %get-tuple-element.31.rest, f32[16,256]{1,0:T(8,128)S(1)} %get-tuple-element.32.dg, f32[8,256]{1,0:T(8,128)S(1)} %get-tuple-element.33.edge, f32[16,256]{1,0:T(8,128)S(1)} %collective-permute-done.8.from_a, ...), custom_call_target="tpu_custom_call" | custom-call | flops 1000000 | bytes 100000 | tf_op jit(solution)/shard_map/pallas_call | solution.py:487
  36.5 0.6 copy-done.8
  37.1 0.7 broadcast_in_dim.10
  37.8 7.5 %all-to-all-start = ((f32[32,8,128]{2,1,0:T(8,128)}), f32[32,8,128]{2,1,0:T(8,128)}, u32[]{:S(2)}, u32[]{:S(2)}) async-start(f32[32,8,128]{2,1,0:T(8,128)} %broadcast_in_dim.10), calls=%async_computation | async-start | bytes 262144 | tf_op jit(solution)/shard_map/all_to_all | solution.py:430
  45.3 0.5 collective-permute-start.6
  45.8 2.1 %collective-permute-start.7 = (f32[8,32,128]{2,1,0:T(8,128)S(1)}, f32[8,32,128]{2,1,0:T(8,128)S(1)}, u32[]{:S(2)}, u32[]{:S(2)}) collective-permute-start(f32[8,32,128]{2,1,0:T(8,128)S(1)} %get-tuple-element.26.b2), channel_id=1, source_target_pairs={{0,15},{1,2},{2,1},{3,4},{4,3},{5,6},{6,5},{7,8},{8,7},{9,10},{10,... | collective-permute-start | bytes 393224 | tf_op jit(solution)/shard_map/ppermute | solution.py:465
  48.0 5.3 %all-to-all-done = f32[32,8,128]{2,1,0:T(8,128)} async-done(((f32[32,8,128]{2,1,0:T(8,128)}), f32[32,8,128]{2,1,0:T(8,128)}, u32[]{:S(2)}, u32[]{:S(2)}) %all-to-all-start) | async-done | bytes 131104 | tf_op jit(solution)/shard_map/all_to_all | solution.py:430
  53.3 0.9 %reduce_sum.18 = f32[8,128]{1,0:T(8,128)S(1)} reduce(f32[32,8,128]{2,1,0:T(8,128)} %all-to-all-done, f32[]{:T(128)} %constant.0.clone.1), dimensions={0}, to_apply=%region_0.0 | reduce | flops 31744 | bytes 135172 | tf_op jit(solution)/shard_map/reduce_sum | solution.py:430
  54.3 0.6 broadcast_in_dim.11
  54.9 3.9 %all-to-all-start.1 = ((f32[8,8,128]{2,1,0:T(8,128)}), f32[8,8,128]{2,1,0:T(8,128)}, u32[]{:S(2)}, u32[]{:S(2)}) async-start(f32[8,8,128]{2,1,0:T(8,128)} %broadcast_in_dim.11), calls=%async_computation.1 | async-start | bytes 65536 | tf_op jit(solution)/shard_map/all_to_all | solution.py:430
  58.8 0.0 collective-permute-done.6.from_a2
  58.8 0.0 collective-permute-done.7.from_b2
  58.9 5.6 %shard_map.123 = (f32[1024,128]{1,0:T(8,128)}, f32[1024,128]{1,0:T(8,128)}, f32[1024,128]{1,0:T(8,128)}) custom-call(f32[1024,128]{1,0:T(8,128)S(1)} %bitcast.21, f32[1024,128]{1,0:T(8,128)S(1)} %bitcast.10, f32[1024,128]{1,0:T(8,128)S(1)} %bitcast.13, f32[1024,128]{1,0:T(8,128)S(1)} %bitcast.16, s32[1024,128]{1,0:T(8,128)S(1)} %bitcast.19, ...), custom_call_target="tpu_custom_call" | custom-call | flops 15728640 | bytes 4194304 | tf_op jit(solution)/shard_map/pallas_call | solution.py:473
  64.4 0.0 copy-start.7
  64.5 1.1 %all-to-all-done.1 = f32[8,8,128]{2,1,0:T(8,128)} async-done(((f32[8,8,128]{2,1,0:T(8,128)}), f32[8,8,128]{2,1,0:T(8,128)}, u32[]{:S(2)}, u32[]{:S(2)}) %all-to-all-start.1) | async-done | bytes 32800 | tf_op jit(solution)/shard_map/all_to_all | solution.py:430
  65.5 0.8 %reduce_sum.19.dots = f32[8,128]{1,0:T(8,128)S(1)} reduce(f32[8,8,128]{2,1,0:T(8,128)} %all-to-all-done.1, f32[]{:T(128)} %constant.0.clone.1), dimensions={0}, to_apply=%region_1.0 | reduce | flops 7168 | bytes 36868 | tf_op jit(solution)/shard_map/reduce_sum | solution.py:430
  66.3 0.8 %shard_map.126 = f32[16,128]{1,0:T(8,128)} custom-call(f32[8,128]{1,0:T(8,128)S(1)} %reduce_sum.19.dots, f32[3,16,128]{2,1,0:T(8,128)S(1)} %copy-done.9, f32[16,128]{1,0:T(8,128)S(1)} %copy-done.7), custom_call_target="tpu_custom_call" | custom-call | flops 100000 | bytes 10000 | tf_op jit(solution)/shard_map/pallas_call | solution.py:492
  (14 shorter events, 0.0 us)
Async XLA Ops:
  0.6 17.1 %copy-start = (f32[64,16,128]{2,1,0:T(8,128)S(1)}, f32[64,16,128]{2,1,0:T(8,128)}, u32[]{:S(2)}) copy-start(f32[64,16,128]{2,1,0:T(8,128)} %param.10) | copy-start | bytes 1572868
  0.6 17.1 %copy-start.1 = (f32[64,16,128]{2,1,0:T(8,128)S(1)}, f32[64,16,128]{2,1,0:T(8,128)}, u32[]{:S(2)}) copy-start(f32[64,16,128]{2,1,0:T(8,128)} %param.11) | copy-start | bytes 1572868
  0.7 17.1 %copy-start.2 = (f32[64,16,128]{2,1,0:T(8,128)S(1)}, f32[64,16,128]{2,1,0:T(8,128)}, u32[]{:S(2)}) copy-start(f32[64,16,128]{2,1,0:T(8,128)} %param.12) | copy-start | bytes 1572868
  0.7 17.1 %copy-start.3 = (s32[64,16,128]{2,1,0:T(8,128)S(1)}, s32[64,16,128]{2,1,0:T(8,128)}, u32[]{:S(2)}) copy-start(s32[64,16,128]{2,1,0:T(8,128)} %param.13) | copy-start | bytes 1572868
  4.6 17.5 %collective-permute-start.2 = (f32[4,32,128]{2,1,0:T(8,128)}, f32[4,32,128]{2,1,0:T(8,128)S(1)}, u32[]{:S(2)}, u32[]{:S(2)}) collective-permute-start(f32[4,32,128]{2,1,0:T(8,128)} %get-tuple-element.25), channel_id=1, source_target_pairs={{0,1},{1,0},{2,3},{3,2},{4,5},{5,4},{6,7},{7,6},{8,9},{9,8},{10,11... | collective-permute-start | bytes 196616 | tf_op jit(solution)/shard_map/ppermute | solution.py:448
  8.5 9.0 %copy-start.10 = (f32[64]{0:T(128)S(1)}, f32[64]{0:T(128)}, u32[]{:S(2)}) copy-start(f32[64]{0:T(128)} %thick.1) | copy-start | bytes 772
  8.5 13.6 %collective-permute-start.3 = (f32[4,32,128]{2,1,0:T(8,128)}, f32[4,32,128]{2,1,0:T(8,128)S(1)}, u32[]{:S(2)}, u32[]{:S(2)}) collective-permute-start(f32[4,32,128]{2,1,0:T(8,128)} %get-tuple-element.27), channel_id=1, source_target_pairs={{0,15},{1,2},{2,1},{3,4},{4,3},{5,6},{6,5},{7,8},{8,7},{9,10},{10,... | collective-permute-start | bytes 196616 | tf_op jit(solution)/shard_map/ppermute | solution.py:447
  15.2 6.9 %collective-permute-start = (f32[6,16,128]{2,1,0:T(8,128)}, f32[6,16,128]{2,1,0:T(8,128)S(1)}, u32[]{:S(2)}, u32[]{:S(2)}) collective-permute-start(f32[6,16,128]{2,1,0:T(8,128)} %get-tuple-element.21.lon), channel_id=1, source_target_pairs={{0,16},{16,0},{32,48},{48,32},{64,80},{80,64},{96,112},{112,96},{1... | collective-permute-start | bytes 147464 | tf_op jit(solution)/shard_map/ppermute | solution.py:450
  16.4 5.7 %collective-permute-start.1 = (f32[6,16,128]{2,1,0:T(8,128)}, f32[6,16,128]{2,1,0:T(8,128)S(1)}, u32[]{:S(2)}, u32[]{:S(2)}) collective-permute-start(f32[6,16,128]{2,1,0:T(8,128)} %get-tuple-element.21.lon), channel_id=1, source_target_pairs={{0,240},{16,32},{32,16},{48,64},{64,48},{80,96},{96,80},{112,128},... | collective-permute-start | bytes 147464 | tf_op jit(solution)/shard_map/ppermute | solution.py:449
  17.7 1.0 %copy-start.4 = (f32[64,16,128]{2,1,0:T(8,128)S(1)}, f32[64,16,128]{2,1,0:T(8,128)}, u32[]{:S(2)}) copy-start(f32[64,16,128]{2,1,0:T(8,128)} %param.9) | copy-start | bytes 1572868
  18.8 3.4 %copy-start.6 = (f32[6,16,128]{2,1,0:T(8,128)S(1)}, f32[6,16,128]{2,1,0:T(8,128)}, u32[]{:S(2)}) copy-start(f32[6,16,128]{2,1,0:T(8,128)} %get-tuple-element.21.lon) | copy-start | bytes 147460
  22.2 13.0 %copy-start.11 = (f32[5,5]{1,0:T(8,128)S(1)}, f32[5,5]{1,0:T(8,128)}, u32[]{:S(2)}) copy-start(f32[5,5]{1,0:T(8,128)} %pc.1) | copy-start | bytes 304
  22.3 36.5 %copy-start.5 = (f32[64,16,128]{2,1,0:T(8,128)S(1)}, f32[64,16,128]{2,1,0:T(8,128)}, u32[]{:S(2)}) copy-start(f32[64,16,128]{2,1,0:T(8,128)} %param.9) | copy-start | bytes 1572868
  22.4 3.2 %collective-permute-start.4 = (f32[72,128]{1,0:T(8,128)S(1)}, f32[72,128]{1,0:T(8,128)S(1)}, u32[]{:S(2)}, u32[]{:S(2)}) collective-permute-start(f32[72,128]{1,0:T(8,128)S(1)} %shard_map.122.msg), channel_id=1, source_target_pairs={{0,16},{16,0},{32,48},{48,32},{64,80},{80,64},{96,112},{112,96},{1... | collective-permute-start | bytes 110600 | tf_op jit(solution)/shard_map/ppermute | solution.py:464
  24.7 3.4 %collective-permute-start.5 = (f32[72,128]{1,0:T(8,128)S(1)}, f32[72,128]{1,0:T(8,128)S(1)}, u32[]{:S(2)}, u32[]{:S(2)}) collective-permute-start(f32[72,128]{1,0:T(8,128)S(1)} %shard_map.122.msg), channel_id=1, source_target_pairs={{0,240},{16,32},{32,16},{48,64},{64,48},{80,96},{96,80},{112,128},... | collective-permute-start | bytes 110600 | tf_op jit(solution)/shard_map/ppermute | solution.py:463
  28.2 3.6 %collective-permute-start.8 = (f32[16,256]{1,0:T(8,128)S(1)}, f32[16,256]{1,0:T(8,128)S(1)}, u32[]{:S(2)}, u32[]{:S(2)}) collective-permute-start(f32[16,256]{1,0:T(8,128)S(1)} %get-tuple-element.34), channel_id=1, source_target_pairs={{0,1},{1,0},{2,3},{3,2},{4,5},{5,4},{6,7},{7,6},{8,9},{9,8},{10,11... | collective-permute-start | bytes 49160 | tf_op jit(solution)/shard_map/ppermute | solution.py:472
  28.3 6.9 %collective-permute-start.9 = (f32[16,256]{1,0:T(8,128)S(1)}, f32[16,256]{1,0:T(8,128)S(1)}, u32[]{:S(2)}, u32[]{:S(2)}) collective-permute-start(f32[16,256]{1,0:T(8,128)S(1)} %get-tuple-element.35), channel_id=1, source_target_pairs={{0,15},{1,2},{2,1},{3,4},{4,3},{5,6},{6,5},{7,8},{8,7},{9,10},{10,... | collective-permute-start | bytes 49160 | tf_op jit(solution)/shard_map/ppermute | solution.py:471
  36.5 0.6 copy-start.8
  37.8 15.5 %all-to-all-start = ((f32[32,8,128]{2,1,0:T(8,128)}), f32[32,8,128]{2,1,0:T(8,128)}, u32[]{:S(2)}, u32[]{:S(2)}) async-start(f32[32,8,128]{2,1,0:T(8,128)} %broadcast_in_dim.10), calls=%async_computation | async-start | bytes 262144 | tf_op jit(solution)/shard_map/all_to_all | solution.py:430
  45.3 13.5 %collective-permute-start.6 = (f32[8,32,128]{2,1,0:T(8,128)S(1)}, f32[8,32,128]{2,1,0:T(8,128)S(1)}, u32[]{:S(2)}, u32[]{:S(2)}) collective-permute-start(f32[8,32,128]{2,1,0:T(8,128)S(1)} %get-tuple-element.24.a2), channel_id=1, source_target_pairs={{0,1},{1,0},{2,3},{3,2},{4,5},{5,4},{6,7},{7,6},{8,9},{9,8},{10,11... | collective-permute-start | bytes 393224 | tf_op jit(solution)/shard_map/ppermute | solution.py:466
  45.8 13.0 %collective-permute-start.7 = (f32[8,32,128]{2,1,0:T(8,128)S(1)}, f32[8,32,128]{2,1,0:T(8,128)S(1)}, u32[]{:S(2)}, u32[]{:S(2)}) collective-permute-start(f32[8,32,128]{2,1,0:T(8,128)S(1)} %get-tuple-element.26.b2), channel_id=1, source_target_pairs={{0,15},{1,2},{2,1},{3,4},{4,3},{5,6},{6,5},{7,8},{8,7},{9,10},{10,... | collective-permute-start | bytes 393224 | tf_op jit(solution)/shard_map/ppermute | solution.py:465
  54.9 10.7 %all-to-all-start.1 = ((f32[8,8,128]{2,1,0:T(8,128)}), f32[8,8,128]{2,1,0:T(8,128)}, u32[]{:S(2)}, u32[]{:S(2)}) async-start(f32[8,8,128]{2,1,0:T(8,128)} %broadcast_in_dim.11), calls=%async_computation.1 | async-start | bytes 65536 | tf_op jit(solution)/shard_map/all_to_all | solution.py:430
  64.4 1.9 %copy-start.7 = (f32[16,128]{1,0:T(8,128)S(1)}, f32[16,128]{1,0:T(8,128)}, u32[]{:S(2)}) copy-start(f32[16,128]{1,0:T(8,128)} %sf.3) | copy-start | bytes 24580
  64.4 1.9 %copy-start.9 = (f32[3,16,128]{2,1,0:T(8,128)S(1)}, f32[3,16,128]{2,1,0:T(8,128)}, u32[]{:S(2)}) copy-start(f32[3,16,128]{2,1,0:T(8,128)} %copy-done.8) | copy-start | bytes 73732

commit v3 on v2

v3 whole, which is shorter than its diff:
```python
import jax
import jax.numpy as jnp
from jax import lax
from jax.experimental import pallas as pl
from jax.experimental.pallas import tpu as pltpu
from jax.sharding import Mesh
from jax.sharding import PartitionSpec as P

DT_ADV = 0.25
DT_VISC = 0.2
TAU = 0.05
SHIFTS = (0.3, 1.3)

LON = ("zl", "x", "c")
LAT = ("y", "zh")
NZ, NR, NC = 64, 16, 128
SWAP_A = [(i, i ^ 1) for i in range(16)]
SWAP_B = [(i, (i + 1) % 16 if i % 2 else (i - 1) % 16) for i in range(16)]

VM = pl.BlockSpec(memory_space=pltpu.VMEM)
SM = pl.BlockSpec(memory_space=pltpu.SMEM)
HBM = pl.BlockSpec(memory_space=pltpu.HBM)
FETCH_VMEM = 53.5
FETCH_UNROLL = 4


def call(kernel, outs, specs, flops, nbytes, scratch=(), place=VM, vmem=4):
    return pl.pallas_call(
        kernel,
        out_shape=[jax.ShapeDtypeStruct(s, jnp.float32) for s in outs],
        in_specs=specs,
        out_specs=place if isinstance(place, list) else [place] * len(outs),
        scratch_shapes=list(scratch),
        compiler_params=pltpu.CompilerParams(vmem_limit_bytes=int(vmem * 1024 * 1024)),
        cost_estimate=pl.CostEstimate(flops=flops, bytes_accessed=nbytes, transcendentals=0),
    )


def lane_of(shape):
    return lax.broadcasted_iota(jnp.int32, shape, len(shape) - 1)


def row_of(shape):
    return lax.broadcasted_iota(jnp.int32, shape, len(shape) - 2)


def even_lon():
    return lax.axis_index("c") == 0


def even_lat():
    return lax.axis_index("zh") % 2 == 0


def lat_index():
    return lax.axis_index("y") * 4 + lax.axis_index("zh")


def b_exists():
    lat = lat_index()
    return jnp.where(jnp.logical_or(lat == 0, lat == 15), 0.0, 1.0).astype(jnp.float32)


HALF = NZ // 2
CHUNKS = 4


def halves():
    mine = jnp.where(even_lat(), 0, HALF)
    return pl.multiple_of(mine, HALF), pl.multiple_of(HALF - mine, HALF)


def edge_row(ref, north, inwards, first, count):
    if isinstance(north, bool):
        row = NR - 1 - inwards if north else inwards
    else:
        row = jnp.where(north, NR - 1 - inwards, inwards)
    return ref[pl.ds(first * NR + row, count, stride=NR), :].astype(jnp.float32)


def pipeline(copies, body, acc, unroll):
    per = NZ // CHUNKS

    def start(c, carry):
        for copy in copies(c):
            copy.start()
        return carry

    def chunk(c, carry):
        for copy in copies(c):
            copy.wait()
        return lax.fori_loop(0, per, lambda i, x: body(c * per + i, x), carry, unroll=unroll)

    lax.fori_loop(0, CHUNKS, start, 0)
    return lax.fori_loop(0, CHUNKS, chunk, acc)


def chunk_copies(pairs, sems):
    span = NZ * NR // CHUNKS

    def copies(c):
        at = pl.ds(pl.multiple_of(c * span, span), span)
        return [
            pltpu.make_async_copy(src.at[at], dst.at[at], sems.at[c, i])
            for i, (src, dst) in enumerate(pairs)
        ]

    return copies


def level(k):
    return pl.ds(pl.multiple_of(k * NR, NR), NR)


def fetch_kernel(
    thick_hbm, u, v, vi, land, lon_out, a_out, b_out, late_a, late_b, out, th_out, uo, vo, vio, lo, thick, sems, th_sem
):
    lane, row = lane_of((NR, NC)), row_of((NR, NC))
    pair = lane // 2
    up = lambda x: pltpu.roll(x, NC - 1, 1)
    north_of = lambda x: pltpu.roll(x, NR - 1, 0)

    def body(k, acc):
        at = level(k)
        wet, uu, vv, visc = lo[at, :].astype(jnp.float32), uo[at, :], vo[at, :], vio[at, :]
        mine = pair == k
        packed = tuple(
            jnp.where(mine, pltpu.roll(x, 2 * k + 1, 1), old)
            for x, old in zip((uu, vv, visc, wet), acc[:4])
        )
        th = jnp.full((1, NC), thick[k], jnp.float32)
        th_out[pl.ds(k, 1), :] = th
        own = wet * th
        half = 0.5 * own
        east = (visc + up(visc)) * (half * up(wet))
        north = (visc + north_of(visc)) * (half * north_of(wet))
        return packed + (
            acc[4] + own * uu,
            acc[5] + east * (up(uu) - uu),
            acc[6] + north * (north_of(uu) - uu),
            acc[7] + own * vv,
            acc[8] + east * (up(vv) - vv),
            acc[9] + north * (north_of(vv) - vv),
            jnp.where(mine[:1], th, acc[10]),
        )

    thick_copy = pltpu.make_async_copy(thick_hbm, thick, th_sem)
    thick_copy.start()
    copies = chunk_copies(((u, uo), (v, vo), (vi, vio), (land, lo)), sems)
    thick_copy.wait()
    zero = jnp.zeros((NR, NC), jnp.float32)
    acc = pipeline(copies, body, (zero,) * 10 + (zero[:1],), FETCH_UNROLL)
    for i in range(4):
        lon_out[i] = acc[i]
    th_out[NZ:, :] = jnp.broadcast_to(acc[10], (8, NC))
    for i in range(2):
        east = jnp.where(lane == NC - 1, 0.0, acc[3 * i + 5])
        north = jnp.where(row == NR - 1, 0.0, acc[3 * i + 6])
        out[i] = acc[3 * i + 4] + DT_VISC * (
            east - pltpu.roll(east, 1, 1) + north - pltpu.roll(north, 1, 0)
        )
    even = even_lat()
    mine, theirs = halves()
    for north, first, rest in ((even, a_out, late_a), (jnp.logical_not(even), b_out, late_b)):
        for i, ref in enumerate((uo, vo, vio, lo)):
            first[i] = edge_row(ref, north, 0, mine, HALF)
            rest[i] = edge_row(ref, north, 0, theirs, HALF)


def late_kernel(pc, t, land, late_a, late_b, lon_out, a_out, b_out, pc_out, to, lo, sems):
    lane = lane_of((NR, NC))
    pair = lane // 2
    half_lane = lane < NC // 2

    def body(k, acc):
        at = level(k)
        first = to[at, :] * lo[at, :].astype(jnp.float32)
        inner = jnp.where(half_lane, pltpu.roll(first, NC - 1, 1), pltpu.roll(first, 1, 1))
        mine = pair == k
        return tuple(
            jnp.where(mine, pltpu.roll(x, 2 * k + 1, 1), old)
            for x, old in zip((first, 7.0 * first - inner), acc)
        )

    copies = chunk_copies(((t, to), (land, lo)), sems)
    acc = pipeline(copies, body, (jnp.zeros((NR, NC), jnp.float32),) * 2, 8)
    lon_out[0] = acc[0]
    lon_out[1] = acc[1]
    for i in range(25):
        pc_out[i : i + 1, :] = jnp.full((1, 2 * NC), pc[i // 5, i % 5], jnp.float32)
    even = even_lat()
    for north, src, dst in ((even, late_a, a_out), (jnp.logical_not(even), late_b, b_out)):
        dst[:4] = src[...]
        for i in range(2):
            first, second = (
                edge_row(to, north, n, i * HALF, HALF) * edge_row(lo, north, n, i * HALF, HALF)
                for n in range(2)
            )
            dst[4 + i] = first
            dst[6 + i] = 7.0 * first - second


def lon_sides(first, second):
    even = even_lon()
    return jnp.where(even, first, second), jnp.where(even, second, first)


def beyond(from_a, from_b):
    east, west = lon_sides(from_a, from_b)
    is_east = lane_of((NR, NC)) % 2 == 0
    return jnp.where(is_east, pltpu.roll(east, NC - 1, 1), pltpu.roll(west, 1, 1))


def face_in(own, other):
    face = 0.5 * (own[2] + other[2]) * (own[3] * other[3])
    return face * (other[0] - own[0]), face * (other[1] - own[1])


MSG = 104


def join_kernel(inner, lon, lon_a, lon_b, lon2, a2, from_a, b2, from_b, th, sf, dg, out):
    lane = lane_of((NR, NC))
    own = [lon[i] for i in range(4)]
    other = [beyond(lon_a[i], lon_b[i]) for i in range(4)]
    is_east = lane % 2 == 0
    for i, grad in enumerate(face_in(own, other)):
        grad = grad * th[NZ : NZ + 1, :]
        east = jnp.sum(jnp.where(is_east, grad, 0.0), axis=1, keepdims=True)
        west = jnp.sum(jnp.where(is_east, 0.0, grad), axis=1, keepdims=True)
        add = jnp.where(lane == NC - 1, east, 0.0) + jnp.where(lane == 0, west, 0.0)
        out[NR * i : NR * (i + 1), :] = inner[i] + DT_VISC * add
    _, theirs = halves()
    weight = DT_VISC * th[pl.ds(theirs, HALF), :]
    lat_a = face_in([a2[i] for i in range(4)], [from_a[i] for i in range(4)])
    weight_b = weight * b_exists()
    lat_b = face_in([b2[i] for i in range(4)], [from_b[i] for i in range(4)])
    sums = [jnp.sum(x * weight, axis=0, keepdims=True) for x in lat_a]
    sums += [jnp.sum(x * weight_b, axis=0, keepdims=True) for x in lat_b]
    out[2 * NR : 2 * NR + 8, :] = jnp.concatenate(sums + [jnp.zeros((4, NC), jnp.float32)], axis=0)
    out[40:56, :] = lon2[0]
    out[56:72, :] = lon2[1]
    out[72:88, :] = sf[...]
    out[88:104, :] = dg[...]


def side_kernel(msg, msg_a, msg_b, rest_out, diag_out, edge_out, a_out, b_out):
    def widen(own, first, second):
        east, west = lon_sides(first, second)
        halo = jnp.where(lane_of(own.shape) < NC // 2, east, west)
        return jnp.concatenate([own, halo], axis=1)

    part = lambda lo, hi: widen(msg[lo:hi, :], msg_a[lo:hi, :], msg_b[lo:hi, :])
    te, tn, faces = part(0, NR), part(NR, 2 * NR), part(2 * NR, 2 * NR + 8)
    sf, dg = part(72, 88), part(88, 104)
    row = row_of((NR, 2 * NC))
    even = even_lat()
    north_u, north_v = (jnp.where(even, faces[i : i + 1], faces[i + 2 : i + 3]) for i in range(2))
    south_u, south_v = (jnp.where(even, faces[i + 2 : i + 3], faces[i : i + 1]) for i in range(2))
    at_north, at_south = row == NR - 1, row == 0
    te = te + jnp.where(at_north, north_u, 0.0) + jnp.where(at_south, south_u, 0.0)
    tn = tn + jnp.where(at_north, north_v, 0.0) + jnp.where(at_south, south_v, 0.0)
    east = lambda x: pltpu.roll(x, 2 * NC - 1, 1)
    west = lambda x: pltpu.roll(x, 1, 1)
    north = lambda x: jnp.where(at_north, 0.0, pltpu.roll(x, NR - 1, 0))
    south = lambda x: jnp.where(at_south, 0.0, pltpu.roll(x, 1, 0))
    across = lambda fu, fv: TAU * (fu - west(fu) + fv)
    rest = sf - TAU * (te - west(te) + tn - south(tn))
    rest = rest - ((4.0 + dg) * sf - (east(sf) + west(sf) + north(sf) + south(sf)))
    rest = rest - jnp.where(at_south, TAU * south_v, 0.0)
    rest_out[...] = rest
    diag_out[...] = dg
    first = TAU * tn[NR - 1 :] + sf[NR - 1 :] + across(north_u, north_v)
    second = -TAU * north_v
    to_south = sf[:1] + across(south_u, south_v)
    zero = jnp.zeros((5, 2 * NC), jnp.float32)
    edge_out[...] = jnp.concatenate([first, second, to_south, zero], axis=0)
    msg_north = jnp.concatenate([rest[8:], dg[11:], first, second, zero[:1]], axis=0)
    msg_south = jnp.concatenate([rest[:9], dg[:6], to_south], axis=0)
    a_out[...] = jnp.where(even, msg_north, msg_south)
    b_out[...] = jnp.where(even, msg_south, msg_north)


def solve_kernel(pc, rest, dg, edge, from_a, from_b, v_hbm, dots_out, v_out, sem):
    rows, wide = 3 * NR, 2 * NC
    even = even_lat()
    exists = b_exists()
    msg_a = from_a[...]
    msg_b = from_b[...] * exists
    north = jnp.where(even, msg_a, msg_b)
    south = jnp.where(even, msg_b, msg_a)
    zeros = lambda n: jnp.zeros((n, wide), jnp.float32)
    row = row_of((rows, wide))
    lat = lat_index()
    low = jnp.where(lat == 0, NR, 0)
    high = jnp.where(lat == 15, 2 * NR, 3 * NR)
    inside = jnp.where(jnp.logical_and(row >= low, row < high), 1.0, 0.0).astype(jnp.float32)
    below = jnp.concatenate([zeros(8), south[:7], south[7:8] + edge[2:3]], axis=0)
    above = jnp.concatenate(
        [north[:1] + edge[0:1], north[1:2] + edge[1:2], north[2:9], zeros(7)], axis=0
    )
    own = rest[...] + jnp.concatenate([south[13:15], zeros(13), north[15:]], axis=0)
    res = jnp.concatenate([below, own, above], axis=0) * inside
    diag = 4.0 + jnp.concatenate([zeros(11), south[8:13], dg[...], north[9:15], zeros(10)], axis=0)

    def lon_shift(x, n):
        return x if n == 0 else pltpu.roll(x, (-n) % wide, 1)

    def lat_shift(x, n):
        return x if n == 0 else pltpu.roll(x, (-n) % rows, 0)

    def operate(x):
        near = lon_shift(x, 1) + lon_shift(x, -1) + lat_shift(x, 1) + lat_shift(x, -1)
        return diag * x - near

    def tap(a, b):
        at = 5 * (a + 2) + b + 2
        return pc[at : at + 1, :]

    def precondition(x):
        moved = [lon_shift(x, b) for b in range(-2, 3)]
        total = None
        for a in range(-2, 3):
            line = tap(a, -2) * moved[0]
            for b in range(1, 5):
                line = line + tap(a, b - 2) * moved[b]
            line = lat_shift(line, a)
            total = line if total is None else total + line
        return total * inside

    scale = 1.0 / (5.0 * tap(0, 0))
    p0 = res
    v0 = precondition(p0)
    a0 = operate(v0)
    p1 = (a0 * scale - SHIFTS[0] * p0) * inside
    v1 = precondition(p1)
    a1 = operate(v1)
    p2 = (a1 * scale - SHIFTS[1] * p1) * inside
    v2 = precondition(p2)
    mine = lambda x: x[NR : 2 * NR, :NC]
    half_a2 = mine(diag * v2 - 2.0 * (lon_shift(v2, 1) + lat_shift(v2, 1)))
    v0, v1, v2, a0, a1, r = (mine(x) for x in (v0, v1, v2, a0, a1, p0))
    v_out[0] = v0
    v_out[1] = v1
    v_out[2] = v2
    pairs = ((v0, a0), (v0, a1), (v2, a0), (v1, a1), (v2, a1), (v2, half_a2), (v0, r), (v1, r), (v2, r))
    copy = pltpu.make_async_copy(v_out, v_hbm, sem)
    copy.start()
    lane = lane_of((1, NC))
    line = jnp.zeros((1, NC), jnp.float32)
    for i, (x, y) in enumerate(pairs):
        total = jnp.sum(jnp.sum(x * y, axis=0, keepdims=True), axis=1, keepdims=True)
        line = line + jnp.where(lane == i, total, 0.0)
    dots_out[...] = jnp.broadcast_to(line[None], dots_out.shape)
    copy.wait()


def relay_kernel(got, out, held, spread, sems):
    copy = pltpu.make_async_copy(got, held, sems.at[0])
    copy.start()
    copy.wait()
    spread[...] = jnp.broadcast_to(jnp.sum(held[...], axis=0, keepdims=True), spread.shape)
    copy = pltpu.make_async_copy(spread, out, sems.at[1])
    copy.start()
    copy.wait()


def step_kernel(got, v, sf, out, held, sem):
    copy = pltpu.make_async_copy(got, held, sem)
    copy.start()
    copy.wait()
    line = jnp.sum(held[...], axis=0)
    lane = lane_of((1, NC))
    h00, h01, h02, h11, h12, h22, g0, g1, g2 = (
        jnp.sum(jnp.where(lane == i, line, 0.0), axis=1, keepdims=True) for i in range(9)
    )
    l1 = h01 / h00
    l2 = h02 / h00
    d1 = h11 - l1 * h01
    e12 = h12 - l1 * h02
    l3 = e12 / d1
    d2 = h22 - l2 * h02 - l3 * e12
    y1 = g1 - l1 * g0
    y2 = g2 - l2 * g0 - l3 * y1
    c2 = y2 / d2
    c1 = y1 / d1 - l3 * c2
    c0 = g0 / h00 - l1 * c1 - l2 * c2
    out[...] = sf[...] + c0 * v[0] + c1 * v[1] + c2 * v[2]


def row_masks():
    lane, row = lane_of((NR, NC)), row_of((NR, NC))
    return lane == NC - 1, lane == 0, row == NR - 1, row == 0


def spread_of(packed, lines):
    at_east, at_west, at_north, at_south = row_masks()

    def spread(k, flux_e, flux_n, i):
        side = pltpu.roll(packed[i], NC - 1 - 2 * k, 1)
        north = jnp.broadcast_to(lines[2 * i, pl.ds(k, 1), :], (NR, NC))
        south = jnp.broadcast_to(lines[2 * i + 1, pl.ds(k, 1), :], (NR, NC))
        flux_e = jnp.where(at_east, side, flux_e)
        flux_n = jnp.where(at_north, north, flux_n)
        back_e = jnp.where(at_west, side, pltpu.roll(flux_e, 1, 1))
        back_n = jnp.where(at_south, south, pltpu.roll(flux_n, 1, 0))
        return flux_e - back_e + (flux_n - back_n)

    return spread


def write_out(body, pairs, sems, unroll):
    per = NZ // CHUNKS
    copies = chunk_copies(pairs, sems)

    def chunk(c, carry):
        lax.fori_loop(0, per, lambda i, x: body(c * per + i, x), 0, unroll=unroll)
        for copy in copies(c):
            copy.start()
        return carry

    def finish(c, carry):
        for copy in copies(c):
            copy.wait()
        return carry

    lax.fori_loop(0, CHUNKS, chunk, 0)
    lax.fori_loop(0, CHUNKS, finish, 0)


def velocity_kernel(
    u, v, vi, w, lon, lon_a, lon_b, from_a, from_a2, from_b, from_b2,
    u_hbm, v_hbm, u_out, v_out, packed, lines, sems,
):
    is_east = lane_of((NR, NC)) % 2 == 0
    own = [lon[i] for i in range(4)]
    other = [beyond(lon_a[i], lon_b[i]) for i in range(4)]
    for i, grad in enumerate(face_in(own, other)):
        packed[i] = DT_VISC * jnp.where(is_east, grad, -grad)
    even = even_lat()
    exists = b_exists()
    mine, theirs = halves()
    for first, there_a, there_b in ((mine, from_a2, from_b2), (theirs, from_a, from_b)):
        at = pl.ds(first, HALF)
        for side in range(2):
            use_a = even if side == 0 else jnp.logical_not(even)
            here = [edge_row(ref, side == 0, 0, first, HALF) for ref in (u, v, vi, w)]
            there = [jnp.where(use_a, there_a[i], there_b[i] * exists) for i in range(4)]
            sign = DT_VISC if side == 0 else -DT_VISC
            for i, grad in enumerate(face_in(here, there)):
                lines[2 * i + side, at, :] = sign * grad
    spread = spread_of(packed, lines)
    lon_up = lambda x: pltpu.roll(x, NC - 1, 1)
    lat_up = lambda x: pltpu.roll(x, NR - 1, 0)

    def body(k, carry):
        at = level(k)
        uu, vv, visc = u[at, :], v[at, :], vi[at, :]
        wet = w[at, :].astype(jnp.float32)
        half = wet * (0.5 * DT_VISC)
        face_e = (visc + lon_up(visc)) * (half * lon_up(wet))
        face_n = (visc + lat_up(visc)) * (half * lat_up(wet))
        u_out[at, :] = wet * (uu + spread(k, face_e * (lon_up(uu) - uu), face_n * (lat_up(uu) - uu), 0))
        v_out[at, :] = wet * (vv + spread(k, face_e * (lon_up(vv) - vv), face_n * (lat_up(vv) - vv), 1))
        return carry

    write_out(body, ((u_out, u_hbm), (v_out, v_hbm)), sems, 8)


def tracer_kernel(
    t, u, v, w, lon, lon_a, lon_b, msg, msg_a, msg_b, from_a, from_a2, from_b, from_b2,
    t_hbm, t_out, packed, lines, sems,
):
    is_east = lane_of((NR, NC)) % 2 == 0
    by = DT_ADV / 12.0
    packed[1] = beyond(msg_a[40:56, :], msg_b[40:56, :])
    far = msg[56:72, :] + beyond(msg_a[56:72, :], msg_b[56:72, :])
    speed = jnp.where(is_east, lon[0], beyond(lon_a[0], lon_b[0]))
    packed[0] = speed * far * (by * lon[3] * beyond(lon_a[3], lon_b[3]))
    even = even_lat()
    exists = b_exists()
    mine, theirs = halves()
    for first, there_a, there_b in ((mine, from_a2, from_b2), (theirs, from_a, from_b)):
        at = pl.ds(first, HALF)
        part = first // HALF
        for side in range(2):
            north = side == 0
            use_a = even if north else jnp.logical_not(even)
            wet_here = edge_row(w, north, 0, first, HALF)
            wet_there = jnp.where(use_a, there_a[3], there_b[3] * exists)
            near = edge_row(t, north, 0, first, HALF) * wet_here
            inner = edge_row(t, north, 1, first, HALF) * edge_row(w, north, 1, first, HALF)
            far = jnp.where(use_a, from_a2[6 + part], from_b2[6 + part]) + (7.0 * near - inner)
            if north:
                speed = edge_row(v, True, 0, first, HALF)
            else:
                speed = jnp.where(use_a, there_a[1], there_b[1])
            lines[side, at, :] = speed * far * (by * wet_here * wet_there)
            lines[2 + side, at, :] = jnp.where(use_a, from_a2[4 + part], from_b2[4 + part] * exists)
    spread = spread_of(packed, lines)
    at_east, at_west, at_north, at_south = row_masks()
    lon_up = lambda x: pltpu.roll(x, NC - 1, 1)
    lat_up = lambda x: pltpu.roll(x, NR - 1, 0)

    def body(k, carry):
        at = level(k)
        tt = t[at, :]
        wet = w[at, :].astype(jnp.float32)
        wt = tt * wet
        side = pltpu.roll(packed[1], NC - 1 - 2 * k, 1)
        north = jnp.broadcast_to(lines[2, pl.ds(k, 1), :], (NR, NC))
        south = jnp.broadcast_to(lines[3, pl.ds(k, 1), :], (NR, NC))
        t_e = jnp.where(at_east, side, lon_up(wt))
        t_w = jnp.where(at_west, side, pltpu.roll(wt, 1, 1))
        t_n = jnp.where(at_north, north, lat_up(wt))
        t_s = jnp.where(at_south, south, pltpu.roll(wt, 1, 0))
        part = by * wet
        flux_e = u[at, :] * (7.0 * (wt + t_e) - (t_w + lon_up(t_e))) * (part * lon_up(wet))
        flux_n = v[at, :] * (7.0 * (wt + t_n) - (t_s + lat_up(t_n))) * (part * lat_up(wet))
        t_out[at, :] = wet * (tt - spread(k, flux_e, flux_n, 0))
        return carry

    write_out(body, ((t_out, t_hbm),), sems, 8)


def local(tracer, east_vel, north_vel, viscosity, land_sea, thickness, surface, surface_diag, precond_kernel):
    flat = (NZ * NR, NC)
    u, v, vi, w, t = (x.reshape(flat) for x in (east_vel, north_vel, viscosity, land_sea, tracer))
    block = NZ * NR * NC * 4
    field = pltpu.VMEM(flat, jnp.float32)
    wets = pltpu.VMEM(flat, jnp.int32)
    dma = pltpu.SemaphoreType.DMA
    rows = (4, HALF, NC)
    lon, a, b, late_a, late_b, inner, th = call(
        fetch_kernel,
        [(4, NR, NC), rows, rows, rows, rows, (2, NR, NC), (NZ + 8, NC)],
        [HBM] * 5,
        50 * NZ * NR * NC,
        4 * block,
        [field] * 3 + [wets, pltpu.SMEM((NZ,), jnp.float32), dma((CHUNKS, 4)), dma],
        vmem=FETCH_VMEM,
    )(thickness, u, v, vi, w)
    from_b = lax.ppermute(b, LAT, SWAP_B)
    from_a = lax.ppermute(a, LAT, SWAP_A)
    lon_b = lax.ppermute(lon, LON, SWAP_B)
    lon_a = lax.ppermute(lon, LON, SWAP_A)
    lon2, a2, b2, taps = call(
        late_kernel,
        [(2, NR, NC), (8, HALF, NC), (8, HALF, NC), (32, 2 * NC)],
        [SM] + [HBM] * 2 + [VM] * 2,
        20 * NZ * NR * NC,
        2 * block,
        [field, wets, dma((CHUNKS, 2))],
        vmem=FETCH_VMEM,
    )(precond_kernel, t, w, late_a, late_b)
    (msg,) = call(join_kernel, [(MSG, NC)], [VM] * 12, 10**6, 10**6)(
        inner, lon, lon_a, lon_b, lon2, late_a, from_a, late_b, from_b, th, surface, surface_diag
    )
    msg, a2, b2 = lax.optimization_barrier((msg, a2, b2))
    msg_b = lax.ppermute(msg, LON, SWAP_B)
    msg_a = lax.ppermute(msg, LON, SWAP_A)
    from_b2 = lax.ppermute(b2, LAT, SWAP_B)
    from_a2 = lax.ppermute(a2, LAT, SWAP_A)
    wide = (NR, 2 * NC)
    rest, dg, edge, side_a, side_b = call(
        side_kernel, [wide, wide, (8, 2 * NC), wide, wide], [VM] * 3, 10**6, 10**5
    )(msg, msg_a, msg_b)
    got_b = lax.ppermute(side_b, LAT, SWAP_B)
    got_a = lax.ppermute(side_a, LAT, SWAP_A)
    lat = (from_a, from_a2, from_b, from_b2)
    u_new, v_new = call(
        velocity_kernel,
        [flat] * 2,
        [VM] * 11,
        60 * NZ * NR * NC,
        6 * block,
        [field] * 2
        + [pltpu.VMEM((2, NR, NC), jnp.float32), pltpu.VMEM((4, NZ, NC), jnp.float32), dma((CHUNKS, 2))],
        HBM,
    )(u, v, vi, w, lon, lon_a, lon_b, *lat)
    got_a, got_b, u_new, v_new = lax.optimization_barrier((got_a, got_b, u_new, v_new))
    t_new = call(
        tracer_kernel,
        [flat],
        [VM] * 14,
        60 * NZ * NR * NC,
        5 * block,
        [field, pltpu.VMEM((2, NR, NC), jnp.float32), pltpu.VMEM((4, NZ, NC), jnp.float32), dma((CHUNKS, 1))],
        HBM,
    )(t, u, v, w, lon, lon_a, lon_b, msg, msg_a, msg_b, *lat)[0]
    vecs, dots = call(
        solve_kernel,
        [(3, NR, NC), (32, 1, NC)],
        [VM] * 6,
        10**6,
        10**5,
        [pltpu.VMEM((3, NR, NC), jnp.float32), dma],
        [HBM, VM],
    )(taps, rest, dg, edge, got_a, got_b)
    dots = lax.all_to_all(dots, ("x", "y", "c"), 0, 0)
    dots, t_new = lax.optimization_barrier((dots, t_new))
    (dots,) = call(
        relay_kernel,
        [(8, 1, NC)],
        [HBM],
        10**4,
        10**4,
        [pltpu.VMEM((32, 1, NC), jnp.float32), pltpu.VMEM((8, 1, NC), jnp.float32), dma((2,))],
        HBM,
    )(dots)
    dots = lax.all_to_all(dots, ("zl", "zh"), 0, 0)
    (surface_new,) = call(
        step_kernel,
        [(NR, NC)],
        [HBM] + [VM] * 2,
        10**5,
        10**4,
        [pltpu.VMEM((8, 1, NC), jnp.float32), dma],
    )(dots, vecs, surface)
    shape = (NZ, NR, NC)
    return t_new.reshape(shape), u_new.reshape(shape), v_new.reshape(shape), surface_new


def solution(mesh):
    sizes = dict(mesh.shape)
    assert sizes == {"lon": 16, "lat": 16} and tuple(mesh.axis_names) == ("lon", "lat")
    fine = Mesh(mesh.devices.reshape(2, 4, 2, 4, 4), ("zl", "x", "c", "y", "zh"))
    deep = P(None, LAT, LON)
    flat = P(LAT, LON)
    return jax.shard_map(
        local,
        mesh=fine,
        in_specs=(deep,) * 5 + (P(), flat, flat, P()),
        out_specs=(deep, deep, deep, flat),
        check_vma=False,
    )
```

time: 67.4 us -> 65.4 us (0.970)
  blocking collectives: 0 us -> 9.5 us
  waiting for transfers between devices: 15.4 us -> 6.99 us
  local copies, waits for them, and re-layouts: 3.24 us -> 0.69 us
  other arithmetic: 1.71 us -> 0 us
  Pallas kernels: 15.1 us -> 16.1 us
    all_to_all x0 -> x1, blocking collectives: none -> 9.5 us  [local(): dots = lax.all_to_all(dots, ('zl', 'zh'), 0, 0)]
    ppermute x1, starting transfers between devices: 0.01 us -> 3.58 us  [local(): msg_b = lax.ppermute(msg, LON, SWAP_B)]
    ppermute x1, waiting for transfers between devices: 3.42 us -> 0.34 us  [local(): got_b = lax.ppermute(side_b, LAT, SWAP_B)]
    all_to_all x2 -> x1, waiting for transfers between devices: 6.42 us -> 4.02 us  [local(): dots = lax.all_to_all(dots, ('x', 'y', 'c'), 0, 0)]
    all_to_all x2 -> x1, starting transfers between devices: 11.5 us -> 9.15 us  [local(): dots = lax.all_to_all(dots, ('x', 'y', 'c'), 0, 0)]
    ppermute x1, starting transfers between devices: 2.32 us -> 0.01 us  [local(): msg_a = lax.ppermute(msg, LON, SWAP_A)]
    ppermute x1, waiting for transfers between devices: 2.2 us -> 0.01 us  [local(): got_a = lax.ppermute(side_a, LAT, SWAP_A)]
    reduce_sum x2 -> x0, other arithmetic: 1.71 us -> none  [shared_sum(): return jnp.sum(lax.all_to_all(spread, axes, 0, 0), axis=0)]
  transfers between devices with their start and end apart: 12 -> 11, of which waited for: 6 -> 4; matrix products, arithmetic and copies ran while one was open for 3% -> 0% of each run, Pallas kernels for 13% -> 15%
where the time goes in v3:
time: 65.4 us; the launch traced here: 65.2 us
  starting transfers between devices  31 us (47%)
  Pallas kernels  16.1 us (25%)
  blocking collectives  9.5 us (15%)
  waiting for transfers between devices  6.99 us (11%)
  between operations  0.83 us (1%)
  local copies, waits for them, and re-layouts  0.69 us (1%)
    all_to_all x1, blocking collectives, local(): dots = lax.all_to_all(dots, ('zl', 'zh'), 0, 0)  9.5 us
    all_to_all x1, starting transfers between devices, local(): dots = lax.all_to_all(dots, ('x', 'y', 'c'), 0, 0)  9.15 us
    ppermute x1, starting transfers between devices, local(): from_b = lax.ppermute(b, LAT, SWAP_B)  6.65 us
    pallas_call x1, Pallas kernels, local(): call(fetch_kernel, [(4, NR, NC), rows, rows, rows, rows, (2, NR, NC), (NZ...  4.15 us
    all_to_all x1, waiting for transfers between devices, local(): dots = lax.all_to_all(dots, ('x', 'y', 'c'), 0, 0)  4.02 us
    ppermute x1, starting transfers between devices, local(): from_a = lax.ppermute(a, LAT, SWAP_A)  3.91 us
    ppermute x1, starting transfers between devices, local(): msg_b = lax.ppermute(msg, LON, SWAP_B)  3.58 us
    pallas_call x1, Pallas kernels, local(): call(velocity_kernel, [flat] * 2, [VM] * 11, 60 * NZ * NR * NC, 6 * block...  3.26 us
  transfers between devices with their start and end apart: 11, of which 4 were waited for; matrix products, arithmetic and copies ran while one was open for 0% of the time, Pallas kernels for 15%

profile of v3, /device:TPU:1, one launch (start us, length us, event | category | flops | bytes accessed | tf_op | source)
XLA Modules:
  0.0 65.2 jit_solution(11379600673770680356)
XLA Ops:
  0.6 0.0 copy-start.8
  0.6 0.6 copy-done.8
  1.3 0.0 copy-start.3
  1.3 4.1 %shard_map.120 = (f32[4,16,128]{2,1,0:T(8,128)S(1)}, f32[4,32,128]{2,1,0:T(8,128)S(1)}, f32[4,32,128]{2,1,0:T(8,128)S(1)}, f32[4,32,128]{2,1,0:T(8,128)S(1)}, f3...) custom-call(f32[64]{0:T(128)S(1)} %copy-done.8, f32[1024,128]{1,0:T(8,128)} %bitcast.12, ...), custom_call_target="tpu_custom_call" | custom-call | flops 6553600 | bytes 2097152 | tf_op jit(solution)/shard_map/pallas_call | solution.py:534
  5.4 3.9 %collective-permute-start.2 = (f32[4,32,128]{2,1,0:T(8,128)S(1)}, f32[4,32,128]{2,1,0:T(8,128)S(1)}, u32[]{:S(2)}, u32[]{:S(2)}) collective-permute-start(f32[4,32,128]{2,1,0:T(8,128)S(1)} %get-tuple-element.39), channel_id=1, source_target_pairs={{0,1},{1,0},{2,3},{3,2},{4,5},{5,4},{6,7},{7,6},{8,9},{9,8},{10,11... | collective-permute-start | bytes 196616 | tf_op jit(solution)/shard_map/ppermute | solution.py:544
  9.3 0.0 copy-start.7
  9.4 6.7 %collective-permute-start.3 = (f32[4,32,128]{2,1,0:T(8,128)S(1)}, f32[4,32,128]{2,1,0:T(8,128)S(1)}, u32[]{:S(2)}, u32[]{:S(2)}) collective-permute-start(f32[4,32,128]{2,1,0:T(8,128)S(1)} %get-tuple-element.40), channel_id=1, source_target_pairs={{0,15},{1,2},{2,1},{3,4},{4,3},{5,6},{6,5},{7,8},{8,7},{9,10},{10,... | collective-permute-start | bytes 196616 | tf_op jit(solution)/shard_map/ppermute | solution.py:543
  16.0 2.3 %collective-permute-start.1 = (f32[4,16,128]{2,1,0:T(8,128)S(1)}, f32[4,16,128]{2,1,0:T(8,128)S(1)}, u32[]{:S(2)}, u32[]{:S(2)}) collective-permute-start(f32[4,16,128]{2,1,0:T(8,128)S(1)} %get-tuple-element.37.lon), channel_id=1, source_target_pairs={{0,240},{16,32},{32,16},{48,64},{64,48},{80,96},{96,80},{112,128},... | collective-permute-start | bytes 98312 | tf_op jit(solution)/shard_map/ppermute | solution.py:545
  18.3 1.0 %collective-permute-start = (f32[4,16,128]{2,1,0:T(8,128)S(1)}, f32[4,16,128]{2,1,0:T(8,128)S(1)}, u32[]{:S(2)}, u32[]{:S(2)}) collective-permute-start(f32[4,16,128]{2,1,0:T(8,128)S(1)} %get-tuple-element.37.lon), channel_id=1, source_target_pairs={{0,16},{16,0},{32,48},{48,32},{64,80},{80,64},{96,112},{112,96},{1... | collective-permute-start | bytes 98312 | tf_op jit(solution)/shard_map/ppermute | solution.py:546
  19.3 0.0 copy-done.7
  19.3 0.0 copy-start.5
  19.3 0.0 copy-start.2
  19.4 3.2 %shard_map.121 = (f32[2,16,128]{2,1,0:T(8,128)S(1)}, f32[8,32,128]{2,1,0:T(8,128)S(1)}, f32[8,32,128]{2,1,0:T(8,128)S(1)}, f32[32,256]{1,0:T(8,128)S(1)}) custom-call(f32[5,5]{1,0:T(8,128)S(1)} %copy-done.7, f32[1024,128]{1,0:T(8,128)} %bitcast.20, s32[1024,128]{1,0:T(8,128)} %bitcast.9, f32[4,32,128]{2,1,0:T(8,128)S(1)} %get-tuple-element.33.late_a.a2, ...), custom_call_target="tpu_custom_call" | custom-call | flops 2621440 | bytes 1048576 | tf_op jit(solution)/shard_map/pallas_call | solution.py:547
  22.6 0.0 copy-start
  22.6 0.0 collective-permute-done.1.lon_b
  22.6 0.0 collective-permute-done.lon_a
  22.6 0.0 collective-permute-done.2.from_a
  22.6 0.0 collective-permute-done.3.from_b
  22.6 0.0 copy-done.5
  22.6 0.0 copy-done.6
  22.6 0.2 shard_map.122.msg
  22.8 0.1 collective-permute-start.8
  22.9 1.5 %collective-permute-start.9 = (f32[8,32,128]{2,1,0:T(8,128)S(1)}, f32[8,32,128]{2,1,0:T(8,128)S(1)}, u32[]{:S(2)}, u32[]{:S(2)}) collective-permute-start(f32[8,32,128]{2,1,0:T(8,128)S(1)} %get-tuple-element.51), channel_id=1, source_target_pairs={{0,15},{1,2},{2,1},{3,4},{4,3},{5,6},{6,5},{7,8},{8,7},{9,10},{10,... | collective-permute-start | bytes 393224 | tf_op jit(solution)/shard_map/ppermute | solution.py:562
  24.4 3.6 %collective-permute-start.5 = (f32[104,128]{1,0:T(8,128)S(1)}, f32[104,128]{1,0:T(8,128)S(1)}, u32[]{:S(2)}, u32[]{:S(2)}) collective-permute-start(f32[104,128]{1,0:T(8,128)S(1)} %shard_map.122.msg), channel_id=1, source_target_pairs={{0,240},{16,32},{32,16},{48,64},{64,48},{80,96},{96,80},{112,128},... | collective-permute-start | bytes 159752 | tf_op jit(solution)/shard_map/ppermute | solution.py:560
  28.0 0.0 collective-permute-start.4
  28.0 2.1 %collective-permute-done.5.msg_b = f32[104,128]{1,0:T(8,128)S(1)} collective-permute-done((f32[104,128]{1,0:T(8,128)S(1)}, f32[104,128]{1,0:T(8,128)S(1)}, u32[]{:S(2)}, u32[]{:S(2)}) %collective-permute-start.5) | collective-permute-done | bytes 53280 | tf_op jit(solution)/shard_map/ppermute | solution.py:560
  30.1 0.0 collective-permute-done.4.msg_a
  30.1 0.1 shard_map.123
  30.2 0.1 collective-permute-start.6
  30.3 0.0 copy-start.4
  30.3 2.7 %collective-permute-start.7 = (f32[16,256]{1,0:T(8,128)S(1)}, f32[16,256]{1,0:T(8,128)S(1)}, u32[]{:S(2)}, u32[]{:S(2)}) collective-permute-start(f32[16,256]{1,0:T(8,128)S(1)} %get-tuple-element.49), channel_id=1, source_target_pairs={{0,15},{1,2},{2,1},{3,4},{4,3},{5,6},{6,5},{7,8},{8,7},{9,10},{10,... | collective-permute-start | bytes 49160 | tf_op jit(solution)/shard_map/ppermute | solution.py:568
  33.1 0.0 collective-permute-done.8.from_a2
  33.1 0.5 collective-permute-done.9.from_b2
  33.6 0.0 copy-done.3
  33.6 0.0 copy-done.1
  33.6 0.0 copy-done.2
  33.6 0.0 copy-done
  33.6 3.3 %shard_map.124 = (f32[1024,128]{1,0:T(8,128)}, f32[1024,128]{1,0:T(8,128)}) custom-call(f32[1024,128]{1,0:T(8,128)S(1)} %bitcast.13, f32[1024,128]{1,0:T(8,128)S(1)} %bitcast.16, f32[1024,128]{1,0:T(8,128)S(1)} %bitcast.19, s32[1024,128]{1,0:T(8,128)S(1)} %bitcast.10, f32[4,16,128]{2,1,0:T(8,128)S(1)} %get-tuple-element.37.lon, ...), custom_call_target="tpu_custom_call" | custom-call | flops 7864320 | bytes 3145728 | tf_op jit(solution)/shard_map/pallas_call | solution.py:571
  36.9 0.0 collective-permute-done.6.from_a
  36.9 0.3 collective-permute-done.7.from_b
  37.2 1.4 %shard_map.125 = (f32[3,16,128]{2,1,0:T(8,128)S(1)}, f32[32,1,128]{2,1,0:T(1,128)}) custom-call(f32[32,256]{1,0:T(8,128)S(1)} %get-tuple-element.35.pc, f32[16,256]{1,0:T(8,128)S(1)} %get-tuple-element.45.rest, f32[16,256]{1,0:T(8,128)S(1)} %get-tuple-element.46.dg, f32[8,256]{1,0:T(8,128)S(1)} %get-tuple-element.47.edge, ...), custom_call_target="tpu_custom_call" | custom-call | flops 1000000 | bytes 100000 | tf_op jit(solution)/shard_map/pallas_call | solution.py:591
  38.6 9.1 %all-to-all-start = ((f32[32,1,128]{2,1,0:T(1,128)}), f32[32,1,128]{2,1,0:T(1,128)S(1)}, u32[]{:S(2)}, u32[]{:S(2)}) async-start(f32[32,1,128]{2,1,0:T(1,128)} %get-tuple-element.56), calls=%async_computation | async-start | bytes 32768 | tf_op jit(solution)/shard_map/all_to_all | solution.py:600
  47.8 0.0 copy-done.4
  47.8 3.0 %shard_map.126 = f32[1024,128]{1,0:T(8,128)} custom-call(f32[1024,128]{1,0:T(8,128)S(1)} %bitcast.21, f32[1024,128]{1,0:T(8,128)S(1)} %bitcast.14, f32[1024,128]{1,0:T(8,128)S(1)} %bitcast.17, s32[1024,128]{1,0:T(8,128)S(1)} %bitcast.11, f32[4,16,128]{2,1,0:T(8,128)S(1)} %get-tuple-element.37.lon, f32[4,16,128]{2,1,0:T(8,128)S(1)} %collective-permute-done.lon_a, ...), custom_call_target="tpu_custom_call" | custom-call | flops 7864320 | bytes 2621440 | tf_op jit(solution)/shard_map/pallas_call | solution.py:582
  50.8 4.0 %all-to-all-done.got = f32[32,1,128]{2,1,0:T(1,128)S(1)} async-done(((f32[32,1,128]{2,1,0:T(1,128)}), f32[32,1,128]{2,1,0:T(1,128)S(1)}, u32[]{:S(2)}, u32[]{:S(2)}) %all-to-all-start) | async-done | bytes 16416 | tf_op jit(solution)/shard_map/all_to_all | solution.py:600
  54.8 0.1 shard_map.127
  54.9 9.5 %all_to_all.10.got = f32[8,1,128]{2,1,0:T(1,128)S(1)} all-to-all(f32[8,1,128]{2,1,0:T(1,128)S(1)} %shard_map.127), channel_id=1, replica_groups=mesh['zl'=2,'x'=4,'c'=2,'y'=4,'zh'=4] {'zl','zh'}, dimensions={0} | all-to-all | bytes 8192 | tf_op jit(solution)/shard_map/all_to_all | solution.py:611
  64.4 0.7 %shard_map.128 = f32[16,128]{1,0:T(8,128)} custom-call(f32[8,1,128]{2,1,0:T(1,128)S(1)} %all_to_all.10.got, f32[3,16,128]{2,1,0:T(8,128)S(1)} %get-tuple-element.61.v, f32[16,128]{1,0:T(8,128)S(1)} %copy-done.5), custom_call_target="tpu_custom_call" | custom-call | flops 100000 | bytes 10000 | tf_op jit(solution)/shard_map/pallas_call | solution.py:612
  (2 shorter events, 0.0 us)
Async XLA Ops:
  0.6 0.7 %copy-start.8 = (f32[64]{0:T(128)S(1)}, f32[64]{0:T(128)}, u32[]{:S(2)}) copy-start(f32[64]{0:T(128)} %thick_hbm.1) | copy-start | bytes 772
  1.3 32.3 %copy-start.3 = (f32[64,16,128]{2,1,0:T(8,128)S(1)}, f32[64,16,128]{2,1,0:T(8,128)}, u32[]{:S(2)}) copy-start(f32[64,16,128]{2,1,0:T(8,128)} %param.12) | copy-start | bytes 1572868
  5.4 17.2 %collective-permute-start.2 = (f32[4,32,128]{2,1,0:T(8,128)S(1)}, f32[4,32,128]{2,1,0:T(8,128)S(1)}, u32[]{:S(2)}, u32[]{:S(2)}) collective-permute-start(f32[4,32,128]{2,1,0:T(8,128)S(1)} %get-tuple-element.39), channel_id=1, source_target_pairs={{0,1},{1,0},{2,3},{3,2},{4,5},{5,4},{6,7},{7,6},{8,9},{9,8},{10,11... | collective-permute-start | bytes 196616 | tf_op jit(solution)/shard_map/ppermute | solution.py:544
  9.3 10.0 %copy-start.7 = (f32[5,5]{1,0:T(8,128)S(1)}, f32[5,5]{1,0:T(8,128)}, u32[]{:S(2)}) copy-start(f32[5,5]{1,0:T(8,128)} %pc.1) | copy-start | bytes 304
  9.4 13.3 %collective-permute-start.3 = (f32[4,32,128]{2,1,0:T(8,128)S(1)}, f32[4,32,128]{2,1,0:T(8,128)S(1)}, u32[]{:S(2)}, u32[]{:S(2)}) collective-permute-start(f32[4,32,128]{2,1,0:T(8,128)S(1)} %get-tuple-element.40), channel_id=1, source_target_pairs={{0,15},{1,2},{2,1},{3,4},{4,3},{5,6},{6,5},{7,8},{8,7},{9,10},{10,... | collective-permute-start | bytes 196616 | tf_op jit(solution)/shard_map/ppermute | solution.py:543
  16.0 6.6 %collective-permute-start.1 = (f32[4,16,128]{2,1,0:T(8,128)S(1)}, f32[4,16,128]{2,1,0:T(8,128)S(1)}, u32[]{:S(2)}, u32[]{:S(2)}) collective-permute-start(f32[4,16,128]{2,1,0:T(8,128)S(1)} %get-tuple-element.37.lon), channel_id=1, source_target_pairs={{0,240},{16,32},{32,16},{48,64},{64,48},{80,96},{96,80},{112,128},... | collective-permute-start | bytes 98312 | tf_op jit(solution)/shard_map/ppermute | solution.py:545
  18.3 4.2 %collective-permute-start = (f32[4,16,128]{2,1,0:T(8,128)S(1)}, f32[4,16,128]{2,1,0:T(8,128)S(1)}, u32[]{:S(2)}, u32[]{:S(2)}) collective-permute-start(f32[4,16,128]{2,1,0:T(8,128)S(1)} %get-tuple-element.37.lon), channel_id=1, source_target_pairs={{0,16},{16,0},{32,48},{48,32},{64,80},{80,64},{96,112},{112,96},{1... | collective-permute-start | bytes 98312 | tf_op jit(solution)/shard_map/ppermute | solution.py:546
  19.3 3.3 %copy-start.5 = (f32[16,128]{1,0:T(8,128)S(1)}, f32[16,128]{1,0:T(8,128)}, u32[]{:S(2)}) copy-start(f32[16,128]{1,0:T(8,128)} %sf.3) | copy-start | bytes 24580
  19.3 3.3 %copy-start.6 = (f32[16,128]{1,0:T(8,128)S(1)}, f32[16,128]{1,0:T(8,128)}, u32[]{:S(2)}) copy-start(f32[16,128]{1,0:T(8,128)} %dg.1) | copy-start | bytes 24580
  19.3 14.2 %copy-start.1 = (f32[64,16,128]{2,1,0:T(8,128)S(1)}, f32[64,16,128]{2,1,0:T(8,128)}, u32[]{:S(2)}) copy-start(f32[64,16,128]{2,1,0:T(8,128)} %param.10) | copy-start | bytes 1572868
  19.3 14.2 %copy-start.2 = (f32[64,16,128]{2,1,0:T(8,128)S(1)}, f32[64,16,128]{2,1,0:T(8,128)}, u32[]{:S(2)}) copy-start(f32[64,16,128]{2,1,0:T(8,128)} %param.11) | copy-start | bytes 1572868
  22.6 11.0 %copy-start = (s32[64,16,128]{2,1,0:T(8,128)S(1)}, s32[64,16,128]{2,1,0:T(8,128)}, u32[]{:S(2)}) copy-start(s32[64,16,128]{2,1,0:T(8,128)} %param.13) | copy-start | bytes 1572868
  22.8 10.2 %collective-permute-start.8 = (f32[8,32,128]{2,1,0:T(8,128)S(1)}, f32[8,32,128]{2,1,0:T(8,128)S(1)}, u32[]{:S(2)}, u32[]{:S(2)}) collective-permute-start(f32[8,32,128]{2,1,0:T(8,128)S(1)} %get-tuple-element.50), channel_id=1, source_target_pairs={{0,1},{1,0},{2,3},{3,2},{4,5},{5,4},{6,7},{7,6},{8,9},{9,8},{10,11... | collective-permute-start | bytes 393224 | tf_op jit(solution)/shard_map/ppermute | solution.py:563
  22.9 10.7 %collective-permute-start.9 = (f32[8,32,128]{2,1,0:T(8,128)S(1)}, f32[8,32,128]{2,1,0:T(8,128)S(1)}, u32[]{:S(2)}, u32[]{:S(2)}) collective-permute-start(f32[8,32,128]{2,1,0:T(8,128)S(1)} %get-tuple-element.51), channel_id=1, source_target_pairs={{0,15},{1,2},{2,1},{3,4},{4,3},{5,6},{6,5},{7,8},{8,7},{9,10},{10,... | collective-permute-start | bytes 393224 | tf_op jit(solution)/shard_map/ppermute | solution.py:562
  24.4 5.7 %collective-permute-start.5 = (f32[104,128]{1,0:T(8,128)S(1)}, f32[104,128]{1,0:T(8,128)S(1)}, u32[]{:S(2)}, u32[]{:S(2)}) collective-permute-start(f32[104,128]{1,0:T(8,128)S(1)} %shard_map.122.msg), channel_id=1, source_target_pairs={{0,240},{16,32},{32,16},{48,64},{64,48},{80,96},{96,80},{112,128},... | collective-permute-start | bytes 159752 | tf_op jit(solution)/shard_map/ppermute | solution.py:560
  28.0 2.1 %collective-permute-start.4 = (f32[104,128]{1,0:T(8,128)S(1)}, f32[104,128]{1,0:T(8,128)S(1)}, u32[]{:S(2)}, u32[]{:S(2)}) collective-permute-start(f32[104,128]{1,0:T(8,128)S(1)} %shard_map.122.msg), channel_id=1, source_target_pairs={{0,16},{16,0},{32,48},{48,32},{64,80},{80,64},{96,112},{112,96},{1... | collective-permute-start | bytes 159752 | tf_op jit(solution)/shard_map/ppermute | solution.py:561
  30.2 6.7 %collective-permute-start.6 = (f32[16,256]{1,0:T(8,128)S(1)}, f32[16,256]{1,0:T(8,128)S(1)}, u32[]{:S(2)}, u32[]{:S(2)}) collective-permute-start(f32[16,256]{1,0:T(8,128)S(1)} %get-tuple-element.48), channel_id=1, source_target_pairs={{0,1},{1,0},{2,3},{3,2},{4,5},{5,4},{6,7},{7,6},{8,9},{9,8},{10,11... | collective-permute-start | bytes 49160 | tf_op jit(solution)/shard_map/ppermute | solution.py:569
  30.3 17.5 %copy-start.4 = (f32[64,16,128]{2,1,0:T(8,128)S(1)}, f32[64,16,128]{2,1,0:T(8,128)}, u32[]{:S(2)}) copy-start(f32[64,16,128]{2,1,0:T(8,128)} %param.9) | copy-start | bytes 1572868
  30.3 6.9 %collective-permute-start.7 = (f32[16,256]{1,0:T(8,128)S(1)}, f32[16,256]{1,0:T(8,128)S(1)}, u32[]{:S(2)}, u32[]{:S(2)}) collective-permute-start(f32[16,256]{1,0:T(8,128)S(1)} %get-tuple-element.49), channel_id=1, source_target_pairs={{0,15},{1,2},{2,1},{3,4},{4,3},{5,6},{6,5},{7,8},{8,7},{9,10},{10,... | collective-permute-start | bytes 49160 | tf_op jit(solution)/shard_map/ppermute | solution.py:568
  38.6 16.2 %all-to-all-start = ((f32[32,1,128]{2,1,0:T(1,128)}), f32[32,1,128]{2,1,0:T(1,128)S(1)}, u32[]{:S(2)}, u32[]{:S(2)}) async-start(f32[32,1,128]{2,1,0:T(1,128)} %get-tuple-element.56), calls=%async_computation | async-start | bytes 32768 | tf_op jit(solution)/shard_map/all_to_all | solution.py:600

commit v4 on v3

--- a/solution.py
+++ b/solution.py
@@ -1,3 +1,5 @@
+import functools
+
 import jax
 import jax.numpy as jnp
 from jax import lax
@@ -20,17 +22,18 @@
 VM = pl.BlockSpec(memory_space=pltpu.VMEM)
 SM = pl.BlockSpec(memory_space=pltpu.SMEM)
 HBM = pl.BlockSpec(memory_space=pltpu.HBM)
-FETCH_VMEM = 53.5
+FETCH_VMEM = 53.25
 FETCH_UNROLL = 4
 
 
-def call(kernel, outs, specs, flops, nbytes, scratch=(), place=VM, vmem=4):
+def call(kernel, outs, specs, flops, nbytes, scratch=(), place=VM, vmem=4, aliases=None):
     return pl.pallas_call(
         kernel,
         out_shape=[jax.ShapeDtypeStruct(s, jnp.float32) for s in outs],
         in_specs=specs,
         out_specs=place if isinstance(place, list) else [place] * len(outs),
         scratch_shapes=list(scratch),
+        input_output_aliases=aliases or {},
         compiler_params=pltpu.CompilerParams(vmem_limit_bytes=int(vmem * 1024 * 1024)),
         cost_estimate=pl.CostEstimate(flops=flops, bytes_accessed=nbytes, transcendentals=0),
     )
@@ -113,10 +116,12 @@
 
 
 def fetch_kernel(
-    thick_hbm, u, v, vi, land, lon_out, a_out, b_out, late_a, late_b, out, th_out, uo, vo, vio, lo, thick, sems, th_sem
+    thick_hbm, u, v, vi, land, t,
+    lon_out, a_out, b_out, late_a, late_b, out, th_out, uo, vo, vio, lo, to, thick, sems, th_sem,
 ):
     lane, row = lane_of((NR, NC)), row_of((NR, NC))
     pair = lane // 2
+    half_lane = lane < NC // 2
     up = lambda x: pltpu.roll(x, NC - 1, 1)
     north_of = lambda x: pltpu.roll(x, NR - 1, 0)
 
@@ -124,9 +129,11 @@
         at = level(k)
         wet, uu, vv, visc = lo[at, :].astype(jnp.float32), uo[at, :], vo[at, :], vio[at, :]
         mine = pair == k
+        first = to[at, :] * wet
+        inner = jnp.where(half_lane, up(first), pltpu.roll(first, 1, 1))
         packed = tuple(
             jnp.where(mine, pltpu.roll(x, 2 * k + 1, 1), old)
-            for x, old in zip((uu, vv, visc, wet), acc[:4])
+            for x, old in zip((uu, vv, visc, wet, first, 7.0 * first - inner), acc[:6])
         )
         th = jnp.full((1, NC), thick[k], jnp.float32)
         th_out[pl.ds(k, 1), :] = th
@@ -135,28 +142,28 @@
         east = (visc + up(visc)) * (half * up(wet))
         north = (visc + north_of(visc)) * (half * north_of(wet))
         return packed + (
-            acc[4] + own * uu,
-            acc[5] + east * (up(uu) - uu),
-            acc[6] + north * (north_of(uu) - uu),
-            acc[7] + own * vv,
-            acc[8] + east * (up(vv) - vv),
-            acc[9] + north * (north_of(vv) - vv),
-            jnp.where(mine[:1], th, acc[10]),
+            acc[6] + own * uu,
+            acc[7] + east * (up(uu) - uu),
+            acc[8] + north * (north_of(uu) - uu),
+            acc[9] + own * vv,
+            acc[10] + east * (up(vv) - vv),
+            acc[11] + north * (north_of(vv) - vv),
+            jnp.where(mine[:1], th, acc[12]),
         )
 
     thick_copy = pltpu.make_async_copy(thick_hbm, thick, th_sem)
     thick_copy.start()
-    copies = chunk_copies(((u, uo), (v, vo), (vi, vio), (land, lo)), sems)
+    copies = chunk_copies(((u, uo), (v, vo), (vi, vio), (land, lo), (t, to)), sems)
     thick_copy.wait()
     zero = jnp.zeros((NR, NC), jnp.float32)
-    acc = pipeline(copies, body, (zero,) * 10 + (zero[:1],), FETCH_UNROLL)
-    for i in range(4):
+    acc = pipeline(copies, body, (zero,) * 12 + (zero[:1],), FETCH_UNROLL)
+    for i in range(6):
         lon_out[i] = acc[i]
-    th_out[NZ:, :] = jnp.broadcast_to(acc[10], (8, NC))
+    th_out[NZ:, :] = jnp.broadcast_to(acc[12], (8, NC))
     for i in range(2):
-        east = jnp.where(lane == NC - 1, 0.0, acc[3 * i + 5])
-        north = jnp.where(row == NR - 1, 0.0, acc[3 * i + 6])
-        out[i] = acc[3 * i + 4] + DT_VISC * (
+        east = jnp.where(lane == NC - 1, 0.0, acc[3 * i + 7])
+        north = jnp.where(row == NR - 1, 0.0, acc[3 * i + 8])
+        out[i] = acc[3 * i + 6] + DT_VISC * (
             east - pltpu.roll(east, 1, 1) + north - pltpu.roll(north, 1, 0)
         )
     even = even_lat()
@@ -165,39 +172,18 @@
         for i, ref in enumerate((uo, vo, vio, lo)):
             first[i] = edge_row(ref, north, 0, mine, HALF)
             rest[i] = edge_row(ref, north, 0, theirs, HALF)
-
-
-def late_kernel(pc, t, land, late_a, late_b, lon_out, a_out, b_out, pc_out, to, lo, sems):
-    lane = lane_of((NR, NC))
-    pair = lane // 2
-    half_lane = lane < NC // 2
-
-    def body(k, acc):
-        at = level(k)
-        first = to[at, :] * lo[at, :].astype(jnp.float32)
-        inner = jnp.where(half_lane, pltpu.roll(first, NC - 1, 1), pltpu.roll(first, 1, 1))
-        mine = pair == k
-        return tuple(
-            jnp.where(mine, pltpu.roll(x, 2 * k + 1, 1), old)
-            for x, old in zip((first, 7.0 * first - inner), acc)
-        )
-
-    copies = chunk_copies(((t, to), (land, lo)), sems)
-    acc = pipeline(copies, body, (jnp.zeros((NR, NC), jnp.float32),) * 2, 8)
-    lon_out[0] = acc[0]
-    lon_out[1] = acc[1]
-    for i in range(25):
-        pc_out[i : i + 1, :] = jnp.full((1, 2 * NC), pc[i // 5, i % 5], jnp.float32)
-    even = even_lat()
-    for north, src, dst in ((even, late_a, a_out), (jnp.logical_not(even), late_b, b_out)):
-        dst[:4] = src[...]
         for i in range(2):
-            first, second = (
+            near, inner = (
                 edge_row(to, north, n, i * HALF, HALF) * edge_row(lo, north, n, i * HALF, HALF)
                 for n in range(2)
             )
-            dst[4 + i] = first
-            dst[6 + i] = 7.0 * first - second
+            rest[4 + i] = near
+            rest[6 + i] = 7.0 * near - inner
+
+
+def taps_kernel(pc, out):
+    for i in range(25):
+        out[i : i + 1, :] = jnp.full((1, 2 * NC), pc[i // 5, i % 5], jnp.float32)
 
 
 def lon_sides(first, second):
@@ -216,10 +202,10 @@
     return face * (other[0] - own[0]), face * (other[1] - own[1])
 
 
-MSG = 104
-
-
-def join_kernel(inner, lon, lon_a, lon_b, lon2, a2, from_a, b2, from_b, th, sf, dg, out):
+MSG = 72
+
+
+def join_kernel(inner, lon, lon_a, lon_b, a2, from_a, b2, from_b, th, sf, dg, out):
     lane = lane_of((NR, NC))
     own = [lon[i] for i in range(4)]
     other = [beyond(lon_a[i], lon_b[i]) for i in range(4)]
@@ -238,10 +224,8 @@
     sums = [jnp.sum(x * weight, axis=0, keepdims=True) for x in lat_a]
     sums += [jnp.sum(x * weight_b, axis=0, keepdims=True) for x in lat_b]
     out[2 * NR : 2 * NR + 8, :] = jnp.concatenate(sums + [jnp.zeros((4, NC), jnp.float32)], axis=0)
-    out[40:56, :] = lon2[0]
-    out[56:72, :] = lon2[1]
-    out[72:88, :] = sf[...]
-    out[88:104, :] = dg[...]
+    out[40:56, :] = sf[...]
+    out[56:72, :] = dg[...]
 
 
 def side_kernel(msg, msg_a, msg_b, rest_out, diag_out, edge_out, a_out, b_out):
@@ -252,7 +236,7 @@
 
     part = lambda lo, hi: widen(msg[lo:hi, :], msg_a[lo:hi, :], msg_b[lo:hi, :])
     te, tn, faces = part(0, NR), part(NR, 2 * NR), part(2 * NR, 2 * NR + 8)
-    sf, dg = part(72, 88), part(88, 104)
+    sf, dg = part(40, 56), part(56, 72)
     row = row_of((NR, 2 * NC))
     even = even_lat()
     north_u, north_v = (jnp.where(even, faces[i : i + 1], faces[i + 2 : i + 3]) for i in range(2))
@@ -409,12 +393,13 @@
     return spread
 
 
-def write_out(body, pairs, sems, unroll):
+def write_out(body, pairs, sems, unroll, first=0, count=NZ):
     per = NZ // CHUNKS
-    copies = chunk_copies(pairs, sems)
+    all_copies = chunk_copies(pairs, sems)
+    copies = lambda c: all_copies(first // per + c)
 
     def chunk(c, carry):
-        lax.fori_loop(0, per, lambda i, x: body(c * per + i, x), 0, unroll=unroll)
+        lax.fori_loop(0, per, lambda i, x: body(first + c * per + i, x), 0, unroll=unroll)
         for copy in copies(c):
             copy.start()
         return carry
@@ -424,14 +409,12 @@
             copy.wait()
         return carry
 
-    lax.fori_loop(0, CHUNKS, chunk, 0)
-    lax.fori_loop(0, CHUNKS, finish, 0)
-
-
-def velocity_kernel(
-    u, v, vi, w, lon, lon_a, lon_b, from_a, from_a2, from_b, from_b2,
-    u_hbm, v_hbm, u_out, v_out, packed, lines, sems,
-):
+    lax.fori_loop(0, count // per, chunk, 0)
+    lax.fori_loop(0, count // per, finish, 0)
+
+
+def velocity_kernel(early, u, v, vi, w, lon, lon_a, lon_b, from_a, from_b, *rest):
+    u_hbm, v_hbm, u_out, v_out, packed, lines, sems = rest[0 if early else 2 :]
     is_east = lane_of((NR, NC)) % 2 == 0
     own = [lon[i] for i in range(4)]
     other = [beyond(lon_a[i], lon_b[i]) for i in range(4)]
@@ -440,15 +423,15 @@
     even = even_lat()
     exists = b_exists()
     mine, theirs = halves()
-    for first, there_a, there_b in ((mine, from_a2, from_b2), (theirs, from_a, from_b)):
-        at = pl.ds(first, HALF)
-        for side in range(2):
-            use_a = even if side == 0 else jnp.logical_not(even)
-            here = [edge_row(ref, side == 0, 0, first, HALF) for ref in (u, v, vi, w)]
-            there = [jnp.where(use_a, there_a[i], there_b[i] * exists) for i in range(4)]
-            sign = DT_VISC if side == 0 else -DT_VISC
-            for i, grad in enumerate(face_in(here, there)):
-                lines[2 * i + side, at, :] = sign * grad
+    first = theirs if early else mine
+    at = pl.ds(first, HALF)
+    for side in range(2):
+        use_a = even if side == 0 else jnp.logical_not(even)
+        here = [edge_row(ref, side == 0, 0, first, HALF) for ref in (u, v, vi, w)]
+        there = [jnp.where(use_a, from_a[i], from_b[i] * exists) for i in range(4)]
+        sign = DT_VISC if side == 0 else -DT_VISC
+        for i, grad in enumerate(face_in(here, there)):
+            lines[2 * i + side, at, :] = sign * grad
     spread = spread_of(packed, lines)
     lon_up = lambda x: pltpu.roll(x, NC - 1, 1)
     lat_up = lambda x: pltpu.roll(x, NR - 1, 0)
@@ -464,17 +447,17 @@
         v_out[at, :] = wet * (vv + spread(k, face_e * (lon_up(vv) - vv), face_n * (lat_up(vv) - vv), 1))
         return carry
 
-    write_out(body, ((u_out, u_hbm), (v_out, v_hbm)), sems, 8)
+    write_out(body, ((u_out, u_hbm), (v_out, v_hbm)), sems, 8, first, HALF)
 
 
 def tracer_kernel(
-    t, u, v, w, lon, lon_a, lon_b, msg, msg_a, msg_b, from_a, from_a2, from_b, from_b2,
+    t, u, v, w, lon, lon_a, lon_b, from_a, from_a2, from_b, from_b2,
     t_hbm, t_out, packed, lines, sems,
 ):
     is_east = lane_of((NR, NC)) % 2 == 0
     by = DT_ADV / 12.0
-    packed[1] = beyond(msg_a[40:56, :], msg_b[40:56, :])
-    far = msg[56:72, :] + beyond(msg_a[56:72, :], msg_b[56:72, :])
+    packed[1] = beyond(lon_a[4], lon_b[4])
+    far = lon[5] + beyond(lon_a[5], lon_b[5])
     speed = jnp.where(is_east, lon[0], beyond(lon_a[0], lon_b[0]))
     packed[0] = speed * far * (by * lon[3] * beyond(lon_a[3], lon_b[3]))
     even = even_lat()
@@ -531,63 +514,32 @@
     wets = pltpu.VMEM(flat, jnp.int32)
     dma = pltpu.SemaphoreType.DMA
     rows = (4, HALF, NC)
-    lon, a, b, late_a, late_b, inner, th = call(
+    late = (8, HALF, NC)
+    lon, a, b, a2, b2, inner, th = call(
         fetch_kernel,
-        [(4, NR, NC), rows, rows, rows, rows, (2, NR, NC), (NZ + 8, NC)],
-        [HBM] * 5,
+        [(6, NR, NC), rows, rows, late, late, (2, NR, NC), (NZ + 8, NC)],
+        [HBM] * 6,
         50 * NZ * NR * NC,
-        4 * block,
-        [field] * 3 + [wets, pltpu.SMEM((NZ,), jnp.float32), dma((CHUNKS, 4)), dma],
+        5 * block,
+        [field] * 3 + [wets, field, pltpu.SMEM((NZ,), jnp.float32), dma((CHUNKS, 5)), dma],
         vmem=FETCH_VMEM,
-    )(thickness, u, v, vi, w)
+    )(thickness, u, v, vi, w, t)
     from_b = lax.ppermute(b, LAT, SWAP_B)
     from_a = lax.ppermute(a, LAT, SWAP_A)
     lon_b = lax.ppermute(lon, LON, SWAP_B)
     lon_a = lax.ppermute(lon, LON, SWAP_A)
-    lon2, a2, b2, taps = call(
-        late_kernel,
-        [(2, NR, NC), (8, HALF, NC), (8, HALF, NC), (32, 2 * NC)],
-        [SM] + [HBM] * 2 + [VM] * 2,
-        20 * NZ * NR * NC,
-        2 * block,
-        [field, wets, dma((CHUNKS, 2))],
-        vmem=FETCH_VMEM,
-    )(precond_kernel, t, w, late_a, late_b)
-    (msg,) = call(join_kernel, [(MSG, NC)], [VM] * 12, 10**6, 10**6)(
-        inner, lon, lon_a, lon_b, lon2, late_a, from_a, late_b, from_b, th, surface, surface_diag
+    (msg,) = call(join_kernel, [(MSG, NC)], [VM] * 11, 10**6, 10**6)(
+        inner, lon, lon_a, lon_b, a2, from_a, b2, from_b, th, surface, surface_diag
     )
-    msg, a2, b2 = lax.optimization_barrier((msg, a2, b2))
     msg_b = lax.ppermute(msg, LON, SWAP_B)
     msg_a = lax.ppermute(msg, LON, SWAP_A)
-    from_b2 = lax.ppermute(b2, LAT, SWAP_B)
-    from_a2 = lax.ppermute(a2, LAT, SWAP_A)
     wide = (NR, 2 * NC)
     rest, dg, edge, side_a, side_b = call(
         side_kernel, [wide, wide, (8, 2 * NC), wide, wide], [VM] * 3, 10**6, 10**5
     )(msg, msg_a, msg_b)
     got_b = lax.ppermute(side_b, LAT, SWAP_B)
     got_a = lax.ppermute(side_a, LAT, SWAP_A)
-    lat = (from_a, from_a2, from_b, from_b2)
-    u_new, v_new = call(
-        velocity_kernel,
-        [flat] * 2,
-        [VM] * 11,
-        60 * NZ * NR * NC,
-        6 * block,
-        [field] * 2
-        + [pltpu.VMEM((2, NR, NC), jnp.float32), pltpu.VMEM((4, NZ, NC), jnp.float32), dma((CHUNKS, 2))],
-        HBM,
-    )(u, v, vi, w, lon, lon_a, lon_b, *lat)
-    got_a, got_b, u_new, v_new = lax.optimization_barrier((got_a, got_b, u_new, v_new))
-    t_new = call(
-        tracer_kernel,
-        [flat],
-        [VM] * 14,
-        60 * NZ * NR * NC,
-        5 * block,
-        [field, pltpu.VMEM((2, NR, NC), jnp.float32), pltpu.VMEM((4, NZ, NC), jnp.float32), dma((CHUNKS, 1))],
-        HBM,
-    )(t, u, v, w, lon, lon_a, lon_b, msg, msg_a, msg_b, *lat)[0]
+    (taps,) = call(taps_kernel, [(32, 2 * NC)], [SM], 10**4, 10**4)(precond_kernel)
     vecs, dots = call(
         solve_kernel,
         [(3, NR, NC), (32, 1, NC)],
@@ -597,8 +549,37 @@
         [pltpu.VMEM((3, NR, NC), jnp.float32), dma],
         [HBM, VM],
     )(taps, rest, dg, edge, got_a, got_b)
+    def velocity(early, edges, written):
+        return call(
+            functools.partial(velocity_kernel, early),
+            [flat] * 2,
+            [VM] * 9 + [HBM] * len(written),
+            30 * NZ * NR * NC,
+            3 * block,
+            [field] * 2
+            + [pltpu.VMEM((2, NR, NC), jnp.float32), pltpu.VMEM((4, NZ, NC), jnp.float32), dma((CHUNKS, 2))],
+            HBM,
+            aliases={9 + i: i for i in range(len(written))},
+        )(u, v, vi, w, lon, lon_a, lon_b, *edges, *written)
+
+    dots, from_a, from_b = lax.optimization_barrier((dots, from_a, from_b))
+    u_half, v_half = velocity(True, (from_a, from_b), ())
+    dots, a2, b2 = lax.optimization_barrier((dots, a2, b2))
+    from_b2 = lax.ppermute(b2, LAT, SWAP_B)
+    from_a2 = lax.ppermute(a2, LAT, SWAP_A)
     dots = lax.all_to_all(dots, ("x", "y", "c"), 0, 0)
-    dots, t_new = lax.optimization_barrier((dots, t_new))
+    dots, u_half, v_half = lax.optimization_barrier((dots, u_half, v_half))
+    lat = (from_a, from_a2, from_b, from_b2)
+    u_new, v_new = velocity(False, (from_a2, from_b2), (u_half, v_half))
+    t_new = call(
+        tracer_kernel,
+        [flat],
+        [VM] * 11,
+        60 * NZ * NR * NC,
+        5 * block,
+        [field, pltpu.VMEM((2, NR, NC), jnp.float32), pltpu.VMEM((4, NZ, NC), jnp.float32), dma((CHUNKS, 1))],
+        HBM,
+    )(t, u, v, w, lon, lon_a, lon_b, *lat)[0]
     (dots,) = call(
         relay_kernel,
         [(8, 1, NC)],
@@ -609,6 +590,7 @@
         HBM,
     )(dots)
     dots = lax.all_to_all(dots, ("zl", "zh"), 0, 0)
+    dots, t_new, u_new, v_new = lax.optimization_barrier((dots, t_new, u_new, v_new))
     (surface_new,) = call(
         step_kernel,
         [(NR, NC)],

time: 65.4 us -> 66 us (level)
  blocking collectives: 9.5 us -> 0 us
  waiting for transfers between devices: 6.99 us -> 15.3 us
  starting transfers between devices: 31 us -> 32.9 us
    all_to_all x1 -> x0, blocking collectives: 9.5 us -> none  [local(): dots = lax.all_to_all(dots, ('zl', 'zh'), 0, 0)]
    all_to_all x0 -> x1, starting transfers between devices: none -> 3.6 us  [local(): dots = lax.all_to_all(dots, ('zl', 'zh'), 0, 0)]
    ppermute x1, starting transfers between devices: 3.58 us -> 0.01 us  [local(): msg_b = lax.ppermute(msg, LON, SWAP_B)]
    ppermute x1, waiting for transfers between devices: 0.34 us -> 3.27 us  [local(): got_b = lax.ppermute(side_b, LAT, SWAP_B)]
    ppermute x1, starting transfers between devices: 0.01 us -> 2.53 us  [local(): msg_a = lax.ppermute(msg, LON, SWAP_A)]
    ppermute x1, waiting for transfers between devices: 0.01 us -> 2.41 us  [local(): lon_b = lax.ppermute(lon, LON, SWAP_B)]
    all_to_all x1, starting transfers between devices: 9.15 us -> 7.68 us  [local(): dots = lax.all_to_all(dots, ('x', 'y', 'c'), 0, 0)]
    ppermute x1, starting transfers between devices: 1.5 us -> 2.9 us  [local(): from_b2 = lax.ppermute(b2, LAT, SWAP_B)]
  transfers between devices with their start and end apart: 11 -> 12, of which waited for: 4 -> 6; matrix products, arithmetic and copies ran while one was open for 0% -> 0% of each run, Pallas kernels for 15% -> 13%
where the time goes in v4:
time: 66 us; the launch traced here: 65.8 us
  starting transfers between devices  32.9 us (50%)
  Pallas kernels  16.1 us (24%)
  waiting for transfers between devices  15.3 us (23%)
  between operations  0.83 us (1%)
  local copies, waits for them, and re-layouts  0.68 us (1%)
    all_to_all x1, starting transfers between devices, local(): dots = lax.all_to_all(dots, ('x', 'y', 'c'), 0, 0)  7.68 us
    ppermute x1, starting transfers between devices, local(): from_b = lax.ppermute(b, LAT, SWAP_B)  6.65 us
    pallas_call x1, Pallas kernels, local(): call(fetch_kernel, [(6, NR, NC), rows, rows, late, late, (2, NR, NC), (NZ...  5.3 us
    all_to_all x1, waiting for transfers between devices, local(): dots = lax.all_to_all(dots, ('x', 'y', 'c'), 0, 0)  4.9 us
    pallas_call x2, Pallas kernels, velocity(): call(functools.partial(velocity_kernel, early), [flat] * 2, [VM] * 9 + [H...  4.07 us
    ppermute x1, starting transfers between devices, local(): from_a = lax.ppermute(a, LAT, SWAP_A)  3.91 us
    all_to_all x1, starting transfers between devices, local(): dots = lax.all_to_all(dots, ('zl', 'zh'), 0, 0)  3.6 us
    ppermute x1, waiting for transfers between devices, local(): got_b = lax.ppermute(side_b, LAT, SWAP_B)  3.27 us
  transfers between devices with their start and end apart: 12, of which 6 were waited for; matrix products, arithmetic and copies ran while one was open for 0% of the time, Pallas kernels for 13%

profile of v4, /device:TPU:1, one launch (start us, length us, event | category | flops | bytes accessed | tf_op | source)
XLA Modules:
  0.0 65.8 jit_solution(4182286193384615175)
XLA Ops:
  0.6 0.0 copy-start.8
  0.6 0.6 copy-done.8
  1.3 0.0 copy-start.5
  1.3 0.0 copy-start.6
  1.3 0.0 copy-start.3
  1.3 5.3 %shard_map.121 = (f32[6,16,128]{2,1,0:T(8,128)S(1)}, f32[4,32,128]{2,1,0:T(8,128)S(1)}, f32[4,32,128]{2,1,0:T(8,128)S(1)}, f32[8,32,128]{2,1,0:T(8,128)S(1)}, f3...) custom-call(f32[64]{0:T(128)S(1)} %copy-done.8, f32[1024,128]{1,0:T(8,128)} %bitcast.8, ...), custom_call_target="tpu_custom_call" | custom-call | flops 6553600 | bytes 2621440 | tf_op jit(solution)/shard_map/pallas_call | solution.py:518
  6.6 0.0 copy-start
  6.6 3.9 %collective-permute-start.2 = (f32[4,32,128]{2,1,0:T(8,128)S(1)}, f32[4,32,128]{2,1,0:T(8,128)S(1)}, u32[]{:S(2)}, u32[]{:S(2)}) collective-permute-start(f32[4,32,128]{2,1,0:T(8,128)S(1)} %get-tuple-element.38), channel_id=1, source_target_pairs={{0,1},{1,0},{2,3},{3,2},{4,5},{5,4},{6,7},{7,6},{8,9},{9,8},{10,11... | collective-permute-start | bytes 196616 | tf_op jit(solution)/shard_map/ppermute | solution.py:528
  10.5 6.7 %collective-permute-start.3 = (f32[4,32,128]{2,1,0:T(8,128)S(1)}, f32[4,32,128]{2,1,0:T(8,128)S(1)}, u32[]{:S(2)}, u32[]{:S(2)}) collective-permute-start(f32[4,32,128]{2,1,0:T(8,128)S(1)} %get-tuple-element.40), channel_id=1, source_target_pairs={{0,15},{1,2},{2,1},{3,4},{4,3},{5,6},{6,5},{7,8},{8,7},{9,10},{10,... | collective-permute-start | bytes 196616 | tf_op jit(solution)/shard_map/ppermute | solution.py:527
  17.2 1.2 %collective-permute-start = (f32[6,16,128]{2,1,0:T(8,128)S(1)}, f32[6,16,128]{2,1,0:T(8,128)S(1)}, u32[]{:S(2)}, u32[]{:S(2)}) collective-permute-start(f32[6,16,128]{2,1,0:T(8,128)S(1)} %get-tuple-element.36.lon), channel_id=1, source_target_pairs={{0,16},{16,0},{32,48},{48,32},{64,80},{80,64},{96,112},{112,96},{1... | collective-permute-start | bytes 147464 | tf_op jit(solution)/shard_map/ppermute | solution.py:530
  18.4 1.1 %collective-permute-start.1 = (f32[6,16,128]{2,1,0:T(8,128)S(1)}, f32[6,16,128]{2,1,0:T(8,128)S(1)}, u32[]{:S(2)}, u32[]{:S(2)}) collective-permute-start(f32[6,16,128]{2,1,0:T(8,128)S(1)} %get-tuple-element.36.lon), channel_id=1, source_target_pairs={{0,240},{16,32},{32,16},{48,64},{64,48},{80,96},{96,80},{112,128},... | collective-permute-start | bytes 147464 | tf_op jit(solution)/shard_map/ppermute | solution.py:529
  19.5 0.0 collective-permute-done.lon_a
  19.5 2.4 %collective-permute-done.1.lon_b = f32[6,16,128]{2,1,0:T(8,128)S(1)} collective-permute-done((f32[6,16,128]{2,1,0:T(8,128)S(1)}, f32[6,16,128]{2,1,0:T(8,128)S(1)}, u32[]{:S(2)}, u32[]{:S(2)}) %collective-permute-start.1) | collective-permute-done | bytes 49184 | tf_op jit(solution)/shard_map/ppermute | solution.py:529
  21.9 0.0 collective-permute-done.2.from_a
  22.0 0.0 collective-permute-done.3.from_b
  22.0 0.0 copy-done.5
  22.0 0.0 copy-done.6
  22.0 0.2 shard_map.122.msg
  22.2 2.5 %collective-permute-start.4 = (f32[72,128]{1,0:T(8,128)S(1)}, f32[72,128]{1,0:T(8,128)S(1)}, u32[]{:S(2)}, u32[]{:S(2)}) collective-permute-start(f32[72,128]{1,0:T(8,128)S(1)} %shard_map.122.msg), channel_id=1, source_target_pairs={{0,16},{16,0},{32,48},{48,32},{64,80},{80,64},{96,112},{112,96},{1... | collective-permute-start | bytes 110600 | tf_op jit(solution)/shard_map/ppermute | solution.py:535
  24.7 0.0 collective-permute-start.5
  24.7 0.9 %collective-permute-done.4.msg_a = f32[72,128]{1,0:T(8,128)S(1)} collective-permute-done((f32[72,128]{1,0:T(8,128)S(1)}, f32[72,128]{1,0:T(8,128)S(1)}, u32[]{:S(2)}, u32[]{:S(2)}) %collective-permute-start.4) | collective-permute-done | bytes 36896 | tf_op jit(solution)/shard_map/ppermute | solution.py:535
  25.5 2.5 %collective-permute-done.5.msg_b = f32[72,128]{1,0:T(8,128)S(1)} collective-permute-done((f32[72,128]{1,0:T(8,128)S(1)}, f32[72,128]{1,0:T(8,128)S(1)}, u32[]{:S(2)}, u32[]{:S(2)}) %collective-permute-start.5) | collective-permute-done | bytes 36896 | tf_op jit(solution)/shard_map/ppermute | solution.py:534
  28.1 0.1 shard_map.123
  28.2 0.1 collective-permute-start.6
  28.3 3.0 %collective-permute-start.7 = (f32[16,256]{1,0:T(8,128)S(1)}, f32[16,256]{1,0:T(8,128)S(1)}, u32[]{:S(2)}, u32[]{:S(2)}) collective-permute-start(f32[16,256]{1,0:T(8,128)S(1)} %get-tuple-element.46), channel_id=1, source_target_pairs={{0,15},{1,2},{2,1},{3,4},{4,3},{5,6},{6,5},{7,8},{8,7},{9,10},{10,... | collective-permute-start | bytes 49160 | tf_op jit(solution)/shard_map/ppermute | solution.py:540
  31.3 0.0 copy-done.7
  31.3 0.6 shard_map.120.pc
  31.9 0.0 collective-permute-done.6.from_a
  31.9 3.3 %collective-permute-done.7.from_b = f32[16,256]{1,0:T(8,128)S(1)} collective-permute-done((f32[16,256]{1,0:T(8,128)S(1)}, f32[16,256]{1,0:T(8,128)S(1)}, u32[]{:S(2)}, u32[]{:S(2)}) %collective-permute-start.7) | collective-permute-done | bytes 16416 | tf_op jit(solution)/shard_map/ppermute | solution.py:540
  35.2 1.4 %shard_map.124 = (f32[3,16,128]{2,1,0:T(8,128)S(1)}, f32[32,1,128]{2,1,0:T(1,128)}) custom-call(f32[32,256]{1,0:T(8,128)S(1)} %shard_map.120.pc, f32[16,256]{1,0:T(8,128)S(1)} %get-tuple-element.42.rest, f32[16,256]{1,0:T(8,128)S(1)} %get-tuple-element.43.dg, f32[8,256]{1,0:T(8,128)S(1)} %get-tuple-element.44.edge, ...), custom_call_target="tpu_custom_call" | custom-call | flops 1000000 | bytes 100000 | tf_op jit(solution)/shard_map/pallas_call | solution.py:543
  36.6 0.3 collective-permute-start.8
  36.8 2.9 %collective-permute-start.9 = (f32[8,32,128]{2,1,0:T(8,128)S(1)}, f32[8,32,128]{2,1,0:T(8,128)S(1)}, u32[]{:S(2)}, u32[]{:S(2)}) collective-permute-start(f32[8,32,128]{2,1,0:T(8,128)S(1)} %get-tuple-element.56.b2), channel_id=1, source_target_pairs={{0,15},{1,2},{2,1},{3,4},{4,3},{5,6},{6,5},{7,8},{8,7},{9,10},{10,... | collective-permute-start | bytes 393224 | tf_op jit(solution)/shard_map/ppermute | solution.py:568
  39.7 7.7 %all-to-all-start = ((f32[32,1,128]{2,1,0:T(1,128)}), f32[32,1,128]{2,1,0:T(1,128)S(1)}, u32[]{:S(2)}, u32[]{:S(2)}) async-start(f32[32,1,128]{2,1,0:T(1,128)} %get-tuple-element.49), calls=%async_computation | async-start | bytes 32768 | tf_op jit(solution)/shard_map/all_to_all | solution.py:570
  47.4 0.0 copy-done.1
  47.4 0.0 copy-done.2
  47.5 0.0 copy-done.3
  47.5 0.0 copy-done
  47.5 2.0 %shard_map.125 = (f32[1024,128]{1,0:T(8,128)}, f32[1024,128]{1,0:T(8,128)}) custom-call(f32[1024,128]{1,0:T(8,128)S(1)} %bitcast.9, f32[1024,128]{1,0:T(8,128)S(1)} %bitcast.13, f32[1024,128]{1,0:T(8,128)S(1)} %bitcast.21, s32[1024,128]{1,0:T(8,128)S(1)} %bitcast.17, f32[6,16,128]{2,1,0:T(8,128)S(1)} %get-tuple-element.36.lon, ...), custom_call_target="tpu_custom_call" | custom-call | flops 3932160 | bytes 1572864 | tf_op jit(solution)/shard_map/pallas_call | solution.py:553
  49.5 4.9 %all-to-all-done.got = f32[32,1,128]{2,1,0:T(1,128)S(1)} async-done(((f32[32,1,128]{2,1,0:T(1,128)}), f32[32,1,128]{2,1,0:T(1,128)S(1)}, u32[]{:S(2)}, u32[]{:S(2)}) %all-to-all-start) | async-done | bytes 16416 | tf_op jit(solution)/shard_map/all_to_all | solution.py:570
  54.4 0.7 shard_map.126
  55.1 3.6 %all-to-all-start.1 = ((f32[8,1,128]{2,1,0:T(1,128)}), f32[8,1,128]{2,1,0:T(1,128)S(1)}, u32[]{:S(2)}, u32[]{:S(2)}) async-start(f32[8,1,128]{2,1,0:T(1,128)} %shard_map.126), calls=%async_computation.1 | async-start | bytes 8192 | tf_op jit(solution)/shard_map/all_to_all | solution.py:592
  58.7 0.0 collective-permute-done.8.from_a2.from_a
  58.7 0.0 collective-permute-done.9.from_b2.from_b
  58.7 2.0 %shard_map.128 = (f32[1024,128]{1,0:T(8,128)}, f32[1024,128]{1,0:T(8,128)}) custom-call(f32[1024,128]{1,0:T(8,128)S(1)} %bitcast.10, f32[1024,128]{1,0:T(8,128)S(1)} %bitcast.14, f32[1024,128]{1,0:T(8,128)S(1)} %bitcast.22, s32[1024,128]{1,0:T(8,128)S(1)} %bitcast.18, ...), custom_call_target="tpu_custom_call", output_to_operand_aliasing={{0}: (9, {}), {1}: (10, {})} | custom-call | flops 3932160 | bytes 1572864 | tf_op jit(solution)/shard_map/pallas_call | solution.py:553
  60.7 0.0 copy-done.4
  60.8 3.0 %shard_map.127 = f32[1024,128]{1,0:T(8,128)} custom-call(f32[1024,128]{1,0:T(8,128)S(1)} %bitcast.24, f32[1024,128]{1,0:T(8,128)S(1)} %bitcast.11, f32[1024,128]{1,0:T(8,128)S(1)} %bitcast.15, s32[1024,128]{1,0:T(8,128)S(1)} %bitcast.19, f32[6,16,128]{2,1,0:T(8,128)S(1)} %get-tuple-element.36.lon, f32[6,16,128]{2,1,0:T(8,128)S(1)} %collective-permute-done.lon_a, ...), custom_call_target="tpu_custom_call" | custom-call | flops 7864320 | bytes 2621440 | tf_op jit(solution)/shard_map/pallas_call | solution.py:574
  63.8 1.3 %all-to-all-done.1.got = f32[8,1,128]{2,1,0:T(1,128)S(1)} async-done(((f32[8,1,128]{2,1,0:T(1,128)}), f32[8,1,128]{2,1,0:T(1,128)S(1)}, u32[]{:S(2)}, u32[]{:S(2)}) %all-to-all-start.1) | async-done | bytes 4128 | tf_op jit(solution)/shard_map/all_to_all | solution.py:592
  65.1 0.7 %shard_map.129 = f32[16,128]{1,0:T(8,128)} custom-call(f32[8,1,128]{2,1,0:T(1,128)S(1)} %all-to-all-done.1.got, f32[3,16,128]{2,1,0:T(8,128)S(1)} %get-tuple-element.65.v, f32[16,128]{1,0:T(8,128)S(1)} %copy-done.5), custom_call_target="tpu_custom_call" | custom-call | flops 100000 | bytes 10000 | tf_op jit(solution)/shard_map/pallas_call | solution.py:594
  (4 shorter events, 0.0 us)
Async XLA Ops:
  0.6 0.7 copy-start.8
  1.3 20.7 %copy-start.5 = (f32[16,128]{1,0:T(8,128)S(1)}, f32[16,128]{1,0:T(8,128)}, u32[]{:S(2)}) copy-start(f32[16,128]{1,0:T(8,128)} %sf.3) | copy-start | bytes 24580
  1.3 20.7 %copy-start.6 = (f32[16,128]{1,0:T(8,128)S(1)}, f32[16,128]{1,0:T(8,128)}, u32[]{:S(2)}) copy-start(f32[16,128]{1,0:T(8,128)} %dg.1) | copy-start | bytes 24580
  1.3 46.1 %copy-start.1 = (f32[64,16,128]{2,1,0:T(8,128)S(1)}, f32[64,16,128]{2,1,0:T(8,128)}, u32[]{:S(2)}) copy-start(f32[64,16,128]{2,1,0:T(8,128)} %param.11) | copy-start | bytes 1572868
  1.3 46.1 %copy-start.2 = (s32[64,16,128]{2,1,0:T(8,128)S(1)}, s32[64,16,128]{2,1,0:T(8,128)}, u32[]{:S(2)}) copy-start(s32[64,16,128]{2,1,0:T(8,128)} %param.13) | copy-start | bytes 1572868
  1.3 46.2 %copy-start.3 = (f32[64,16,128]{2,1,0:T(8,128)S(1)}, f32[64,16,128]{2,1,0:T(8,128)}, u32[]{:S(2)}) copy-start(f32[64,16,128]{2,1,0:T(8,128)} %param.12) | copy-start | bytes 1572868
  6.6 40.8 %copy-start = (f32[64,16,128]{2,1,0:T(8,128)S(1)}, f32[64,16,128]{2,1,0:T(8,128)}, u32[]{:S(2)}) copy-start(f32[64,16,128]{2,1,0:T(8,128)} %param.10) | copy-start | bytes 1572868
  6.6 15.3 %collective-permute-start.2 = (f32[4,32,128]{2,1,0:T(8,128)S(1)}, f32[4,32,128]{2,1,0:T(8,128)S(1)}, u32[]{:S(2)}, u32[]{:S(2)}) collective-permute-start(f32[4,32,128]{2,1,0:T(8,128)S(1)} %get-tuple-element.38), channel_id=1, source_target_pairs={{0,1},{1,0},{2,3},{3,2},{4,5},{5,4},{6,7},{7,6},{8,9},{9,8},{10,11... | collective-permute-start | bytes 196616 | tf_op jit(solution)/shard_map/ppermute | solution.py:528
  10.5 11.4 %collective-permute-start.3 = (f32[4,32,128]{2,1,0:T(8,128)S(1)}, f32[4,32,128]{2,1,0:T(8,128)S(1)}, u32[]{:S(2)}, u32[]{:S(2)}) collective-permute-start(f32[4,32,128]{2,1,0:T(8,128)S(1)} %get-tuple-element.40), channel_id=1, source_target_pairs={{0,15},{1,2},{2,1},{3,4},{4,3},{5,6},{6,5},{7,8},{8,7},{9,10},{10,... | collective-permute-start | bytes 196616 | tf_op jit(solution)/shard_map/ppermute | solution.py:527
  17.2 2.3 %collective-permute-start = (f32[6,16,128]{2,1,0:T(8,128)S(1)}, f32[6,16,128]{2,1,0:T(8,128)S(1)}, u32[]{:S(2)}, u32[]{:S(2)}) collective-permute-start(f32[6,16,128]{2,1,0:T(8,128)S(1)} %get-tuple-element.36.lon), channel_id=1, source_target_pairs={{0,16},{16,0},{32,48},{48,32},{64,80},{80,64},{96,112},{112,96},{1... | collective-permute-start | bytes 147464 | tf_op jit(solution)/shard_map/ppermute | solution.py:530
  18.4 3.5 %collective-permute-start.1 = (f32[6,16,128]{2,1,0:T(8,128)S(1)}, f32[6,16,128]{2,1,0:T(8,128)S(1)}, u32[]{:S(2)}, u32[]{:S(2)}) collective-permute-start(f32[6,16,128]{2,1,0:T(8,128)S(1)} %get-tuple-element.36.lon), channel_id=1, source_target_pairs={{0,240},{16,32},{32,16},{48,64},{64,48},{80,96},{96,80},{112,128},... | collective-permute-start | bytes 147464 | tf_op jit(solution)/shard_map/ppermute | solution.py:529
  22.2 3.4 %collective-permute-start.4 = (f32[72,128]{1,0:T(8,128)S(1)}, f32[72,128]{1,0:T(8,128)S(1)}, u32[]{:S(2)}, u32[]{:S(2)}) collective-permute-start(f32[72,128]{1,0:T(8,128)S(1)} %shard_map.122.msg), channel_id=1, source_target_pairs={{0,16},{16,0},{32,48},{48,32},{64,80},{80,64},{96,112},{112,96},{1... | collective-permute-start | bytes 110600 | tf_op jit(solution)/shard_map/ppermute | solution.py:535
  24.7 3.4 %collective-permute-start.5 = (f32[72,128]{1,0:T(8,128)S(1)}, f32[72,128]{1,0:T(8,128)S(1)}, u32[]{:S(2)}, u32[]{:S(2)}) collective-permute-start(f32[72,128]{1,0:T(8,128)S(1)} %shard_map.122.msg), channel_id=1, source_target_pairs={{0,240},{16,32},{32,16},{48,64},{64,48},{80,96},{96,80},{112,128},... | collective-permute-start | bytes 110600 | tf_op jit(solution)/shard_map/ppermute | solution.py:534
  28.1 3.2 %copy-start.7 = (f32[5,5]{1,0:T(8,128)S(1)}, f32[5,5]{1,0:T(8,128)}, u32[]{:S(2)}) copy-start(f32[5,5]{1,0:T(8,128)} %pc.1) | copy-start | bytes 304
  28.2 3.7 %collective-permute-start.6 = (f32[16,256]{1,0:T(8,128)S(1)}, f32[16,256]{1,0:T(8,128)S(1)}, u32[]{:S(2)}, u32[]{:S(2)}) collective-permute-start(f32[16,256]{1,0:T(8,128)S(1)} %get-tuple-element.45), channel_id=1, source_target_pairs={{0,1},{1,0},{2,3},{3,2},{4,5},{5,4},{6,7},{7,6},{8,9},{9,8},{10,11... | collective-permute-start | bytes 49160 | tf_op jit(solution)/shard_map/ppermute | solution.py:541
  28.3 6.9 %collective-permute-start.7 = (f32[16,256]{1,0:T(8,128)S(1)}, f32[16,256]{1,0:T(8,128)S(1)}, u32[]{:S(2)}, u32[]{:S(2)}) collective-permute-start(f32[16,256]{1,0:T(8,128)S(1)} %get-tuple-element.46), channel_id=1, source_target_pairs={{0,15},{1,2},{2,1},{3,4},{4,3},{5,6},{6,5},{7,8},{8,7},{9,10},{10,... | collective-permute-start | bytes 49160 | tf_op jit(solution)/shard_map/ppermute | solution.py:540
  36.6 22.1 %collective-permute-start.8 = (f32[8,32,128]{2,1,0:T(8,128)S(1)}, f32[8,32,128]{2,1,0:T(8,128)S(1)}, u32[]{:S(2)}, u32[]{:S(2)}) collective-permute-start(f32[8,32,128]{2,1,0:T(8,128)S(1)} %get-tuple-element.55.a2), channel_id=1, source_target_pairs={{0,1},{1,0},{2,3},{3,2},{4,5},{5,4},{6,7},{7,6},{8,9},{9,8},{10,11... | collective-permute-start | bytes 393224 | tf_op jit(solution)/shard_map/ppermute | solution.py:569
  36.8 21.8 %collective-permute-start.9 = (f32[8,32,128]{2,1,0:T(8,128)S(1)}, f32[8,32,128]{2,1,0:T(8,128)S(1)}, u32[]{:S(2)}, u32[]{:S(2)}) collective-permute-start(f32[8,32,128]{2,1,0:T(8,128)S(1)} %get-tuple-element.56.b2), channel_id=1, source_target_pairs={{0,15},{1,2},{2,1},{3,4},{4,3},{5,6},{6,5},{7,8},{8,7},{9,10},{10,... | collective-permute-start | bytes 393224 | tf_op jit(solution)/shard_map/ppermute | solution.py:568
  39.7 14.7 %all-to-all-start = ((f32[32,1,128]{2,1,0:T(1,128)}), f32[32,1,128]{2,1,0:T(1,128)S(1)}, u32[]{:S(2)}, u32[]{:S(2)}) async-start(f32[32,1,128]{2,1,0:T(1,128)} %get-tuple-element.49), calls=%async_computation | async-start | bytes 32768 | tf_op jit(solution)/shard_map/all_to_all | solution.py:570
  55.1 10.0 %all-to-all-start.1 = ((f32[8,1,128]{2,1,0:T(1,128)}), f32[8,1,128]{2,1,0:T(1,128)S(1)}, u32[]{:S(2)}, u32[]{:S(2)}) async-start(f32[8,1,128]{2,1,0:T(1,128)} %shard_map.126), calls=%async_computation.1 | async-start | bytes 8192 | tf_op jit(solution)/shard_map/all_to_all | solution.py:592
  58.7 2.1 %copy-start.4 = (f32[64,16,128]{2,1,0:T(8,128)S(1)}, f32[64,16,128]{2,1,0:T(8,128)}, u32[]{:S(2)}) copy-start(f32[64,16,128]{2,1,0:T(8,128)} %param.9) | copy-start | bytes 1572868

commit v5 on v4

--- a/solution.py
+++ b/solution.py
@@ -343,7 +343,7 @@
     copy = pltpu.make_async_copy(got, held, sems.at[0])
     copy.start()
     copy.wait()
-    spread[...] = jnp.broadcast_to(jnp.sum(held[...], axis=0, keepdims=True), spread.shape)
+    spread[...] = jnp.broadcast_to(jnp.sum(held[...], axis=0, keepdims=True)[:, :1], spread.shape)
     copy = pltpu.make_async_copy(spread, out, sems.at[1])
     copy.start()
     copy.wait()
@@ -540,15 +540,6 @@
     got_b = lax.ppermute(side_b, LAT, SWAP_B)
     got_a = lax.ppermute(side_a, LAT, SWAP_A)
     (taps,) = call(taps_kernel, [(32, 2 * NC)], [SM], 10**4, 10**4)(precond_kernel)
-    vecs, dots = call(
-        solve_kernel,
-        [(3, NR, NC), (32, 1, NC)],
-        [VM] * 6,
-        10**6,
-        10**5,
-        [pltpu.VMEM((3, NR, NC), jnp.float32), dma],
-        [HBM, VM],
-    )(taps, rest, dg, edge, got_a, got_b)
     def velocity(early, edges, written):
         return call(
             functools.partial(velocity_kernel, early),
@@ -562,13 +553,21 @@
             aliases={9 + i: i for i in range(len(written))},
         )(u, v, vi, w, lon, lon_a, lon_b, *edges, *written)
 
-    dots, from_a, from_b = lax.optimization_barrier((dots, from_a, from_b))
     u_half, v_half = velocity(True, (from_a, from_b), ())
+    got_a, got_b, u_half, v_half = lax.optimization_barrier((got_a, got_b, u_half, v_half))
+    vecs, dots = call(
+        solve_kernel,
+        [(3, NR, NC), (32, 8, NC)],
+        [VM] * 6,
+        10**6,
+        10**5,
+        [pltpu.VMEM((3, NR, NC), jnp.float32), dma],
+        [HBM, VM],
+    )(taps, rest, dg, edge, got_a, got_b)
     dots, a2, b2 = lax.optimization_barrier((dots, a2, b2))
     from_b2 = lax.ppermute(b2, LAT, SWAP_B)
     from_a2 = lax.ppermute(a2, LAT, SWAP_A)
     dots = lax.all_to_all(dots, ("x", "y", "c"), 0, 0)
-    dots, u_half, v_half = lax.optimization_barrier((dots, u_half, v_half))
     lat = (from_a, from_a2, from_b, from_b2)
     u_new, v_new = velocity(False, (from_a2, from_b2), (u_half, v_half))
     t_new = call(
@@ -586,7 +585,7 @@
         [HBM],
         10**4,
         10**4,
-        [pltpu.VMEM((32, 1, NC), jnp.float32), pltpu.VMEM((8, 1, NC), jnp.float32), dma((2,))],
+        [pltpu.VMEM((32, 8, NC), jnp.float32), pltpu.VMEM((8, 1, NC), jnp.float32), dma((2,))],
         HBM,
     )(dots)
     dots = lax.all_to_all(dots, ("zl", "zh"), 0, 0)

time: 66 us -> 62.8 us (0.952)
  waiting for transfers between devices: 15.3 us -> 7.4 us
  starting transfers between devices: 32.9 us -> 37.4 us
    ppermute x1, waiting for transfers between devices: 2.52 us -> 0.01 us  [local(): msg_b = lax.ppermute(msg, LON, SWAP_B)]
    ppermute x1, waiting for transfers between devices: 3.27 us -> 1.06 us  [local(): got_b = lax.ppermute(side_b, LAT, SWAP_B)]
    ppermute x1, starting transfers between devices: 0.01 us -> 1.72 us  [local(): msg_b = lax.ppermute(msg, LON, SWAP_B)]
    ppermute x1, waiting for transfers between devices: 2.41 us -> 0.78 us  [local(): lon_b = lax.ppermute(lon, LON, SWAP_B)]
    all_to_all x1, waiting for transfers between devices: 4.9 us -> 3.36 us  [local(): dots = lax.all_to_all(dots, ('x', 'y', 'c'), 0, 0)]
    ppermute x1, starting transfers between devices: 1.1 us -> 2.33 us  [local(): lon_b = lax.ppermute(lon, LON, SWAP_B)]
    ppermute x1, starting transfers between devices: 2.9 us -> 4.03 us  [local(): from_b2 = lax.ppermute(b2, LAT, SWAP_B)]
  transfers between devices with their start and end apart: 12 -> 12, of which waited for: 6 -> 6; matrix products, arithmetic and copies ran while one was open for 0% -> 0% of each run, Pallas kernels for 13% -> 14%
where the time goes in v5:
time: 62.8 us; the launch traced here: 62.6 us
  starting transfers between devices  37.4 us (60%)
  Pallas kernels  16.3 us (26%)
  waiting for transfers between devices  7.4 us (12%)
  between operations  0.84 us (1%)
  local copies, waits for them, and re-layouts  0.68 us (1%)
    all_to_all x1, starting transfers between devices, local(): dots = lax.all_to_all(dots, ('x', 'y', 'c'), 0, 0)  7.57 us
    ppermute x1, starting transfers between devices, local(): from_b = lax.ppermute(b, LAT, SWAP_B)  6.65 us
    pallas_call x1, Pallas kernels, local(): call(fetch_kernel, [(6, NR, NC), rows, rows, late, late, (2, NR, NC), (NZ...  5.3 us
    pallas_call x2, Pallas kernels, velocity(): call(functools.partial(velocity_kernel, early), [flat] * 2, [VM] * 9 + [H...  4.07 us
    ppermute x1, starting transfers between devices, local(): from_b2 = lax.ppermute(b2, LAT, SWAP_B)  4.03 us
    ppermute x1, starting transfers between devices, local(): from_a = lax.ppermute(a, LAT, SWAP_A)  3.91 us
    all_to_all x1, waiting for transfers between devices, local(): dots = lax.all_to_all(dots, ('x', 'y', 'c'), 0, 0)  3.36 us
    all_to_all x1, starting transfers between devices, local(): dots = lax.all_to_all(dots, ('zl', 'zh'), 0, 0)  3.32 us
  transfers between devices with their start and end apart: 12, of which 6 were waited for; matrix products, arithmetic and copies ran while one was open for 0% of the time, Pallas kernels for 14%

profile of v5, /device:TPU:1, one launch (start us, length us, event | category | flops | bytes accessed | tf_op | source)
XLA Modules:
  0.0 62.6 jit_solution(17425241874825603900)
XLA Ops:
  0.6 0.0 copy-start.8
  0.6 0.6 %copy-done.8 = f32[64]{0:T(128)S(1)} copy-done((f32[64]{0:T(128)S(1)}, f32[64]{0:T(128)}, u32[]{:S(2)}) %copy-start.8) | copy-done | bytes 280
  1.3 0.0 copy-start.5
  1.3 0.0 copy-start.3
  1.3 5.3 %shard_map.121 = (f32[6,16,128]{2,1,0:T(8,128)S(1)}, f32[4,32,128]{2,1,0:T(8,128)S(1)}, f32[4,32,128]{2,1,0:T(8,128)S(1)}, f32[8,32,128]{2,1,0:T(8,128)S(1)}, f3...) custom-call(f32[64]{0:T(128)S(1)} %copy-done.8, f32[1024,128]{1,0:T(8,128)} %bitcast.8, ...), custom_call_target="tpu_custom_call" | custom-call | flops 6553600 | bytes 2621440 | tf_op jit(solution)/shard_map/pallas_call | solution.py:518
  6.6 0.0 copy-start
  6.6 3.9 %collective-permute-start.2 = (f32[4,32,128]{2,1,0:T(8,128)S(1)}, f32[4,32,128]{2,1,0:T(8,128)S(1)}, u32[]{:S(2)}, u32[]{:S(2)}) collective-permute-start(f32[4,32,128]{2,1,0:T(8,128)S(1)} %get-tuple-element.36), channel_id=1, source_target_pairs={{0,1},{1,0},{2,3},{3,2},{4,5},{5,4},{6,7},{7,6},{8,9},{9,8},{10,11... | collective-permute-start | bytes 196616 | tf_op jit(solution)/shard_map/ppermute | solution.py:528
  10.5 6.7 %collective-permute-start.3 = (f32[4,32,128]{2,1,0:T(8,128)S(1)}, f32[4,32,128]{2,1,0:T(8,128)S(1)}, u32[]{:S(2)}, u32[]{:S(2)}) collective-permute-start(f32[4,32,128]{2,1,0:T(8,128)S(1)} %get-tuple-element.38), channel_id=1, source_target_pairs={{0,15},{1,2},{2,1},{3,4},{4,3},{5,6},{6,5},{7,8},{8,7},{9,10},{10,... | collective-permute-start | bytes 196616 | tf_op jit(solution)/shard_map/ppermute | solution.py:527
  17.2 2.3 %collective-permute-start.1 = (f32[6,16,128]{2,1,0:T(8,128)S(1)}, f32[6,16,128]{2,1,0:T(8,128)S(1)}, u32[]{:S(2)}, u32[]{:S(2)}) collective-permute-start(f32[6,16,128]{2,1,0:T(8,128)S(1)} %get-tuple-element.34.lon), channel_id=1, source_target_pairs={{0,240},{16,32},{32,16},{48,64},{64,48},{80,96},{96,80},{112,128},... | collective-permute-start | bytes 147464 | tf_op jit(solution)/shard_map/ppermute | solution.py:529
  19.5 1.0 %collective-permute-start = (f32[6,16,128]{2,1,0:T(8,128)S(1)}, f32[6,16,128]{2,1,0:T(8,128)S(1)}, u32[]{:S(2)}, u32[]{:S(2)}) collective-permute-start(f32[6,16,128]{2,1,0:T(8,128)S(1)} %get-tuple-element.34.lon), channel_id=1, source_target_pairs={{0,16},{16,0},{32,48},{48,32},{64,80},{80,64},{96,112},{112,96},{1... | collective-permute-start | bytes 147464 | tf_op jit(solution)/shard_map/ppermute | solution.py:530
  20.5 0.8 %collective-permute-done.1.lon_b = f32[6,16,128]{2,1,0:T(8,128)S(1)} collective-permute-done((f32[6,16,128]{2,1,0:T(8,128)S(1)}, f32[6,16,128]{2,1,0:T(8,128)S(1)}, u32[]{:S(2)}, u32[]{:S(2)}) %collective-permute-start.1) | collective-permute-done | bytes 49184 | tf_op jit(solution)/shard_map/ppermute | solution.py:529
  21.3 0.1 collective-permute-done.lon_a
  21.4 0.0 collective-permute-done.2.from_a
  21.4 0.0 collective-permute-done.3.from_b
  21.4 0.0 copy-done.5
  21.4 0.0 copy-done.6
  21.4 0.2 shard_map.122.msg
  21.6 1.7 %collective-permute-start.5 = (f32[72,128]{1,0:T(8,128)S(1)}, f32[72,128]{1,0:T(8,128)S(1)}, u32[]{:S(2)}, u32[]{:S(2)}) collective-permute-start(f32[72,128]{1,0:T(8,128)S(1)} %shard_map.122.msg), channel_id=1, source_target_pairs={{0,240},{16,32},{32,16},{48,64},{64,48},{80,96},{96,80},{112,128},... | collective-permute-start | bytes 110600 | tf_op jit(solution)/shard_map/ppermute | solution.py:534
  23.3 3.1 %collective-permute-start.4 = (f32[72,128]{1,0:T(8,128)S(1)}, f32[72,128]{1,0:T(8,128)S(1)}, u32[]{:S(2)}, u32[]{:S(2)}) collective-permute-start(f32[72,128]{1,0:T(8,128)S(1)} %shard_map.122.msg), channel_id=1, source_target_pairs={{0,16},{16,0},{32,48},{48,32},{64,80},{80,64},{96,112},{112,96},{1... | collective-permute-start | bytes 110600 | tf_op jit(solution)/shard_map/ppermute | solution.py:535
  26.4 0.0 collective-permute-done.5.msg_b
  26.4 0.9 %collective-permute-done.4.msg_a = f32[72,128]{1,0:T(8,128)S(1)} collective-permute-done((f32[72,128]{1,0:T(8,128)S(1)}, f32[72,128]{1,0:T(8,128)S(1)}, u32[]{:S(2)}, u32[]{:S(2)}) %collective-permute-start.4) | collective-permute-done | bytes 36896 | tf_op jit(solution)/shard_map/ppermute | solution.py:535
  27.3 0.1 shard_map.123
  27.4 0.1 collective-permute-start.6
  27.5 3.1 %collective-permute-start.7 = (f32[16,256]{1,0:T(8,128)S(1)}, f32[16,256]{1,0:T(8,128)S(1)}, u32[]{:S(2)}, u32[]{:S(2)}) collective-permute-start(f32[16,256]{1,0:T(8,128)S(1)} %get-tuple-element.44), channel_id=1, source_target_pairs={{0,15},{1,2},{2,1},{3,4},{4,3},{5,6},{6,5},{7,8},{8,7},{9,10},{10,... | collective-permute-start | bytes 49160 | tf_op jit(solution)/shard_map/ppermute | solution.py:540
  30.6 0.0 copy-done.7
  30.6 0.6 shard_map.120.pc
  31.2 0.0 copy-done.1
  31.3 0.0 copy-done.2
  31.3 0.0 copy-done.3
  31.3 0.0 copy-done
  31.3 2.0 %shard_map.124 = (f32[1024,128]{1,0:T(8,128)}, f32[1024,128]{1,0:T(8,128)}) custom-call(f32[1024,128]{1,0:T(8,128)S(1)} %bitcast.9, f32[1024,128]{1,0:T(8,128)S(1)} %bitcast.13, f32[1024,128]{1,0:T(8,128)S(1)} %bitcast.21, s32[1024,128]{1,0:T(8,128)S(1)} %bitcast.17, f32[6,16,128]{2,1,0:T(8,128)S(1)} %get-tuple-element.34.lon, ...), custom_call_target="tpu_custom_call" | custom-call | flops 3932160 | bytes 1572864 | tf_op jit(solution)/shard_map/pallas_call | solution.py:544
  33.3 0.0 collective-permute-done.6.from_a
  33.3 1.1 %collective-permute-done.7.from_b = f32[16,256]{1,0:T(8,128)S(1)} collective-permute-done((f32[16,256]{1,0:T(8,128)S(1)}, f32[16,256]{1,0:T(8,128)S(1)}, u32[]{:S(2)}, u32[]{:S(2)}) %collective-permute-start.7) | collective-permute-done | bytes 16416 | tf_op jit(solution)/shard_map/ppermute | solution.py:540
  34.4 1.5 %shard_map.125 = (f32[3,16,128]{2,1,0:T(8,128)S(1)}, f32[32,8,128]{2,1,0:T(8,128)}) custom-call(f32[32,256]{1,0:T(8,128)S(1)} %shard_map.120.pc, f32[16,256]{1,0:T(8,128)S(1)} %get-tuple-element.40.rest, f32[16,256]{1,0:T(8,128)S(1)} %get-tuple-element.41.dg, f32[8,256]{1,0:T(8,128)S(1)} %get-tuple-element.42.edge, ...), custom_call_target="tpu_custom_call" | custom-call | flops 1000000 | bytes 100000 | tf_op jit(solution)/shard_map/pallas_call | solution.py:558
  35.9 7.6 %all-to-all-start = ((f32[32,8,128]{2,1,0:T(8,128)}), f32[32,8,128]{2,1,0:T(8,128)S(1)}, u32[]{:S(2)}, u32[]{:S(2)}) async-start(f32[32,8,128]{2,1,0:T(8,128)} %get-tuple-element.50), calls=%async_computation | async-start | bytes 262144 | tf_op jit(solution)/shard_map/all_to_all | solution.py:570
  43.5 0.5 collective-permute-start.8
  44.0 4.0 %collective-permute-start.9 = (f32[8,32,128]{2,1,0:T(8,128)S(1)}, f32[8,32,128]{2,1,0:T(8,128)S(1)}, u32[]{:S(2)}, u32[]{:S(2)}) collective-permute-start(f32[8,32,128]{2,1,0:T(8,128)S(1)} %get-tuple-element.52.b2), channel_id=1, source_target_pairs={{0,15},{1,2},{2,1},{3,4},{4,3},{5,6},{6,5},{7,8},{8,7},{9,10},{10,... | collective-permute-start | bytes 393224 | tf_op jit(solution)/shard_map/ppermute | solution.py:568
  48.0 3.4 %all-to-all-done.got = f32[32,8,128]{2,1,0:T(8,128)S(1)} async-done(((f32[32,8,128]{2,1,0:T(8,128)}), f32[32,8,128]{2,1,0:T(8,128)S(1)}, u32[]{:S(2)}, u32[]{:S(2)}) %all-to-all-start) | async-done | bytes 131104 | tf_op jit(solution)/shard_map/all_to_all | solution.py:570
  51.4 0.8 %shard_map.126 = f32[8,1,128]{2,1,0:T(1,128)} custom-call(f32[32,8,128]{2,1,0:T(8,128)S(1)} %all-to-all-done.got), custom_call_target="tpu_custom_call" | custom-call | flops 10000 | bytes 10000 | tf_op jit(solution)/shard_map/pallas_call | solution.py:582
  52.2 3.3 %all-to-all-start.1 = ((f32[8,1,128]{2,1,0:T(1,128)}), f32[8,1,128]{2,1,0:T(1,128)S(1)}, u32[]{:S(2)}, u32[]{:S(2)}) async-start(f32[8,1,128]{2,1,0:T(1,128)} %shard_map.126), calls=%async_computation.1 | async-start | bytes 8192 | tf_op jit(solution)/shard_map/all_to_all | solution.py:591
  55.5 0.0 copy-start.4
  55.5 0.0 collective-permute-done.8.from_a2.from_a
  55.5 0.0 collective-permute-done.9.from_b2.from_b
  55.5 2.0 %shard_map.128 = (f32[1024,128]{1,0:T(8,128)}, f32[1024,128]{1,0:T(8,128)}) custom-call(f32[1024,128]{1,0:T(8,128)S(1)} %bitcast.10, f32[1024,128]{1,0:T(8,128)S(1)} %bitcast.14, f32[1024,128]{1,0:T(8,128)S(1)} %bitcast.22, s32[1024,128]{1,0:T(8,128)S(1)} %bitcast.18, ...), custom_call_target="tpu_custom_call", output_to_operand_aliasing={{0}: (9, {}), {1}: (10, {})} | custom-call | flops 3932160 | bytes 1572864 | tf_op jit(solution)/shard_map/pallas_call | solution.py:544
  57.6 0.0 copy-done.4
  57.6 3.0 %shard_map.127 = f32[1024,128]{1,0:T(8,128)} custom-call(f32[1024,128]{1,0:T(8,128)S(1)} %bitcast.24, f32[1024,128]{1,0:T(8,128)S(1)} %bitcast.11, f32[1024,128]{1,0:T(8,128)S(1)} %bitcast.15, s32[1024,128]{1,0:T(8,128)S(1)} %bitcast.19, f32[6,16,128]{2,1,0:T(8,128)S(1)} %get-tuple-element.34.lon, f32[6,16,128]{2,1,0:T(8,128)S(1)} %collective-permute-done.lon_a, ...), custom_call_target="tpu_custom_call" | custom-call | flops 7864320 | bytes 2621440 | tf_op jit(solution)/shard_map/pallas_call | solution.py:573
  60.6 1.2 %all-to-all-done.1.got = f32[8,1,128]{2,1,0:T(1,128)S(1)} async-done(((f32[8,1,128]{2,1,0:T(1,128)}), f32[8,1,128]{2,1,0:T(1,128)S(1)}, u32[]{:S(2)}, u32[]{:S(2)}) %all-to-all-start.1) | async-done | bytes 4128 | tf_op jit(solution)/shard_map/all_to_all | solution.py:591
  61.8 0.7 %shard_map.129 = f32[16,128]{1,0:T(8,128)} custom-call(f32[8,1,128]{2,1,0:T(1,128)S(1)} %all-to-all-done.1.got, f32[3,16,128]{2,1,0:T(8,128)S(1)} %get-tuple-element.61.v, f32[16,128]{1,0:T(8,128)S(1)} %copy-done.5), custom_call_target="tpu_custom_call" | custom-call | flops 100000 | bytes 10000 | tf_op jit(solution)/shard_map/pallas_call | solution.py:593
  (4 shorter events, 0.0 us)
Async XLA Ops:
  0.6 0.7 %copy-start.8 = (f32[64]{0:T(128)S(1)}, f32[64]{0:T(128)}, u32[]{:S(2)}) copy-start(f32[64]{0:T(128)} %thick_hbm.1) | copy-start | bytes 772
  1.3 20.1 %copy-start.5 = (f32[16,128]{1,0:T(8,128)S(1)}, f32[16,128]{1,0:T(8,128)}, u32[]{:S(2)}) copy-start(f32[16,128]{1,0:T(8,128)} %sf.3) | copy-start | bytes 24580
  1.3 20.1 %copy-start.6 = (f32[16,128]{1,0:T(8,128)S(1)}, f32[16,128]{1,0:T(8,128)}, u32[]{:S(2)}) copy-start(f32[16,128]{1,0:T(8,128)} %dg.1) | copy-start | bytes 24580
  1.3 30.0 %copy-start.1 = (f32[64,16,128]{2,1,0:T(8,128)S(1)}, f32[64,16,128]{2,1,0:T(8,128)}, u32[]{:S(2)}) copy-start(f32[64,16,128]{2,1,0:T(8,128)} %param.11) | copy-start | bytes 1572868
  1.3 30.0 %copy-start.2 = (s32[64,16,128]{2,1,0:T(8,128)S(1)}, s32[64,16,128]{2,1,0:T(8,128)}, u32[]{:S(2)}) copy-start(s32[64,16,128]{2,1,0:T(8,128)} %param.13) | copy-start | bytes 1572868
  1.3 30.0 %copy-start.3 = (f32[64,16,128]{2,1,0:T(8,128)S(1)}, f32[64,16,128]{2,1,0:T(8,128)}, u32[]{:S(2)}) copy-start(f32[64,16,128]{2,1,0:T(8,128)} %param.12) | copy-start | bytes 1572868
  6.6 24.7 %copy-start = (f32[64,16,128]{2,1,0:T(8,128)S(1)}, f32[64,16,128]{2,1,0:T(8,128)}, u32[]{:S(2)}) copy-start(f32[64,16,128]{2,1,0:T(8,128)} %param.10) | copy-start | bytes 1572868
  6.6 14.8 %collective-permute-start.2 = (f32[4,32,128]{2,1,0:T(8,128)S(1)}, f32[4,32,128]{2,1,0:T(8,128)S(1)}, u32[]{:S(2)}, u32[]{:S(2)}) collective-permute-start(f32[4,32,128]{2,1,0:T(8,128)S(1)} %get-tuple-element.36), channel_id=1, source_target_pairs={{0,1},{1,0},{2,3},{3,2},{4,5},{5,4},{6,7},{7,6},{8,9},{9,8},{10,11... | collective-permute-start | bytes 196616 | tf_op jit(solution)/shard_map/ppermute | solution.py:528
  10.5 10.9 %collective-permute-start.3 = (f32[4,32,128]{2,1,0:T(8,128)S(1)}, f32[4,32,128]{2,1,0:T(8,128)S(1)}, u32[]{:S(2)}, u32[]{:S(2)}) collective-permute-start(f32[4,32,128]{2,1,0:T(8,128)S(1)} %get-tuple-element.38), channel_id=1, source_target_pairs={{0,15},{1,2},{2,1},{3,4},{4,3},{5,6},{6,5},{7,8},{8,7},{9,10},{10,... | collective-permute-start | bytes 196616 | tf_op jit(solution)/shard_map/ppermute | solution.py:527
  17.2 4.1 %collective-permute-start.1 = (f32[6,16,128]{2,1,0:T(8,128)S(1)}, f32[6,16,128]{2,1,0:T(8,128)S(1)}, u32[]{:S(2)}, u32[]{:S(2)}) collective-permute-start(f32[6,16,128]{2,1,0:T(8,128)S(1)} %get-tuple-element.34.lon), channel_id=1, source_target_pairs={{0,240},{16,32},{32,16},{48,64},{64,48},{80,96},{96,80},{112,128},... | collective-permute-start | bytes 147464 | tf_op jit(solution)/shard_map/ppermute | solution.py:529
  19.5 1.9 %collective-permute-start = (f32[6,16,128]{2,1,0:T(8,128)S(1)}, f32[6,16,128]{2,1,0:T(8,128)S(1)}, u32[]{:S(2)}, u32[]{:S(2)}) collective-permute-start(f32[6,16,128]{2,1,0:T(8,128)S(1)} %get-tuple-element.34.lon), channel_id=1, source_target_pairs={{0,16},{16,0},{32,48},{48,32},{64,80},{80,64},{96,112},{112,96},{1... | collective-permute-start | bytes 147464 | tf_op jit(solution)/shard_map/ppermute | solution.py:530
  21.6 4.8 %collective-permute-start.5 = (f32[72,128]{1,0:T(8,128)S(1)}, f32[72,128]{1,0:T(8,128)S(1)}, u32[]{:S(2)}, u32[]{:S(2)}) collective-permute-start(f32[72,128]{1,0:T(8,128)S(1)} %shard_map.122.msg), channel_id=1, source_target_pairs={{0,240},{16,32},{32,16},{48,64},{64,48},{80,96},{96,80},{112,128},... | collective-permute-start | bytes 110600 | tf_op jit(solution)/shard_map/ppermute | solution.py:534
  23.3 4.0 %collective-permute-start.4 = (f32[72,128]{1,0:T(8,128)S(1)}, f32[72,128]{1,0:T(8,128)S(1)}, u32[]{:S(2)}, u32[]{:S(2)}) collective-permute-start(f32[72,128]{1,0:T(8,128)S(1)} %shard_map.122.msg), channel_id=1, source_target_pairs={{0,16},{16,0},{32,48},{48,32},{64,80},{80,64},{96,112},{112,96},{1... | collective-permute-start | bytes 110600 | tf_op jit(solution)/shard_map/ppermute | solution.py:535
  27.3 3.3 %copy-start.7 = (f32[5,5]{1,0:T(8,128)S(1)}, f32[5,5]{1,0:T(8,128)}, u32[]{:S(2)}) copy-start(f32[5,5]{1,0:T(8,128)} %pc.1) | copy-start | bytes 304
  27.4 5.9 %collective-permute-start.6 = (f32[16,256]{1,0:T(8,128)S(1)}, f32[16,256]{1,0:T(8,128)S(1)}, u32[]{:S(2)}, u32[]{:S(2)}) collective-permute-start(f32[16,256]{1,0:T(8,128)S(1)} %get-tuple-element.43), channel_id=1, source_target_pairs={{0,1},{1,0},{2,3},{3,2},{4,5},{5,4},{6,7},{7,6},{8,9},{9,8},{10,11... | collective-permute-start | bytes 49160 | tf_op jit(solution)/shard_map/ppermute | solution.py:541
  27.5 6.9 %collective-permute-start.7 = (f32[16,256]{1,0:T(8,128)S(1)}, f32[16,256]{1,0:T(8,128)S(1)}, u32[]{:S(2)}, u32[]{:S(2)}) collective-permute-start(f32[16,256]{1,0:T(8,128)S(1)} %get-tuple-element.44), channel_id=1, source_target_pairs={{0,15},{1,2},{2,1},{3,4},{4,3},{5,6},{6,5},{7,8},{8,7},{9,10},{10,... | collective-permute-start | bytes 49160 | tf_op jit(solution)/shard_map/ppermute | solution.py:540
  35.9 15.5 %all-to-all-start = ((f32[32,8,128]{2,1,0:T(8,128)}), f32[32,8,128]{2,1,0:T(8,128)S(1)}, u32[]{:S(2)}, u32[]{:S(2)}) async-start(f32[32,8,128]{2,1,0:T(8,128)} %get-tuple-element.50), calls=%async_computation | async-start | bytes 262144 | tf_op jit(solution)/shard_map/all_to_all | solution.py:570
  43.5 12.1 %collective-permute-start.8 = (f32[8,32,128]{2,1,0:T(8,128)S(1)}, f32[8,32,128]{2,1,0:T(8,128)S(1)}, u32[]{:S(2)}, u32[]{:S(2)}) collective-permute-start(f32[8,32,128]{2,1,0:T(8,128)S(1)} %get-tuple-element.51.a2), channel_id=1, source_target_pairs={{0,1},{1,0},{2,3},{3,2},{4,5},{5,4},{6,7},{7,6},{8,9},{9,8},{10,11... | collective-permute-start | bytes 393224 | tf_op jit(solution)/shard_map/ppermute | solution.py:569
  44.0 11.5 %collective-permute-start.9 = (f32[8,32,128]{2,1,0:T(8,128)S(1)}, f32[8,32,128]{2,1,0:T(8,128)S(1)}, u32[]{:S(2)}, u32[]{:S(2)}) collective-permute-start(f32[8,32,128]{2,1,0:T(8,128)S(1)} %get-tuple-element.52.b2), channel_id=1, source_target_pairs={{0,15},{1,2},{2,1},{3,4},{4,3},{5,6},{6,5},{7,8},{8,7},{9,10},{10,... | collective-permute-start | bytes 393224 | tf_op jit(solution)/shard_map/ppermute | solution.py:568
  52.2 9.7 %all-to-all-start.1 = ((f32[8,1,128]{2,1,0:T(1,128)}), f32[8,1,128]{2,1,0:T(1,128)S(1)}, u32[]{:S(2)}, u32[]{:S(2)}) async-start(f32[8,1,128]{2,1,0:T(1,128)} %shard_map.126), calls=%async_computation.1 | async-start | bytes 8192 | tf_op jit(solution)/shard_map/all_to_all | solution.py:591
  55.5 2.1 %copy-start.4 = (f32[64,16,128]{2,1,0:T(8,128)S(1)}, f32[64,16,128]{2,1,0:T(8,128)}, u32[]{:S(2)}) copy-start(f32[64,16,128]{2,1,0:T(8,128)} %param.9) | copy-start | bytes 1572868

commit v6 on v5

--- a/solution.py
+++ b/solution.py
@@ -23,7 +23,6 @@
 SM = pl.BlockSpec(memory_space=pltpu.SMEM)
 HBM = pl.BlockSpec(memory_space=pltpu.HBM)
 FETCH_VMEM = 53.25
-FETCH_UNROLL = 4
 
 
 def call(kernel, outs, specs, flops, nbytes, scratch=(), place=VM, vmem=4, aliases=None):
@@ -115,70 +114,93 @@
     return pl.ds(pl.multiple_of(k * NR, NR), NR)
 
 
-def fetch_kernel(
-    thick_hbm, u, v, vi, land, t,
-    lon_out, a_out, b_out, late_a, late_b, out, th_out, uo, vo, vio, lo, to, thick, sems, th_sem,
-):
+def fetch_kernel(u, v, vi, land, lon_out, a_out, b_out, other_a, other_b, uo, vo, vio, lo, sems):
+    pair = lane_of((NR, NC)) // 2
+
+    def body(k, acc):
+        at = level(k)
+        values = (uo[at, :], vo[at, :], vio[at, :], lo[at, :].astype(jnp.float32))
+        mine = pair == k
+        return tuple(
+            jnp.where(mine, pltpu.roll(x, 2 * k + 1, 1), old) for x, old in zip(values, acc)
+        )
+
+    copies = chunk_copies(((u, uo), (v, vo), (vi, vio), (land, lo)), sems)
+    acc = pipeline(copies, body, (jnp.zeros((NR, NC), jnp.float32),) * 4, 8)
+    for i in range(4):
+        lon_out[i] = acc[i]
+    even = even_lat()
+    mine, theirs = halves()
+    for north, first, rest in ((even, a_out, other_a), (jnp.logical_not(even), b_out, other_b)):
+        for i, ref in enumerate((uo, vo, vio, lo)):
+            first[i] = edge_row(ref, north, 0, mine, HALF)
+            rest[i] = edge_row(ref, north, 0, theirs, HALF)
+
+
+def inner_kernel(thick, u, v, vi, w, out, th_out):
     lane, row = lane_of((NR, NC)), row_of((NR, NC))
-    pair = lane // 2
-    half_lane = lane < NC // 2
+    pair = lane[:1] // 2
     up = lambda x: pltpu.roll(x, NC - 1, 1)
     north_of = lambda x: pltpu.roll(x, NR - 1, 0)
 
     def body(k, acc):
         at = level(k)
-        wet, uu, vv, visc = lo[at, :].astype(jnp.float32), uo[at, :], vo[at, :], vio[at, :]
-        mine = pair == k
-        first = to[at, :] * wet
-        inner = jnp.where(half_lane, up(first), pltpu.roll(first, 1, 1))
-        packed = tuple(
-            jnp.where(mine, pltpu.roll(x, 2 * k + 1, 1), old)
-            for x, old in zip((uu, vv, visc, wet, first, 7.0 * first - inner), acc[:6])
-        )
+        wet, uu, vv, visc = w[at, :].astype(jnp.float32), u[at, :], v[at, :], vi[at, :]
         th = jnp.full((1, NC), thick[k], jnp.float32)
         th_out[pl.ds(k, 1), :] = th
         own = wet * th
         half = 0.5 * own
         east = (visc + up(visc)) * (half * up(wet))
         north = (visc + north_of(visc)) * (half * north_of(wet))
-        return packed + (
-            acc[6] + own * uu,
-            acc[7] + east * (up(uu) - uu),
-            acc[8] + north * (north_of(uu) - uu),
-            acc[9] + own * vv,
-            acc[10] + east * (up(vv) - vv),
-            acc[11] + north * (north_of(vv) - vv),
-            jnp.where(mine[:1], th, acc[12]),
+        return (
+            acc[0] + own * uu,
+            acc[1] + east * (up(uu) - uu),
+            acc[2] + north * (north_of(uu) - uu),
+            acc[3] + own * vv,
+            acc[4] + east * (up(vv) - vv),
+            acc[5] + north * (north_of(vv) - vv),
+            jnp.where(pair == k, th, acc[6]),
         )
 
-    thick_copy = pltpu.make_async_copy(thick_hbm, thick, th_sem)
-    thick_copy.start()
-    copies = chunk_copies(((u, uo), (v, vo), (vi, vio), (land, lo), (t, to)), sems)
-    thick_copy.wait()
     zero = jnp.zeros((NR, NC), jnp.float32)
-    acc = pipeline(copies, body, (zero,) * 12 + (zero[:1],), FETCH_UNROLL)
-    for i in range(6):
-        lon_out[i] = acc[i]
-    th_out[NZ:, :] = jnp.broadcast_to(acc[12], (8, NC))
+    acc = lax.fori_loop(0, NZ, body, (zero,) * 6 + (zero[:1],), unroll=4)
+    th_out[NZ:, :] = jnp.broadcast_to(acc[6], (8, NC))
     for i in range(2):
-        east = jnp.where(lane == NC - 1, 0.0, acc[3 * i + 7])
-        north = jnp.where(row == NR - 1, 0.0, acc[3 * i + 8])
-        out[i] = acc[3 * i + 6] + DT_VISC * (
+        east = jnp.where(lane == NC - 1, 0.0, acc[3 * i + 1])
+        north = jnp.where(row == NR - 1, 0.0, acc[3 * i + 2])
+        out[i] = acc[3 * i] + DT_VISC * (
             east - pltpu.roll(east, 1, 1) + north - pltpu.roll(north, 1, 0)
         )
+
+
+def late_kernel(t, w, other_a, other_b, lon_out, a_out, b_out):
+    lane = lane_of((NR, NC))
+    pair = lane // 2
+    half_lane = lane < NC // 2
+
+    def body(k, acc):
+        at = level(k)
+        first = t[at, :] * w[at, :].astype(jnp.float32)
+        inner = jnp.where(half_lane, pltpu.roll(first, NC - 1, 1), pltpu.roll(first, 1, 1))
+        mine = pair == k
+        return tuple(
+            jnp.where(mine, pltpu.roll(x, 2 * k + 1, 1), old)
+            for x, old in zip((first, 7.0 * first - inner), acc)
+        )
+
+    acc = lax.fori_loop(0, NZ, body, (jnp.zeros((NR, NC), jnp.float32),) * 2, unroll=8)
+    lon_out[0] = acc[0]
+    lon_out[1] = acc[1]
     even = even_lat()
-    mine, theirs = halves()
-    for north, first, rest in ((even, a_out, late_a), (jnp.logical_not(even), b_out, late_b)):
-        for i, ref in enumerate((uo, vo, vio, lo)):
-            first[i] = edge_row(ref, north, 0, mine, HALF)
-            rest[i] = edge_row(ref, north, 0, theirs, HALF)
+    for north, src, dst in ((even, other_a, a_out), (jnp.logical_not(even), other_b, b_out)):
+        dst[:4] = src[...]
         for i in range(2):
             near, inner = (
-                edge_row(to, north, n, i * HALF, HALF) * edge_row(lo, north, n, i * HALF, HALF)
+                edge_row(t, north, n, i * HALF, HALF) * edge_row(w, north, n, i * HALF, HALF)
                 for n in range(2)
             )
-            rest[4 + i] = near
-            rest[6 + i] = 7.0 * near - inner
+            dst[4 + i] = near
+            dst[6 + i] = 7.0 * near - inner
 
 
 def taps_kernel(pc, out):
@@ -266,7 +288,7 @@
 
 
 def solve_kernel(pc, rest, dg, edge, from_a, from_b, v_hbm, dots_out, v_out, sem):
-    rows, wide = 3 * NR, 2 * NC
+    rows, wide = 2 * NR, 2 * NC
     even = even_lat()
     exists = b_exists()
     msg_a = from_a[...]
@@ -274,24 +296,25 @@
     north = jnp.where(even, msg_a, msg_b)
     south = jnp.where(even, msg_b, msg_a)
     zeros = lambda n: jnp.zeros((n, wide), jnp.float32)
-    row = row_of((rows, wide))
+    row = row_of((rows + 8, wide))
     lat = lat_index()
-    low = jnp.where(lat == 0, NR, 0)
-    high = jnp.where(lat == 15, 2 * NR, 3 * NR)
+    low = jnp.where(lat == 0, 8, 0)
+    high = jnp.where(lat == 15, 8 + NR, rows + 8)
     inside = jnp.where(jnp.logical_and(row >= low, row < high), 1.0, 0.0).astype(jnp.float32)
-    below = jnp.concatenate([zeros(8), south[:7], south[7:8] + edge[2:3]], axis=0)
+    below = jnp.concatenate([south[:7], south[7:8] + edge[2:3]], axis=0)
     above = jnp.concatenate(
         [north[:1] + edge[0:1], north[1:2] + edge[1:2], north[2:9], zeros(7)], axis=0
     )
     own = rest[...] + jnp.concatenate([south[13:15], zeros(13), north[15:]], axis=0)
     res = jnp.concatenate([below, own, above], axis=0) * inside
-    diag = 4.0 + jnp.concatenate([zeros(11), south[8:13], dg[...], north[9:15], zeros(10)], axis=0)
+    inside = inside[:rows]
+    diag = 4.0 + jnp.concatenate([zeros(3), south[8:13], dg[...], north[9:15], zeros(2)], axis=0)
 
     def lon_shift(x, n):
         return x if n == 0 else pltpu.roll(x, (-n) % wide, 1)
 
     def lat_shift(x, n):
-        return x if n == 0 else pltpu.roll(x, (-n) % rows, 0)
+        return x if n == 0 else pltpu.roll(x, (-n) % x.shape[0], 0)
 
     def operate(x):
         near = lon_shift(x, 1) + lon_shift(x, -1) + lat_shift(x, 1) + lat_shift(x, -1)
@@ -308,7 +331,7 @@
             line = tap(a, -2) * moved[0]
             for b in range(1, 5):
                 line = line + tap(a, b - 2) * moved[b]
-            line = lat_shift(line, a)
+            line = lat_shift(line, a)[:rows]
             total = line if total is None else total + line
         return total * inside
 
@@ -316,12 +339,12 @@
     p0 = res
     v0 = precondition(p0)
     a0 = operate(v0)
-    p1 = (a0 * scale - SHIFTS[0] * p0) * inside
+    p1 = (a0 * scale - SHIFTS[0] * p0[:rows]) * inside
     v1 = precondition(p1)
     a1 = operate(v1)
     p2 = (a1 * scale - SHIFTS[1] * p1) * inside
     v2 = precondition(p2)
-    mine = lambda x: x[NR : 2 * NR, :NC]
+    mine = lambda x: x[8 : 8 + NR, :NC]
     half_a2 = mine(diag * v2 - 2.0 * (lon_shift(v2, 1) + lat_shift(v2, 1)))
     v0, v1, v2, a0, a1, r = (mine(x) for x in (v0, v1, v2, a0, a1, p0))
     v_out[0] = v0
@@ -339,21 +362,12 @@
     copy.wait()
 
 
-def relay_kernel(got, out, held, spread, sems):
-    copy = pltpu.make_async_copy(got, held, sems.at[0])
-    copy.start()
-    copy.wait()
-    spread[...] = jnp.broadcast_to(jnp.sum(held[...], axis=0, keepdims=True)[:, :1], spread.shape)
-    copy = pltpu.make_async_copy(spread, out, sems.at[1])
-    copy.start()
-    copy.wait()
-
-
-def step_kernel(got, v, sf, out, held, sem):
-    copy = pltpu.make_async_copy(got, held, sem)
-    copy.start()
-    copy.wait()
-    line = jnp.sum(held[...], axis=0)
+def relay_kernel(got, out):
+    out[...] = jnp.broadcast_to(jnp.sum(got[...], axis=0, keepdims=True)[:, :1], out.shape)
+
+
+def step_kernel(got, v, sf, out):
+    line = jnp.sum(got[...], axis=0)
     lane = lane_of((1, NC))
     h00, h01, h02, h11, h12, h22, g0, g1, g2 = (
         jnp.sum(jnp.where(lane == i, line, 0.0), axis=1, keepdims=True) for i in range(9)
@@ -451,13 +465,13 @@
 
 
 def tracer_kernel(
-    t, u, v, w, lon, lon_a, lon_b, from_a, from_a2, from_b, from_b2,
+    t, u, v, w, lon, lon_a, lon_b, lon2, lon2_a, lon2_b, from_a, from_a2, from_b, from_b2,
     t_hbm, t_out, packed, lines, sems,
 ):
     is_east = lane_of((NR, NC)) % 2 == 0
     by = DT_ADV / 12.0
-    packed[1] = beyond(lon_a[4], lon_b[4])
-    far = lon[5] + beyond(lon_a[5], lon_b[5])
+    packed[1] = beyond(lon2_a[0], lon2_b[0])
+    far = lon2[1] + beyond(lon2_a[1], lon2_b[1])
     speed = jnp.where(is_east, lon[0], beyond(lon_a[0], lon_b[0]))
     packed[0] = speed * far * (by * lon[3] * beyond(lon_a[3], lon_b[3]))
     even = even_lat()
@@ -515,24 +529,31 @@
     dma = pltpu.SemaphoreType.DMA
     rows = (4, HALF, NC)
     late = (8, HALF, NC)
-    lon, a, b, a2, b2, inner, th = call(
+    lon, a, b, other_a, other_b = call(
         fetch_kernel,
-        [(6, NR, NC), rows, rows, late, late, (2, NR, NC), (NZ + 8, NC)],
-        [HBM] * 6,
-        50 * NZ * NR * NC,
-        5 * block,
-        [field] * 3 + [wets, field, pltpu.SMEM((NZ,), jnp.float32), dma((CHUNKS, 5)), dma],
+        [(4, NR, NC), rows, rows, rows, rows],
+        [HBM] * 4,
+        20 * NZ * NR * NC,
+        4 * block,
+        [field] * 3 + [wets, dma((CHUNKS, 4))],
         vmem=FETCH_VMEM,
-    )(thickness, u, v, vi, w, t)
+    )(u, v, vi, w)
     from_b = lax.ppermute(b, LAT, SWAP_B)
     from_a = lax.ppermute(a, LAT, SWAP_A)
     lon_b = lax.ppermute(lon, LON, SWAP_B)
     lon_a = lax.ppermute(lon, LON, SWAP_A)
+    inner, th = call(
+        inner_kernel, [(2, NR, NC), (NZ + 8, NC)], [SM] + [VM] * 4, 40 * NZ * NR * NC, 4 * block
+    )(thickness, u, v, vi, w)
     (msg,) = call(join_kernel, [(MSG, NC)], [VM] * 11, 10**6, 10**6)(
-        inner, lon, lon_a, lon_b, a2, from_a, b2, from_b, th, surface, surface_diag
+        inner, lon, lon_a, lon_b, other_a, from_a, other_b, from_b, th, surface, surface_diag
     )
     msg_b = lax.ppermute(msg, LON, SWAP_B)
     msg_a = lax.ppermute(msg, LON, SWAP_A)
+    lon2, a2, b2 = call(
+        late_kernel, [(2, NR, NC), late, late], [VM] * 4, 20 * NZ * NR * NC, 2 * block
+    )(t, w, other_a, other_b)
+    msg_a, msg_b, lon2, a2, b2 = lax.optimization_barrier((msg_a, msg_b, lon2, a2, b2))
     wide = (NR, 2 * NC)
     rest, dg, edge, side_a, side_b = call(
         side_kernel, [wide, wide, (8, 2 * NC), wide, wide], [VM] * 3, 10**6, 10**5
@@ -564,40 +585,27 @@
         [pltpu.VMEM((3, NR, NC), jnp.float32), dma],
         [HBM, VM],
     )(taps, rest, dg, edge, got_a, got_b)
-    dots, a2, b2 = lax.optimization_barrier((dots, a2, b2))
+    dots, a2, b2, lon2 = lax.optimization_barrier((dots, a2, b2, lon2))
     from_b2 = lax.ppermute(b2, LAT, SWAP_B)
     from_a2 = lax.ppermute(a2, LAT, SWAP_A)
+    lon2_b = lax.ppermute(lon2, LON, SWAP_B)
+    lon2_a = lax.ppermute(lon2, LON, SWAP_A)
     dots = lax.all_to_all(dots, ("x", "y", "c"), 0, 0)
     lat = (from_a, from_a2, from_b, from_b2)
     u_new, v_new = velocity(False, (from_a2, from_b2), (u_half, v_half))
     t_new = call(
         tracer_kernel,
         [flat],
-        [VM] * 11,
+        [VM] * 14,
         60 * NZ * NR * NC,
         5 * block,
         [field, pltpu.VMEM((2, NR, NC), jnp.float32), pltpu.VMEM((4, NZ, NC), jnp.float32), dma((CHUNKS, 1))],
         HBM,
-    )(t, u, v, w, lon, lon_a, lon_b, *lat)[0]
-    (dots,) = call(
-        relay_kernel,
-        [(8, 1, NC)],
-        [HBM],
-        10**4,
-        10**4,
-        [pltpu.VMEM((32, 8, NC), jnp.float32), pltpu.VMEM((8, 1, NC), jnp.float32), dma((2,))],
-        HBM,
-    )(dots)
+    )(t, u, v, w, lon, lon_a, lon_b, lon2, lon2_a, lon2_b, *lat)[0]
+    (dots,) = call(relay_kernel, [(8, 1, NC)], [VM], 10**4, 10**4)(dots)
     dots = lax.all_to_all(dots, ("zl", "zh"), 0, 0)
     dots, t_new, u_new, v_new = lax.optimization_barrier((dots, t_new, u_new, v_new))
-    (surface_new,) = call(
-        step_kernel,
-        [(NR, NC)],
-        [HBM] + [VM] * 2,
-        10**5,
-        10**4,
-        [pltpu.VMEM((8, 1, NC), jnp.float32), dma],
-    )(dots, vecs, surface)
+    (surface_new,) = call(step_kernel, [(NR, NC)], [VM] * 3, 10**5, 10**4)(dots, vecs, surface)
     shape = (NZ, NR, NC)
     return t_new.reshape(shape), u_new.reshape(shape), v_new.reshape(shape), surface_new
 

time: 62.8 us -> 58.9 us (0.938)
  waiting for transfers between devices: 7.4 us -> 2.96 us
  Pallas kernels: 16.3 us -> 17.9 us
  local copies, waits for them, and re-layouts: 0.68 us -> 0.04 us
    all_to_all x1, waiting for transfers between devices: 3.36 us -> 0.01 us  [local(): dots = lax.all_to_all(dots, ('x', 'y', 'c'), 0, 0)]
    ppermute x0 -> x2, starting transfers between devices: none -> 3.09 us  [the longest x1 1.99 us: local(): lon2_b = lax.ppermute(lon2, LON, SWAP_B)]
    pallas_call x4 -> x6, Pallas kernels: 9.84 us -> 11.5 us  [the longest x1 3.02 us: local(): call(tracer_kernel, [flat], [VM] * 14, 60 * NZ * NR * NC, 5 * block, [fie...]
    all_to_all x1, starting transfers between devices: 7.57 us -> 6.14 us  [local(): dots = lax.all_to_all(dots, ('x', 'y', 'c'), 0, 0)]
    ppermute x1, starting transfers between devices: 1.72 us -> 0.68 us  [local(): msg_b = lax.ppermute(msg, LON, SWAP_B)]
    ppermute x1, waiting for transfers between devices: 0.86 us -> 0.01 us  [local(): msg_a = lax.ppermute(msg, LON, SWAP_A)]
    ppermute x1, waiting for transfers between devices: 0.78 us -> 0.01 us  [local(): lon_b = lax.ppermute(lon, LON, SWAP_B)]
    ppermute x1, starting transfers between devices: 3.1 us -> 2.44 us  [local(): msg_a = lax.ppermute(msg, LON, SWAP_A)]
  transfers between devices with their start and end apart: 12 -> 14, of which waited for: 6 -> 2; matrix products, arithmetic and copies ran while one was open for 0% -> 0% of each run, Pallas kernels for 14% -> 22%
where the time goes in v6:
time: 58.9 us; the launch traced here: 58.7 us
  starting transfers between devices  37 us (63%)
  Pallas kernels  17.9 us (30%)
  waiting for transfers between devices  2.96 us (5%)
  between operations  0.87 us (1%)
    ppermute x1, starting transfers between devices, local(): from_b = lax.ppermute(b, LAT, SWAP_B)  6.65 us
    all_to_all x1, starting transfers between devices, local(): dots = lax.all_to_all(dots, ('x', 'y', 'c'), 0, 0)  6.14 us
    ppermute x1, starting transfers between devices, local(): from_b2 = lax.ppermute(b2, LAT, SWAP_B)  4.32 us
    pallas_call x2, Pallas kernels, velocity(): call(functools.partial(velocity_kernel, early), [flat] * 2, [VM] * 9 + [H...  4.07 us
    ppermute x1, starting transfers between devices, local(): from_a = lax.ppermute(a, LAT, SWAP_A)  3.91 us
    all_to_all x1, starting transfers between devices, local(): dots = lax.all_to_all(dots, ('zl', 'zh'), 0, 0)  3.31 us
    pallas_call x1, Pallas kernels, local(): call(tracer_kernel, [flat], [VM] * 14, 60 * NZ * NR * NC, 5 * block, [fie...  3.02 us
    pallas_call x1, Pallas kernels, local(): call(fetch_kernel, [(4, NR, NC), rows, rows, rows, rows], [HBM] * 4, 20 *...  2.63 us
  transfers between devices with their start and end apart: 14, of which 2 were waited for; matrix products, arithmetic and copies ran while one was open for 0% of the time, Pallas kernels for 22%

profile of v6, /device:TPU:1, one launch (start us, length us, event | category | flops | bytes accessed | tf_op | source)
XLA Modules:
  0.0 58.7 jit_solution(12853408101354140409)
XLA Ops:
  0.6 0.0 copy-start
  0.6 0.0 copy-start.1
  0.7 2.6 %shard_map.122 = (f32[4,16,128]{2,1,0:T(8,128)S(1)}, f32[4,32,128]{2,1,0:T(8,128)S(1)}, f32[4,32,128]{2,1,0:T(8,128)S(1)}, f32[4,32,128]{2,1,0:T(8,128)S(1)}, f32[4,32,128]{2,1,0:T(8,128)S(1)}) custom-call(f32[1024,128]{1,0:T(8,128)} %bitcast.14, f32[1024,128]{1,0:T(8,128)} %bitcast.19, f32[1024,128]{1,0:T(8,128)} %bitcast.24, s32[1024,128]{1,0:T(8,128)} %bitcast.8), custom_call_target="tpu_custom_call" | custom-call | flops 2621440 | bytes 2097152 | tf_op jit(solution)/shard_map/pallas_call | solution.py:532
  3.3 3.9 %collective-permute-start.2 = (f32[4,32,128]{2,1,0:T(8,128)S(1)}, f32[4,32,128]{2,1,0:T(8,128)S(1)}, u32[]{:S(2)}, u32[]{:S(2)}) collective-permute-start(f32[4,32,128]{2,1,0:T(8,128)S(1)} %get-tuple-element.45), channel_id=1, source_target_pairs={{0,1},{1,0},{2,3},{3,2},{4,5},{5,4},{6,7},{7,6},{8,9},{9,8},{10,11... | collective-permute-start | bytes 196616 | tf_op jit(solution)/shard_map/ppermute | solution.py:542
  7.2 6.7 %collective-permute-start.3 = (f32[4,32,128]{2,1,0:T(8,128)S(1)}, f32[4,32,128]{2,1,0:T(8,128)S(1)}, u32[]{:S(2)}, u32[]{:S(2)}) collective-permute-start(f32[4,32,128]{2,1,0:T(8,128)S(1)} %get-tuple-element.47), channel_id=1, source_target_pairs={{0,15},{1,2},{2,1},{3,4},{4,3},{5,6},{6,5},{7,8},{8,7},{9,10},{10,... | collective-permute-start | bytes 196616 | tf_op jit(solution)/shard_map/ppermute | solution.py:541
  13.9 2.3 %collective-permute-start.1 = (f32[4,16,128]{2,1,0:T(8,128)S(1)}, f32[4,16,128]{2,1,0:T(8,128)S(1)}, u32[]{:S(2)}, u32[]{:S(2)}) collective-permute-start(f32[4,16,128]{2,1,0:T(8,128)S(1)} %get-tuple-element.43.lon), channel_id=1, source_target_pairs={{0,240},{16,32},{32,16},{48,64},{64,48},{80,96},{96,80},{112,128},... | collective-permute-start | bytes 98312 | tf_op jit(solution)/shard_map/ppermute | solution.py:543
  16.2 1.0 %collective-permute-start = (f32[4,16,128]{2,1,0:T(8,128)S(1)}, f32[4,16,128]{2,1,0:T(8,128)S(1)}, u32[]{:S(2)}, u32[]{:S(2)}) collective-permute-start(f32[4,16,128]{2,1,0:T(8,128)S(1)} %get-tuple-element.43.lon), channel_id=1, source_target_pairs={{0,16},{16,0},{32,48},{48,32},{64,80},{80,64},{96,112},{112,96},{1... | collective-permute-start | bytes 98312 | tf_op jit(solution)/shard_map/ppermute | solution.py:544
  17.2 0.0 copy-done.3
  17.2 0.0 copy-done.8
  17.2 0.0 copy-start.5
  17.2 0.0 copy-start.6
  17.2 0.0 copy-start.4
  17.3 2.3 %shard_map.121 = (f32[2,16,128]{2,1,0:T(8,128)S(1)}, f32[72,128]{1,0:T(8,128)S(1)}) custom-call(f32[64]{0:T(128)S(1)} %copy-done.8, f32[1024,128]{1,0:T(8,128)S(1)} %bitcast.15, f32[1024,128]{1,0:T(8,128)S(1)} %bitcast.20, f32[1024,128]{1,0:T(8,128)S(1)} %bitcast.25, s32[1024,128]{1,0:T(8,128)S(1)} %bitcast.9), custom_call_target="tpu_custom_call" | custom-call | flops 5242880 | bytes 2097152 | tf_op jit(solution)/shard_map/pallas_call | solution.py:545
  19.6 0.0 collective-permute-done.1.lon_b
  19.6 0.0 collective-permute-done.lon_a
  19.6 0.0 collective-permute-done.2.from_a
  19.6 0.0 collective-permute-done.3.from_b
  19.6 0.2 shard_map.123.msg
  19.8 0.7 %collective-permute-start.5 = (f32[72,128]{1,0:T(8,128)S(1)}, f32[72,128]{1,0:T(8,128)S(1)}, u32[]{:S(2)}, u32[]{:S(2)}) collective-permute-start(f32[72,128]{1,0:T(8,128)S(1)} %shard_map.123.msg), channel_id=1, source_target_pairs={{0,240},{16,32},{32,16},{48,64},{64,48},{80,96},{96,80},{112,128},... | collective-permute-start | bytes 110600 | tf_op jit(solution)/shard_map/ppermute | solution.py:551
  20.5 2.4 %collective-permute-start.4 = (f32[72,128]{1,0:T(8,128)S(1)}, f32[72,128]{1,0:T(8,128)S(1)}, u32[]{:S(2)}, u32[]{:S(2)}) collective-permute-start(f32[72,128]{1,0:T(8,128)S(1)} %shard_map.123.msg), channel_id=1, source_target_pairs={{0,16},{16,0},{32,48},{48,32},{64,80},{80,64},{96,112},{112,96},{1... | collective-permute-start | bytes 110600 | tf_op jit(solution)/shard_map/ppermute | solution.py:552
  22.9 2.2 %shard_map.124 = (f32[2,16,128]{2,1,0:T(8,128)S(1)}, f32[8,32,128]{2,1,0:T(8,128)}, f32[8,32,128]{2,1,0:T(8,128)S(1)}) custom-call(f32[1024,128]{1,0:T(8,128)S(1)} %bitcast.28, s32[1024,128]{1,0:T(8,128)S(1)} %bitcast.10, f32[4,32,128]{2,1,0:T(8,128)S(1)} %get-tuple-element.44.a2.other_a, f32[4,32,128]{2,1,0:T(8,128)S(1)} %get-tuple-element.46.b2.other_b), custom_call_target="tpu_custom_call" | custom-call | flops 2621440 | bytes 1048576 | tf_op jit(solution)/shard_map/pallas_call | solution.py:553
  25.1 0.0 collective-permute-done.5.msg_b
  25.1 0.0 collective-permute-done.4.msg_a
  25.1 0.1 shard_map.125
  25.2 0.1 collective-permute-start.6
  25.3 2.5 %collective-permute-start.7 = (f32[16,256]{1,0:T(8,128)S(1)}, f32[16,256]{1,0:T(8,128)S(1)}, u32[]{:S(2)}, u32[]{:S(2)}) collective-permute-start(f32[16,256]{1,0:T(8,128)S(1)} %get-tuple-element.58), channel_id=1, source_target_pairs={{0,15},{1,2},{2,1},{3,4},{4,3},{5,6},{6,5},{7,8},{8,7},{9,10},{10,... | collective-permute-start | bytes 49160 | tf_op jit(solution)/shard_map/ppermute | solution.py:561
  27.9 0.0 copy-done.7
  27.9 0.6 %shard_map.120.pc = f32[32,256]{1,0:T(8,128)S(1)} custom-call(f32[5,5]{1,0:T(8,128)S(1)} %copy-done.7), custom_call_target="tpu_custom_call" | custom-call | flops 10000 | bytes 10000 | tf_op jit(solution)/shard_map/pallas_call | solution.py:563
  28.5 2.0 %shard_map.126 = (f32[1024,128]{1,0:T(8,128)}, f32[1024,128]{1,0:T(8,128)}) custom-call(f32[1024,128]{1,0:T(8,128)S(1)} %bitcast.16, f32[1024,128]{1,0:T(8,128)S(1)} %bitcast.21, f32[1024,128]{1,0:T(8,128)S(1)} %bitcast.26, s32[1024,128]{1,0:T(8,128)S(1)} %bitcast.11, f32[4,16,128]{2,1,0:T(8,128)S(1)} %get-tuple-element.43.lon, ...), custom_call_target="tpu_custom_call" | custom-call | flops 3932160 | bytes 1572864 | tf_op jit(solution)/shard_map/pallas_call | solution.py:565
  30.5 0.0 collective-permute-done.6.from_a
  30.5 1.7 %collective-permute-done.7.from_b = f32[16,256]{1,0:T(8,128)S(1)} collective-permute-done((f32[16,256]{1,0:T(8,128)S(1)}, f32[16,256]{1,0:T(8,128)S(1)}, u32[]{:S(2)}, u32[]{:S(2)}) %collective-permute-start.7) | collective-permute-done | bytes 16416 | tf_op jit(solution)/shard_map/ppermute | solution.py:561
  32.2 1.4 %shard_map.127 = (f32[3,16,128]{2,1,0:T(8,128)S(1)}, f32[32,8,128]{2,1,0:T(8,128)}) custom-call(f32[32,256]{1,0:T(8,128)S(1)} %shard_map.120.pc, f32[16,256]{1,0:T(8,128)S(1)} %get-tuple-element.54.rest, f32[16,256]{1,0:T(8,128)S(1)} %get-tuple-element.55.dg, f32[8,256]{1,0:T(8,128)S(1)} %get-tuple-element.56.edge, ...), custom_call_target="tpu_custom_call" | custom-call | flops 1000000 | bytes 100000 | tf_op jit(solution)/shard_map/pallas_call | solution.py:579
  33.7 6.1 %all-to-all-start = ((f32[32,8,128]{2,1,0:T(8,128)}), f32[32,8,128]{2,1,0:T(8,128)S(1)}, u32[]{:S(2)}, u32[]{:S(2)}) async-start(f32[32,8,128]{2,1,0:T(8,128)} %get-tuple-element.67), calls=%async_computation | async-start | bytes 262144 | tf_op jit(solution)/shard_map/all_to_all | solution.py:593
  39.8 0.5 collective-permute-start.10
  40.3 4.3 %collective-permute-start.11 = (f32[8,32,128]{2,1,0:T(8,128)S(1)}, f32[8,32,128]{2,1,0:T(8,128)S(1)}, u32[]{:S(2)}, u32[]{:S(2)}) collective-permute-start(f32[8,32,128]{2,1,0:T(8,128)S(1)} %get-tuple-element.70), channel_id=1, source_target_pairs={{0,15},{1,2},{2,1},{3,4},{4,3},{5,6},{6,5},{7,8},{8,7},{9,10},{10,... | collective-permute-start | bytes 393224 | tf_op jit(solution)/shard_map/ppermute | solution.py:589
  44.6 2.0 %collective-permute-start.9 = (f32[2,16,128]{2,1,0:T(8,128)S(1)}, f32[2,16,128]{2,1,0:T(8,128)S(1)}, u32[]{:S(2)}, u32[]{:S(2)}) collective-permute-start(f32[2,16,128]{2,1,0:T(8,128)S(1)} %get-tuple-element.68.lon2), channel_id=1, source_target_pairs={{0,240},{16,32},{32,16},{48,64},{64,48},{80,96},{96,80},{112,128},... | collective-permute-start | bytes 49160 | tf_op jit(solution)/shard_map/ppermute | solution.py:591
  46.6 1.1 %collective-permute-start.8 = (f32[2,16,128]{2,1,0:T(8,128)S(1)}, f32[2,16,128]{2,1,0:T(8,128)S(1)}, u32[]{:S(2)}, u32[]{:S(2)}) collective-permute-start(f32[2,16,128]{2,1,0:T(8,128)S(1)} %get-tuple-element.68.lon2), channel_id=1, source_target_pairs={{0,16},{16,0},{32,48},{48,32},{64,80},{80,64},{96,112},{112,96},{1... | collective-permute-start | bytes 49160 | tf_op jit(solution)/shard_map/ppermute | solution.py:592
  47.7 0.0 all-to-all-done.got
  47.7 0.6 %shard_map.128 = f32[8,1,128]{2,1,0:T(1,128)} custom-call(f32[32,8,128]{2,1,0:T(8,128)S(1)} %all-to-all-done.got), custom_call_target="tpu_custom_call" | custom-call | flops 10000 | bytes 10000 | tf_op jit(solution)/shard_map/pallas_call | solution.py:605
  48.4 3.3 %all-to-all-start.1 = ((f32[8,1,128]{2,1,0:T(1,128)}), f32[8,1,128]{2,1,0:T(1,128)S(1)}, u32[]{:S(2)}, u32[]{:S(2)}) async-start(f32[8,1,128]{2,1,0:T(1,128)} %shard_map.128), calls=%async_computation.1 | async-start | bytes 8192 | tf_op jit(solution)/shard_map/all_to_all | solution.py:606
  51.7 0.0 collective-permute-done.10.from_a2.from_a
  51.7 0.0 collective-permute-done.11.from_b2.from_b
  51.7 2.0 %shard_map.130 = (f32[1024,128]{1,0:T(8,128)}, f32[1024,128]{1,0:T(8,128)}) custom-call(f32[1024,128]{1,0:T(8,128)S(1)} %bitcast.17, f32[1024,128]{1,0:T(8,128)S(1)} %bitcast.22, f32[1024,128]{1,0:T(8,128)S(1)} %bitcast.27, s32[1024,128]{1,0:T(8,128)S(1)} %bitcast.12, ...), custom_call_target="tpu_custom_call", output_to_operand_aliasing={{0}: (9, {}), {1}: (10, {})} | custom-call | flops 3932160 | bytes 1572864 | tf_op jit(solution)/shard_map/pallas_call | solution.py:565
  53.7 0.0 collective-permute-done.9.lon2_b
  53.8 0.0 collective-permute-done.8.lon2_a
  53.8 3.0 %shard_map.129 = f32[1024,128]{1,0:T(8,128)} custom-call(f32[1024,128]{1,0:T(8,128)S(1)} %bitcast.29, f32[1024,128]{1,0:T(8,128)S(1)} %bitcast.18, f32[1024,128]{1,0:T(8,128)S(1)} %bitcast.23, s32[1024,128]{1,0:T(8,128)S(1)} %bitcast.13, f32[4,16,128]{2,1,0:T(8,128)S(1)} %get-tuple-element.43.lon, f32[4,16,128]{2,1,0:T(8,128)S(1)} %collective-permute-done.lon_a, ...), custom_call_target="tpu_custom_call" | custom-call | flops 7864320 | bytes 2621440 | tf_op jit(solution)/shard_map/pallas_call | solution.py:596
  56.8 1.2 %all-to-all-done.1.got = f32[8,1,128]{2,1,0:T(1,128)S(1)} async-done(((f32[8,1,128]{2,1,0:T(1,128)}), f32[8,1,128]{2,1,0:T(1,128)S(1)}, u32[]{:S(2)}, u32[]{:S(2)}) %all-to-all-start.1) | async-done | bytes 4128 | tf_op jit(solution)/shard_map/all_to_all | solution.py:606
  58.0 0.7 %shard_map.131 = f32[16,128]{1,0:T(8,128)} custom-call(f32[8,1,128]{2,1,0:T(1,128)S(1)} %all-to-all-done.1.got, f32[3,16,128]{2,1,0:T(8,128)S(1)} %get-tuple-element.79.v, f32[16,128]{1,0:T(8,128)S(1)} %copy-done.5), custom_call_target="tpu_custom_call" | custom-call | flops 100000 | bytes 10000 | tf_op jit(solution)/shard_map/pallas_call | solution.py:608
  (10 shorter events, 0.0 us)
Async XLA Ops:
  0.6 16.6 %copy-start = (s32[64,16,128]{2,1,0:T(8,128)S(1)}, s32[64,16,128]{2,1,0:T(8,128)}, u32[]{:S(2)}) copy-start(s32[64,16,128]{2,1,0:T(8,128)} %param.13) | copy-start | bytes 1572868
  0.6 16.6 %copy-start.1 = (f32[64,16,128]{2,1,0:T(8,128)S(1)}, f32[64,16,128]{2,1,0:T(8,128)}, u32[]{:S(2)}) copy-start(f32[64,16,128]{2,1,0:T(8,128)} %param.10) | copy-start | bytes 1572868
  0.7 16.6 %copy-start.2 = (f32[64,16,128]{2,1,0:T(8,128)S(1)}, f32[64,16,128]{2,1,0:T(8,128)}, u32[]{:S(2)}) copy-start(f32[64,16,128]{2,1,0:T(8,128)} %param.11) | copy-start | bytes 1572868
  0.7 16.6 %copy-start.3 = (f32[64,16,128]{2,1,0:T(8,128)S(1)}, f32[64,16,128]{2,1,0:T(8,128)}, u32[]{:S(2)}) copy-start(f32[64,16,128]{2,1,0:T(8,128)} %param.12) | copy-start | bytes 1572868
  3.3 16.3 %collective-permute-start.2 = (f32[4,32,128]{2,1,0:T(8,128)S(1)}, f32[4,32,128]{2,1,0:T(8,128)S(1)}, u32[]{:S(2)}, u32[]{:S(2)}) collective-permute-start(f32[4,32,128]{2,1,0:T(8,128)S(1)} %get-tuple-element.45), channel_id=1, source_target_pairs={{0,1},{1,0},{2,3},{3,2},{4,5},{5,4},{6,7},{7,6},{8,9},{9,8},{10,11... | collective-permute-start | bytes 196616 | tf_op jit(solution)/shard_map/ppermute | solution.py:542
  7.2 10.0 %copy-start.8 = (f32[64]{0:T(128)S(1)}, f32[64]{0:T(128)}, u32[]{:S(2)}) copy-start(f32[64]{0:T(128)} %thick.1) | copy-start | bytes 772
  7.2 12.4 %collective-permute-start.3 = (f32[4,32,128]{2,1,0:T(8,128)S(1)}, f32[4,32,128]{2,1,0:T(8,128)S(1)}, u32[]{:S(2)}, u32[]{:S(2)}) collective-permute-start(f32[4,32,128]{2,1,0:T(8,128)S(1)} %get-tuple-element.47), channel_id=1, source_target_pairs={{0,15},{1,2},{2,1},{3,4},{4,3},{5,6},{6,5},{7,8},{8,7},{9,10},{10,... | collective-permute-start | bytes 196616 | tf_op jit(solution)/shard_map/ppermute | solution.py:541
  13.9 5.7 %collective-permute-start.1 = (f32[4,16,128]{2,1,0:T(8,128)S(1)}, f32[4,16,128]{2,1,0:T(8,128)S(1)}, u32[]{:S(2)}, u32[]{:S(2)}) collective-permute-start(f32[4,16,128]{2,1,0:T(8,128)S(1)} %get-tuple-element.43.lon), channel_id=1, source_target_pairs={{0,240},{16,32},{32,16},{48,64},{64,48},{80,96},{96,80},{112,128},... | collective-permute-start | bytes 98312 | tf_op jit(solution)/shard_map/ppermute | solution.py:543
  16.2 3.4 %collective-permute-start = (f32[4,16,128]{2,1,0:T(8,128)S(1)}, f32[4,16,128]{2,1,0:T(8,128)S(1)}, u32[]{:S(2)}, u32[]{:S(2)}) collective-permute-start(f32[4,16,128]{2,1,0:T(8,128)S(1)} %get-tuple-element.43.lon), channel_id=1, source_target_pairs={{0,16},{16,0},{32,48},{48,32},{64,80},{80,64},{96,112},{112,96},{1... | collective-permute-start | bytes 98312 | tf_op jit(solution)/shard_map/ppermute | solution.py:544
  17.2 2.4 %copy-start.5 = (f32[16,128]{1,0:T(8,128)S(1)}, f32[16,128]{1,0:T(8,128)}, u32[]{:S(2)}) copy-start(f32[16,128]{1,0:T(8,128)} %sf.3) | copy-start | bytes 24580
  17.2 2.4 %copy-start.6 = (f32[16,128]{1,0:T(8,128)S(1)}, f32[16,128]{1,0:T(8,128)}, u32[]{:S(2)}) copy-start(f32[16,128]{1,0:T(8,128)} %dg.1) | copy-start | bytes 24580
  17.2 5.7 %copy-start.4 = (f32[64,16,128]{2,1,0:T(8,128)S(1)}, f32[64,16,128]{2,1,0:T(8,128)}, u32[]{:S(2)}) copy-start(f32[64,16,128]{2,1,0:T(8,128)} %param.9) | copy-start | bytes 1572868
  19.8 5.3 %collective-permute-start.5 = (f32[72,128]{1,0:T(8,128)S(1)}, f32[72,128]{1,0:T(8,128)S(1)}, u32[]{:S(2)}, u32[]{:S(2)}) collective-permute-start(f32[72,128]{1,0:T(8,128)S(1)} %shard_map.123.msg), channel_id=1, source_target_pairs={{0,240},{16,32},{32,16},{48,64},{64,48},{80,96},{96,80},{112,128},... | collective-permute-start | bytes 110600 | tf_op jit(solution)/shard_map/ppermute | solution.py:551
  20.5 4.6 %collective-permute-start.4 = (f32[72,128]{1,0:T(8,128)S(1)}, f32[72,128]{1,0:T(8,128)S(1)}, u32[]{:S(2)}, u32[]{:S(2)}) collective-permute-start(f32[72,128]{1,0:T(8,128)S(1)} %shard_map.123.msg), channel_id=1, source_target_pairs={{0,16},{16,0},{32,48},{48,32},{64,80},{80,64},{96,112},{112,96},{1... | collective-permute-start | bytes 110600 | tf_op jit(solution)/shard_map/ppermute | solution.py:552
  25.1 2.7 %copy-start.7 = (f32[5,5]{1,0:T(8,128)S(1)}, f32[5,5]{1,0:T(8,128)}, u32[]{:S(2)}) copy-start(f32[5,5]{1,0:T(8,128)} %pc.1) | copy-start | bytes 304
  25.2 5.3 %collective-permute-start.6 = (f32[16,256]{1,0:T(8,128)S(1)}, f32[16,256]{1,0:T(8,128)S(1)}, u32[]{:S(2)}, u32[]{:S(2)}) collective-permute-start(f32[16,256]{1,0:T(8,128)S(1)} %get-tuple-element.57), channel_id=1, source_target_pairs={{0,1},{1,0},{2,3},{3,2},{4,5},{5,4},{6,7},{7,6},{8,9},{9,8},{10,11... | collective-permute-start | bytes 49160 | tf_op jit(solution)/shard_map/ppermute | solution.py:562
  25.3 6.9 %collective-permute-start.7 = (f32[16,256]{1,0:T(8,128)S(1)}, f32[16,256]{1,0:T(8,128)S(1)}, u32[]{:S(2)}, u32[]{:S(2)}) collective-permute-start(f32[16,256]{1,0:T(8,128)S(1)} %get-tuple-element.58), channel_id=1, source_target_pairs={{0,15},{1,2},{2,1},{3,4},{4,3},{5,6},{6,5},{7,8},{8,7},{9,10},{10,... | collective-permute-start | bytes 49160 | tf_op jit(solution)/shard_map/ppermute | solution.py:561
  33.7 14.1 %all-to-all-start = ((f32[32,8,128]{2,1,0:T(8,128)}), f32[32,8,128]{2,1,0:T(8,128)S(1)}, u32[]{:S(2)}, u32[]{:S(2)}) async-start(f32[32,8,128]{2,1,0:T(8,128)} %get-tuple-element.67), calls=%async_computation | async-start | bytes 262144 | tf_op jit(solution)/shard_map/all_to_all | solution.py:593
  39.8 11.9 %collective-permute-start.10 = (f32[8,32,128]{2,1,0:T(8,128)}, f32[8,32,128]{2,1,0:T(8,128)S(1)}, u32[]{:S(2)}, u32[]{:S(2)}) collective-permute-start(f32[8,32,128]{2,1,0:T(8,128)} %get-tuple-element.69), channel_id=1, source_target_pairs={{0,1},{1,0},{2,3},{3,2},{4,5},{5,4},{6,7},{7,6},{8,9},{9,8},{10,11... | collective-permute-start | bytes 393224 | tf_op jit(solution)/shard_map/ppermute | solution.py:590
  40.3 11.4 %collective-permute-start.11 = (f32[8,32,128]{2,1,0:T(8,128)S(1)}, f32[8,32,128]{2,1,0:T(8,128)S(1)}, u32[]{:S(2)}, u32[]{:S(2)}) collective-permute-start(f32[8,32,128]{2,1,0:T(8,128)S(1)} %get-tuple-element.70), channel_id=1, source_target_pairs={{0,15},{1,2},{2,1},{3,4},{4,3},{5,6},{6,5},{7,8},{8,7},{9,10},{10,... | collective-permute-start | bytes 393224 | tf_op jit(solution)/shard_map/ppermute | solution.py:589
  44.6 9.1 %collective-permute-start.9 = (f32[2,16,128]{2,1,0:T(8,128)S(1)}, f32[2,16,128]{2,1,0:T(8,128)S(1)}, u32[]{:S(2)}, u32[]{:S(2)}) collective-permute-start(f32[2,16,128]{2,1,0:T(8,128)S(1)} %get-tuple-element.68.lon2), channel_id=1, source_target_pairs={{0,240},{16,32},{32,16},{48,64},{64,48},{80,96},{96,80},{112,128},... | collective-permute-start | bytes 49160 | tf_op jit(solution)/shard_map/ppermute | solution.py:591
  46.6 7.1 %collective-permute-start.8 = (f32[2,16,128]{2,1,0:T(8,128)S(1)}, f32[2,16,128]{2,1,0:T(8,128)S(1)}, u32[]{:S(2)}, u32[]{:S(2)}) collective-permute-start(f32[2,16,128]{2,1,0:T(8,128)S(1)} %get-tuple-element.68.lon2), channel_id=1, source_target_pairs={{0,16},{16,0},{32,48},{48,32},{64,80},{80,64},{96,112},{112,96},{1... | collective-permute-start | bytes 49160 | tf_op jit(solution)/shard_map/ppermute | solution.py:592
  48.4 9.7 %all-to-all-start.1 = ((f32[8,1,128]{2,1,0:T(1,128)}), f32[8,1,128]{2,1,0:T(1,128)S(1)}, u32[]{:S(2)}, u32[]{:S(2)}) async-start(f32[8,1,128]{2,1,0:T(1,128)} %shard_map.128), calls=%async_computation.1 | async-start | bytes 8192 | tf_op jit(solution)/shard_map/all_to_all | solution.py:606

commit v7 on v6

--- a/solution.py
+++ b/solution.py
@@ -114,7 +114,16 @@
     return pl.ds(pl.multiple_of(k * NR, NR), NR)
 
 
-def fetch_kernel(u, v, vi, land, lon_out, a_out, b_out, other_a, other_b, uo, vo, vio, lo, sems):
+def squeeze(rows, shift):
+    group = lane_of((8, NC)) // 32
+    out = None
+    for g in range(4):
+        part = pltpu.roll(rows[8 * g : 8 * g + 8], (shift + 32 * g) % NC, 1)
+        out = part if g == 0 else jnp.where(group == g, part, out)
+    return out
+
+
+def fetch_kernel(u, v, vi, land, lon_out, a_out, b_out, other_a, other_b, corners, uo, vo, vio, lo, sems):
     pair = lane_of((NR, NC)) // 2
 
     def body(k, acc):
@@ -135,9 +144,30 @@
         for i, ref in enumerate((uo, vo, vio, lo)):
             first[i] = edge_row(ref, north, 0, mine, HALF)
             rest[i] = edge_row(ref, north, 0, theirs, HALF)
-
-
-def inner_kernel(thick, u, v, vi, w, out, th_out):
+    for n, ref in enumerate((a_out, other_a, b_out, other_b)):
+        for i in range(4):
+            corners[4 * n + i] = squeeze(ref[i], 16)
+
+
+AT_CORNER, AT_FIELDS, MSG = 32, 96, 112
+
+
+def put_side_by_side(first, second, step, high):
+    left = lane_of(first.shape) % (2 * step) < step
+    high_pair = jnp.where(left, first, pltpu.roll(second, step, 1))
+    low_pair = jnp.where(left, pltpu.roll(first, NC - step, 1), second)
+    return jnp.where(high, high_pair, low_pair)
+
+
+def take_across(east, west, which, step, east_first):
+    left = lane_of(east.shape) % (2 * step) < step
+    place = 0 if east_first else 1
+    east = east if which == place else pltpu.roll(east, step if which < place else NC - step, 1)
+    west = west if which != place else pltpu.roll(west, NC - step if which else step, 1)
+    return jnp.where(left, east, west) if east_first else jnp.where(left, west, east)
+
+
+def inner_kernel(thick, u, v, vi, w, lon, corners, sf, dg, out, msg_a, msg_b, th_out):
     lane, row = lane_of((NR, NC)), row_of((NR, NC))
     pair = lane[:1] // 2
     up = lambda x: pltpu.roll(x, NC - 1, 1)
@@ -171,6 +201,20 @@
         out[i] = acc[3 * i] + DT_VISC * (
             east - pltpu.roll(east, 1, 1) + north - pltpu.roll(north, 1, 0)
         )
+    fields = (out[0], out[1], sf[...], dg[...])
+    for msg, high in ((msg_a, even_lon()), (msg_b, jnp.logical_not(even_lon()))):
+        for i in range(2):
+            msg[NR * i : NR * (i + 1), :] = put_side_by_side(lon[2 * i], lon[2 * i + 1], 1, high)
+        for n in range(2):
+            for i in range(4):
+                at = AT_CORNER + 32 * n + 8 * i
+                first, second = corners[8 * n + i], corners[8 * n + 4 + i]
+                msg[at : at + 8, :] = put_side_by_side(first, second, 16, high)
+        line = None
+        for f, x in enumerate(fields):
+            part = jnp.where(high, pltpu.roll(x, 16 * (f + 1) % NC, 1), pltpu.roll(x, 16 * f, 1) if f else x)
+            line = part if f == 0 else jnp.where(lane // 16 == f, part, line)
+        msg[AT_FIELDS:, :] = line
 
 
 def late_kernel(t, w, other_a, other_b, lon_out, a_out, b_out):
@@ -219,50 +263,67 @@
     return jnp.where(is_east, pltpu.roll(east, NC - 1, 1), pltpu.roll(west, 1, 1))
 
 
+def edge_across(msg_a, msg_b, i):
+    at = slice(NR * (i // 2), NR * (i // 2 + 1))
+    return take_across(*lon_sides(msg_a[at, :], msg_b[at, :]), i % 2, 1, True)
+
+
 def face_in(own, other):
     face = 0.5 * (own[2] + other[2]) * (own[3] * other[3])
     return face * (other[0] - own[0]), face * (other[1] - own[1])
 
 
-MSG = 72
-
-
-def join_kernel(inner, lon, lon_a, lon_b, a2, from_a, b2, from_b, th, sf, dg, out):
+LAT_MSG = 96
+
+
+def side_kernel(
+    inner, lon, sf_own, dg_own, msg_a, msg_b, a2, from_a, b2, from_b, th,
+    rest_out, diag_out, edge_out, corner_out, a_out, b_out,
+):
     lane = lane_of((NR, NC))
-    own = [lon[i] for i in range(4)]
-    other = [beyond(lon_a[i], lon_b[i]) for i in range(4)]
     is_east = lane % 2 == 0
-    for i, grad in enumerate(face_in(own, other)):
-        grad = grad * th[NZ : NZ + 1, :]
+    packed = [lon[i] for i in range(4)]
+    other = [edge_across(msg_a, msg_b, i) for i in range(4)]
+    far_east, far_west = lon_sides(msg_a[AT_FIELDS:, :], msg_b[AT_FIELDS:, :])
+
+    def widen(own, f):
+        east = pltpu.roll(far_east, (NC - 16 * f) % NC, 1) if f else far_east
+        west = pltpu.roll(far_west, (NC - 16 - 16 * f) % NC, 1)
+        halo = jnp.where(lane < 16, east, jnp.where(lane >= NC - 16, west, 0.0))
+        return jnp.concatenate([own, halo], axis=1)
+
+    wide_lane = lane_of((NR, 2 * NC))
+    te, tn = widen(inner[0], 0), widen(inner[1], 1)
+    sf, dg = widen(sf_own[...], 2), widen(dg_own[...], 3)
+    add = []
+    for grad in face_in(packed, other):
+        grad = grad * (DT_VISC * th[NZ : NZ + 1, :])
         east = jnp.sum(jnp.where(is_east, grad, 0.0), axis=1, keepdims=True)
         west = jnp.sum(jnp.where(is_east, 0.0, grad), axis=1, keepdims=True)
-        add = jnp.where(lane == NC - 1, east, 0.0) + jnp.where(lane == 0, west, 0.0)
-        out[NR * i : NR * (i + 1), :] = inner[i] + DT_VISC * add
+        here = jnp.where(wide_lane == NC - 1, east, 0.0) + jnp.where(wide_lane == 0, west, 0.0)
+        there = jnp.where(wide_lane == NC, east, 0.0) + jnp.where(wide_lane == 2 * NC - 1, west, 0.0)
+        add.append(here - there)
+    te = te + add[0]
+    tn = tn + add[1]
     _, theirs = halves()
     weight = DT_VISC * th[pl.ds(theirs, HALF), :]
     lat_a = face_in([a2[i] for i in range(4)], [from_a[i] for i in range(4)])
     weight_b = weight * b_exists()
     lat_b = face_in([b2[i] for i in range(4)], [from_b[i] for i in range(4)])
-    sums = [jnp.sum(x * weight, axis=0, keepdims=True) for x in lat_a]
-    sums += [jnp.sum(x * weight_b, axis=0, keepdims=True) for x in lat_b]
-    out[2 * NR : 2 * NR + 8, :] = jnp.concatenate(sums + [jnp.zeros((4, NC), jnp.float32)], axis=0)
-    out[40:56, :] = sf[...]
-    out[56:72, :] = dg[...]
-
-
-def side_kernel(msg, msg_a, msg_b, rest_out, diag_out, edge_out, a_out, b_out):
-    def widen(own, first, second):
-        east, west = lon_sides(first, second)
-        halo = jnp.where(lane_of(own.shape) < NC // 2, east, west)
-        return jnp.concatenate([own, halo], axis=1)
-
-    part = lambda lo, hi: widen(msg[lo:hi, :], msg_a[lo:hi, :], msg_b[lo:hi, :])
-    te, tn, faces = part(0, NR), part(NR, 2 * NR), part(2 * NR, 2 * NR + 8)
-    sf, dg = part(40, 56), part(56, 72)
+    faces = [jnp.sum(x * weight, axis=0, keepdims=True) for x in lat_a]
+    faces += [jnp.sum(x * weight_b, axis=0, keepdims=True) for x in lat_b]
+    faces = [jnp.concatenate([x, jnp.zeros((1, NC), jnp.float32)], axis=1) for x in faces]
+    for n in range(2):
+        for i in range(4):
+            at = AT_CORNER + 32 * n + 8 * i
+            sides = lon_sides(msg_a[at : at + 8, :], msg_b[at : at + 8, :])
+            for h in range(2):
+                to = 64 * n + 32 * h + 8 * i
+                corner_out[to : to + 8, :] = take_across(*sides, h, 16, False)
     row = row_of((NR, 2 * NC))
     even = even_lat()
-    north_u, north_v = (jnp.where(even, faces[i : i + 1], faces[i + 2 : i + 3]) for i in range(2))
-    south_u, south_v = (jnp.where(even, faces[i + 2 : i + 3], faces[i : i + 1]) for i in range(2))
+    north_u, north_v = (jnp.where(even, faces[i], faces[i + 2]) for i in range(2))
+    south_u, south_v = (jnp.where(even, faces[i + 2], faces[i]) for i in range(2))
     at_north, at_south = row == NR - 1, row == 0
     te = te + jnp.where(at_north, north_u, 0.0) + jnp.where(at_south, south_u, 0.0)
     tn = tn + jnp.where(at_north, north_v, 0.0) + jnp.where(at_south, south_v, 0.0)
@@ -283,16 +344,23 @@
     edge_out[...] = jnp.concatenate([first, second, to_south, zero], axis=0)
     msg_north = jnp.concatenate([rest[8:], dg[11:], first, second, zero[:1]], axis=0)
     msg_south = jnp.concatenate([rest[:9], dg[:6], to_south], axis=0)
-    a_out[...] = jnp.where(even, msg_north, msg_south)
-    b_out[...] = jnp.where(even, msg_south, msg_north)
-
-
-def solve_kernel(pc, rest, dg, edge, from_a, from_b, v_hbm, dots_out, v_out, sem):
+    for n, (out, lines) in enumerate(
+        (
+            (a_out, jnp.where(even, msg_north, msg_south)),
+            (b_out, jnp.where(even, msg_south, msg_north)),
+        )
+    ):
+        out[:NR, :] = lines[:, :NC]
+        out[NR : 2 * NR, :] = lines[:, NC:]
+        out[2 * NR :, :] = corner_out[64 * n : 64 * (n + 1), :]
+
+
+def solve_kernel(pc, th, corner, rest, dg, edge, from_a, from_b, v_hbm, dots_out, v_out, sem):
     rows, wide = 2 * NR, 2 * NC
     even = even_lat()
     exists = b_exists()
-    msg_a = from_a[...]
-    msg_b = from_b[...] * exists
+    msg_a = jnp.concatenate([from_a[:NR, :], from_a[NR : 2 * NR, :]], axis=1)
+    msg_b = jnp.concatenate([from_b[:NR, :], from_b[NR : 2 * NR, :]], axis=1) * exists
     north = jnp.where(even, msg_a, msg_b)
     south = jnp.where(even, msg_b, msg_a)
     zeros = lambda n: jnp.zeros((n, wide), jnp.float32)
@@ -306,7 +374,47 @@
         [north[:1] + edge[0:1], north[1:2] + edge[1:2], north[2:9], zeros(7)], axis=0
     )
     own = rest[...] + jnp.concatenate([south[13:15], zeros(13), north[15:]], axis=0)
-    res = jnp.concatenate([below, own, above], axis=0) * inside
+    res = jnp.concatenate([below, own, above], axis=0)
+    group = lane_of((8, NC)) // 32
+    weights = []
+    for first in halves():
+        line = None
+        for g in range(4):
+            part = th[pl.ds(pl.multiple_of(first + 8 * g, 8), 8), :]
+            line = part if g == 0 else jnp.where(group == g, part, line)
+        weights.append(DT_VISC * line)
+    sums = []
+    for n, got in enumerate((from_a, from_b)):
+        total = None
+        for h in range(2):
+            here = [corner[64 * n + 32 * h + 8 * i : 64 * n + 32 * h + 8 * (i + 1), :] for i in range(4)]
+            at = 2 * NR + 32 * (1 - h)
+            there = [got[at + 8 * i : at + 8 * (i + 1), :] for i in range(4)]
+            part = [x * weights[h] for x in face_in(here, there)]
+            total = part if h == 0 else [x + y for x, y in zip(total, part)]
+        for x in total:
+            x = jnp.sum(x, axis=0, keepdims=True)
+            x = x + pltpu.roll(x, 32, 1)
+            x = x + pltpu.roll(x, 64, 1)
+            edge_lane = lane_of((1, NC))
+            near = jnp.logical_or(edge_lane < 16, edge_lane >= NC - 16)
+            x = jnp.where(near, pltpu.roll(x, NC - 16, 1), 0.0)
+            sums.append(jnp.concatenate([jnp.zeros((1, NC), jnp.float32), x], axis=1))
+    sums[2] = sums[2] * exists
+    sums[3] = sums[3] * exists
+    north_u, north_v = (jnp.where(even, sums[i], sums[i + 2]) for i in range(2))
+    south_u, south_v = (jnp.where(even, sums[i + 2], sums[i]) for i in range(2))
+    across = lambda fu, fv: TAU * (fu - pltpu.roll(fu, 1, 1) + fv)
+    for at, line in (
+        (7 + NR, -across(north_u, north_v)),
+        (8 + NR, across(north_u, north_v) + TAU * north_v),
+        (9 + NR, -TAU * north_v),
+        (7, across(south_u, south_v)),
+        (8, -across(south_u, south_v) - TAU * south_v),
+        (9, TAU * south_v),
+    ):
+        res = res + jnp.where(row == at, line, 0.0)
+    res = res * inside
     inside = inside[:rows]
     diag = 4.0 + jnp.concatenate([zeros(3), south[8:13], dg[...], north[9:15], zeros(2)], axis=0)
 
@@ -427,11 +535,11 @@
     lax.fori_loop(0, count // per, finish, 0)
 
 
-def velocity_kernel(early, u, v, vi, w, lon, lon_a, lon_b, from_a, from_b, *rest):
+def velocity_kernel(early, u, v, vi, w, lon, msg_a, msg_b, from_a, from_b, *rest):
     u_hbm, v_hbm, u_out, v_out, packed, lines, sems = rest[0 if early else 2 :]
     is_east = lane_of((NR, NC)) % 2 == 0
     own = [lon[i] for i in range(4)]
-    other = [beyond(lon_a[i], lon_b[i]) for i in range(4)]
+    other = [edge_across(msg_a, msg_b, i) for i in range(4)]
     for i, grad in enumerate(face_in(own, other)):
         packed[i] = DT_VISC * jnp.where(is_east, grad, -grad)
     even = even_lat()
@@ -465,15 +573,16 @@
 
 
 def tracer_kernel(
-    t, u, v, w, lon, lon_a, lon_b, lon2, lon2_a, lon2_b, from_a, from_a2, from_b, from_b2,
+    t, u, v, w, lon, msg_a, msg_b, lon2, lon2_a, lon2_b, from_a, from_a2, from_b, from_b2,
     t_hbm, t_out, packed, lines, sems,
 ):
     is_east = lane_of((NR, NC)) % 2 == 0
     by = DT_ADV / 12.0
     packed[1] = beyond(lon2_a[0], lon2_b[0])
     far = lon2[1] + beyond(lon2_a[1], lon2_b[1])
-    speed = jnp.where(is_east, lon[0], beyond(lon_a[0], lon_b[0]))
-    packed[0] = speed * far * (by * lon[3] * beyond(lon_a[3], lon_b[3]))
+    speed = jnp.where(is_east, lon[0], edge_across(msg_a, msg_b, 0))
+    wets = edge_across(msg_a, msg_b, 3) * lon[3]
+    packed[0] = speed * far * (by * wets)
     even = even_lat()
     exists = b_exists()
     mine, theirs = halves()
@@ -529,9 +638,9 @@
     dma = pltpu.SemaphoreType.DMA
     rows = (4, HALF, NC)
     late = (8, HALF, NC)
-    lon, a, b, other_a, other_b = call(
+    lon, a, b, other_a, other_b, corners = call(
         fetch_kernel,
-        [(4, NR, NC), rows, rows, rows, rows],
+        [(4, NR, NC), rows, rows, rows, rows, (16, 8, NC)],
         [HBM] * 4,
         20 * NZ * NR * NC,
         4 * block,
@@ -540,24 +649,27 @@
     )(u, v, vi, w)
     from_b = lax.ppermute(b, LAT, SWAP_B)
     from_a = lax.ppermute(a, LAT, SWAP_A)
-    lon_b = lax.ppermute(lon, LON, SWAP_B)
-    lon_a = lax.ppermute(lon, LON, SWAP_A)
-    inner, th = call(
-        inner_kernel, [(2, NR, NC), (NZ + 8, NC)], [SM] + [VM] * 4, 40 * NZ * NR * NC, 4 * block
-    )(thickness, u, v, vi, w)
-    (msg,) = call(join_kernel, [(MSG, NC)], [VM] * 11, 10**6, 10**6)(
-        inner, lon, lon_a, lon_b, other_a, from_a, other_b, from_b, th, surface, surface_diag
-    )
-    msg_b = lax.ppermute(msg, LON, SWAP_B)
-    msg_a = lax.ppermute(msg, LON, SWAP_A)
+    inner, to_a, to_b, th = call(
+        inner_kernel,
+        [(2, NR, NC), (MSG, NC), (MSG, NC), (NZ + 8, NC)],
+        [SM] + [VM] * 8,
+        40 * NZ * NR * NC,
+        4 * block,
+    )(thickness, u, v, vi, w, lon, corners, surface, surface_diag)
+    msg_b = lax.ppermute(to_b, LON, SWAP_B)
+    msg_a = lax.ppermute(to_a, LON, SWAP_A)
     lon2, a2, b2 = call(
         late_kernel, [(2, NR, NC), late, late], [VM] * 4, 20 * NZ * NR * NC, 2 * block
     )(t, w, other_a, other_b)
     msg_a, msg_b, lon2, a2, b2 = lax.optimization_barrier((msg_a, msg_b, lon2, a2, b2))
     wide = (NR, 2 * NC)
-    rest, dg, edge, side_a, side_b = call(
-        side_kernel, [wide, wide, (8, 2 * NC), wide, wide], [VM] * 3, 10**6, 10**5
-    )(msg, msg_a, msg_b)
+    rest, dg, edge, corner, side_a, side_b = call(
+        side_kernel,
+        [wide, wide, (8, 2 * NC), (128, NC), (LAT_MSG, NC), (LAT_MSG, NC)],
+        [VM] * 11,
+        10**6,
+        10**5,
+    )(inner, lon, surface, surface_diag, msg_a, msg_b, other_a, from_a, other_b, from_b, th)
     got_b = lax.ppermute(side_b, LAT, SWAP_B)
     got_a = lax.ppermute(side_a, LAT, SWAP_A)
     (taps,) = call(taps_kernel, [(32, 2 * NC)], [SM], 10**4, 10**4)(precond_kernel)
@@ -572,19 +684,19 @@
             + [pltpu.VMEM((2, NR, NC), jnp.float32), pltpu.VMEM((4, NZ, NC), jnp.float32), dma((CHUNKS, 2))],
             HBM,
             aliases={9 + i: i for i in range(len(written))},
-        )(u, v, vi, w, lon, lon_a, lon_b, *edges, *written)
+        )(u, v, vi, w, lon, msg_a, msg_b, *edges, *written)
 
     u_half, v_half = velocity(True, (from_a, from_b), ())
     got_a, got_b, u_half, v_half = lax.optimization_barrier((got_a, got_b, u_half, v_half))
     vecs, dots = call(
         solve_kernel,
         [(3, NR, NC), (32, 8, NC)],
-        [VM] * 6,
+        [VM] * 8,
         10**6,
         10**5,
         [pltpu.VMEM((3, NR, NC), jnp.float32), dma],
         [HBM, VM],
-    )(taps, rest, dg, edge, got_a, got_b)
+    )(taps, th, corner, rest, dg, edge, got_a, got_b)
     dots, a2, b2, lon2 = lax.optimization_barrier((dots, a2, b2, lon2))
     from_b2 = lax.ppermute(b2, LAT, SWAP_B)
     from_a2 = lax.ppermute(a2, LAT, SWAP_A)
@@ -601,7 +713,7 @@
         5 * block,
         [field, pltpu.VMEM((2, NR, NC), jnp.float32), pltpu.VMEM((4, NZ, NC), jnp.float32), dma((CHUNKS, 1))],
         HBM,
-    )(t, u, v, w, lon, lon_a, lon_b, lon2, lon2_a, lon2_b, *lat)[0]
+    )(t, u, v, w, lon, msg_a, msg_b, lon2, lon2_a, lon2_b, *lat)[0]
     (dots,) = call(relay_kernel, [(8, 1, NC)], [VM], 10**4, 10**4)(dots)
     dots = lax.all_to_all(dots, ("zl", "zh"), 0, 0)
     dots, t_new, u_new, v_new = lax.optimization_barrier((dots, t_new, u_new, v_new))

time: 58.9 us -> 58.2 us (0.988)
  starting transfers between devices: 37 us -> 31.3 us
  waiting for transfers between devices: 2.96 us -> 6.25 us
  local copies, waits for them, and re-layouts: 0.04 us -> 1.35 us
    ppermute x4 -> x2, starting transfers between devices: 6.45 us -> 2.52 us  [the longest x1 1.32 us: local(): msg_a = lax.ppermute(to_a, LON, SWAP_A)]
    ppermute x1, waiting for transfers between devices: 1.7 us -> 3.49 us  [local(): got_b = lax.ppermute(side_b, LAT, SWAP_B)]
    ppermute x1, starting transfers between devices: 2.52 us -> 0.9 us  [local(): got_b = lax.ppermute(side_b, LAT, SWAP_B)]
    unnamed x18, local copies, waits for them, and re-layouts: 0.04 us -> 1.35 us
    ppermute x1, starting transfers between devices: 4.32 us -> 3.22 us  [local(): from_b2 = lax.ppermute(b2, LAT, SWAP_B)]
    all_to_all x1, waiting for transfers between devices: 0.01 us -> 1.01 us  [local(): dots = lax.all_to_all(dots, ('x', 'y', 'c'), 0, 0)]
    all_to_all x1, starting transfers between devices: 6.14 us -> 6.88 us  [local(): dots = lax.all_to_all(dots, ('x', 'y', 'c'), 0, 0)]
    pallas_call x5 -> x4, Pallas kernels: 6.65 us -> 7.06 us  [the longest x1 2.7 us: local(): call(fetch_kernel, [(4, NR, NC), rows, rows, rows, rows, (16, 8, NC)], [H...]
  transfers between devices with their start and end apart: 14 -> 12, of which waited for: 2 -> 5; matrix products, arithmetic and copies ran while one was open for 0% -> 0% of each run, Pallas kernels for 22% -> 22%
where the time goes in v7:
time: 58.2 us; the launch traced here: 57.9 us
  starting transfers between devices  31.3 us (54%)
  Pallas kernels  18.3 us (31%)
  waiting for transfers between devices  6.25 us (11%)
  local copies, waits for them, and re-layouts  1.35 us (2%)
  between operations  0.82 us (1%)
    all_to_all x1, starting transfers between devices, local(): dots = lax.all_to_all(dots, ('x', 'y', 'c'), 0, 0)  6.88 us
    ppermute x1, starting transfers between devices, local(): from_b = lax.ppermute(b, LAT, SWAP_B)  6.65 us
    pallas_call x2, Pallas kernels, velocity(): call(functools.partial(velocity_kernel, early), [flat] * 2, [VM] * 9 + [H...  4.06 us
    ppermute x1, starting transfers between devices, local(): from_a = lax.ppermute(a, LAT, SWAP_A)  3.91 us
    ppermute x1, waiting for transfers between devices, local(): got_b = lax.ppermute(side_b, LAT, SWAP_B)  3.49 us
    all_to_all x1, starting transfers between devices, local(): dots = lax.all_to_all(dots, ('zl', 'zh'), 0, 0)  3.31 us
    ppermute x1, starting transfers between devices, local(): from_b2 = lax.ppermute(b2, LAT, SWAP_B)  3.22 us
    pallas_call x1, Pallas kernels, local(): call(tracer_kernel, [flat], [VM] * 14, 60 * NZ * NR * NC, 5 * block, [fie...  3.02 us
  transfers between devices with their start and end apart: 12, of which 5 were waited for; matrix products, arithmetic and copies ran while one was open for 0% of the time, Pallas kernels for 22%

profile of v7, /device:TPU:1, one launch (start us, length us, event | category | flops | bytes accessed | tf_op | source)
XLA Modules:
  0.0 57.9 jit_solution(9960694967241553410)
XLA Ops:
  0.6 0.0 copy-start.5
  0.6 0.0 copy-start
  0.7 0.0 copy-start.1
  0.7 0.0 copy-start.2
  0.7 0.0 copy-start.3
  0.7 2.7 %shard_map.121 = (f32[4,16,128]{2,1,0:T(8,128)S(1)}, f32[4,32,128]{2,1,0:T(8,128)S(1)}, f32[4,32,128]{2,1,0:T(8,128)S(1)}, f32[4,32,128]{2,1,0:T(8,128)S(1)}, f3...) custom-call(f32[1024,128]{1,0:T(8,128)} %bitcast.14, f32[1024,128]{1,0:T(8,128)} %bitcast.19, f32[1024,128]{1,0:T(8,128)} %bitcast.24, ...), custom_call_target="tpu_custom_call" | custom-call | flops 2621440 | bytes 2097152 | tf_op jit(solution)/shard_map/pallas_call | solution.py:641
  3.4 3.9 %collective-permute-start.2 = (f32[4,32,128]{2,1,0:T(8,128)S(1)}, f32[4,32,128]{2,1,0:T(8,128)S(1)}, u32[]{:S(2)}, u32[]{:S(2)}) collective-permute-start(f32[4,32,128]{2,1,0:T(8,128)S(1)} %get-tuple-element.59), channel_id=1, source_target_pairs={{0,1},{1,0},{2,3},{3,2},{4,5},{5,4},{6,7},{7,6},{8,9},{9,8},{10,11... | collective-permute-start | bytes 196616 | tf_op jit(solution)/shard_map/ppermute | solution.py:651
  7.3 6.7 %collective-permute-start.3 = (f32[4,32,128]{2,1,0:T(8,128)S(1)}, f32[4,32,128]{2,1,0:T(8,128)S(1)}, u32[]{:S(2)}, u32[]{:S(2)}) collective-permute-start(f32[4,32,128]{2,1,0:T(8,128)S(1)} %get-tuple-element.60), channel_id=1, source_target_pairs={{0,15},{1,2},{2,1},{3,4},{4,3},{5,6},{6,5},{7,8},{8,7},{9,10},{10,... | collective-permute-start | bytes 196616 | tf_op jit(solution)/shard_map/ppermute | solution.py:650
  13.9 0.0 copy-done.5
  14.0 0.0 copy-done
  14.0 0.0 copy-done.1
  14.0 0.0 copy-done.2
  14.0 0.0 copy-done.3
  14.0 0.6 %copy-done.8 = f32[64]{0:T(128)S(1)} copy-done((f32[64]{0:T(128)S(1)}, f32[64]{0:T(128)}, u32[]{:S(2)}) %copy-start.8) | copy-done | bytes 280
  14.6 0.7 %copy-done.6 = f32[16,128]{1,0:T(8,128)S(1)} copy-done((f32[16,128]{1,0:T(8,128)S(1)}, f32[16,128]{1,0:T(8,128)}, u32[]{:S(2)}) %copy-start.6) | copy-done | bytes 8216
  15.3 2.4 %shard_map.122 = (f32[2,16,128]{2,1,0:T(8,128)S(1)}, f32[112,128]{1,0:T(8,128)S(1)}, f32[112,128]{1,0:T(8,128)S(1)}, f32[72,128]{1,0:T(8,128)S(1)}) custom-call(f32[64]{0:T(128)S(1)} %copy-done.8, f32[1024,128]{1,0:T(8,128)S(1)} %bitcast.15, f32[1024,128]{1,0:T(8,128)S(1)} %bitcast.20, f32[1024,128]{1,0:T(8,128)S(1)} %bitcast.25, s32[1024,128]{1,0:T(8,128)S(1)} %bitcast.9, ...), custom_call_target="tpu_custom_call" | custom-call | flops 5242880 | bytes 2097152 | tf_op jit(solution)/shard_map/pallas_call | solution.py:652
  17.7 1.3 %collective-permute-start = (f32[112,128]{1,0:T(8,128)S(1)}, f32[112,128]{1,0:T(8,128)S(1)}, u32[]{:S(2)}, u32[]{:S(2)}) collective-permute-start(f32[112,128]{1,0:T(8,128)S(1)} %get-tuple-element.50), channel_id=1, source_target_pairs={{0,16},{16,0},{32,48},{48,32},{64,80},{80,64},{96,112},{112,96},{1... | collective-permute-start | bytes 172040 | tf_op jit(solution)/shard_map/ppermute | solution.py:660
  19.0 1.2 %collective-permute-start.1 = (f32[112,128]{1,0:T(8,128)S(1)}, f32[112,128]{1,0:T(8,128)S(1)}, u32[]{:S(2)}, u32[]{:S(2)}) collective-permute-start(f32[112,128]{1,0:T(8,128)S(1)} %get-tuple-element.51), channel_id=1, source_target_pairs={{0,240},{16,32},{32,16},{48,64},{64,48},{80,96},{96,80},{112,128},... | collective-permute-start | bytes 172040 | tf_op jit(solution)/shard_map/ppermute | solution.py:659
  20.2 0.0 copy-done.4
  20.2 2.2 %shard_map.123 = (f32[2,16,128]{2,1,0:T(8,128)S(1)}, f32[8,32,128]{2,1,0:T(8,128)}, f32[8,32,128]{2,1,0:T(8,128)S(1)}) custom-call(f32[1024,128]{1,0:T(8,128)S(1)} %bitcast.28, s32[1024,128]{1,0:T(8,128)S(1)} %bitcast.10, f32[4,32,128]{2,1,0:T(8,128)S(1)} %get-tuple-element.52.other_a.a2, f32[4,32,128]{2,1,0:T(8,128)S(1)} %get-tuple-element.53.other_b.b2), custom_call_target="tpu_custom_call" | custom-call | flops 2621440 | bytes 1048576 | tf_op jit(solution)/shard_map/pallas_call | solution.py:661
  22.4 0.0 collective-permute-done.msg_a
  22.4 0.2 collective-permute-done.1.msg_b
  22.6 0.0 collective-permute-done.2.from_a
  22.6 0.0 collective-permute-done.3.from_b
  22.6 0.3 shard_map.124
  22.9 0.1 collective-permute-start.4
  23.0 0.9 %collective-permute-start.5 = (f32[96,128]{1,0:T(8,128)S(1)}, f32[96,128]{1,0:T(8,128)S(1)}, u32[]{:S(2)}, u32[]{:S(2)}) collective-permute-start(f32[96,128]{1,0:T(8,128)S(1)} %get-tuple-element.66), channel_id=1, source_target_pairs={{0,15},{1,2},{2,1},{3,4},{4,3},{5,6},{6,5},{7,8},{8,7},{9,10},{10,... | collective-permute-start | bytes 147464 | tf_op jit(solution)/shard_map/ppermute | solution.py:673
  23.9 0.6 %shard_map.120.pc = f32[32,256]{1,0:T(8,128)S(1)} custom-call(f32[5,5]{1,0:T(8,128)S(1)} %copy-done.7), custom_call_target="tpu_custom_call" | custom-call | flops 10000 | bytes 10000 | tf_op jit(solution)/shard_map/pallas_call | solution.py:675
  24.5 2.0 %shard_map.125 = (f32[1024,128]{1,0:T(8,128)}, f32[1024,128]{1,0:T(8,128)}) custom-call(f32[1024,128]{1,0:T(8,128)S(1)} %bitcast.16, f32[1024,128]{1,0:T(8,128)S(1)} %bitcast.21, f32[1024,128]{1,0:T(8,128)S(1)} %bitcast.26, s32[1024,128]{1,0:T(8,128)S(1)} %bitcast.11, f32[4,16,128]{2,1,0:T(8,128)S(1)} %get-tuple-element.46.lon, ...), custom_call_target="tpu_custom_call" | custom-call | flops 3932160 | bytes 1572864 | tf_op jit(solution)/shard_map/pallas_call | solution.py:677
  26.6 0.3 collective-permute-done.4.from_a
  26.8 3.5 %collective-permute-done.5.from_b = f32[96,128]{1,0:T(8,128)S(1)} collective-permute-done((f32[96,128]{1,0:T(8,128)S(1)}, f32[96,128]{1,0:T(8,128)S(1)}, u32[]{:S(2)}, u32[]{:S(2)}) %collective-permute-start.5) | collective-permute-done | bytes 49184 | tf_op jit(solution)/shard_map/ppermute | solution.py:673
  30.3 1.7 %shard_map.126 = (f32[3,16,128]{2,1,0:T(8,128)S(1)}, f32[32,8,128]{2,1,0:T(8,128)}) custom-call(f32[32,256]{1,0:T(8,128)S(1)} %shard_map.120.pc, f32[72,128]{1,0:T(8,128)S(1)} %get-tuple-element.48.th, f32[128,128]{1,0:T(8,128)S(1)} %get-tuple-element.61.corner, f32[16,256]{1,0:T(8,128)S(1)} %get-tuple-element.62.rest, f32[16,256]{1,0:T(8,128)S(1)} %get-tuple-element.63.dg, ...), custom_call_target="tpu_custom_call" | custom-call | flops 1000000 | bytes 100000 | tf_op jit(solution)/shard_map/pallas_call | solution.py:691
  32.0 6.9 %all-to-all-start = ((f32[32,8,128]{2,1,0:T(8,128)}), f32[32,8,128]{2,1,0:T(8,128)S(1)}, u32[]{:S(2)}, u32[]{:S(2)}) async-start(f32[32,8,128]{2,1,0:T(8,128)} %get-tuple-element.75), calls=%async_computation | async-start | bytes 262144 | tf_op jit(solution)/shard_map/all_to_all | solution.py:705
  38.9 0.5 collective-permute-start.8
  39.4 3.2 %collective-permute-start.9 = (f32[8,32,128]{2,1,0:T(8,128)S(1)}, f32[8,32,128]{2,1,0:T(8,128)S(1)}, u32[]{:S(2)}, u32[]{:S(2)}) collective-permute-start(f32[8,32,128]{2,1,0:T(8,128)S(1)} %get-tuple-element.78), channel_id=1, source_target_pairs={{0,15},{1,2},{2,1},{3,4},{4,3},{5,6},{6,5},{7,8},{8,7},{9,10},{10,... | collective-permute-start | bytes 393224 | tf_op jit(solution)/shard_map/ppermute | solution.py:701
  42.6 2.0 %collective-permute-start.7 = (f32[2,16,128]{2,1,0:T(8,128)S(1)}, f32[2,16,128]{2,1,0:T(8,128)S(1)}, u32[]{:S(2)}, u32[]{:S(2)}) collective-permute-start(f32[2,16,128]{2,1,0:T(8,128)S(1)} %get-tuple-element.76.lon2), channel_id=1, source_target_pairs={{0,240},{16,32},{32,16},{48,64},{64,48},{80,96},{96,80},{112,128},... | collective-permute-start | bytes 49160 | tf_op jit(solution)/shard_map/ppermute | solution.py:703
  44.6 1.3 %collective-permute-start.6 = (f32[2,16,128]{2,1,0:T(8,128)S(1)}, f32[2,16,128]{2,1,0:T(8,128)S(1)}, u32[]{:S(2)}, u32[]{:S(2)}) collective-permute-start(f32[2,16,128]{2,1,0:T(8,128)S(1)} %get-tuple-element.76.lon2), channel_id=1, source_target_pairs={{0,16},{16,0},{32,48},{48,32},{64,80},{80,64},{96,112},{112,96},{1... | collective-permute-start | bytes 49160 | tf_op jit(solution)/shard_map/ppermute | solution.py:704
  45.9 1.0 %all-to-all-done.got = f32[32,8,128]{2,1,0:T(8,128)S(1)} async-done(((f32[32,8,128]{2,1,0:T(8,128)}), f32[32,8,128]{2,1,0:T(8,128)S(1)}, u32[]{:S(2)}, u32[]{:S(2)}) %all-to-all-start) | async-done | bytes 131104 | tf_op jit(solution)/shard_map/all_to_all | solution.py:705
  46.9 0.6 %shard_map.127 = f32[8,1,128]{2,1,0:T(1,128)} custom-call(f32[32,8,128]{2,1,0:T(8,128)S(1)} %all-to-all-done.got), custom_call_target="tpu_custom_call" | custom-call | flops 10000 | bytes 10000 | tf_op jit(solution)/shard_map/pallas_call | solution.py:717
  47.6 3.3 %all-to-all-start.1 = ((f32[8,1,128]{2,1,0:T(1,128)}), f32[8,1,128]{2,1,0:T(1,128)S(1)}, u32[]{:S(2)}, u32[]{:S(2)}) async-start(f32[8,1,128]{2,1,0:T(1,128)} %shard_map.127), calls=%async_computation.1 | async-start | bytes 8192 | tf_op jit(solution)/shard_map/all_to_all | solution.py:718
  50.9 0.0 collective-permute-done.8.from_a2.from_a
  50.9 0.0 collective-permute-done.9.from_b2.from_b
  50.9 2.0 %shard_map.129 = (f32[1024,128]{1,0:T(8,128)}, f32[1024,128]{1,0:T(8,128)}) custom-call(f32[1024,128]{1,0:T(8,128)S(1)} %bitcast.17, f32[1024,128]{1,0:T(8,128)S(1)} %bitcast.22, f32[1024,128]{1,0:T(8,128)S(1)} %bitcast.27, s32[1024,128]{1,0:T(8,128)S(1)} %bitcast.12, ...), custom_call_target="tpu_custom_call", output_to_operand_aliasing={{0}: (9, {}), {1}: (10, {})} | custom-call | flops 3932160 | bytes 1572864 | tf_op jit(solution)/shard_map/pallas_call | solution.py:677
  52.9 0.0 collective-permute-done.7.lon2_b
  53.0 0.0 collective-permute-done.6.lon2_a
  53.0 3.0 %shard_map.128 = f32[1024,128]{1,0:T(8,128)} custom-call(f32[1024,128]{1,0:T(8,128)S(1)} %bitcast.29, f32[1024,128]{1,0:T(8,128)S(1)} %bitcast.18, f32[1024,128]{1,0:T(8,128)S(1)} %bitcast.23, s32[1024,128]{1,0:T(8,128)S(1)} %bitcast.13, f32[4,16,128]{2,1,0:T(8,128)S(1)} %get-tuple-element.46.lon, f32[112,128]{1,0:T(8,128)S(1)} %collective-permute-done.msg_a, ...), custom_call_target="tpu_custom_call" | custom-call | flops 7864320 | bytes 2621440 | tf_op jit(solution)/shard_map/pallas_call | solution.py:708
  56.0 1.2 %all-to-all-done.1.got = f32[8,1,128]{2,1,0:T(1,128)S(1)} async-done(((f32[8,1,128]{2,1,0:T(1,128)}), f32[8,1,128]{2,1,0:T(1,128)S(1)}, u32[]{:S(2)}, u32[]{:S(2)}) %all-to-all-start.1) | async-done | bytes 4128 | tf_op jit(solution)/shard_map/all_to_all | solution.py:718
  57.2 0.7 %shard_map.130 = f32[16,128]{1,0:T(8,128)} custom-call(f32[8,1,128]{2,1,0:T(1,128)S(1)} %all-to-all-done.1.got, f32[3,16,128]{2,1,0:T(8,128)S(1)} %get-tuple-element.87.v, f32[16,128]{1,0:T(8,128)S(1)} %copy-done.5), custom_call_target="tpu_custom_call" | custom-call | flops 100000 | bytes 10000 | tf_op jit(solution)/shard_map/pallas_call | solution.py:720
  (5 shorter events, 0.0 us)
Async XLA Ops:
  0.6 13.3 %copy-start.5 = (f32[16,128]{1,0:T(8,128)S(1)}, f32[16,128]{1,0:T(8,128)}, u32[]{:S(2)}) copy-start(f32[16,128]{1,0:T(8,128)} %sf.3) | copy-start | bytes 24580
  0.6 13.3 %copy-start = (s32[64,16,128]{2,1,0:T(8,128)S(1)}, s32[64,16,128]{2,1,0:T(8,128)}, u32[]{:S(2)}) copy-start(s32[64,16,128]{2,1,0:T(8,128)} %param.13) | copy-start | bytes 1572868
  0.7 13.3 %copy-start.1 = (f32[64,16,128]{2,1,0:T(8,128)S(1)}, f32[64,16,128]{2,1,0:T(8,128)}, u32[]{:S(2)}) copy-start(f32[64,16,128]{2,1,0:T(8,128)} %param.10) | copy-start | bytes 1572868
  0.7 13.3 %copy-start.2 = (f32[64,16,128]{2,1,0:T(8,128)S(1)}, f32[64,16,128]{2,1,0:T(8,128)}, u32[]{:S(2)}) copy-start(f32[64,16,128]{2,1,0:T(8,128)} %param.11) | copy-start | bytes 1572868
  0.7 13.3 %copy-start.3 = (f32[64,16,128]{2,1,0:T(8,128)S(1)}, f32[64,16,128]{2,1,0:T(8,128)}, u32[]{:S(2)}) copy-start(f32[64,16,128]{2,1,0:T(8,128)} %param.12) | copy-start | bytes 1572868
  3.4 19.2 %collective-permute-start.2 = (f32[4,32,128]{2,1,0:T(8,128)S(1)}, f32[4,32,128]{2,1,0:T(8,128)S(1)}, u32[]{:S(2)}, u32[]{:S(2)}) collective-permute-start(f32[4,32,128]{2,1,0:T(8,128)S(1)} %get-tuple-element.59), channel_id=1, source_target_pairs={{0,1},{1,0},{2,3},{3,2},{4,5},{5,4},{6,7},{7,6},{8,9},{9,8},{10,11... | collective-permute-start | bytes 196616 | tf_op jit(solution)/shard_map/ppermute | solution.py:651
  7.3 15.3 %collective-permute-start.3 = (f32[4,32,128]{2,1,0:T(8,128)S(1)}, f32[4,32,128]{2,1,0:T(8,128)S(1)}, u32[]{:S(2)}, u32[]{:S(2)}) collective-permute-start(f32[4,32,128]{2,1,0:T(8,128)S(1)} %get-tuple-element.60), channel_id=1, source_target_pairs={{0,15},{1,2},{2,1},{3,4},{4,3},{5,6},{6,5},{7,8},{8,7},{9,10},{10,... | collective-permute-start | bytes 196616 | tf_op jit(solution)/shard_map/ppermute | solution.py:650
  13.9 0.7 %copy-start.8 = (f32[64]{0:T(128)S(1)}, f32[64]{0:T(128)}, u32[]{:S(2)}) copy-start(f32[64]{0:T(128)} %thick.1) | copy-start | bytes 772
  14.6 0.7 %copy-start.6 = (f32[16,128]{1,0:T(8,128)S(1)}, f32[16,128]{1,0:T(8,128)}, u32[]{:S(2)}) copy-start(f32[16,128]{1,0:T(8,128)} %dg_own.1) | copy-start | bytes 24580
  15.3 4.9 %copy-start.4 = (f32[64,16,128]{2,1,0:T(8,128)S(1)}, f32[64,16,128]{2,1,0:T(8,128)}, u32[]{:S(2)}) copy-start(f32[64,16,128]{2,1,0:T(8,128)} %param.9) | copy-start | bytes 1572868
  17.7 4.7 %collective-permute-start = (f32[112,128]{1,0:T(8,128)S(1)}, f32[112,128]{1,0:T(8,128)S(1)}, u32[]{:S(2)}, u32[]{:S(2)}) collective-permute-start(f32[112,128]{1,0:T(8,128)S(1)} %get-tuple-element.50), channel_id=1, source_target_pairs={{0,16},{16,0},{32,48},{48,32},{64,80},{80,64},{96,112},{112,96},{1... | collective-permute-start | bytes 172040 | tf_op jit(solution)/shard_map/ppermute | solution.py:660
  19.0 3.6 %collective-permute-start.1 = (f32[112,128]{1,0:T(8,128)S(1)}, f32[112,128]{1,0:T(8,128)S(1)}, u32[]{:S(2)}, u32[]{:S(2)}) collective-permute-start(f32[112,128]{1,0:T(8,128)S(1)} %get-tuple-element.51), channel_id=1, source_target_pairs={{0,240},{16,32},{32,16},{48,64},{64,48},{80,96},{96,80},{112,128},... | collective-permute-start | bytes 172040 | tf_op jit(solution)/shard_map/ppermute | solution.py:659
  22.6 1.3 %copy-start.7 = (f32[5,5]{1,0:T(8,128)S(1)}, f32[5,5]{1,0:T(8,128)}, u32[]{:S(2)}) copy-start(f32[5,5]{1,0:T(8,128)} %pc.1) | copy-start | bytes 304
  22.9 3.9 %collective-permute-start.4 = (f32[96,128]{1,0:T(8,128)S(1)}, f32[96,128]{1,0:T(8,128)S(1)}, u32[]{:S(2)}, u32[]{:S(2)}) collective-permute-start(f32[96,128]{1,0:T(8,128)S(1)} %get-tuple-element.65), channel_id=1, source_target_pairs={{0,1},{1,0},{2,3},{3,2},{4,5},{5,4},{6,7},{7,6},{8,9},{9,8},{10,11... | collective-permute-start | bytes 147464 | tf_op jit(solution)/shard_map/ppermute | solution.py:674
  23.0 7.3 %collective-permute-start.5 = (f32[96,128]{1,0:T(8,128)S(1)}, f32[96,128]{1,0:T(8,128)S(1)}, u32[]{:S(2)}, u32[]{:S(2)}) collective-permute-start(f32[96,128]{1,0:T(8,128)S(1)} %get-tuple-element.66), channel_id=1, source_target_pairs={{0,15},{1,2},{2,1},{3,4},{4,3},{5,6},{6,5},{7,8},{8,7},{9,10},{10,... | collective-permute-start | bytes 147464 | tf_op jit(solution)/shard_map/ppermute | solution.py:673
  32.0 14.9 %all-to-all-start = ((f32[32,8,128]{2,1,0:T(8,128)}), f32[32,8,128]{2,1,0:T(8,128)S(1)}, u32[]{:S(2)}, u32[]{:S(2)}) async-start(f32[32,8,128]{2,1,0:T(8,128)} %get-tuple-element.75), calls=%async_computation | async-start | bytes 262144 | tf_op jit(solution)/shard_map/all_to_all | solution.py:705
  38.9 12.0 %collective-permute-start.8 = (f32[8,32,128]{2,1,0:T(8,128)}, f32[8,32,128]{2,1,0:T(8,128)S(1)}, u32[]{:S(2)}, u32[]{:S(2)}) collective-permute-start(f32[8,32,128]{2,1,0:T(8,128)} %get-tuple-element.77), channel_id=1, source_target_pairs={{0,1},{1,0},{2,3},{3,2},{4,5},{5,4},{6,7},{7,6},{8,9},{9,8},{10,11... | collective-permute-start | bytes 393224 | tf_op jit(solution)/shard_map/ppermute | solution.py:702
  39.4 11.5 %collective-permute-start.9 = (f32[8,32,128]{2,1,0:T(8,128)S(1)}, f32[8,32,128]{2,1,0:T(8,128)S(1)}, u32[]{:S(2)}, u32[]{:S(2)}) collective-permute-start(f32[8,32,128]{2,1,0:T(8,128)S(1)} %get-tuple-element.78), channel_id=1, source_target_pairs={{0,15},{1,2},{2,1},{3,4},{4,3},{5,6},{6,5},{7,8},{8,7},{9,10},{10,... | collective-permute-start | bytes 393224 | tf_op jit(solution)/shard_map/ppermute | solution.py:701
  42.6 10.3 %collective-permute-start.7 = (f32[2,16,128]{2,1,0:T(8,128)S(1)}, f32[2,16,128]{2,1,0:T(8,128)S(1)}, u32[]{:S(2)}, u32[]{:S(2)}) collective-permute-start(f32[2,16,128]{2,1,0:T(8,128)S(1)} %get-tuple-element.76.lon2), channel_id=1, source_target_pairs={{0,240},{16,32},{32,16},{48,64},{64,48},{80,96},{96,80},{112,128},... | collective-permute-start | bytes 49160 | tf_op jit(solution)/shard_map/ppermute | solution.py:703
  44.6 8.4 %collective-permute-start.6 = (f32[2,16,128]{2,1,0:T(8,128)S(1)}, f32[2,16,128]{2,1,0:T(8,128)S(1)}, u32[]{:S(2)}, u32[]{:S(2)}) collective-permute-start(f32[2,16,128]{2,1,0:T(8,128)S(1)} %get-tuple-element.76.lon2), channel_id=1, source_target_pairs={{0,16},{16,0},{32,48},{48,32},{64,80},{80,64},{96,112},{112,96},{1... | collective-permute-start | bytes 49160 | tf_op jit(solution)/shard_map/ppermute | solution.py:704
  47.6 9.7 %all-to-all-start.1 = ((f32[8,1,128]{2,1,0:T(1,128)}), f32[8,1,128]{2,1,0:T(1,128)S(1)}, u32[]{:S(2)}, u32[]{:S(2)}) async-start(f32[8,1,128]{2,1,0:T(1,128)} %shard_map.127), calls=%async_computation.1 | async-start | bytes 8192 | tf_op jit(solution)/shard_map/all_to_all | solution.py:718

commit v8 on v7

--- a/solution.py
+++ b/solution.py
@@ -123,7 +123,7 @@
     return out
 
 
-def fetch_kernel(u, v, vi, land, lon_out, a_out, b_out, other_a, other_b, corners, uo, vo, vio, lo, sems):
+def fetch_kernel(u, v, vi, land, lon_out, a_out, b_out, corners, uo, vo, vio, lo, sems):
     pair = lane_of((NR, NC)) // 2
 
     def body(k, acc):
@@ -140,13 +140,11 @@
         lon_out[i] = acc[i]
     even = even_lat()
     mine, theirs = halves()
-    for north, first, rest in ((even, a_out, other_a), (jnp.logical_not(even), b_out, other_b)):
+    for n, (north, out) in enumerate(((even, a_out), (jnp.logical_not(even), b_out))):
         for i, ref in enumerate((uo, vo, vio, lo)):
-            first[i] = edge_row(ref, north, 0, mine, HALF)
-            rest[i] = edge_row(ref, north, 0, theirs, HALF)
-    for n, ref in enumerate((a_out, other_a, b_out, other_b)):
-        for i in range(4):
-            corners[4 * n + i] = squeeze(ref[i], 16)
+            out[i] = edge_row(ref, north, 0, mine, HALF)
+            corners[8 * n + i] = squeeze(out[i], 16)
+            corners[8 * n + 4 + i] = squeeze(edge_row(ref, north, 0, theirs, HALF), 16)
 
 
 AT_CORNER, AT_FIELDS, MSG = 32, 96, 112
@@ -217,7 +215,7 @@
         msg[AT_FIELDS:, :] = line
 
 
-def late_kernel(t, w, other_a, other_b, lon_out, a_out, b_out):
+def late_kernel(t, u, v, vi, w, lon_out, a_out, b_out):
     lane = lane_of((NR, NC))
     pair = lane // 2
     half_lane = lane < NC // 2
@@ -236,8 +234,10 @@
     lon_out[0] = acc[0]
     lon_out[1] = acc[1]
     even = even_lat()
-    for north, src, dst in ((even, other_a, a_out), (jnp.logical_not(even), other_b, b_out)):
-        dst[:4] = src[...]
+    _, theirs = halves()
+    for north, dst in ((even, a_out), (jnp.logical_not(even), b_out)):
+        for i, ref in enumerate((u, v, vi, w)):
+            dst[i] = edge_row(ref, north, 0, theirs, HALF)
         for i in range(2):
             near, inner = (
                 edge_row(t, north, n, i * HALF, HALF) * edge_row(w, north, n, i * HALF, HALF)
@@ -277,7 +277,7 @@
 
 
 def side_kernel(
-    inner, lon, sf_own, dg_own, msg_a, msg_b, a2, from_a, b2, from_b, th,
+    inner, lon, sf_own, dg_own, msg_a, msg_b, u, v, vi, w, from_a, from_b, th,
     rest_out, diag_out, edge_out, corner_out, a_out, b_out,
 ):
     lane = lane_of((NR, NC))
@@ -307,9 +307,11 @@
     tn = tn + add[1]
     _, theirs = halves()
     weight = DT_VISC * th[pl.ds(theirs, HALF), :]
-    lat_a = face_in([a2[i] for i in range(4)], [from_a[i] for i in range(4)])
+    even = even_lat()
+    rows_of = lambda north: [edge_row(ref, north, 0, theirs, HALF) for ref in (u, v, vi, w)]
+    lat_a = face_in(rows_of(even), [from_a[i] for i in range(4)])
     weight_b = weight * b_exists()
-    lat_b = face_in([b2[i] for i in range(4)], [from_b[i] for i in range(4)])
+    lat_b = face_in(rows_of(jnp.logical_not(even)), [from_b[i] for i in range(4)])
     faces = [jnp.sum(x * weight, axis=0, keepdims=True) for x in lat_a]
     faces += [jnp.sum(x * weight_b, axis=0, keepdims=True) for x in lat_b]
     faces = [jnp.concatenate([x, jnp.zeros((1, NC), jnp.float32)], axis=1) for x in faces]
@@ -638,9 +640,9 @@
     dma = pltpu.SemaphoreType.DMA
     rows = (4, HALF, NC)
     late = (8, HALF, NC)
-    lon, a, b, other_a, other_b, corners = call(
+    lon, a, b, corners = call(
         fetch_kernel,
-        [(4, NR, NC), rows, rows, rows, rows, (16, 8, NC)],
+        [(4, NR, NC), rows, rows, (16, 8, NC)],
         [HBM] * 4,
         20 * NZ * NR * NC,
         4 * block,
@@ -659,17 +661,19 @@
     msg_b = lax.ppermute(to_b, LON, SWAP_B)
     msg_a = lax.ppermute(to_a, LON, SWAP_A)
     lon2, a2, b2 = call(
-        late_kernel, [(2, NR, NC), late, late], [VM] * 4, 20 * NZ * NR * NC, 2 * block
-    )(t, w, other_a, other_b)
-    msg_a, msg_b, lon2, a2, b2 = lax.optimization_barrier((msg_a, msg_b, lon2, a2, b2))
+        late_kernel, [(2, NR, NC), late, late], [VM] * 5, 20 * NZ * NR * NC, 2 * block
+    )(t, u, v, vi, w)
+    lon2_b = lax.ppermute(lon2, LON, SWAP_B)
+    lon2_a = lax.ppermute(lon2, LON, SWAP_A)
+    msg_a, msg_b, a2, b2 = lax.optimization_barrier((msg_a, msg_b, a2, b2))
     wide = (NR, 2 * NC)
     rest, dg, edge, corner, side_a, side_b = call(
         side_kernel,
         [wide, wide, (8, 2 * NC), (128, NC), (LAT_MSG, NC), (LAT_MSG, NC)],
-        [VM] * 11,
+        [VM] * 13,
         10**6,
         10**5,
-    )(inner, lon, surface, surface_diag, msg_a, msg_b, other_a, from_a, other_b, from_b, th)
+    )(inner, lon, surface, surface_diag, msg_a, msg_b, u, v, vi, w, from_a, from_b, th)
     got_b = lax.ppermute(side_b, LAT, SWAP_B)
     got_a = lax.ppermute(side_a, LAT, SWAP_A)
     (taps,) = call(taps_kernel, [(32, 2 * NC)], [SM], 10**4, 10**4)(precond_kernel)
@@ -687,7 +691,9 @@
         )(u, v, vi, w, lon, msg_a, msg_b, *edges, *written)
 
     u_half, v_half = velocity(True, (from_a, from_b), ())
-    got_a, got_b, u_half, v_half = lax.optimization_barrier((got_a, got_b, u_half, v_half))
+    got_a, got_b, u_half, v_half, lon2_a, lon2_b = lax.optimization_barrier(
+        (got_a, got_b, u_half, v_half, lon2_a, lon2_b)
+    )
     vecs, dots = call(
         solve_kernel,
         [(3, NR, NC), (32, 8, NC)],
@@ -697,11 +703,9 @@
         [pltpu.VMEM((3, NR, NC), jnp.float32), dma],
         [HBM, VM],
     )(taps, th, corner, rest, dg, edge, got_a, got_b)
-    dots, a2, b2, lon2 = lax.optimization_barrier((dots, a2, b2, lon2))
+    dots, a2, b2 = lax.optimization_barrier((dots, a2, b2))
     from_b2 = lax.ppermute(b2, LAT, SWAP_B)
     from_a2 = lax.ppermute(a2, LAT, SWAP_A)
-    lon2_b = lax.ppermute(lon2, LON, SWAP_B)
-    lon2_a = lax.ppermute(lon2, LON, SWAP_A)
     dots = lax.all_to_all(dots, ("x", "y", "c"), 0, 0)
     lat = (from_a, from_a2, from_b, from_b2)
     u_new, v_new = velocity(False, (from_a2, from_b2), (u_half, v_half))

time: 58.2 us -> 59.4 us (1.021)
  starting transfers between devices: 31.3 us -> 35.1 us
  waiting for transfers between devices: 6.25 us -> 3.43 us
    ppermute x1, waiting for transfers between devices: 3.49 us -> 0.01 us  [local(): got_b = lax.ppermute(side_b, LAT, SWAP_B)]
    ppermute x1, starting transfers between devices: 3.22 us -> 5.3 us  [local(): from_b2 = lax.ppermute(b2, LAT, SWAP_B)]
    ppermute x1, starting transfers between devices: 1.33 us -> 3.41 us  [local(): lon2_a = lax.ppermute(lon2, LON, SWAP_A)]
    all_to_all x1, starting transfers between devices: 6.88 us -> 5.16 us  [local(): dots = lax.all_to_all(dots, ('x', 'y', 'c'), 0, 0)]
    all_to_all x1, starting transfers between devices: 3.31 us -> 4.45 us  [local(): dots = lax.all_to_all(dots, ('zl', 'zh'), 0, 0)]
    all_to_all x1, waiting for transfers between devices: 1.01 us -> 1.9 us  [local(): dots = lax.all_to_all(dots, ('x', 'y', 'c'), 0, 0)]
  transfers between devices with their start and end apart: 12 -> 12, of which waited for: 5 -> 3; matrix products, arithmetic and copies ran while one was open for 0% -> 0% of each run, Pallas kernels for 22% -> 22%
where the time goes in v8:
time: 59.4 us; the launch traced here: 59.1 us
  starting transfers between devices  35.1 us (59%)
  Pallas kernels  18.4 us (31%)
  waiting for transfers between devices  3.43 us (6%)
  local copies, waits for them, and re-layouts  1.35 us (2%)
  between operations  0.83 us (1%)
    ppermute x1, starting transfers between devices, local(): from_b = lax.ppermute(b, LAT, SWAP_B)  6.65 us
    ppermute x1, starting transfers between devices, local(): from_b2 = lax.ppermute(b2, LAT, SWAP_B)  5.3 us
    all_to_all x1, starting transfers between devices, local(): dots = lax.all_to_all(dots, ('x', 'y', 'c'), 0, 0)  5.16 us
    all_to_all x1, starting transfers between devices, local(): dots = lax.all_to_all(dots, ('zl', 'zh'), 0, 0)  4.45 us
    pallas_call x2, Pallas kernels, velocity(): call(functools.partial(velocity_kernel, early), [flat] * 2, [VM] * 9 + [H...  4.06 us
    ppermute x1, starting transfers between devices, local(): from_a = lax.ppermute(a, LAT, SWAP_A)  3.91 us
    ppermute x1, starting transfers between devices, local(): lon2_a = lax.ppermute(lon2, LON, SWAP_A)  3.41 us
    pallas_call x1, Pallas kernels, local(): call(tracer_kernel, [flat], [VM] * 14, 60 * NZ * NR * NC, 5 * block, [fie...  3.02 us
  transfers between devices with their start and end apart: 12, of which 3 were waited for; matrix products, arithmetic and copies ran while one was open for 0% of the time, Pallas kernels for 22%

profile of v8, /device:TPU:1, one launch (start us, length us, event | category | flops | bytes accessed | tf_op | source)
XLA Modules:
  0.0 59.1 jit_solution(2190854396740329019)
XLA Ops:
  0.6 0.0 copy-start.5
  0.6 0.0 copy-start
  0.7 0.0 copy-start.1
  0.7 0.0 copy-start.2
  0.7 0.0 copy-start.3
  0.7 2.7 %shard_map.121 = (f32[4,16,128]{2,1,0:T(8,128)S(1)}, f32[4,32,128]{2,1,0:T(8,128)S(1)}, f32[4,32,128]{2,1,0:T(8,128)S(1)}, f32[16,8,128]{2,1,0:T(8,128)S(1)}) custom-call(f32[1024,128]{1,0:T(8,128)} %bitcast.8, f32[1024,128]{1,0:T(8,128)} %bitcast.15, f32[1024,128]{1,0:T(8,128)} %bitcast.29, s32[1024,128]{1,0:T(8,128)} %bitcast.22), custom_call_target="tpu_custom_call" | custom-call | flops 2621440 | bytes 2097152 | tf_op jit(solution)/shard_map/pallas_call | solution.py:643
  3.4 3.9 %collective-permute-start.2 = (f32[4,32,128]{2,1,0:T(8,128)S(1)}, f32[4,32,128]{2,1,0:T(8,128)S(1)}, u32[]{:S(2)}, u32[]{:S(2)}) collective-permute-start(f32[4,32,128]{2,1,0:T(8,128)S(1)} %get-tuple-element.54), channel_id=1, source_target_pairs={{0,1},{1,0},{2,3},{3,2},{4,5},{5,4},{6,7},{7,6},{8,9},{9,8},{10,11... | collective-permute-start | bytes 196616 | tf_op jit(solution)/shard_map/ppermute | solution.py:653
  7.3 6.7 %collective-permute-start.3 = (f32[4,32,128]{2,1,0:T(8,128)S(1)}, f32[4,32,128]{2,1,0:T(8,128)S(1)}, u32[]{:S(2)}, u32[]{:S(2)}) collective-permute-start(f32[4,32,128]{2,1,0:T(8,128)S(1)} %get-tuple-element.55), channel_id=1, source_target_pairs={{0,15},{1,2},{2,1},{3,4},{4,3},{5,6},{6,5},{7,8},{8,7},{9,10},{10,... | collective-permute-start | bytes 196616 | tf_op jit(solution)/shard_map/ppermute | solution.py:652
  14.0 0.0 copy-done.5
  14.0 0.0 copy-done
  14.0 0.0 copy-done.1
  14.0 0.0 copy-done.2
  14.0 0.6 %copy-done.8 = f32[64]{0:T(128)S(1)} copy-done((f32[64]{0:T(128)S(1)}, f32[64]{0:T(128)}, u32[]{:S(2)}) %copy-start.8) | copy-done | bytes 280
  14.6 0.7 %copy-done.6 = f32[16,128]{1,0:T(8,128)S(1)} copy-done((f32[16,128]{1,0:T(8,128)S(1)}, f32[16,128]{1,0:T(8,128)}, u32[]{:S(2)}) %copy-start.6) | copy-done | bytes 8216
  15.3 2.4 %shard_map.122 = (f32[2,16,128]{2,1,0:T(8,128)S(1)}, f32[112,128]{1,0:T(8,128)S(1)}, f32[112,128]{1,0:T(8,128)S(1)}, f32[72,128]{1,0:T(8,128)S(1)}) custom-call(f32[64]{0:T(128)S(1)} %copy-done.8, f32[1024,128]{1,0:T(8,128)S(1)} %bitcast.9, f32[1024,128]{1,0:T(8,128)S(1)} %bitcast.16, f32[1024,128]{1,0:T(8,128)S(1)} %bitcast.30, s32[1024,128]{1,0:T(8,128)S(1)} %bitcast.23, ...), custom_call_target="tpu_custom_call" | custom-call | flops 5242880 | bytes 2097152 | tf_op jit(solution)/shard_map/pallas_call | solution.py:654
  17.7 1.3 %collective-permute-start = (f32[112,128]{1,0:T(8,128)S(1)}, f32[112,128]{1,0:T(8,128)S(1)}, u32[]{:S(2)}, u32[]{:S(2)}) collective-permute-start(f32[112,128]{1,0:T(8,128)S(1)} %get-tuple-element.48), channel_id=1, source_target_pairs={{0,16},{16,0},{32,48},{48,32},{64,80},{80,64},{96,112},{112,96},{1... | collective-permute-start | bytes 172040 | tf_op jit(solution)/shard_map/ppermute | solution.py:662
  19.0 1.2 %collective-permute-start.1 = (f32[112,128]{1,0:T(8,128)S(1)}, f32[112,128]{1,0:T(8,128)S(1)}, u32[]{:S(2)}, u32[]{:S(2)}) collective-permute-start(f32[112,128]{1,0:T(8,128)S(1)} %get-tuple-element.49), channel_id=1, source_target_pairs={{0,240},{16,32},{32,16},{48,64},{64,48},{80,96},{96,80},{112,128},... | collective-permute-start | bytes 172040 | tf_op jit(solution)/shard_map/ppermute | solution.py:661
  20.2 2.2 %shard_map.123 = (f32[2,16,128]{2,1,0:T(8,128)S(1)}, f32[8,32,128]{2,1,0:T(8,128)}, f32[8,32,128]{2,1,0:T(8,128)S(1)}) custom-call(f32[1024,128]{1,0:T(8,128)S(1)} %bitcast.35, f32[1024,128]{1,0:T(8,128)S(1)} %bitcast.10, f32[1024,128]{1,0:T(8,128)S(1)} %bitcast.17, f32[1024,128]{1,0:T(8,128)S(1)} %bitcast.31, s32[1024,128]{1,0:T(8,128)S(1)} %bitcast.24), custom_call_target="tpu_custom_call" | custom-call | flops 2621440 | bytes 1048576 | tf_op jit(solution)/shard_map/pallas_call | solution.py:663
  22.4 0.0 collective-permute-done.msg_a
  22.4 0.2 collective-permute-done.1.msg_b
  22.6 0.0 collective-permute-done.2.from_a
  22.6 0.0 collective-permute-done.3.from_b
  22.6 0.3 shard_map.124
  22.9 0.0 copy-start.7
  22.9 0.1 collective-permute-start.4
  23.0 0.9 %collective-permute-start.5 = (f32[96,128]{1,0:T(8,128)S(1)}, f32[96,128]{1,0:T(8,128)S(1)}, u32[]{:S(2)}, u32[]{:S(2)}) collective-permute-start(f32[96,128]{1,0:T(8,128)S(1)} %get-tuple-element.61), channel_id=1, source_target_pairs={{0,15},{1,2},{2,1},{3,4},{4,3},{5,6},{6,5},{7,8},{8,7},{9,10},{10,... | collective-permute-start | bytes 147464 | tf_op jit(solution)/shard_map/ppermute | solution.py:677
  23.9 2.0 %collective-permute-start.7 = (f32[2,16,128]{2,1,0:T(8,128)S(1)}, f32[2,16,128]{2,1,0:T(8,128)S(1)}, u32[]{:S(2)}, u32[]{:S(2)}) collective-permute-start(f32[2,16,128]{2,1,0:T(8,128)S(1)} %get-tuple-element.64.lon2), channel_id=1, source_target_pairs={{0,240},{16,32},{32,16},{48,64},{64,48},{80,96},{96,80},{112,128},... | collective-permute-start | bytes 49160 | tf_op jit(solution)/shard_map/ppermute | solution.py:666
  26.0 3.4 %collective-permute-start.6 = (f32[2,16,128]{2,1,0:T(8,128)S(1)}, f32[2,16,128]{2,1,0:T(8,128)S(1)}, u32[]{:S(2)}, u32[]{:S(2)}) collective-permute-start(f32[2,16,128]{2,1,0:T(8,128)S(1)} %get-tuple-element.64.lon2), channel_id=1, source_target_pairs={{0,16},{16,0},{32,48},{48,32},{64,80},{80,64},{96,112},{112,96},{1... | collective-permute-start | bytes 49160 | tf_op jit(solution)/shard_map/ppermute | solution.py:667
  29.4 0.0 copy-done.7
  29.4 0.6 %shard_map.120.pc = f32[32,256]{1,0:T(8,128)S(1)} custom-call(f32[5,5]{1,0:T(8,128)S(1)} %copy-done.7), custom_call_target="tpu_custom_call" | custom-call | flops 10000 | bytes 10000 | tf_op jit(solution)/shard_map/pallas_call | solution.py:679
  30.0 2.0 %shard_map.125 = (f32[1024,128]{1,0:T(8,128)}, f32[1024,128]{1,0:T(8,128)}) custom-call(f32[1024,128]{1,0:T(8,128)S(1)} %bitcast.12, f32[1024,128]{1,0:T(8,128)S(1)} %bitcast.19, f32[1024,128]{1,0:T(8,128)S(1)} %bitcast.33, s32[1024,128]{1,0:T(8,128)S(1)} %bitcast.26, f32[4,16,128]{2,1,0:T(8,128)S(1)} %get-tuple-element.44.lon, ...), custom_call_target="tpu_custom_call" | custom-call | flops 3932160 | bytes 1572864 | tf_op jit(solution)/shard_map/pallas_call | solution.py:681
  32.0 0.0 collective-permute-done.7.lon2_b
  32.0 0.0 collective-permute-done.6.lon2_a
  32.0 0.0 collective-permute-done.4.from_a
  32.1 0.0 collective-permute-done.5.from_b
  32.1 1.7 %shard_map.126 = (f32[3,16,128]{2,1,0:T(8,128)S(1)}, f32[32,8,128]{2,1,0:T(8,128)}) custom-call(f32[32,256]{1,0:T(8,128)S(1)} %shard_map.120.pc, f32[72,128]{1,0:T(8,128)S(1)} %get-tuple-element.46.th, f32[128,128]{1,0:T(8,128)S(1)} %get-tuple-element.56.corner, f32[16,256]{1,0:T(8,128)S(1)} %get-tuple-element.57.rest, f32[16,256]{1,0:T(8,128)S(1)} %get-tuple-element.58.dg, ...), custom_call_target="tpu_custom_call" | custom-call | flops 1000000 | bytes 100000 | tf_op jit(solution)/shard_map/pallas_call | solution.py:697
  33.8 5.2 %all-to-all-start = ((f32[32,8,128]{2,1,0:T(8,128)}), f32[32,8,128]{2,1,0:T(8,128)S(1)}, u32[]{:S(2)}, u32[]{:S(2)}) async-start(f32[32,8,128]{2,1,0:T(8,128)} %get-tuple-element.70), calls=%async_computation | async-start | bytes 262144 | tf_op jit(solution)/shard_map/all_to_all | solution.py:709
  39.0 0.7 %collective-permute-start.8 = (f32[8,32,128]{2,1,0:T(8,128)}, f32[8,32,128]{2,1,0:T(8,128)S(1)}, u32[]{:S(2)}, u32[]{:S(2)}) collective-permute-start(f32[8,32,128]{2,1,0:T(8,128)} %get-tuple-element.73), channel_id=1, source_target_pairs={{0,1},{1,0},{2,3},{3,2},{4,5},{5,4},{6,7},{7,6},{8,9},{9,8},{10,11... | collective-permute-start | bytes 393224 | tf_op jit(solution)/shard_map/ppermute | solution.py:708
  39.7 5.3 %collective-permute-start.9 = (f32[8,32,128]{2,1,0:T(8,128)S(1)}, f32[8,32,128]{2,1,0:T(8,128)S(1)}, u32[]{:S(2)}, u32[]{:S(2)}) collective-permute-start(f32[8,32,128]{2,1,0:T(8,128)S(1)} %get-tuple-element.74), channel_id=1, source_target_pairs={{0,15},{1,2},{2,1},{3,4},{4,3},{5,6},{6,5},{7,8},{8,7},{9,10},{10,... | collective-permute-start | bytes 393224 | tf_op jit(solution)/shard_map/ppermute | solution.py:707
  45.0 1.9 %all-to-all-done.got = f32[32,8,128]{2,1,0:T(8,128)S(1)} async-done(((f32[32,8,128]{2,1,0:T(8,128)}), f32[32,8,128]{2,1,0:T(8,128)S(1)}, u32[]{:S(2)}, u32[]{:S(2)}) %all-to-all-start) | async-done | bytes 131104 | tf_op jit(solution)/shard_map/all_to_all | solution.py:709
  46.9 0.6 %shard_map.127 = f32[8,1,128]{2,1,0:T(1,128)} custom-call(f32[32,8,128]{2,1,0:T(8,128)S(1)} %all-to-all-done.got), custom_call_target="tpu_custom_call" | custom-call | flops 10000 | bytes 10000 | tf_op jit(solution)/shard_map/pallas_call | solution.py:721
  47.5 4.4 %all-to-all-start.1 = ((f32[8,1,128]{2,1,0:T(1,128)}), f32[8,1,128]{2,1,0:T(1,128)S(1)}, u32[]{:S(2)}, u32[]{:S(2)}) async-start(f32[8,1,128]{2,1,0:T(1,128)} %shard_map.127), calls=%async_computation.1 | async-start | bytes 8192 | tf_op jit(solution)/shard_map/all_to_all | solution.py:722
  51.9 0.0 collective-permute-done.8.from_a2.from_a
  52.0 0.0 collective-permute-done.9.from_b2.from_b
  52.0 2.0 %shard_map.129 = (f32[1024,128]{1,0:T(8,128)}, f32[1024,128]{1,0:T(8,128)}) custom-call(f32[1024,128]{1,0:T(8,128)S(1)} %bitcast.13, f32[1024,128]{1,0:T(8,128)S(1)} %bitcast.20, f32[1024,128]{1,0:T(8,128)S(1)} %bitcast.34, s32[1024,128]{1,0:T(8,128)S(1)} %bitcast.27, ...), custom_call_target="tpu_custom_call", output_to_operand_aliasing={{0}: (9, {}), {1}: (10, {})} | custom-call | flops 3932160 | bytes 1572864 | tf_op jit(solution)/shard_map/pallas_call | solution.py:681
  54.0 3.0 %shard_map.128 = f32[1024,128]{1,0:T(8,128)} custom-call(f32[1024,128]{1,0:T(8,128)S(1)} %bitcast.36, f32[1024,128]{1,0:T(8,128)S(1)} %bitcast.14, f32[1024,128]{1,0:T(8,128)S(1)} %bitcast.21, s32[1024,128]{1,0:T(8,128)S(1)} %bitcast.28, f32[4,16,128]{2,1,0:T(8,128)S(1)} %get-tuple-element.44.lon, f32[112,128]{1,0:T(8,128)S(1)} %collective-permute-done.msg_a, ...), custom_call_target="tpu_custom_call" | custom-call | flops 7864320 | bytes 2621440 | tf_op jit(solution)/shard_map/pallas_call | solution.py:712
  57.0 1.3 %all-to-all-done.1.got = f32[8,1,128]{2,1,0:T(1,128)S(1)} async-done(((f32[8,1,128]{2,1,0:T(1,128)}), f32[8,1,128]{2,1,0:T(1,128)S(1)}, u32[]{:S(2)}, u32[]{:S(2)}) %all-to-all-start.1) | async-done | bytes 4128 | tf_op jit(solution)/shard_map/all_to_all | solution.py:722
  58.4 0.7 %shard_map.130 = f32[16,128]{1,0:T(8,128)} custom-call(f32[8,1,128]{2,1,0:T(1,128)S(1)} %all-to-all-done.1.got, f32[3,16,128]{2,1,0:T(8,128)S(1)} %get-tuple-element.83.v, f32[16,128]{1,0:T(8,128)S(1)} %copy-done.5), custom_call_target="tpu_custom_call" | custom-call | flops 100000 | bytes 10000 | tf_op jit(solution)/shard_map/pallas_call | solution.py:724
  (5 shorter events, 0.0 us)
Async XLA Ops:
  0.6 13.3 %copy-start.5 = (f32[16,128]{1,0:T(8,128)S(1)}, f32[16,128]{1,0:T(8,128)}, u32[]{:S(2)}) copy-start(f32[16,128]{1,0:T(8,128)} %sf.3) | copy-start | bytes 24580
  0.6 13.3 %copy-start = (f32[64,16,128]{2,1,0:T(8,128)S(1)}, f32[64,16,128]{2,1,0:T(8,128)}, u32[]{:S(2)}) copy-start(f32[64,16,128]{2,1,0:T(8,128)} %param.10) | copy-start | bytes 1572868
  0.7 13.3 %copy-start.1 = (f32[64,16,128]{2,1,0:T(8,128)S(1)}, f32[64,16,128]{2,1,0:T(8,128)}, u32[]{:S(2)}) copy-start(f32[64,16,128]{2,1,0:T(8,128)} %param.11) | copy-start | bytes 1572868
  0.7 13.3 %copy-start.2 = (s32[64,16,128]{2,1,0:T(8,128)S(1)}, s32[64,16,128]{2,1,0:T(8,128)}, u32[]{:S(2)}) copy-start(s32[64,16,128]{2,1,0:T(8,128)} %param.13) | copy-start | bytes 1572868
  0.7 13.3 %copy-start.3 = (f32[64,16,128]{2,1,0:T(8,128)S(1)}, f32[64,16,128]{2,1,0:T(8,128)}, u32[]{:S(2)}) copy-start(f32[64,16,128]{2,1,0:T(8,128)} %param.12) | copy-start | bytes 1572868
  3.4 19.2 %collective-permute-start.2 = (f32[4,32,128]{2,1,0:T(8,128)S(1)}, f32[4,32,128]{2,1,0:T(8,128)S(1)}, u32[]{:S(2)}, u32[]{:S(2)}) collective-permute-start(f32[4,32,128]{2,1,0:T(8,128)S(1)} %get-tuple-element.54), channel_id=1, source_target_pairs={{0,1},{1,0},{2,3},{3,2},{4,5},{5,4},{6,7},{7,6},{8,9},{9,8},{10,11... | collective-permute-start | bytes 196616 | tf_op jit(solution)/shard_map/ppermute | solution.py:653
  7.3 15.3 %collective-permute-start.3 = (f32[4,32,128]{2,1,0:T(8,128)S(1)}, f32[4,32,128]{2,1,0:T(8,128)S(1)}, u32[]{:S(2)}, u32[]{:S(2)}) collective-permute-start(f32[4,32,128]{2,1,0:T(8,128)S(1)} %get-tuple-element.55), channel_id=1, source_target_pairs={{0,15},{1,2},{2,1},{3,4},{4,3},{5,6},{6,5},{7,8},{8,7},{9,10},{10,... | collective-permute-start | bytes 196616 | tf_op jit(solution)/shard_map/ppermute | solution.py:652
  14.0 0.7 %copy-start.8 = (f32[64]{0:T(128)S(1)}, f32[64]{0:T(128)}, u32[]{:S(2)}) copy-start(f32[64]{0:T(128)} %thick.1) | copy-start | bytes 772
  14.6 0.7 %copy-start.6 = (f32[16,128]{1,0:T(8,128)S(1)}, f32[16,128]{1,0:T(8,128)}, u32[]{:S(2)}) copy-start(f32[16,128]{1,0:T(8,128)} %dg_own.1) | copy-start | bytes 24580
  15.3 4.9 %copy-start.4 = (f32[64,16,128]{2,1,0:T(8,128)S(1)}, f32[64,16,128]{2,1,0:T(8,128)}, u32[]{:S(2)}) copy-start(f32[64,16,128]{2,1,0:T(8,128)} %param.9) | copy-start | bytes 1572868
  17.7 4.8 %collective-permute-start = (f32[112,128]{1,0:T(8,128)S(1)}, f32[112,128]{1,0:T(8,128)S(1)}, u32[]{:S(2)}, u32[]{:S(2)}) collective-permute-start(f32[112,128]{1,0:T(8,128)S(1)} %get-tuple-element.48), channel_id=1, source_target_pairs={{0,16},{16,0},{32,48},{48,32},{64,80},{80,64},{96,112},{112,96},{1... | collective-permute-start | bytes 172040 | tf_op jit(solution)/shard_map/ppermute | solution.py:662
  19.0 3.6 %collective-permute-start.1 = (f32[112,128]{1,0:T(8,128)S(1)}, f32[112,128]{1,0:T(8,128)S(1)}, u32[]{:S(2)}, u32[]{:S(2)}) collective-permute-start(f32[112,128]{1,0:T(8,128)S(1)} %get-tuple-element.49), channel_id=1, source_target_pairs={{0,240},{16,32},{32,16},{48,64},{64,48},{80,96},{96,80},{112,128},... | collective-permute-start | bytes 172040 | tf_op jit(solution)/shard_map/ppermute | solution.py:661
  22.9 6.5 %copy-start.7 = (f32[5,5]{1,0:T(8,128)S(1)}, f32[5,5]{1,0:T(8,128)}, u32[]{:S(2)}) copy-start(f32[5,5]{1,0:T(8,128)} %pc.1) | copy-start | bytes 304
  22.9 9.1 %collective-permute-start.4 = (f32[96,128]{1,0:T(8,128)S(1)}, f32[96,128]{1,0:T(8,128)S(1)}, u32[]{:S(2)}, u32[]{:S(2)}) collective-permute-start(f32[96,128]{1,0:T(8,128)S(1)} %get-tuple-element.60), channel_id=1, source_target_pairs={{0,1},{1,0},{2,3},{3,2},{4,5},{5,4},{6,7},{7,6},{8,9},{9,8},{10,11... | collective-permute-start | bytes 147464 | tf_op jit(solution)/shard_map/ppermute | solution.py:678
  23.0 9.0 %collective-permute-start.5 = (f32[96,128]{1,0:T(8,128)S(1)}, f32[96,128]{1,0:T(8,128)S(1)}, u32[]{:S(2)}, u32[]{:S(2)}) collective-permute-start(f32[96,128]{1,0:T(8,128)S(1)} %get-tuple-element.61), channel_id=1, source_target_pairs={{0,15},{1,2},{2,1},{3,4},{4,3},{5,6},{6,5},{7,8},{8,7},{9,10},{10,... | collective-permute-start | bytes 147464 | tf_op jit(solution)/shard_map/ppermute | solution.py:677
  23.9 8.1 %collective-permute-start.7 = (f32[2,16,128]{2,1,0:T(8,128)S(1)}, f32[2,16,128]{2,1,0:T(8,128)S(1)}, u32[]{:S(2)}, u32[]{:S(2)}) collective-permute-start(f32[2,16,128]{2,1,0:T(8,128)S(1)} %get-tuple-element.64.lon2), channel_id=1, source_target_pairs={{0,240},{16,32},{32,16},{48,64},{64,48},{80,96},{96,80},{112,128},... | collective-permute-start | bytes 49160 | tf_op jit(solution)/shard_map/ppermute | solution.py:666
  26.0 6.1 %collective-permute-start.6 = (f32[2,16,128]{2,1,0:T(8,128)S(1)}, f32[2,16,128]{2,1,0:T(8,128)S(1)}, u32[]{:S(2)}, u32[]{:S(2)}) collective-permute-start(f32[2,16,128]{2,1,0:T(8,128)S(1)} %get-tuple-element.64.lon2), channel_id=1, source_target_pairs={{0,16},{16,0},{32,48},{48,32},{64,80},{80,64},{96,112},{112,96},{1... | collective-permute-start | bytes 49160 | tf_op jit(solution)/shard_map/ppermute | solution.py:667
  33.8 13.1 %all-to-all-start = ((f32[32,8,128]{2,1,0:T(8,128)}), f32[32,8,128]{2,1,0:T(8,128)S(1)}, u32[]{:S(2)}, u32[]{:S(2)}) async-start(f32[32,8,128]{2,1,0:T(8,128)} %get-tuple-element.70), calls=%async_computation | async-start | bytes 262144 | tf_op jit(solution)/shard_map/all_to_all | solution.py:709
  39.0 13.0 %collective-permute-start.8 = (f32[8,32,128]{2,1,0:T(8,128)}, f32[8,32,128]{2,1,0:T(8,128)S(1)}, u32[]{:S(2)}, u32[]{:S(2)}) collective-permute-start(f32[8,32,128]{2,1,0:T(8,128)} %get-tuple-element.73), channel_id=1, source_target_pairs={{0,1},{1,0},{2,3},{3,2},{4,5},{5,4},{6,7},{7,6},{8,9},{9,8},{10,11... | collective-permute-start | bytes 393224 | tf_op jit(solution)/shard_map/ppermute | solution.py:708
  39.7 12.3 %collective-permute-start.9 = (f32[8,32,128]{2,1,0:T(8,128)S(1)}, f32[8,32,128]{2,1,0:T(8,128)S(1)}, u32[]{:S(2)}, u32[]{:S(2)}) collective-permute-start(f32[8,32,128]{2,1,0:T(8,128)S(1)} %get-tuple-element.74), channel_id=1, source_target_pairs={{0,15},{1,2},{2,1},{3,4},{4,3},{5,6},{6,5},{7,8},{8,7},{9,10},{10,... | collective-permute-start | bytes 393224 | tf_op jit(solution)/shard_map/ppermute | solution.py:707
  47.5 10.9 %all-to-all-start.1 = ((f32[8,1,128]{2,1,0:T(1,128)}), f32[8,1,128]{2,1,0:T(1,128)S(1)}, u32[]{:S(2)}, u32[]{:S(2)}) async-start(f32[8,1,128]{2,1,0:T(1,128)} %shard_map.127), calls=%async_computation.1 | async-start | bytes 8192 | tf_op jit(solution)/shard_map/all_to_all | solution.py:722

commit v9 on v7

--- a/solution.py
+++ b/solution.py
@@ -193,7 +193,7 @@
         )
 
     zero = jnp.zeros((NR, NC), jnp.float32)
-    acc = lax.fori_loop(0, NZ, body, (zero,) * 6 + (zero[:1],), unroll=4)
+    acc = lax.fori_loop(0, NZ, body, (zero,) * 6 + (zero[:1],), unroll=16)
     th_out[NZ:, :] = jnp.broadcast_to(acc[6], (8, NC))
     for i in range(2):
         east = jnp.where(lane == NC - 1, 0.0, acc[3 * i + 1])

time: 58.2 us -> 57.2 us (0.983)
  waiting for transfers between devices: 6.25 us -> 5.36 us
  Pallas kernels: 18.3 us -> 17.5 us
  starting transfers between devices: 31.3 us -> 31.9 us
    all_to_all x1, waiting for transfers between devices: 1.01 us -> 0.13 us  [local(): dots = lax.all_to_all(dots, ('x', 'y', 'c'), 0, 0)]
    pallas_call x1, Pallas kernels: 2.38 us -> 1.58 us  [local(): call(inner_kernel, [(2, NR, NC), (MSG, NC), (MSG, NC), (NZ + 8, NC)], [SM...]
    ppermute x1, starting transfers between devices: 3.22 us -> 3.94 us  [local(): from_b2 = lax.ppermute(b2, LAT, SWAP_B)]
  transfers between devices with their start and end apart: 12 -> 12, of which waited for: 5 -> 5; matrix products, arithmetic and copies ran while one was open for 0% -> 0% of each run, Pallas kernels for 22% -> 21%
where the time goes in v9:
time: 57.2 us; the launch traced here: 56.9 us
  starting transfers between devices  31.9 us (56%)
  Pallas kernels  17.5 us (31%)
  waiting for transfers between devices  5.36 us (9%)
  local copies, waits for them, and re-layouts  1.35 us (2%)
  between operations  0.82 us (1%)
    all_to_all x1, starting transfers between devices, local(): dots = lax.all_to_all(dots, ('x', 'y', 'c'), 0, 0)  6.88 us
    ppermute x1, starting transfers between devices, local(): from_b = lax.ppermute(b, LAT, SWAP_B)  6.65 us
    pallas_call x2, Pallas kernels, velocity(): call(functools.partial(velocity_kernel, early), [flat] * 2, [VM] * 9 + [H...  4.06 us
    ppermute x1, starting transfers between devices, local(): from_b2 = lax.ppermute(b2, LAT, SWAP_B)  3.94 us
    ppermute x1, starting transfers between devices, local(): from_a = lax.ppermute(a, LAT, SWAP_A)  3.91 us
    ppermute x1, waiting for transfers between devices, local(): got_b = lax.ppermute(side_b, LAT, SWAP_B)  3.49 us
    all_to_all x1, starting transfers between devices, local(): dots = lax.all_to_all(dots, ('zl', 'zh'), 0, 0)  3.31 us
    pallas_call x1, Pallas kernels, local(): call(tracer_kernel, [flat], [VM] * 14, 60 * NZ * NR * NC, 5 * block, [fie...  3.02 us
  transfers between devices with their start and end apart: 12, of which 5 were waited for; matrix products, arithmetic and copies ran while one was open for 0% of the time, Pallas kernels for 21%

profile of v9, /device:TPU:1, one launch (start us, length us, event | category | flops | bytes accessed | tf_op | source)
XLA Modules:
  0.0 56.9 jit_solution(18030191282329911227)
XLA Ops:
  0.6 0.0 copy-start.5
  0.6 0.0 copy-start
  0.7 0.0 copy-start.1
  0.7 0.0 copy-start.2
  0.7 0.0 copy-start.3
  0.7 2.7 %shard_map.121 = (f32[4,16,128]{2,1,0:T(8,128)S(1)}, f32[4,32,128]{2,1,0:T(8,128)S(1)}, f32[4,32,128]{2,1,0:T(8,128)S(1)}, f32[4,32,128]{2,1,0:T(8,128)S(1)}, f3...) custom-call(f32[1024,128]{1,0:T(8,128)} %bitcast.14, f32[1024,128]{1,0:T(8,128)} %bitcast.19, f32[1024,128]{1,0:T(8,128)} %bitcast.24, ...), custom_call_target="tpu_custom_call" | custom-call | flops 2621440 | bytes 2097152 | tf_op jit(solution)/shard_map/pallas_call | solution.py:641
  3.4 3.9 %collective-permute-start.2 = (f32[4,32,128]{2,1,0:T(8,128)S(1)}, f32[4,32,128]{2,1,0:T(8,128)S(1)}, u32[]{:S(2)}, u32[]{:S(2)}) collective-permute-start(f32[4,32,128]{2,1,0:T(8,128)S(1)} %get-tuple-element.59), channel_id=1, source_target_pairs={{0,1},{1,0},{2,3},{3,2},{4,5},{5,4},{6,7},{7,6},{8,9},{9,8},{10,11... | collective-permute-start | bytes 196616 | tf_op jit(solution)/shard_map/ppermute | solution.py:651
  7.3 6.7 %collective-permute-start.3 = (f32[4,32,128]{2,1,0:T(8,128)S(1)}, f32[4,32,128]{2,1,0:T(8,128)S(1)}, u32[]{:S(2)}, u32[]{:S(2)}) collective-permute-start(f32[4,32,128]{2,1,0:T(8,128)S(1)} %get-tuple-element.60), channel_id=1, source_target_pairs={{0,15},{1,2},{2,1},{3,4},{4,3},{5,6},{6,5},{7,8},{8,7},{9,10},{10,... | collective-permute-start | bytes 196616 | tf_op jit(solution)/shard_map/ppermute | solution.py:650
  13.9 0.0 copy-done.5
  14.0 0.0 copy-done
  14.0 0.0 copy-done.1
  14.0 0.0 copy-done.2
  14.0 0.0 copy-done.3
  14.0 0.6 %copy-done.8 = f32[64]{0:T(128)S(1)} copy-done((f32[64]{0:T(128)S(1)}, f32[64]{0:T(128)}, u32[]{:S(2)}) %copy-start.8) | copy-done | bytes 280
  14.6 0.7 %copy-done.6 = f32[16,128]{1,0:T(8,128)S(1)} copy-done((f32[16,128]{1,0:T(8,128)S(1)}, f32[16,128]{1,0:T(8,128)}, u32[]{:S(2)}) %copy-start.6) | copy-done | bytes 8216
  15.3 1.6 %shard_map.122 = (f32[2,16,128]{2,1,0:T(8,128)S(1)}, f32[112,128]{1,0:T(8,128)S(1)}, f32[112,128]{1,0:T(8,128)S(1)}, f32[72,128]{1,0:T(8,128)S(1)}) custom-call(f32[64]{0:T(128)S(1)} %copy-done.8, f32[1024,128]{1,0:T(8,128)S(1)} %bitcast.15, f32[1024,128]{1,0:T(8,128)S(1)} %bitcast.20, f32[1024,128]{1,0:T(8,128)S(1)} %bitcast.25, s32[1024,128]{1,0:T(8,128)S(1)} %bitcast.9, ...), custom_call_target="tpu_custom_call" | custom-call | flops 5242880 | bytes 2097152 | tf_op jit(solution)/shard_map/pallas_call | solution.py:652
  16.9 1.3 %collective-permute-start = (f32[112,128]{1,0:T(8,128)S(1)}, f32[112,128]{1,0:T(8,128)S(1)}, u32[]{:S(2)}, u32[]{:S(2)}) collective-permute-start(f32[112,128]{1,0:T(8,128)S(1)} %get-tuple-element.50), channel_id=1, source_target_pairs={{0,16},{16,0},{32,48},{48,32},{64,80},{80,64},{96,112},{112,96},{1... | collective-permute-start | bytes 172040 | tf_op jit(solution)/shard_map/ppermute | solution.py:660
  18.2 1.2 %collective-permute-start.1 = (f32[112,128]{1,0:T(8,128)S(1)}, f32[112,128]{1,0:T(8,128)S(1)}, u32[]{:S(2)}, u32[]{:S(2)}) collective-permute-start(f32[112,128]{1,0:T(8,128)S(1)} %get-tuple-element.51), channel_id=1, source_target_pairs={{0,240},{16,32},{32,16},{48,64},{64,48},{80,96},{96,80},{112,128},... | collective-permute-start | bytes 172040 | tf_op jit(solution)/shard_map/ppermute | solution.py:659
  19.4 0.0 copy-done.4
  19.4 2.2 %shard_map.123 = (f32[2,16,128]{2,1,0:T(8,128)S(1)}, f32[8,32,128]{2,1,0:T(8,128)}, f32[8,32,128]{2,1,0:T(8,128)S(1)}) custom-call(f32[1024,128]{1,0:T(8,128)S(1)} %bitcast.28, s32[1024,128]{1,0:T(8,128)S(1)} %bitcast.10, f32[4,32,128]{2,1,0:T(8,128)S(1)} %get-tuple-element.52.other_a.a2, f32[4,32,128]{2,1,0:T(8,128)S(1)} %get-tuple-element.53.other_b.b2), custom_call_target="tpu_custom_call" | custom-call | flops 2621440 | bytes 1048576 | tf_op jit(solution)/shard_map/pallas_call | solution.py:661
  21.6 0.0 collective-permute-done.msg_a
  21.6 0.2 collective-permute-done.1.msg_b
  21.8 0.0 collective-permute-done.2.from_a
  21.8 0.0 collective-permute-done.3.from_b
  21.8 0.3 shard_map.124
  22.1 0.1 collective-permute-start.4
  22.2 0.9 %collective-permute-start.5 = (f32[96,128]{1,0:T(8,128)S(1)}, f32[96,128]{1,0:T(8,128)S(1)}, u32[]{:S(2)}, u32[]{:S(2)}) collective-permute-start(f32[96,128]{1,0:T(8,128)S(1)} %get-tuple-element.66), channel_id=1, source_target_pairs={{0,15},{1,2},{2,1},{3,4},{4,3},{5,6},{6,5},{7,8},{8,7},{9,10},{10,... | collective-permute-start | bytes 147464 | tf_op jit(solution)/shard_map/ppermute | solution.py:673
  23.1 0.6 %shard_map.120.pc = f32[32,256]{1,0:T(8,128)S(1)} custom-call(f32[5,5]{1,0:T(8,128)S(1)} %copy-done.7), custom_call_target="tpu_custom_call" | custom-call | flops 10000 | bytes 10000 | tf_op jit(solution)/shard_map/pallas_call | solution.py:675
  23.7 2.0 %shard_map.125 = (f32[1024,128]{1,0:T(8,128)}, f32[1024,128]{1,0:T(8,128)}) custom-call(f32[1024,128]{1,0:T(8,128)S(1)} %bitcast.16, f32[1024,128]{1,0:T(8,128)S(1)} %bitcast.21, f32[1024,128]{1,0:T(8,128)S(1)} %bitcast.26, s32[1024,128]{1,0:T(8,128)S(1)} %bitcast.11, f32[4,16,128]{2,1,0:T(8,128)S(1)} %get-tuple-element.46.lon, ...), custom_call_target="tpu_custom_call" | custom-call | flops 3932160 | bytes 1572864 | tf_op jit(solution)/shard_map/pallas_call | solution.py:677
  25.8 0.3 collective-permute-done.4.from_a
  26.0 3.5 %collective-permute-done.5.from_b = f32[96,128]{1,0:T(8,128)S(1)} collective-permute-done((f32[96,128]{1,0:T(8,128)S(1)}, f32[96,128]{1,0:T(8,128)S(1)}, u32[]{:S(2)}, u32[]{:S(2)}) %collective-permute-start.5) | collective-permute-done | bytes 49184 | tf_op jit(solution)/shard_map/ppermute | solution.py:673
  29.5 1.7 %shard_map.126 = (f32[3,16,128]{2,1,0:T(8,128)S(1)}, f32[32,8,128]{2,1,0:T(8,128)}) custom-call(f32[32,256]{1,0:T(8,128)S(1)} %shard_map.120.pc, f32[72,128]{1,0:T(8,128)S(1)} %get-tuple-element.48.th, f32[128,128]{1,0:T(8,128)S(1)} %get-tuple-element.61.corner, f32[16,256]{1,0:T(8,128)S(1)} %get-tuple-element.62.rest, f32[16,256]{1,0:T(8,128)S(1)} %get-tuple-element.63.dg, ...), custom_call_target="tpu_custom_call" | custom-call | flops 1000000 | bytes 100000 | tf_op jit(solution)/shard_map/pallas_call | solution.py:691
  31.2 6.9 %all-to-all-start = ((f32[32,8,128]{2,1,0:T(8,128)}), f32[32,8,128]{2,1,0:T(8,128)S(1)}, u32[]{:S(2)}, u32[]{:S(2)}) async-start(f32[32,8,128]{2,1,0:T(8,128)} %get-tuple-element.75), calls=%async_computation | async-start | bytes 262144 | tf_op jit(solution)/shard_map/all_to_all | solution.py:705
  38.1 0.5 collective-permute-start.8
  38.6 3.9 %collective-permute-start.9 = (f32[8,32,128]{2,1,0:T(8,128)S(1)}, f32[8,32,128]{2,1,0:T(8,128)S(1)}, u32[]{:S(2)}, u32[]{:S(2)}) collective-permute-start(f32[8,32,128]{2,1,0:T(8,128)S(1)} %get-tuple-element.78), channel_id=1, source_target_pairs={{0,15},{1,2},{2,1},{3,4},{4,3},{5,6},{6,5},{7,8},{8,7},{9,10},{10,... | collective-permute-start | bytes 393224 | tf_op jit(solution)/shard_map/ppermute | solution.py:701
  42.5 1.7 %collective-permute-start.7 = (f32[2,16,128]{2,1,0:T(8,128)S(1)}, f32[2,16,128]{2,1,0:T(8,128)S(1)}, u32[]{:S(2)}, u32[]{:S(2)}) collective-permute-start(f32[2,16,128]{2,1,0:T(8,128)S(1)} %get-tuple-element.76.lon2), channel_id=1, source_target_pairs={{0,240},{16,32},{32,16},{48,64},{64,48},{80,96},{96,80},{112,128},... | collective-permute-start | bytes 49160 | tf_op jit(solution)/shard_map/ppermute | solution.py:703
  44.2 1.6 %collective-permute-start.6 = (f32[2,16,128]{2,1,0:T(8,128)S(1)}, f32[2,16,128]{2,1,0:T(8,128)S(1)}, u32[]{:S(2)}, u32[]{:S(2)}) collective-permute-start(f32[2,16,128]{2,1,0:T(8,128)S(1)} %get-tuple-element.76.lon2), channel_id=1, source_target_pairs={{0,16},{16,0},{32,48},{48,32},{64,80},{80,64},{96,112},{112,96},{1... | collective-permute-start | bytes 49160 | tf_op jit(solution)/shard_map/ppermute | solution.py:704
  45.8 0.1 all-to-all-done.got
  45.9 0.6 %shard_map.127 = f32[8,1,128]{2,1,0:T(1,128)} custom-call(f32[32,8,128]{2,1,0:T(8,128)S(1)} %all-to-all-done.got), custom_call_target="tpu_custom_call" | custom-call | flops 10000 | bytes 10000 | tf_op jit(solution)/shard_map/pallas_call | solution.py:717
  46.6 3.3 %all-to-all-start.1 = ((f32[8,1,128]{2,1,0:T(1,128)}), f32[8,1,128]{2,1,0:T(1,128)S(1)}, u32[]{:S(2)}, u32[]{:S(2)}) async-start(f32[8,1,128]{2,1,0:T(1,128)} %shard_map.127), calls=%async_computation.1 | async-start | bytes 8192 | tf_op jit(solution)/shard_map/all_to_all | solution.py:718
  49.9 0.0 collective-permute-done.8.from_a2.from_a
  49.9 0.0 collective-permute-done.9.from_b2.from_b
  49.9 2.0 %shard_map.129 = (f32[1024,128]{1,0:T(8,128)}, f32[1024,128]{1,0:T(8,128)}) custom-call(f32[1024,128]{1,0:T(8,128)S(1)} %bitcast.17, f32[1024,128]{1,0:T(8,128)S(1)} %bitcast.22, f32[1024,128]{1,0:T(8,128)S(1)} %bitcast.27, s32[1024,128]{1,0:T(8,128)S(1)} %bitcast.12, ...), custom_call_target="tpu_custom_call", output_to_operand_aliasing={{0}: (9, {}), {1}: (10, {})} | custom-call | flops 3932160 | bytes 1572864 | tf_op jit(solution)/shard_map/pallas_call | solution.py:677
  51.9 0.0 collective-permute-done.7.lon2_b
  52.0 0.0 collective-permute-done.6.lon2_a
  52.0 3.0 %shard_map.128 = f32[1024,128]{1,0:T(8,128)} custom-call(f32[1024,128]{1,0:T(8,128)S(1)} %bitcast.29, f32[1024,128]{1,0:T(8,128)S(1)} %bitcast.18, f32[1024,128]{1,0:T(8,128)S(1)} %bitcast.23, s32[1024,128]{1,0:T(8,128)S(1)} %bitcast.13, f32[4,16,128]{2,1,0:T(8,128)S(1)} %get-tuple-element.46.lon, f32[112,128]{1,0:T(8,128)S(1)} %collective-permute-done.msg_a, ...), custom_call_target="tpu_custom_call" | custom-call | flops 7864320 | bytes 2621440 | tf_op jit(solution)/shard_map/pallas_call | solution.py:708
  55.0 1.2 %all-to-all-done.1.got = f32[8,1,128]{2,1,0:T(1,128)S(1)} async-done(((f32[8,1,128]{2,1,0:T(1,128)}), f32[8,1,128]{2,1,0:T(1,128)S(1)}, u32[]{:S(2)}, u32[]{:S(2)}) %all-to-all-start.1) | async-done | bytes 4128 | tf_op jit(solution)/shard_map/all_to_all | solution.py:718
  56.2 0.7 %shard_map.130 = f32[16,128]{1,0:T(8,128)} custom-call(f32[8,1,128]{2,1,0:T(1,128)S(1)} %all-to-all-done.1.got, f32[3,16,128]{2,1,0:T(8,128)S(1)} %get-tuple-element.87.v, f32[16,128]{1,0:T(8,128)S(1)} %copy-done.5), custom_call_target="tpu_custom_call" | custom-call | flops 100000 | bytes 10000 | tf_op jit(solution)/shard_map/pallas_call | solution.py:720
  (5 shorter events, 0.0 us)
Async XLA Ops:
  0.6 13.3 %copy-start.5 = (f32[16,128]{1,0:T(8,128)S(1)}, f32[16,128]{1,0:T(8,128)}, u32[]{:S(2)}) copy-start(f32[16,128]{1,0:T(8,128)} %sf.3) | copy-start | bytes 24580
  0.6 13.3 %copy-start = (s32[64,16,128]{2,1,0:T(8,128)S(1)}, s32[64,16,128]{2,1,0:T(8,128)}, u32[]{:S(2)}) copy-start(s32[64,16,128]{2,1,0:T(8,128)} %param.13) | copy-start | bytes 1572868
  0.7 13.3 %copy-start.1 = (f32[64,16,128]{2,1,0:T(8,128)S(1)}, f32[64,16,128]{2,1,0:T(8,128)}, u32[]{:S(2)}) copy-start(f32[64,16,128]{2,1,0:T(8,128)} %param.10) | copy-start | bytes 1572868
  0.7 13.3 %copy-start.2 = (f32[64,16,128]{2,1,0:T(8,128)S(1)}, f32[64,16,128]{2,1,0:T(8,128)}, u32[]{:S(2)}) copy-start(f32[64,16,128]{2,1,0:T(8,128)} %param.11) | copy-start | bytes 1572868
  0.7 13.3 %copy-start.3 = (f32[64,16,128]{2,1,0:T(8,128)S(1)}, f32[64,16,128]{2,1,0:T(8,128)}, u32[]{:S(2)}) copy-start(f32[64,16,128]{2,1,0:T(8,128)} %param.12) | copy-start | bytes 1572868
  3.4 18.4 %collective-permute-start.2 = (f32[4,32,128]{2,1,0:T(8,128)S(1)}, f32[4,32,128]{2,1,0:T(8,128)S(1)}, u32[]{:S(2)}, u32[]{:S(2)}) collective-permute-start(f32[4,32,128]{2,1,0:T(8,128)S(1)} %get-tuple-element.59), channel_id=1, source_target_pairs={{0,1},{1,0},{2,3},{3,2},{4,5},{5,4},{6,7},{7,6},{8,9},{9,8},{10,11... | collective-permute-start | bytes 196616 | tf_op jit(solution)/shard_map/ppermute | solution.py:651
  7.3 14.5 %collective-permute-start.3 = (f32[4,32,128]{2,1,0:T(8,128)S(1)}, f32[4,32,128]{2,1,0:T(8,128)S(1)}, u32[]{:S(2)}, u32[]{:S(2)}) collective-permute-start(f32[4,32,128]{2,1,0:T(8,128)S(1)} %get-tuple-element.60), channel_id=1, source_target_pairs={{0,15},{1,2},{2,1},{3,4},{4,3},{5,6},{6,5},{7,8},{8,7},{9,10},{10,... | collective-permute-start | bytes 196616 | tf_op jit(solution)/shard_map/ppermute | solution.py:650
  13.9 0.7 %copy-start.8 = (f32[64]{0:T(128)S(1)}, f32[64]{0:T(128)}, u32[]{:S(2)}) copy-start(f32[64]{0:T(128)} %thick.1) | copy-start | bytes 772
  14.6 0.7 %copy-start.6 = (f32[16,128]{1,0:T(8,128)S(1)}, f32[16,128]{1,0:T(8,128)}, u32[]{:S(2)}) copy-start(f32[16,128]{1,0:T(8,128)} %dg_own.1) | copy-start | bytes 24580
  15.3 4.1 %copy-start.4 = (f32[64,16,128]{2,1,0:T(8,128)S(1)}, f32[64,16,128]{2,1,0:T(8,128)}, u32[]{:S(2)}) copy-start(f32[64,16,128]{2,1,0:T(8,128)} %param.9) | copy-start | bytes 1572868
  16.9 4.7 %collective-permute-start = (f32[112,128]{1,0:T(8,128)S(1)}, f32[112,128]{1,0:T(8,128)S(1)}, u32[]{:S(2)}, u32[]{:S(2)}) collective-permute-start(f32[112,128]{1,0:T(8,128)S(1)} %get-tuple-element.50), channel_id=1, source_target_pairs={{0,16},{16,0},{32,48},{48,32},{64,80},{80,64},{96,112},{112,96},{1... | collective-permute-start | bytes 172040 | tf_op jit(solution)/shard_map/ppermute | solution.py:660
  18.2 3.6 %collective-permute-start.1 = (f32[112,128]{1,0:T(8,128)S(1)}, f32[112,128]{1,0:T(8,128)S(1)}, u32[]{:S(2)}, u32[]{:S(2)}) collective-permute-start(f32[112,128]{1,0:T(8,128)S(1)} %get-tuple-element.51), channel_id=1, source_target_pairs={{0,240},{16,32},{32,16},{48,64},{64,48},{80,96},{96,80},{112,128},... | collective-permute-start | bytes 172040 | tf_op jit(solution)/shard_map/ppermute | solution.py:659
  21.8 1.3 %copy-start.7 = (f32[5,5]{1,0:T(8,128)S(1)}, f32[5,5]{1,0:T(8,128)}, u32[]{:S(2)}) copy-start(f32[5,5]{1,0:T(8,128)} %pc.1) | copy-start | bytes 304
  22.1 3.9 %collective-permute-start.4 = (f32[96,128]{1,0:T(8,128)S(1)}, f32[96,128]{1,0:T(8,128)S(1)}, u32[]{:S(2)}, u32[]{:S(2)}) collective-permute-start(f32[96,128]{1,0:T(8,128)S(1)} %get-tuple-element.65), channel_id=1, source_target_pairs={{0,1},{1,0},{2,3},{3,2},{4,5},{5,4},{6,7},{7,6},{8,9},{9,8},{10,11... | collective-permute-start | bytes 147464 | tf_op jit(solution)/shard_map/ppermute | solution.py:674
  22.2 7.3 %collective-permute-start.5 = (f32[96,128]{1,0:T(8,128)S(1)}, f32[96,128]{1,0:T(8,128)S(1)}, u32[]{:S(2)}, u32[]{:S(2)}) collective-permute-start(f32[96,128]{1,0:T(8,128)S(1)} %get-tuple-element.66), channel_id=1, source_target_pairs={{0,15},{1,2},{2,1},{3,4},{4,3},{5,6},{6,5},{7,8},{8,7},{9,10},{10,... | collective-permute-start | bytes 147464 | tf_op jit(solution)/shard_map/ppermute | solution.py:673
  31.2 14.7 %all-to-all-start = ((f32[32,8,128]{2,1,0:T(8,128)}), f32[32,8,128]{2,1,0:T(8,128)S(1)}, u32[]{:S(2)}, u32[]{:S(2)}) async-start(f32[32,8,128]{2,1,0:T(8,128)} %get-tuple-element.75), calls=%async_computation | async-start | bytes 262144 | tf_op jit(solution)/shard_map/all_to_all | solution.py:705
  38.1 11.8 %collective-permute-start.8 = (f32[8,32,128]{2,1,0:T(8,128)}, f32[8,32,128]{2,1,0:T(8,128)S(1)}, u32[]{:S(2)}, u32[]{:S(2)}) collective-permute-start(f32[8,32,128]{2,1,0:T(8,128)} %get-tuple-element.77), channel_id=1, source_target_pairs={{0,1},{1,0},{2,3},{3,2},{4,5},{5,4},{6,7},{7,6},{8,9},{9,8},{10,11... | collective-permute-start | bytes 393224 | tf_op jit(solution)/shard_map/ppermute | solution.py:702
  38.6 11.3 %collective-permute-start.9 = (f32[8,32,128]{2,1,0:T(8,128)S(1)}, f32[8,32,128]{2,1,0:T(8,128)S(1)}, u32[]{:S(2)}, u32[]{:S(2)}) collective-permute-start(f32[8,32,128]{2,1,0:T(8,128)S(1)} %get-tuple-element.78), channel_id=1, source_target_pairs={{0,15},{1,2},{2,1},{3,4},{4,3},{5,6},{6,5},{7,8},{8,7},{9,10},{10,... | collective-permute-start | bytes 393224 | tf_op jit(solution)/shard_map/ppermute | solution.py:701
  42.5 9.4 %collective-permute-start.7 = (f32[2,16,128]{2,1,0:T(8,128)S(1)}, f32[2,16,128]{2,1,0:T(8,128)S(1)}, u32[]{:S(2)}, u32[]{:S(2)}) collective-permute-start(f32[2,16,128]{2,1,0:T(8,128)S(1)} %get-tuple-element.76.lon2), channel_id=1, source_target_pairs={{0,240},{16,32},{32,16},{48,64},{64,48},{80,96},{96,80},{112,128},... | collective-permute-start | bytes 49160 | tf_op jit(solution)/shard_map/ppermute | solution.py:703
  44.2 7.7 %collective-permute-start.6 = (f32[2,16,128]{2,1,0:T(8,128)S(1)}, f32[2,16,128]{2,1,0:T(8,128)S(1)}, u32[]{:S(2)}, u32[]{:S(2)}) collective-permute-start(f32[2,16,128]{2,1,0:T(8,128)S(1)} %get-tuple-element.76.lon2), channel_id=1, source_target_pairs={{0,16},{16,0},{32,48},{48,32},{64,80},{80,64},{96,112},{112,96},{1... | collective-permute-start | bytes 49160 | tf_op jit(solution)/shard_map/ppermute | solution.py:704
  46.6 9.7 %all-to-all-start.1 = ((f32[8,1,128]{2,1,0:T(1,128)}), f32[8,1,128]{2,1,0:T(1,128)S(1)}, u32[]{:S(2)}, u32[]{:S(2)}) async-start(f32[8,1,128]{2,1,0:T(1,128)} %shard_map.127), calls=%async_computation.1 | async-start | bytes 8192 | tf_op jit(solution)/shard_map/all_to_all | solution.py:718

commit v10 on v9

--- a/solution.py
+++ b/solution.py
@@ -532,7 +532,7 @@
         return carry
 
     lax.fori_loop(0, count // per, chunk, 0)
-    lax.fori_loop(0, count // per, finish, 0)
+    return lambda: lax.fori_loop(0, count // per, finish, 0)
 
 
 def velocity_kernel(early, u, v, vi, w, lon, msg_a, msg_b, from_a, from_b, *rest):
@@ -569,7 +569,10 @@
         v_out[at, :] = wet * (vv + spread(k, face_e * (lon_up(vv) - vv), face_n * (lat_up(vv) - vv), 1))
         return carry
 
-    write_out(body, ((u_out, u_hbm), (v_out, v_hbm)), sems, 8, first, HALF)
+    finish = write_out(body, ((u_out, u_hbm), (v_out, v_hbm)), sems, 8, first, HALF)
+    if not early:
+        return finish
+    finish()
 
 
 def tracer_kernel(
@@ -626,7 +629,23 @@
         t_out[at, :] = wet * (tt - spread(k, flux_e, flux_n, 0))
         return carry
 
-    write_out(body, ((t_out, t_hbm),), sems, 8)
+    return write_out(body, ((t_out, t_hbm),), sems, 8)
+
+
+def last_kernel(
+    t, u, v, vi, w, lon, msg_a, msg_b, lon2, lon2_a, lon2_b, from_a, from_a2, from_b, from_b2, u_half, v_half,
+    u_hbm, v_hbm, t_hbm, u_out, v_out, packed, lines, sems, t_out, t_packed, t_lines, t_sems,
+):
+    finish_velocity = velocity_kernel(
+        False, u, v, vi, w, lon, msg_a, msg_b, from_a2, from_b2, u_half, v_half,
+        u_hbm, v_hbm, u_out, v_out, packed, lines, sems,
+    )
+    finish_tracer = tracer_kernel(
+        t, u, v, w, lon, msg_a, msg_b, lon2, lon2_a, lon2_b, from_a, from_a2, from_b, from_b2,
+        t_hbm, t_out, t_packed, t_lines, t_sems,
+    )
+    finish_velocity()
+    finish_tracer()
 
 
 def local(tracer, east_vel, north_vel, viscosity, land_sea, thickness, surface, surface_diag, precond_kernel):
@@ -703,17 +722,20 @@
     lon2_b = lax.ppermute(lon2, LON, SWAP_B)
     lon2_a = lax.ppermute(lon2, LON, SWAP_A)
     dots = lax.all_to_all(dots, ("x", "y", "c"), 0, 0)
-    lat = (from_a, from_a2, from_b, from_b2)
-    u_new, v_new = velocity(False, (from_a2, from_b2), (u_half, v_half))
-    t_new = call(
-        tracer_kernel,
-        [flat],
-        [VM] * 14,
-        60 * NZ * NR * NC,
-        5 * block,
-        [field, pltpu.VMEM((2, NR, NC), jnp.float32), pltpu.VMEM((4, NZ, NC), jnp.float32), dma((CHUNKS, 1))],
+    small = [pltpu.VMEM((2, NR, NC), jnp.float32), pltpu.VMEM((4, NZ, NC), jnp.float32)]
+    u_new, v_new, t_new = call(
+        last_kernel,
+        [flat] * 3,
+        [VM] * 15 + [HBM] * 2,
+        90 * NZ * NR * NC,
+        7 * block,
+        [field] * 2 + small + [dma((CHUNKS, 2)), field] + small + [dma((CHUNKS, 1))],
         HBM,
-    )(t, u, v, w, lon, msg_a, msg_b, lon2, lon2_a, lon2_b, *lat)[0]
+        aliases={15: 0, 16: 1},
+    )(
+        t, u, v, vi, w, lon, msg_a, msg_b, lon2, lon2_a, lon2_b,
+        from_a, from_a2, from_b, from_b2, u_half, v_half,
+    )
     (dots,) = call(relay_kernel, [(8, 1, NC)], [VM], 10**4, 10**4)(dots)
     dots = lax.all_to_all(dots, ("zl", "zh"), 0, 0)
     dots, t_new, u_new, v_new = lax.optimization_barrier((dots, t_new, u_new, v_new))

time: 57.2 us -> 57.2 us (level)
  Pallas kernels: 17.5 us -> 16.7 us
  waiting for transfers between devices: 5.36 us -> 6.1 us
    pallas_call x2 -> x1, Pallas kernels: 4.06 us -> 2.03 us  [velocity(): call(functools.partial(velocity_kernel, early), [flat] * 2, [VM] * 9 + [H...]
    pallas_call x1, Pallas kernels: 3.02 us -> 4.32 us  [local(): call(last_kernel, [flat] * 3, [VM] * 15 + [HBM] * 2, 90 * NZ * NR * NC, 7...]
    all_to_all x1, waiting for transfers between devices: 1.22 us -> 1.96 us  [local(): dots = lax.all_to_all(dots, ('zl', 'zh'), 0, 0)]
  transfers between devices with their start and end apart: 12 -> 12, of which waited for: 5 -> 5; matrix products, arithmetic and copies ran while one was open for 0% -> 0% of each run, Pallas kernels for 21% -> 20%
where the time goes in v10:
time: 57.2 us; the launch traced here: 56.9 us
  starting transfers between devices  31.9 us (56%)
  Pallas kernels  16.7 us (29%)
  waiting for transfers between devices  6.1 us (11%)
  local copies, waits for them, and re-layouts  1.35 us (2%)
  between operations  0.81 us (1%)
    all_to_all x1, starting transfers between devices, local(): dots = lax.all_to_all(dots, ('x', 'y', 'c'), 0, 0)  6.88 us
    ppermute x1, starting transfers between devices, local(): from_b = lax.ppermute(b, LAT, SWAP_B)  6.65 us
    pallas_call x1, Pallas kernels, local(): call(last_kernel, [flat] * 3, [VM] * 15 + [HBM] * 2, 90 * NZ * NR * NC, 7...  4.32 us
    ppermute x1, starting transfers between devices, local(): from_b2 = lax.ppermute(b2, LAT, SWAP_B)  3.94 us
    ppermute x1, starting transfers between devices, local(): from_a = lax.ppermute(a, LAT, SWAP_A)  3.91 us
    ppermute x1, waiting for transfers between devices, local(): got_b = lax.ppermute(side_b, LAT, SWAP_B)  3.49 us
    all_to_all x1, starting transfers between devices, local(): dots = lax.all_to_all(dots, ('zl', 'zh'), 0, 0)  3.31 us
    pallas_call x1, Pallas kernels, local(): call(fetch_kernel, [(4, NR, NC), rows, rows, rows, rows, (16, 8, NC)], [H...  2.7 us
  transfers between devices with their start and end apart: 12, of which 5 were waited for; matrix products, arithmetic and copies ran while one was open for 0% of the time, Pallas kernels for 20%

profile of v10, /device:TPU:1, one launch (start us, length us, event | category | flops | bytes accessed | tf_op | source)
XLA Modules:
  0.0 56.9 jit_solution(14503577855495237852)
XLA Ops:
  0.6 0.0 copy-start.5
  0.6 0.0 copy-start
  0.7 0.0 copy-start.1
  0.7 0.0 copy-start.2
  0.7 0.0 copy-start.3
  0.7 2.7 %shard_map.121 = (f32[4,16,128]{2,1,0:T(8,128)S(1)}, f32[4,32,128]{2,1,0:T(8,128)S(1)}, f32[4,32,128]{2,1,0:T(8,128)S(1)}, f32[4,32,128]{2,1,0:T(8,128)S(1)}, f3...) custom-call(f32[1024,128]{1,0:T(8,128)} %bitcast.13, f32[1024,128]{1,0:T(8,128)} %bitcast.17, f32[1024,128]{1,0:T(8,128)} %bitcast.21, ...), custom_call_target="tpu_custom_call" | custom-call | flops 2621440 | bytes 2097152 | tf_op jit(solution)/shard_map/pallas_call | solution.py:660
  3.4 3.9 %collective-permute-start.2 = (f32[4,32,128]{2,1,0:T(8,128)S(1)}, f32[4,32,128]{2,1,0:T(8,128)S(1)}, u32[]{:S(2)}, u32[]{:S(2)}) collective-permute-start(f32[4,32,128]{2,1,0:T(8,128)S(1)} %get-tuple-element.60), channel_id=1, source_target_pairs={{0,1},{1,0},{2,3},{3,2},{4,5},{5,4},{6,7},{7,6},{8,9},{9,8},{10,11... | collective-permute-start | bytes 196616 | tf_op jit(solution)/shard_map/ppermute | solution.py:670
  7.3 6.7 %collective-permute-start.3 = (f32[4,32,128]{2,1,0:T(8,128)S(1)}, f32[4,32,128]{2,1,0:T(8,128)S(1)}, u32[]{:S(2)}, u32[]{:S(2)}) collective-permute-start(f32[4,32,128]{2,1,0:T(8,128)S(1)} %get-tuple-element.61), channel_id=1, source_target_pairs={{0,15},{1,2},{2,1},{3,4},{4,3},{5,6},{6,5},{7,8},{8,7},{9,10},{10,... | collective-permute-start | bytes 196616 | tf_op jit(solution)/shard_map/ppermute | solution.py:669
  13.9 0.0 copy-done.5
  14.0 0.0 copy-done
  14.0 0.0 copy-done.1
  14.0 0.0 copy-done.2
  14.0 0.0 copy-done.3
  14.0 0.6 %copy-done.8 = f32[64]{0:T(128)S(1)} copy-done((f32[64]{0:T(128)S(1)}, f32[64]{0:T(128)}, u32[]{:S(2)}) %copy-start.8) | copy-done | bytes 280
  14.6 0.7 %copy-done.6 = f32[16,128]{1,0:T(8,128)S(1)} copy-done((f32[16,128]{1,0:T(8,128)S(1)}, f32[16,128]{1,0:T(8,128)}, u32[]{:S(2)}) %copy-start.6) | copy-done | bytes 8216
  15.3 1.6 %shard_map.122 = (f32[2,16,128]{2,1,0:T(8,128)S(1)}, f32[112,128]{1,0:T(8,128)S(1)}, f32[112,128]{1,0:T(8,128)S(1)}, f32[72,128]{1,0:T(8,128)S(1)}) custom-call(f32[64]{0:T(128)S(1)} %copy-done.8, f32[1024,128]{1,0:T(8,128)S(1)} %bitcast.14, f32[1024,128]{1,0:T(8,128)S(1)} %bitcast.18, f32[1024,128]{1,0:T(8,128)S(1)} %bitcast.22, s32[1024,128]{1,0:T(8,128)S(1)} %bitcast.9, ...), custom_call_target="tpu_custom_call" | custom-call | flops 5242880 | bytes 2097152 | tf_op jit(solution)/shard_map/pallas_call | solution.py:671
  16.9 1.3 %collective-permute-start = (f32[112,128]{1,0:T(8,128)S(1)}, f32[112,128]{1,0:T(8,128)S(1)}, u32[]{:S(2)}, u32[]{:S(2)}) collective-permute-start(f32[112,128]{1,0:T(8,128)S(1)} %get-tuple-element.51), channel_id=1, source_target_pairs={{0,16},{16,0},{32,48},{48,32},{64,80},{80,64},{96,112},{112,96},{1... | collective-permute-start | bytes 172040 | tf_op jit(solution)/shard_map/ppermute | solution.py:679
  18.2 1.2 %collective-permute-start.1 = (f32[112,128]{1,0:T(8,128)S(1)}, f32[112,128]{1,0:T(8,128)S(1)}, u32[]{:S(2)}, u32[]{:S(2)}) collective-permute-start(f32[112,128]{1,0:T(8,128)S(1)} %get-tuple-element.52), channel_id=1, source_target_pairs={{0,240},{16,32},{32,16},{48,64},{64,48},{80,96},{96,80},{112,128},... | collective-permute-start | bytes 172040 | tf_op jit(solution)/shard_map/ppermute | solution.py:678
  19.4 0.0 copy-done.4
  19.4 2.2 %shard_map.123 = (f32[2,16,128]{2,1,0:T(8,128)S(1)}, f32[8,32,128]{2,1,0:T(8,128)}, f32[8,32,128]{2,1,0:T(8,128)S(1)}) custom-call(f32[1024,128]{1,0:T(8,128)S(1)} %bitcast.25, s32[1024,128]{1,0:T(8,128)S(1)} %bitcast.10, f32[4,32,128]{2,1,0:T(8,128)S(1)} %get-tuple-element.53.other_a.a2, f32[4,32,128]{2,1,0:T(8,128)S(1)} %get-tuple-element.54.other_b.b2), custom_call_target="tpu_custom_call" | custom-call | flops 2621440 | bytes 1048576 | tf_op jit(solution)/shard_map/pallas_call | solution.py:680
  21.6 0.0 collective-permute-done.msg_a
  21.6 0.2 collective-permute-done.1.msg_b
  21.8 0.0 collective-permute-done.2.from_a
  21.8 0.0 collective-permute-done.3.from_b
  21.8 0.3 shard_map.124
  22.1 0.1 collective-permute-start.4
  22.2 0.9 %collective-permute-start.5 = (f32[96,128]{1,0:T(8,128)S(1)}, f32[96,128]{1,0:T(8,128)S(1)}, u32[]{:S(2)}, u32[]{:S(2)}) collective-permute-start(f32[96,128]{1,0:T(8,128)S(1)} %get-tuple-element.67), channel_id=1, source_target_pairs={{0,15},{1,2},{2,1},{3,4},{4,3},{5,6},{6,5},{7,8},{8,7},{9,10},{10,... | collective-permute-start | bytes 147464 | tf_op jit(solution)/shard_map/ppermute | solution.py:692
  23.1 0.0 copy-done.7
  23.1 0.6 %shard_map.120.pc = f32[32,256]{1,0:T(8,128)S(1)} custom-call(f32[5,5]{1,0:T(8,128)S(1)} %copy-done.7), custom_call_target="tpu_custom_call" | custom-call | flops 10000 | bytes 10000 | tf_op jit(solution)/shard_map/pallas_call | solution.py:694
  23.7 2.0 %shard_map.125 = (f32[1024,128]{1,0:T(8,128)}, f32[1024,128]{1,0:T(8,128)}) custom-call(f32[1024,128]{1,0:T(8,128)S(1)} %bitcast.15, f32[1024,128]{1,0:T(8,128)S(1)} %bitcast.19, f32[1024,128]{1,0:T(8,128)S(1)} %bitcast.23, s32[1024,128]{1,0:T(8,128)S(1)} %bitcast.11, f32[4,16,128]{2,1,0:T(8,128)S(1)} %get-tuple-element.47.lon, ...), custom_call_target="tpu_custom_call" | custom-call | flops 3932160 | bytes 1572864 | tf_op jit(solution)/shard_map/pallas_call | solution.py:696
  25.8 0.3 collective-permute-done.4.from_a
  26.0 3.5 %collective-permute-done.5.from_b = f32[96,128]{1,0:T(8,128)S(1)} collective-permute-done((f32[96,128]{1,0:T(8,128)S(1)}, f32[96,128]{1,0:T(8,128)S(1)}, u32[]{:S(2)}, u32[]{:S(2)}) %collective-permute-start.5) | collective-permute-done | bytes 49184 | tf_op jit(solution)/shard_map/ppermute | solution.py:692
  29.5 1.7 %shard_map.126 = (f32[3,16,128]{2,1,0:T(8,128)S(1)}, f32[32,8,128]{2,1,0:T(8,128)}) custom-call(f32[32,256]{1,0:T(8,128)S(1)} %shard_map.120.pc, f32[72,128]{1,0:T(8,128)S(1)} %get-tuple-element.49.th, f32[128,128]{1,0:T(8,128)S(1)} %get-tuple-element.62.corner, f32[16,256]{1,0:T(8,128)S(1)} %get-tuple-element.63.rest, f32[16,256]{1,0:T(8,128)S(1)} %get-tuple-element.64.dg, ...), custom_call_target="tpu_custom_call" | custom-call | flops 1000000 | bytes 100000 | tf_op jit(solution)/shard_map/pallas_call | solution.py:710
  31.2 6.9 %all-to-all-start = ((f32[32,8,128]{2,1,0:T(8,128)}), f32[32,8,128]{2,1,0:T(8,128)S(1)}, u32[]{:S(2)}, u32[]{:S(2)}) async-start(f32[32,8,128]{2,1,0:T(8,128)} %get-tuple-element.76), calls=%async_computation | async-start | bytes 262144 | tf_op jit(solution)/shard_map/all_to_all | solution.py:724
  38.1 0.5 collective-permute-start.8
  38.6 3.9 %collective-permute-start.9 = (f32[8,32,128]{2,1,0:T(8,128)S(1)}, f32[8,32,128]{2,1,0:T(8,128)S(1)}, u32[]{:S(2)}, u32[]{:S(2)}) collective-permute-start(f32[8,32,128]{2,1,0:T(8,128)S(1)} %get-tuple-element.79), channel_id=1, source_target_pairs={{0,15},{1,2},{2,1},{3,4},{4,3},{5,6},{6,5},{7,8},{8,7},{9,10},{10,... | collective-permute-start | bytes 393224 | tf_op jit(solution)/shard_map/ppermute | solution.py:720
  42.5 1.7 %collective-permute-start.7 = (f32[2,16,128]{2,1,0:T(8,128)S(1)}, f32[2,16,128]{2,1,0:T(8,128)S(1)}, u32[]{:S(2)}, u32[]{:S(2)}) collective-permute-start(f32[2,16,128]{2,1,0:T(8,128)S(1)} %get-tuple-element.77.lon2), channel_id=1, source_target_pairs={{0,240},{16,32},{32,16},{48,64},{64,48},{80,96},{96,80},{112,128},... | collective-permute-start | bytes 49160 | tf_op jit(solution)/shard_map/ppermute | solution.py:722
  44.2 1.6 %collective-permute-start.6 = (f32[2,16,128]{2,1,0:T(8,128)S(1)}, f32[2,16,128]{2,1,0:T(8,128)S(1)}, u32[]{:S(2)}, u32[]{:S(2)}) collective-permute-start(f32[2,16,128]{2,1,0:T(8,128)S(1)} %get-tuple-element.77.lon2), channel_id=1, source_target_pairs={{0,16},{16,0},{32,48},{48,32},{64,80},{80,64},{96,112},{112,96},{1... | collective-permute-start | bytes 49160 | tf_op jit(solution)/shard_map/ppermute | solution.py:723
  45.8 0.1 all-to-all-done.got
  45.9 0.6 %shard_map.127 = f32[8,1,128]{2,1,0:T(1,128)} custom-call(f32[32,8,128]{2,1,0:T(8,128)S(1)} %all-to-all-done.got), custom_call_target="tpu_custom_call" | custom-call | flops 10000 | bytes 10000 | tf_op jit(solution)/shard_map/pallas_call | solution.py:739
  46.6 3.3 %all-to-all-start.1 = ((f32[8,1,128]{2,1,0:T(1,128)}), f32[8,1,128]{2,1,0:T(1,128)S(1)}, u32[]{:S(2)}, u32[]{:S(2)}) async-start(f32[8,1,128]{2,1,0:T(1,128)} %shard_map.127), calls=%async_computation.1 | async-start | bytes 8192 | tf_op jit(solution)/shard_map/all_to_all | solution.py:740
  49.9 0.0 collective-permute-done.7.lon2_b
  49.9 0.0 collective-permute-done.6.lon2_a
  49.9 0.0 collective-permute-done.8.from_a2
  49.9 0.0 collective-permute-done.9.from_b2
  49.9 4.3 %shard_map.128 = (f32[1024,128]{1,0:T(8,128)}, f32[1024,128]{1,0:T(8,128)}, f32[1024,128]{1,0:T(8,128)}) custom-call(f32[1024,128]{1,0:T(8,128)S(1)} %bitcast.26, f32[1024,128]{1,0:T(8,128)S(1)} %bitcast.16, f32[1024,128]{1,0:T(8,128)S(1)} %bitcast.20, f32[1024,128]{1,0:T(8,128)S(1)} %bitcast.24, ...), custom_call_target="tpu_custom_call", output_to_operand_aliasing={{0}: (15, {}), {1}: (16, {})} | custom-call | flops 11796480 | bytes 3670016 | tf_op jit(solution)/shard_map/pallas_call | solution.py:726
  54.3 2.0 %all-to-all-done.1.got = f32[8,1,128]{2,1,0:T(1,128)S(1)} async-done(((f32[8,1,128]{2,1,0:T(1,128)}), f32[8,1,128]{2,1,0:T(1,128)S(1)}, u32[]{:S(2)}, u32[]{:S(2)}) %all-to-all-start.1) | async-done | bytes 4128 | tf_op jit(solution)/shard_map/all_to_all | solution.py:740
  56.2 0.7 %shard_map.129 = f32[16,128]{1,0:T(8,128)} custom-call(f32[8,1,128]{2,1,0:T(1,128)S(1)} %all-to-all-done.1.got, f32[3,16,128]{2,1,0:T(8,128)S(1)} %get-tuple-element.89.v, f32[16,128]{1,0:T(8,128)S(1)} %copy-done.5), custom_call_target="tpu_custom_call" | custom-call | flops 100000 | bytes 10000 | tf_op jit(solution)/shard_map/pallas_call | solution.py:742
  (4 shorter events, 0.0 us)
Async XLA Ops:
  0.6 13.3 %copy-start.5 = (f32[16,128]{1,0:T(8,128)S(1)}, f32[16,128]{1,0:T(8,128)}, u32[]{:S(2)}) copy-start(f32[16,128]{1,0:T(8,128)} %sf.3) | copy-start | bytes 24580
  0.6 13.3 %copy-start = (s32[64,16,128]{2,1,0:T(8,128)S(1)}, s32[64,16,128]{2,1,0:T(8,128)}, u32[]{:S(2)}) copy-start(s32[64,16,128]{2,1,0:T(8,128)} %param.13) | copy-start | bytes 1572868
  0.7 13.3 %copy-start.1 = (f32[64,16,128]{2,1,0:T(8,128)S(1)}, f32[64,16,128]{2,1,0:T(8,128)}, u32[]{:S(2)}) copy-start(f32[64,16,128]{2,1,0:T(8,128)} %param.10) | copy-start | bytes 1572868
  0.7 13.3 %copy-start.2 = (f32[64,16,128]{2,1,0:T(8,128)S(1)}, f32[64,16,128]{2,1,0:T(8,128)}, u32[]{:S(2)}) copy-start(f32[64,16,128]{2,1,0:T(8,128)} %param.11) | copy-start | bytes 1572868
  0.7 13.3 %copy-start.3 = (f32[64,16,128]{2,1,0:T(8,128)S(1)}, f32[64,16,128]{2,1,0:T(8,128)}, u32[]{:S(2)}) copy-start(f32[64,16,128]{2,1,0:T(8,128)} %param.12) | copy-start | bytes 1572868
  3.4 18.4 %collective-permute-start.2 = (f32[4,32,128]{2,1,0:T(8,128)S(1)}, f32[4,32,128]{2,1,0:T(8,128)S(1)}, u32[]{:S(2)}, u32[]{:S(2)}) collective-permute-start(f32[4,32,128]{2,1,0:T(8,128)S(1)} %get-tuple-element.60), channel_id=1, source_target_pairs={{0,1},{1,0},{2,3},{3,2},{4,5},{5,4},{6,7},{7,6},{8,9},{9,8},{10,11... | collective-permute-start | bytes 196616 | tf_op jit(solution)/shard_map/ppermute | solution.py:670
  7.3 14.5 %collective-permute-start.3 = (f32[4,32,128]{2,1,0:T(8,128)S(1)}, f32[4,32,128]{2,1,0:T(8,128)S(1)}, u32[]{:S(2)}, u32[]{:S(2)}) collective-permute-start(f32[4,32,128]{2,1,0:T(8,128)S(1)} %get-tuple-element.61), channel_id=1, source_target_pairs={{0,15},{1,2},{2,1},{3,4},{4,3},{5,6},{6,5},{7,8},{8,7},{9,10},{10,... | collective-permute-start | bytes 196616 | tf_op jit(solution)/shard_map/ppermute | solution.py:669
  13.9 0.7 %copy-start.8 = (f32[64]{0:T(128)S(1)}, f32[64]{0:T(128)}, u32[]{:S(2)}) copy-start(f32[64]{0:T(128)} %thick.1) | copy-start | bytes 772
  14.6 0.7 %copy-start.6 = (f32[16,128]{1,0:T(8,128)S(1)}, f32[16,128]{1,0:T(8,128)}, u32[]{:S(2)}) copy-start(f32[16,128]{1,0:T(8,128)} %dg_own.1) | copy-start | bytes 24580
  15.3 4.1 %copy-start.4 = (f32[64,16,128]{2,1,0:T(8,128)S(1)}, f32[64,16,128]{2,1,0:T(8,128)}, u32[]{:S(2)}) copy-start(f32[64,16,128]{2,1,0:T(8,128)} %param.9) | copy-start | bytes 1572868
  16.9 4.7 %collective-permute-start = (f32[112,128]{1,0:T(8,128)S(1)}, f32[112,128]{1,0:T(8,128)S(1)}, u32[]{:S(2)}, u32[]{:S(2)}) collective-permute-start(f32[112,128]{1,0:T(8,128)S(1)} %get-tuple-element.51), channel_id=1, source_target_pairs={{0,16},{16,0},{32,48},{48,32},{64,80},{80,64},{96,112},{112,96},{1... | collective-permute-start | bytes 172040 | tf_op jit(solution)/shard_map/ppermute | solution.py:679
  18.2 3.6 %collective-permute-start.1 = (f32[112,128]{1,0:T(8,128)S(1)}, f32[112,128]{1,0:T(8,128)S(1)}, u32[]{:S(2)}, u32[]{:S(2)}) collective-permute-start(f32[112,128]{1,0:T(8,128)S(1)} %get-tuple-element.52), channel_id=1, source_target_pairs={{0,240},{16,32},{32,16},{48,64},{64,48},{80,96},{96,80},{112,128},... | collective-permute-start | bytes 172040 | tf_op jit(solution)/shard_map/ppermute | solution.py:678
  21.8 1.3 %copy-start.7 = (f32[5,5]{1,0:T(8,128)S(1)}, f32[5,5]{1,0:T(8,128)}, u32[]{:S(2)}) copy-start(f32[5,5]{1,0:T(8,128)} %pc.1) | copy-start | bytes 304
  22.1 3.9 %collective-permute-start.4 = (f32[96,128]{1,0:T(8,128)S(1)}, f32[96,128]{1,0:T(8,128)S(1)}, u32[]{:S(2)}, u32[]{:S(2)}) collective-permute-start(f32[96,128]{1,0:T(8,128)S(1)} %get-tuple-element.66), channel_id=1, source_target_pairs={{0,1},{1,0},{2,3},{3,2},{4,5},{5,4},{6,7},{7,6},{8,9},{9,8},{10,11... | collective-permute-start | bytes 147464 | tf_op jit(solution)/shard_map/ppermute | solution.py:693
  22.2 7.3 %collective-permute-start.5 = (f32[96,128]{1,0:T(8,128)S(1)}, f32[96,128]{1,0:T(8,128)S(1)}, u32[]{:S(2)}, u32[]{:S(2)}) collective-permute-start(f32[96,128]{1,0:T(8,128)S(1)} %get-tuple-element.67), channel_id=1, source_target_pairs={{0,15},{1,2},{2,1},{3,4},{4,3},{5,6},{6,5},{7,8},{8,7},{9,10},{10,... | collective-permute-start | bytes 147464 | tf_op jit(solution)/shard_map/ppermute | solution.py:692
  31.2 14.7 %all-to-all-start = ((f32[32,8,128]{2,1,0:T(8,128)}), f32[32,8,128]{2,1,0:T(8,128)S(1)}, u32[]{:S(2)}, u32[]{:S(2)}) async-start(f32[32,8,128]{2,1,0:T(8,128)} %get-tuple-element.76), calls=%async_computation | async-start | bytes 262144 | tf_op jit(solution)/shard_map/all_to_all | solution.py:724
  38.1 11.8 %collective-permute-start.8 = (f32[8,32,128]{2,1,0:T(8,128)}, f32[8,32,128]{2,1,0:T(8,128)S(1)}, u32[]{:S(2)}, u32[]{:S(2)}) collective-permute-start(f32[8,32,128]{2,1,0:T(8,128)} %get-tuple-element.78), channel_id=1, source_target_pairs={{0,1},{1,0},{2,3},{3,2},{4,5},{5,4},{6,7},{7,6},{8,9},{9,8},{10,11... | collective-permute-start | bytes 393224 | tf_op jit(solution)/shard_map/ppermute | solution.py:721
  38.6 11.3 %collective-permute-start.9 = (f32[8,32,128]{2,1,0:T(8,128)S(1)}, f32[8,32,128]{2,1,0:T(8,128)S(1)}, u32[]{:S(2)}, u32[]{:S(2)}) collective-permute-start(f32[8,32,128]{2,1,0:T(8,128)S(1)} %get-tuple-element.79), channel_id=1, source_target_pairs={{0,15},{1,2},{2,1},{3,4},{4,3},{5,6},{6,5},{7,8},{8,7},{9,10},{10,... | collective-permute-start | bytes 393224 | tf_op jit(solution)/shard_map/ppermute | solution.py:720
  42.5 7.4 %collective-permute-start.7 = (f32[2,16,128]{2,1,0:T(8,128)S(1)}, f32[2,16,128]{2,1,0:T(8,128)S(1)}, u32[]{:S(2)}, u32[]{:S(2)}) collective-permute-start(f32[2,16,128]{2,1,0:T(8,128)S(1)} %get-tuple-element.77.lon2), channel_id=1, source_target_pairs={{0,240},{16,32},{32,16},{48,64},{64,48},{80,96},{96,80},{112,128},... | collective-permute-start | bytes 49160 | tf_op jit(solution)/shard_map/ppermute | solution.py:722
  44.2 5.7 %collective-permute-start.6 = (f32[2,16,128]{2,1,0:T(8,128)S(1)}, f32[2,16,128]{2,1,0:T(8,128)S(1)}, u32[]{:S(2)}, u32[]{:S(2)}) collective-permute-start(f32[2,16,128]{2,1,0:T(8,128)S(1)} %get-tuple-element.77.lon2), channel_id=1, source_target_pairs={{0,16},{16,0},{32,48},{48,32},{64,80},{80,64},{96,112},{112,96},{1... | collective-permute-start | bytes 49160 | tf_op jit(solution)/shard_map/ppermute | solution.py:723
  46.6 9.7 %all-to-all-start.1 = ((f32[8,1,128]{2,1,0:T(1,128)}), f32[8,1,128]{2,1,0:T(1,128)S(1)}, u32[]{:S(2)}, u32[]{:S(2)}) async-start(f32[8,1,128]{2,1,0:T(1,128)} %shard_map.127), calls=%async_computation.1 | async-start | bytes 8192 | tf_op jit(solution)/shard_map/all_to_all | solution.py:740
